TPU v7x, 32 devices: a whole 2x2x4 slice. The times are simulated.
32 devices in a mesh: seq: 8 (over z, x), ch: 4 (over y, core).
Axes of the slice: x: 2, y: 2, z: 4, core: 2. Of those that a mesh axis runs over, the one named last changes fastest.
Arguments:
- features: bfloat16 [1024, 8192], P('seq', 'ch'), may hold values from -6 to 6
- qkv_weight: bfloat16 [1664, 3, 8192], P('seq', None, 'ch'), may hold values from -0.0625 to 0.0625
- grad_out: bfloat16 [1664, 1024], P('ch', 'seq'), may hold values from -6 to 6
- residues: float32 [1664, 16], P('ch'), may hold values from -1 to 1
- log_rates: float32 [1664, 16], P('ch'), may hold values from -10 to -1, as said below
- skip_gain: float32 [1664], P('ch'), may hold values from -1 to 1
Outputs:
- weight_grad: float32 [1664, 3, 8192], P('seq', None, 'ch')
- residue_grad: float32 [1664, 16], P('ch')
- rate_grad: float32 [1664, 16], P('ch')
- skip_grad: float32 [1664], P('ch')
Inputs may be any that keep to these rules, and one draw needn't show every extreme that they name: Each channel's decay rates exp(log_rates) lie between about 1 / 1024 and 3 / 20.
All inputs are finite; a program needn't handle non-finite values.
Results may differ from a plain program's by a relative error of at most 0.029.
Values may be sent and summed in bfloat16 or wider, within the bound.
No kernel may reach another device: no remote copies, remote signals or barrier semaphores. Data moves between devices by JAX's collectives and lax.ppermute only.
A program may use at most 64 MiB of HBM per device.

v0:
```python
import functools
import math

import jax
import jax.numpy as jnp
import ml_dtypes
import numpy as np
from jax import lax
from jax.experimental import pallas as pl
from jax.experimental.pallas import tpu as pltpu
from jax.sharding import PartitionSpec as P

F32 = jnp.float32
BF16 = jnp.bfloat16
VMEM_BYTES = 56 * 1024 * 1024


def round_up(value, multiple):
    return -(-value // multiple) * multiple


def wave_tables(tokens):
    odd = 2 * np.arange(tokens, dtype=np.int64) + 1
    angles = (odd[:, None] * odd[None, :] % (8 * tokens)) * (math.pi / (4 * tokens))
    twist = odd * (math.pi / (4 * tokens))
    return (
        np.cos(angles).astype(ml_dtypes.bfloat16),
        np.sin(angles).astype(ml_dtypes.bfloat16),
        np.stack([np.cos(twist), np.sin(twist)]).astype(np.float32),
    )


def dot(left, right):
    return jnp.dot(left, right, preferred_element_type=F32)


def two_parts(value):
    high = value.astype(BF16)
    low = (value - high.astype(F32)).astype(BF16)
    return jnp.concatenate([high, low], 0)


def wide_dot(value, table):
    rows = value.shape[0]
    both = dot(two_parts(value), table)
    return both[:rows] + both[rows:]


def taps_kernel(poles_ref, cos_ref, sin_ref, twist_ref, hc_ref, hs_ref, *, order):
    rows, tokens = hc_ref.shape
    steps = lax.broadcasted_iota(jnp.int32, (rows, tokens), 1).astype(F32)
    taps = jnp.zeros((rows, tokens), F32)
    for pole in range(order):
        residue = poles_ref[:, pole : pole + 1]
        rate = jnp.exp(poles_ref[:, order + pole : order + pole + 1])
        taps = taps + residue * jnp.exp(-rate * steps)
    even = wide_dot(taps, cos_ref[...])
    uneven = wide_dot(taps, sin_ref[...])
    cos_half = twist_ref[0:1, :]
    sin_half = twist_ref[1:2, :]
    hc_ref[...] = cos_half * even + sin_half * uneven
    hs_ref[...] = cos_half * uneven - sin_half * even


def project_kernel(starts_ref, weight_ref, *refs, pieces):
    feature_refs = refs[:pieces]
    out_refs = refs[pieces:-2]
    features_ref, sums_ref = refs[-2:]
    gates, _, _ = weight_ref.shape
    part = out_refs[0].shape[1]
    row = 0
    for feature_ref in feature_refs:
        features_ref[row : row + feature_ref.shape[0], :] = feature_ref[...]
        row += feature_ref.shape[0]
    for gate in range(gates):
        sums_ref[gate] = lax.dot_general(
            weight_ref[gate], features_ref[...], (((1,), (1,)), ((), ())),
            preferred_element_type=F32,
        )
    for step, out_ref in enumerate(out_refs):
        start = pl.multiple_of(starts_ref[step], 8)
        out_ref[...] = sums_ref[:, pl.ds(start, part), :].astype(out_ref.dtype)


def conv_kernel(slots_ref, *refs, order, group_slots, shares):
    partial_refs = refs[: len(group_slots) * shares]
    (
        gout_ref, poles_ref, hc_ref, hs_ref, cos_ref, sin_ref, twist_ref,
        grad_ref, tgc_ref, tgs_ref, skip_ref, proj_ref,
    ) = refs[len(group_slots) * shares :]
    rows, tokens = hc_ref.shape
    blocks, _, _, block_len = proj_ref.shape
    slot = 0
    for group, count in enumerate(group_slots):
        own_ref, *other_refs = partial_refs[group * shares : (group + 1) * shares]
        total = own_ref[...]
        for other_ref in other_refs:
            total = total + other_ref[...].astype(F32)
        total = total.astype(BF16).astype(F32)
        for place in range(count):
            proj_ref[slot] = total[:, :, place * block_len : (place + 1) * block_len]
            slot += 1

    def in_order(gate):
        return jnp.concatenate([proj_ref[slots_ref[b], gate] for b in range(blocks)], 1)

    queries = in_order(0)
    keys = in_order(1)
    values = in_order(2)
    upper = jnp.concatenate(
        [gout_ref[slots_ref[blocks + b]].astype(F32) for b in range(blocks)], 1
    )
    product = keys * values
    middle = upper * queries
    signals = jnp.concatenate([product, middle], 0)
    parts = two_parts(signals)
    even = dot(parts, cos_ref[...])
    uneven = dot(parts, sin_ref[...])
    even = even[: 2 * rows] + even[2 * rows :]
    uneven = uneven[: 2 * rows] + uneven[2 * rows :]
    ac, mc = even[:rows], even[rows:]
    as_, ms = uneven[:rows], uneven[rows:]
    hc = hc_ref[...]
    hs = hs_ref[...]
    scale = 1.0 / tokens
    cos_sums = jnp.concatenate([hc * ac - hs * as_, hc * mc + hs * ms], 0) * scale
    sin_sums = jnp.concatenate([hc * as_ + hs * ac, hc * ms - hs * mc], 0) * scale
    tc = (ac * mc + as_ * ms) * scale
    ts = (ac * ms - as_ * mc) * scale
    cos_half = twist_ref[0:1, :]
    sin_half = twist_ref[1:2, :]
    tgc_ref[...] = tc * cos_half - ts * sin_half
    tgs_ref[...] = ts * cos_half + tc * sin_half
    restored = wide_dot(cos_sums, cos_ref[...]) + wide_dot(sin_sums, sin_ref[...])
    skip = poles_ref[:, 2 * order : 2 * order + 1]
    mix = restored[rows:] + skip * middle
    grads = (upper * (restored[:rows] + skip * product), mix * values, mix * keys)
    for gate, grad in enumerate(grads):
        for b in range(blocks):
            place = pl.multiple_of(slots_ref[b] * block_len, block_len)
            grad_ref[gate, :, pl.ds(place, block_len)] = grad[
                :, b * block_len : (b + 1) * block_len
            ].astype(BF16)
    skip_ref[...] = jnp.sum(product * middle, axis=1, keepdims=True)


def pole_kernel(poles_ref, tgc_ref, tgs_ref, cos_ref, sin_ref, skip_ref, out_ref, *, order):
    rows, tokens = tgc_ref.shape
    taps_grad = wide_dot(tgc_ref[...], cos_ref[...]) + wide_dot(tgs_ref[...], sin_ref[...])
    steps = lax.broadcasted_iota(jnp.int32, (rows, tokens), 1).astype(F32)
    for pole in range(order):
        residue = poles_ref[:, pole : pole + 1]
        rate = jnp.exp(poles_ref[:, order + pole : order + pole + 1])
        decayed = taps_grad * jnp.exp(-rate * steps)
        out_ref[:, pole : pole + 1] = jnp.sum(decayed, axis=1, keepdims=True)
        moment = jnp.sum(decayed * steps, axis=1, keepdims=True)
        out_ref[:, order + pole : order + pole + 1] = -residue * rate * moment
    out_ref[:, 2 * order : 2 * order + 1] = skip_ref[...]


def weight_kernel(starts_ref, *refs, shares):
    grad_refs = refs[:shares]
    feature_ref, out_ref, wide_ref, rows_ref = refs[shares:]
    gates = out_ref.shape[0]
    part = grad_refs[0].shape[1]

    @pl.when(pl.program_id(0) == 0)
    def _():
        for share, grad_ref in enumerate(grad_refs):
            start = pl.multiple_of(starts_ref[share], 8)
            wide_ref[:, pl.ds(start, part), :] = grad_ref[...].astype(F32)
        rows_ref[...] = wide_ref[...].astype(BF16)

    for gate in range(gates):
        out_ref[gate] = dot(rows_ref[gate], feature_ref[...])


def call(kernel, outs, flops, transcendentals, *operands, scratch=(), indexed=False):
    size = sum(a.size * a.dtype.itemsize for a in operands) + sum(
        o.size * o.dtype.itemsize for o in outs
    )
    whole = pl.BlockSpec(memory_space=pltpu.VMEM)
    specs = [whole] * len(operands)
    if indexed:
        specs[0] = pl.BlockSpec(memory_space=pltpu.SMEM)
    return pl.pallas_call(
        kernel,
        out_shape=outs,
        in_specs=specs,
        out_specs=[whole] * len(outs),
        scratch_shapes=scratch,
        compiler_params=pltpu.CompilerParams(vmem_limit_bytes=VMEM_BYTES),
        cost_estimate=pl.CostEstimate(
            flops=flops, bytes_accessed=size, transcendentals=transcendentals
        ),
    )(*operands)


def picked(table, index):
    return jnp.asarray(np.asarray(table, np.int32))[index]


def ring_gather(features, ring):
    count = len(ring)
    half = features.shape[0] // 2
    ahead = [(ring[i], ring[(i + 1) % count]) for i in range(count)]
    behind = [(b, a) for a, b in ahead]
    own = (features[:half], features[half:])
    slots = [own]
    from_behind, from_ahead = own, own
    for _ in range(count // 2 - 1):
        from_behind = tuple(lax.ppermute(a, "seq", ahead) for a in from_behind)
        from_ahead = tuple(lax.ppermute(a, "seq", behind) for a in from_ahead)
        slots += [from_behind, from_ahead]
    slots.append(
        (lax.ppermute(from_behind[0], "seq", ahead), lax.ppermute(from_ahead[1], "seq", behind))
    )
    return slots


def local(features, qkv_weight, grad_out, residues, log_rates, skip_gain):
    n_seq = lax.axis_size("seq")
    n_ch = lax.axis_size("ch")
    seq_index = lax.axis_index("seq")
    ch_index = lax.axis_index("ch")
    rows, gates, width = qkv_weight.shape
    block_len = features.shape[0]
    tokens = n_seq * block_len
    order = residues.shape[1]
    part = round_up(-(-rows // n_ch), 8)
    starts = [min(h * part, rows - part) for h in range(n_ch)]
    per_ch = n_seq // n_ch
    cos_table, sin_table, twist = (jnp.asarray(a) for a in wave_tables(tokens))

    ring = list(range(0, n_seq, 2)) + list(range(n_seq - 1, 0, -2))
    offsets = [0] + [o for k in range(1, n_seq // 2) for o in (-k, k)] + [n_seq // 2]
    slot_of = np.zeros((n_seq, n_seq), np.int32)
    for place, index in enumerate(ring):
        for slot, offset in enumerate(offsets):
            slot_of[index, ring[(place + offset) % n_seq]] = slot
    slots = ring_gather(features, ring)

    piece_starts = [(j // n_ch) * rows + starts[j % n_ch] for j in range(n_seq)]
    spread = [((q % n_seq) * n_ch + q // n_seq, q) for q in range(n_seq * n_ch)]
    gather_back = [(b, a) for a, b in spread]

    packed = jnp.concatenate([residues, log_rates, skip_gain[:, None]], 1)
    poles = lax.dynamic_slice_in_dim(packed, picked(piece_starts, seq_index), part, 0)
    poles = lax.ppermute(poles, ("seq", "ch"), spread)

    upper = []
    for k in range(n_seq):
        route = [
            (((q % n_seq + k) % n_seq) * n_ch + q // n_seq, q) for q in range(n_seq * n_ch)
        ]
        begin = picked([piece_starts[(s - k) % n_seq] for s in range(n_seq)], seq_index)
        sent = lax.dynamic_slice_in_dim(grad_out, begin, part, 0)
        upper.append(lax.ppermute(sent, ("seq", "ch"), route))
    upper = jnp.stack(upper)
    own_piece = (seq_index * n_ch + ch_index) % n_seq
    upper_slots = (jnp.arange(n_seq, dtype=jnp.int32) - own_piece) % n_seq
    conv_slots = jnp.concatenate([picked(slot_of, seq_index), upper_slots.astype(jnp.int32)])

    square = part * tokens * tokens
    spectrum = jax.ShapeDtypeStruct((part, tokens), F32)
    hc, hs = call(
        functools.partial(taps_kernel, order=order), (spectrum, spectrum),
        8 * square, part * tokens * order, poles, cos_table, sin_table, twist,
    )

    weight = qkv_weight.transpose(1, 0, 2)
    ahead_starts = picked(
        [[starts[(h + d) % n_ch] for d in range(n_ch)] for h in range(n_ch)], ch_index
    )
    behind_starts = picked(
        [[starts[(h - d) % n_ch] for d in range(n_ch)] for h in range(n_ch)], ch_index
    )
    groups = [slots[:3]] + [slots[i : i + 2] for i in range(3, n_seq, 2)]
    group_slots = [len(group) for group in groups]
    partials = []
    for group in groups:
        pieces = [piece for slot in group for piece in slot]
        span = len(group) * block_len
        sums = call(
            functools.partial(project_kernel, pieces=len(pieces)),
            [
                jax.ShapeDtypeStruct((gates, part, span), F32 if d == 0 else BF16)
                for d in range(n_ch)
            ],
            2 * gates * rows * width * span, 0, ahead_starts, weight, *pieces,
            scratch=[pltpu.VMEM((span, width), BF16), pltpu.VMEM((gates, rows, span), F32)],
            indexed=True,
        )
        partials.append(sums[0])
        for d in range(1, n_ch):
            partials.append(
                lax.ppermute(sums[d], "ch", [(h, (h + d) % n_ch) for h in range(n_ch)])
            )

    grads, tgc, tgs, skip_sum = call(
        functools.partial(conv_kernel, order=order, group_slots=group_slots, shares=n_ch),
        (
            jax.ShapeDtypeStruct((gates, part, tokens), BF16),
            spectrum,
            spectrum,
            jax.ShapeDtypeStruct((part, 1), F32),
        ),
        32 * square, 0, conv_slots, *partials, upper, poles, hc, hs,
        cos_table, sin_table, twist,
        scratch=[pltpu.VMEM((n_seq, gates, part, block_len), F32)], indexed=True,
    )

    held = [grads] + [
        lax.ppermute(grads, "ch", [(h, (h + d) % n_ch) for h in range(n_ch)])
        for d in range(2, n_ch, 2)
    ]
    swap = [(h, h ^ 1) for h in range(n_ch)]
    held += [lax.ppermute(a, "ch", swap) for a in held]
    order_of = [
        [starts[((h ^ core) - d) % n_ch] for core in (0, 1) for d in range(0, n_ch, 2)]
        for h in range(n_ch)
    ]

    (pole_sums,) = call(
        functools.partial(pole_kernel, order=order),
        (jax.ShapeDtypeStruct((part, 2 * order + 1), F32),),
        8 * square, part * tokens * order, poles, tgc, tgs, cos_table, sin_table, skip_sum,
    )

    every_feature = jnp.concatenate([piece for slot in slots for piece in slot], 0)
    tile = min(512, width)
    weight_grad = pl.pallas_call(
        functools.partial(weight_kernel, shares=n_ch),
        out_shape=jax.ShapeDtypeStruct((gates, rows, width), F32),
        grid=(width // tile,),
        in_specs=[pl.BlockSpec(memory_space=pltpu.SMEM)]
        + [pl.BlockSpec((gates, part, tokens), lambda i: (0, 0, 0))] * n_ch
        + [pl.BlockSpec((tokens, tile), lambda i: (0, i))],
        out_specs=pl.BlockSpec((gates, rows, tile), lambda i: (0, 0, i)),
        scratch_shapes=[
            pltpu.VMEM((gates, rows, tokens), F32),
            pltpu.VMEM((gates, rows, tokens), BF16),
        ],
        compiler_params=pltpu.CompilerParams(vmem_limit_bytes=VMEM_BYTES),
        cost_estimate=pl.CostEstimate(
            flops=2 * gates * rows * width * tokens,
            bytes_accessed=4 * gates * rows * width + 2 * tokens * (width + gates * rows),
            transcendentals=0,
        ),
    )(picked(order_of, ch_index), *held, every_feature)
    weight_grad = weight_grad.transpose(1, 0, 2)

    returned = lax.ppermute(pole_sums, ("seq", "ch"), gather_back)[None]
    reach = 1
    while reach < n_seq:
        other = lax.ppermute(returned, "seq", [(s, s ^ reach) for s in range(n_seq)])
        returned = jnp.concatenate([returned, other], 0)
        reach *= 2
    returned = returned[jnp.arange(n_seq) ^ seq_index]
    pieces = []
    for block in range(per_ch):
        filled = 0
        for h, begin in enumerate(starts):
            if begin + part > filled:
                pieces.append(returned[block * n_ch + h, filled - begin :])
                filled = begin + part
    sums = jnp.concatenate(pieces, 0)
    return (weight_grad, sums[:, :order], sums[:, order : 2 * order], sums[:, 2 * order])


def solution(mesh):
    placed = (
        P("seq", "ch"),
        P("seq", None, "ch"),
        P("ch", "seq"),
        P("ch", None),
        P("ch", None),
        P("ch"),
    )
    return jax.shard_map(
        local,
        mesh=mesh,
        in_specs=placed,
        out_specs=(P("seq", None, "ch"), P("ch", None), P("ch", None), P("ch")),
        check_vma=False,
    )
```

profile of v0, /device:TPU:4, one launch (start us, length us, event | category | flops | bytes accessed | tf_op | source)
XLA Modules:
  0.0 211.1 jit_solution(3743851796973554199)
XLA Ops:
  9.9 4.4 %collective-permute-start.34 = (f32[56,33]{1,0:T(8,128)S(1)}, f32[56,33]{1,0:T(8,128)S(1)}, u32[]{:S(2)}, u32[]{:S(2)}) collective-permute-start(f32[56,33]{1,0:T(8,128)S(1)} %copy.43), channel_id=1, source_target_pairs={{0,0},{4,1},{8,2},{12,3},{16,4},{20,5},{24,6},{28,7},{1,8},{5,9},{... | collective-permute-start | bytes 22184 | tf_op jit(solution)/shard_map/ppermute | solution.py:249
  43.1 3.2 %collective-permute-start.26 = (bf16[56,128]{1,0:T(8,128)(2,1)S(1)}, bf16[56,128]{1,0:T(8,128)(2,1)S(1)}, u32[]{:S(2)}, u32[]{:S(2)}) collective-permute-start(bf16[56,128]{1,0:T(8,128)(2,1)S(1)} %get-tuple-element.72), channel_id=1, source_target_pairs={{0,0},{4,1},{8,2},{12,3},{16,4},{20,5},{24,6},{28,7},{1,8},{5,9},{... | collective-permute-start | bytes 43016 | tf_op jit(solution)/shard_map/ppermute | solution.py:258
  46.3 4.5 %shard_map.232 = (f32[56,1024]{1,0:T(8,128)}, f32[56,1024]{1,0:T(8,128)}) custom-call(f32[56,33]{1,0:T(8,128)} %copy-done.24, bf16[1024,1024]{1,0:T(8,128)(2,1)} %constant.65.clone.cos_ref.refs_20_, bf16[1024,1024]{1,0:T(8,128)(2,1)} %constant.66.clone.sin_ref.refs_21_, f32[2,1024]{1,0:T(2,128)} %constant.67.clone.twist_ref.refs_22_), custom_call_target="tpu_custom_call" | custom-call | flops 469762048 | bytes 4668640 | tf_op jit(solution)/shard_map/pallas_call | solution.py:186
  50.8 2.2 %collective-permute-start.27 = (bf16[56,128]{1,0:T(8,128)(2,1)S(1)}, bf16[56,128]{1,0:T(8,128)(2,1)S(1)}, u32[]{:S(2)}, u32[]{:S(2)}) collective-permute-start(bf16[56,128]{1,0:T(8,128)(2,1)S(1)} %get-tuple-element.71), channel_id=1, source_target_pairs={{4,0},{8,1},{12,2},{16,3},{20,4},{24,5},{28,6},{0,7},{5,8},{9,9},{... | collective-permute-start | bytes 43016 | tf_op jit(solution)/shard_map/ppermute | solution.py:258
  53.0 5.2 %collective-permute-done.27 = bf16[56,128]{1,0:T(8,128)(2,1)S(1)} collective-permute-done((bf16[56,128]{1,0:T(8,128)(2,1)S(1)}, bf16[56,128]{1,0:T(8,128)(2,1)S(1)}, u32[]{:S(2)}, u32[]{:S(2)}) %collective-permute-start.27) | collective-permute-done | bytes 14368 | tf_op jit(solution)/shard_map/ppermute | solution.py:258
  60.2 5.5 %collective-permute-done.28 = bf16[56,128]{1,0:T(8,128)(2,1)S(1)} collective-permute-done((bf16[56,128]{1,0:T(8,128)(2,1)S(1)}, bf16[56,128]{1,0:T(8,128)(2,1)S(1)}, u32[]{:S(2)}, u32[]{:S(2)}) %collective-permute-start.28) | collective-permute-done | bytes 14368 | tf_op jit(solution)/shard_map/ppermute | solution.py:258
  67.5 6.4 %collective-permute-done.29 = bf16[56,128]{1,0:T(8,128)(2,1)S(1)} collective-permute-done((bf16[56,128]{1,0:T(8,128)(2,1)S(1)}, bf16[56,128]{1,0:T(8,128)(2,1)S(1)}, u32[]{:S(2)}, u32[]{:S(2)}) %collective-permute-start.29) | collective-permute-done | bytes 14368 | tf_op jit(solution)/shard_map/ppermute | solution.py:258
  73.9 6.4 %collective-permute-done.30 = bf16[56,128]{1,0:T(8,128)(2,1)S(1)} collective-permute-done((bf16[56,128]{1,0:T(8,128)(2,1)S(1)}, bf16[56,128]{1,0:T(8,128)(2,1)S(1)}, u32[]{:S(2)}, u32[]{:S(2)}) %collective-permute-start.30) | collective-permute-done | bytes 14368 | tf_op jit(solution)/shard_map/ppermute | solution.py:258
  80.3 1.9 collective-permute-start.31
  82.3 7.3 %collective-permute-done.31 = bf16[56,128]{1,0:T(8,128)(2,1)S(1)} collective-permute-done((bf16[56,128]{1,0:T(8,128)(2,1)S(1)}, bf16[56,128]{1,0:T(8,128)(2,1)S(1)}, u32[]{:S(2)}, u32[]{:S(2)}) %collective-permute-start.31) | collective-permute-done | bytes 14368 | tf_op jit(solution)/shard_map/ppermute | solution.py:258
  91.5 3.7 %collective-permute-done.32 = bf16[56,128]{1,0:T(8,128)(2,1)S(1)} collective-permute-done((bf16[56,128]{1,0:T(8,128)(2,1)S(1)}, bf16[56,128]{1,0:T(8,128)(2,1)S(1)}, u32[]{:S(2)}, u32[]{:S(2)}) %collective-permute-start.32) | collective-permute-done | bytes 14368 | tf_op jit(solution)/shard_map/ppermute | solution.py:258
  97.1 4.6 %collective-permute-done.33 = bf16[56,128]{1,0:T(8,128)(2,1)S(1)} collective-permute-done((bf16[56,128]{1,0:T(8,128)(2,1)S(1)}, bf16[56,128]{1,0:T(8,128)(2,1)S(1)}, u32[]{:S(2)}, u32[]{:S(2)}) %collective-permute-start.33) | collective-permute-done | bytes 14368 | tf_op jit(solution)/shard_map/ppermute | solution.py:258
  102.7 4.7 %shard_map.228 = (f32[3,56,384]{2,1,0:T(8,128)}, bf16[3,56,384]{2,1,0:T(8,128)(2,1)}, bf16[3,56,384]{2,1,0:T(8,128)(2,1)}, bf16[3,56,384]{2,1,0:T(8,128)(2,1)}) custom-call(s32[4]{0:T(128)} %fusion.6.starts_ref, bf16[3,208,2048]{2,1,0:T(8,128)(2,1)} %bitcast.53, bf16[64,2048]{1,0:T(8,128)(2,1)} %copy-done.9, bf16[64,2048]{1,0:T(8,128)(2,1)} %copy-done.8, ...), custom_call_target="tpu_custom_call" | custom-call | flops 981467136 | bytes 4773904 | tf_op jit(solution)/shard_map/pallas_call | solution.py:186
  107.4 2.0 collective-permute-start.8
  109.5 2.0 collective-permute-start.7
  118.3 2.0 collective-permute-start.15
  122.0 2.1 %collective-permute-start.14 = (bf16[64,2048]{1,0:T(8,128)(2,1)S(1)}, bf16[64,2048]{1,0:T(8,128)(2,1)S(1)}, u32[]{:S(2)}, u32[]{:S(2)}) collective-permute-start(bf16[64,2048]{1,0:T(8,128)(2,1)S(1)} %collective-permute-done.7.refs_0_), channel_id=1, source_target_pairs={{0,8},{8,16},{16,24},{24,28},{28,20},{20,12},{12,4},{4,0},{1,9},{9... | collective-permute-start | bytes 786440 | tf_op jit(solution)/shard_map/ppermute | solution.py:212
  128.3 5.0 %collective-permute-done.14.refs_0_ = bf16[64,2048]{1,0:T(8,128)(2,1)S(1)} collective-permute-done((bf16[64,2048]{1,0:T(8,128)(2,1)S(1)}, bf16[64,2048]{1,0:T(8,128)(2,1)S(1)}, u32[]{:S(2)}, u32[]{:S(2)}) %collective-permute-start.14) | collective-permute-done | bytes 262176 | tf_op jit(solution)/shard_map/ppermute | solution.py:212
  133.2 2.1 %collective-permute-start.21 = (bf16[64,2048]{1,0:T(8,128)(2,1)S(1)}, bf16[64,2048]{1,0:T(8,128)(2,1)S(1)}, u32[]{:S(2)}, u32[]{:S(2)}) collective-permute-start(bf16[64,2048]{1,0:T(8,128)(2,1)S(1)} %collective-permute-done.14.refs_0_), channel_id=1, source_target_pairs={{0,8},{8,16},{16,24},{24,28},{28,20},{20,12},{12,4},{4,0},{1,9},{9... | collective-permute-start | bytes 786440 | tf_op jit(solution)/shard_map/ppermute | solution.py:216
  136.1 3.9 %shard_map.229 = (f32[3,56,256]{2,1,0:T(8,128)}, bf16[3,56,256]{2,1,0:T(8,128)(2,1)}, bf16[3,56,256]{2,1,0:T(8,128)(2,1)}, bf16[3,56,256]{2,1,0:T(8,128)(2,1)}) custom-call(s32[4]{0:T(128)} %fusion.6.starts_ref, bf16[3,208,2048]{2,1,0:T(8,128)(2,1)} %bitcast.54, bf16[64,2048]{1,0:T(8,128)(2,1)} %copy-done.19, bf16[64,2048]{1,0:T(8,128)(2,1)} %copy-done.17, ...), custom_call_target="tpu_custom_call" | custom-call | flops 654311424 | bytes 4034576 | tf_op jit(solution)/shard_map/pallas_call | solution.py:186
  140.7 3.9 %shard_map.230 = (f32[3,56,256]{2,1,0:T(8,128)}, bf16[3,56,256]{2,1,0:T(8,128)(2,1)}, bf16[3,56,256]{2,1,0:T(8,128)(2,1)}, bf16[3,56,256]{2,1,0:T(8,128)(2,1)}) custom-call(s32[4]{0:T(128)} %fusion.6.starts_ref, bf16[3,208,2048]{2,1,0:T(8,128)(2,1)} %bitcast.55, bf16[64,2048]{1,0:T(8,128)(2,1)} %copy-done.15, bf16[64,2048]{1,0:T(8,128)(2,1)} %copy-done.14, ...), custom_call_target="tpu_custom_call" | custom-call | flops 654311424 | bytes 4034576 | tf_op jit(solution)/shard_map/pallas_call | solution.py:186
  149.1 3.4 %shard_map.231 = (f32[3,56,128]{2,1,0:T(8,128)}, bf16[3,56,128]{2,1,0:T(8,128)(2,1)}, bf16[3,56,128]{2,1,0:T(8,128)(2,1)}, bf16[3,56,128]{2,1,0:T(8,128)(2,1)}) custom-call(s32[4]{0:T(128)} %fusion.6.starts_ref, bf16[3,208,2048]{2,1,0:T(8,128)(2,1)} %bitcast.56, bf16[64,2048]{1,0:T(8,128)(2,1)} %copy-done.6, bf16[64,2048]{1,0:T(8,128)(2,1)} %copy-done.4), custom_call_target="tpu_custom_call" | custom-call | flops 327155712 | bytes 3295248 | tf_op jit(solution)/shard_map/pallas_call | solution.py:186
  161.0 6.4 %shard_map.233 = (bf16[3,56,1024]{2,1,0:T(8,128)(2,1)}, f32[56,1024]{1,0:T(8,128)}, f32[56,1024]{1,0:T(8,128)}, f32[56,1]{1,0:T(8,128)}) custom-call(s32[16]{0:T(128)} %pad_add_fusion.slots_ref, f32[3,56,384]{2,1,0:T(8,128)} %get-tuple-element.26.refs_0_, bf16[3,56,384]{2,1,0:T(8,128)(2,1)} %copy-done.26, bf16[3,56,384]{2,1,0:T(8,128)(2,1)} %copy-done.27, ...), custom_call_target="tpu_custom_call" | custom-call | flops 1879048192 | bytes 7306752 | tf_op jit(solution)/shard_map/pallas_call | solution.py:186
  167.5 5.1 %shard_map.235 = f32[56,33]{1,0:T(8,128)} custom-call(f32[56,33]{1,0:T(8,128)} %copy-done.24, f32[56,1024]{1,0:T(8,128)} %get-tuple-element.45.tgc_ref, f32[56,1024]{1,0:T(8,128)} %get-tuple-element.46.tgs_ref, bf16[1024,1024]{1,0:T(8,128)(2,1)} %constant.65.clone.cos_ref.refs_20_, bf16[1024,1024]{1,0:T(8,128)(2,1)} %constant.66.clone.sin_ref.refs_21_, ...), custom_call_target="tpu_custom_call" | custom-call | flops 469762048 | bytes 4668064 | tf_op jit(solution)/shard_map/pallas_call | solution.py:186
  172.6 2.8 %collective-permute-start.38 = (f32[56,33]{1,0:T(8,128)}, f32[56,33]{1,0:T(8,128)S(1)}, u32[]{:S(2)}, u32[]{:S(2)}) collective-permute-start(f32[56,33]{1,0:T(8,128)} %shard_map.235), channel_id=1, source_target_pairs={{0,0},{1,4},{2,8},{3,12},{4,16},{5,20},{6,24},{7,28},{8,1},{9,5},{... | collective-permute-start | bytes 22184 | tf_op jit(solution)/shard_map/ppermute | solution.py:353
  176.2 4.2 %collective-permute-done.38 = f32[56,33]{1,0:T(8,128)S(1)} collective-permute-done((f32[56,33]{1,0:T(8,128)}, f32[56,33]{1,0:T(8,128)S(1)}, u32[]{:S(2)}, u32[]{:S(2)}) %collective-permute-start.38) | collective-permute-done | bytes 7424 | tf_op jit(solution)/shard_map/ppermute | solution.py:353
  181.3 2.9 %collective-permute-done.39 = f32[1,56,33]{2,1,0:T(8,128)S(1)} collective-permute-done((f32[1,56,33]{2,1,0:T(8,128)S(1)}, f32[1,56,33]{2,1,0:T(8,128)S(1)}, u32[]{:S(2)}, u32[]{:S(2)}) %collective-permute-start.39) | collective-permute-done | bytes 7424 | tf_op jit(solution)/shard_map/ppermute | solution.py:356
  185.1 3.4 %collective-permute-done.40 = f32[2,56,33]{2,1,0:T(8,128)S(1)} collective-permute-done((f32[2,56,33]{2,1,0:T(8,128)S(1)}, f32[2,56,33]{2,1,0:T(8,128)S(1)}, u32[]{:S(2)}, u32[]{:S(2)}) %collective-permute-start.40) | collective-permute-done | bytes 14816 | tf_op jit(solution)/shard_map/ppermute | solution.py:356
  189.3 2.3 %collective-permute-start.35 = (bf16[3,56,1024]{2,1,0:T(8,128)(2,1)S(1)}, bf16[3,56,1024]{2,1,0:T(8,128)(2,1)S(1)}, u32[]{:S(2)}, u32[]{:S(2)}) collective-permute-start(bf16[3,56,1024]{2,1,0:T(8,128)(2,1)S(1)} %copy-done.20), channel_id=1, source_target_pairs={{0,2},{1,3},{2,0},{3,1},{4,6},{5,7},{6,4},{7,5},{8,10},{9,11},{10,... | collective-permute-start | bytes 1032200 | tf_op jit(solution)/shard_map/ppermute | solution.py:314
  191.6 3.4 %collective-permute-done.41 = f32[4,56,33]{2,1,0:T(8,128)S(1)} collective-permute-done((f32[4,56,33]{2,1,0:T(8,128)S(1)}, f32[4,56,33]{2,1,0:T(8,128)S(1)}, u32[]{:S(2)}, u32[]{:S(2)}) %collective-permute-start.41) | collective-permute-done | bytes 29600 | tf_op jit(solution)/shard_map/ppermute | solution.py:356
  195.7 4.6 %collective-permute-done.35.refs_1_ = bf16[3,56,1024]{2,1,0:T(8,128)(2,1)S(1)} collective-permute-done((bf16[3,56,1024]{2,1,0:T(8,128)(2,1)S(1)}, bf16[3,56,1024]{2,1,0:T(8,128)(2,1)S(1)}, u32[]{:S(2)}, u32[]{:S(2)}) %collective-permute-start.35) | collective-permute-done | bytes 344096 | tf_op jit(solution)/shard_map/ppermute | solution.py:314
  203.8 7.3 %shard_map.234 = f32[3,208,2048]{2,1,0:T(8,128)} custom-call(s32[4]{0:T(128)} %fusion.4.starts_ref, bf16[3,56,1024]{2,1,0:T(8,128)(2,1)} %get-tuple-element.44.refs_0_, bf16[3,56,1024]{2,1,0:T(8,128)(2,1)} %copy-done.22, bf16[3,56,1024]{2,1,0:T(8,128)(2,1)} %copy-done.21, bf16[3,56,1024]{2,1,0:T(8,128)(2,1)} %copy-done.23, ...), custom_call_target="tpu_custom_call" | custom-call | flops 2617245696 | bytes 10584064 | tf_op jit(solution)/shard_map/pallas_call | solution.py:332
  (197 shorter events, 65.8 us)
Async XLA Ops:
  1.7 99.9 %collective-permute-start.3 = (bf16[64,2048]{1,0:T(8,128)(2,1)S(1)}, bf16[64,2048]{1,0:T(8,128)(2,1)S(1)}, u32[]{:S(2)}, u32[]{:S(2)}) collective-permute-start(bf16[64,2048]{1,0:T(8,128)(2,1)S(1)} %get-tuple-element.56.refs_1_), channel_id=1, source_target_pairs={{8,0},{16,8},{24,16},{28,24},{20,28},{12,20},{4,12},{0,4},{9,1},{1... | collective-permute-start | bytes 786440 | tf_op jit(solution)/shard_map/ppermute | solution.py:213
  3.3 98.4 %collective-permute-start.1 = (bf16[64,2048]{1,0:T(8,128)(2,1)S(1)}, bf16[64,2048]{1,0:T(8,128)(2,1)S(1)}, u32[]{:S(2)}, u32[]{:S(2)}) collective-permute-start(bf16[64,2048]{1,0:T(8,128)(2,1)S(1)} %get-tuple-element.56.refs_1_), channel_id=1, source_target_pairs={{0,8},{8,16},{16,24},{24,28},{28,20},{20,12},{12,4},{4,0},{1,9},{9... | collective-permute-start | bytes 786440 | tf_op jit(solution)/shard_map/ppermute | solution.py:212
  3.8 97.9 %collective-permute-start.2 = (bf16[64,2048]{1,0:T(8,128)(2,1)S(1)}, bf16[64,2048]{1,0:T(8,128)(2,1)S(1)}, u32[]{:S(2)}, u32[]{:S(2)}) collective-permute-start(bf16[64,2048]{1,0:T(8,128)(2,1)S(1)} %get-tuple-element.57.refs_0_), channel_id=1, source_target_pairs={{8,0},{16,8},{24,16},{28,24},{20,28},{12,20},{4,12},{0,4},{9,1},{1... | collective-permute-start | bytes 786440 | tf_op jit(solution)/shard_map/ppermute | solution.py:213
  5.3 96.4 %collective-permute-start = (bf16[64,2048]{1,0:T(8,128)(2,1)S(1)}, bf16[64,2048]{1,0:T(8,128)(2,1)S(1)}, u32[]{:S(2)}, u32[]{:S(2)}) collective-permute-start(bf16[64,2048]{1,0:T(8,128)(2,1)S(1)} %get-tuple-element.57.refs_0_), channel_id=1, source_target_pairs={{0,8},{8,16},{16,24},{24,28},{28,20},{20,12},{12,4},{4,0},{1,9},{9... | collective-permute-start | bytes 786440 | tf_op jit(solution)/shard_map/ppermute | solution.py:212
  9.9 33.2 %collective-permute-start.34 = (f32[56,33]{1,0:T(8,128)S(1)}, f32[56,33]{1,0:T(8,128)S(1)}, u32[]{:S(2)}, u32[]{:S(2)}) collective-permute-start(f32[56,33]{1,0:T(8,128)S(1)} %copy.43), channel_id=1, source_target_pairs={{0,0},{4,1},{8,2},{12,3},{16,4},{20,5},{24,6},{28,7},{1,8},{5,9},{... | collective-permute-start | bytes 22184 | tf_op jit(solution)/shard_map/ppermute | solution.py:249
  43.1 7.7 %collective-permute-start.26 = (bf16[56,128]{1,0:T(8,128)(2,1)S(1)}, bf16[56,128]{1,0:T(8,128)(2,1)S(1)}, u32[]{:S(2)}, u32[]{:S(2)}) collective-permute-start(bf16[56,128]{1,0:T(8,128)(2,1)S(1)} %get-tuple-element.72), channel_id=1, source_target_pairs={{0,0},{4,1},{8,2},{12,3},{16,4},{20,5},{24,6},{28,7},{1,8},{5,9},{... | collective-permute-start | bytes 43016 | tf_op jit(solution)/shard_map/ppermute | solution.py:258
  50.8 7.4 %collective-permute-start.27 = (bf16[56,128]{1,0:T(8,128)(2,1)S(1)}, bf16[56,128]{1,0:T(8,128)(2,1)S(1)}, u32[]{:S(2)}, u32[]{:S(2)}) collective-permute-start(bf16[56,128]{1,0:T(8,128)(2,1)S(1)} %get-tuple-element.71), channel_id=1, source_target_pairs={{4,0},{8,1},{12,2},{16,3},{20,4},{24,5},{28,6},{0,7},{5,8},{9,9},{... | collective-permute-start | bytes 43016 | tf_op jit(solution)/shard_map/ppermute | solution.py:258
  58.2 7.4 %collective-permute-start.28 = (bf16[56,128]{1,0:T(8,128)(2,1)S(1)}, bf16[56,128]{1,0:T(8,128)(2,1)S(1)}, u32[]{:S(2)}, u32[]{:S(2)}) collective-permute-start(bf16[56,128]{1,0:T(8,128)(2,1)S(1)} %get-tuple-element.70), channel_id=1, source_target_pairs={{8,0},{12,1},{16,2},{20,3},{24,4},{28,5},{0,6},{4,7},{9,8},{13,9},... | collective-permute-start | bytes 43016 | tf_op jit(solution)/shard_map/ppermute | solution.py:258
  65.6 8.3 %collective-permute-start.29 = (bf16[56,128]{1,0:T(8,128)(2,1)S(1)}, bf16[56,128]{1,0:T(8,128)(2,1)S(1)}, u32[]{:S(2)}, u32[]{:S(2)}) collective-permute-start(bf16[56,128]{1,0:T(8,128)(2,1)S(1)} %get-tuple-element.69), channel_id=1, source_target_pairs={{12,0},{16,1},{20,2},{24,3},{28,4},{0,5},{4,6},{8,7},{13,8},{17,9}... | collective-permute-start | bytes 43016 | tf_op jit(solution)/shard_map/ppermute | solution.py:258
  80.3 9.2 %collective-permute-start.31 = (bf16[56,128]{1,0:T(8,128)(2,1)S(1)}, bf16[56,128]{1,0:T(8,128)(2,1)S(1)}, u32[]{:S(2)}, u32[]{:S(2)}) collective-permute-start(bf16[56,128]{1,0:T(8,128)(2,1)S(1)} %get-tuple-element.67), channel_id=1, source_target_pairs={{20,0},{24,1},{28,2},{0,3},{4,4},{8,5},{12,6},{16,7},{21,8},{25,9}... | collective-permute-start | bytes 43016 | tf_op jit(solution)/shard_map/ppermute | solution.py:258
  95.1 6.5 %collective-permute-start.33 = (bf16[56,128]{1,0:T(8,128)(2,1)S(1)}, bf16[56,128]{1,0:T(8,128)(2,1)S(1)}, u32[]{:S(2)}, u32[]{:S(2)}) collective-permute-start(bf16[56,128]{1,0:T(8,128)(2,1)S(1)} %get-tuple-element.66), channel_id=1, source_target_pairs={{28,0},{0,1},{4,2},{8,3},{12,4},{16,5},{20,6},{24,7},{29,8},{1,9},... | collective-permute-start | bytes 43016 | tf_op jit(solution)/shard_map/ppermute | solution.py:258
  107.4 37.3 %collective-permute-start.4 = (bf16[3,56,384]{2,1,0:T(8,128)(2,1)}, bf16[3,56,384]{2,1,0:T(8,128)(2,1)S(1)}, u32[]{:S(2)}, u32[]{:S(2)}) collective-permute-start(bf16[3,56,384]{2,1,0:T(8,128)(2,1)} %get-tuple-element.27), channel_id=1, source_target_pairs={{0,1},{1,2},{2,3},{3,0},{4,5},{5,6},{6,7},{7,4},{8,9},{9,10},{10,1... | collective-permute-start | bytes 387080 | tf_op jit(solution)/shard_map/ppermute | solution.py:297
  107.4 10.8 %collective-permute-start.10 = (bf16[64,2048]{1,0:T(8,128)(2,1)}, bf16[64,2048]{1,0:T(8,128)(2,1)S(1)}, u32[]{:S(2)}, u32[]{:S(2)}) collective-permute-start(bf16[64,2048]{1,0:T(8,128)(2,1)} %copy-done.3), channel_id=1, source_target_pairs={{8,0},{16,8},{24,16},{28,24},{20,28},{12,20},{4,12},{0,4},{9,1},{1... | collective-permute-start | bytes 786440 | tf_op jit(solution)/shard_map/ppermute | solution.py:213
  107.4 10.8 %collective-permute-start.8 = (bf16[64,2048]{1,0:T(8,128)(2,1)}, bf16[64,2048]{1,0:T(8,128)(2,1)S(1)}, u32[]{:S(2)}, u32[]{:S(2)}) collective-permute-start(bf16[64,2048]{1,0:T(8,128)(2,1)} %copy-done.1), channel_id=1, source_target_pairs={{0,8},{8,16},{16,24},{24,28},{28,20},{20,12},{12,4},{4,0},{1,9},{9... | collective-permute-start | bytes 786440 | tf_op jit(solution)/shard_map/ppermute | solution.py:212
  109.4 16.1 %collective-permute-start.9 = (bf16[64,2048]{1,0:T(8,128)(2,1)}, bf16[64,2048]{1,0:T(8,128)(2,1)S(1)}, u32[]{:S(2)}, u32[]{:S(2)}) collective-permute-start(bf16[64,2048]{1,0:T(8,128)(2,1)} %copy-done), channel_id=1, source_target_pairs={{8,0},{16,8},{24,16},{28,24},{20,28},{12,20},{4,12},{0,4},{9,1},{1... | collective-permute-start | bytes 786440 | tf_op jit(solution)/shard_map/ppermute | solution.py:213
  109.5 12.5 %collective-permute-start.7 = (bf16[64,2048]{1,0:T(8,128)(2,1)}, bf16[64,2048]{1,0:T(8,128)(2,1)S(1)}, u32[]{:S(2)}, u32[]{:S(2)}) collective-permute-start(bf16[64,2048]{1,0:T(8,128)(2,1)} %copy-done.2), channel_id=1, source_target_pairs={{0,8},{8,16},{16,24},{24,28},{28,20},{20,12},{12,4},{4,0},{1,9},{9... | collective-permute-start | bytes 786440 | tf_op jit(solution)/shard_map/ppermute | solution.py:212
  118.2 10.0 %collective-permute-start.17 = (bf16[64,2048]{1,0:T(8,128)(2,1)S(1)}, bf16[64,2048]{1,0:T(8,128)(2,1)S(1)}, u32[]{:S(2)}, u32[]{:S(2)}) collective-permute-start(bf16[64,2048]{1,0:T(8,128)(2,1)S(1)} %collective-permute-done.10.refs_3_), channel_id=1, source_target_pairs={{8,0},{16,8},{24,16},{28,24},{20,28},{12,20},{4,12},{0,4},{9,1},{1... | collective-permute-start | bytes 786440 | tf_op jit(solution)/shard_map/ppermute | solution.py:213
  118.3 9.9 %collective-permute-start.15 = (bf16[64,2048]{1,0:T(8,128)(2,1)S(1)}, bf16[64,2048]{1,0:T(8,128)(2,1)S(1)}, u32[]{:S(2)}, u32[]{:S(2)}) collective-permute-start(bf16[64,2048]{1,0:T(8,128)(2,1)S(1)} %collective-permute-done.8.refs_1_), channel_id=1, source_target_pairs={{0,8},{8,16},{16,24},{24,28},{28,20},{20,12},{12,4},{4,0},{1,9},{9... | collective-permute-start | bytes 786440 | tf_op jit(solution)/shard_map/ppermute | solution.py:212
  122.0 11.2 %collective-permute-start.14 = (bf16[64,2048]{1,0:T(8,128)(2,1)S(1)}, bf16[64,2048]{1,0:T(8,128)(2,1)S(1)}, u32[]{:S(2)}, u32[]{:S(2)}) collective-permute-start(bf16[64,2048]{1,0:T(8,128)(2,1)S(1)} %collective-permute-done.7.refs_0_), channel_id=1, source_target_pairs={{0,8},{8,16},{16,24},{24,28},{28,20},{20,12},{12,4},{4,0},{1,9},{9... | collective-permute-start | bytes 786440 | tf_op jit(solution)/shard_map/ppermute | solution.py:212
  125.6 19.3 %collective-permute-start.5 = (bf16[3,56,384]{2,1,0:T(8,128)(2,1)}, bf16[3,56,384]{2,1,0:T(8,128)(2,1)S(1)}, u32[]{:S(2)}, u32[]{:S(2)}) collective-permute-start(bf16[3,56,384]{2,1,0:T(8,128)(2,1)} %get-tuple-element.28), channel_id=1, source_target_pairs={{0,2},{1,3},{2,0},{3,1},{4,6},{5,7},{6,4},{7,5},{8,10},{9,11},{10,... | collective-permute-start | bytes 387080 | tf_op jit(solution)/shard_map/ppermute | solution.py:297
  128.1 11.9 %collective-permute-start.16 = (bf16[64,2048]{1,0:T(8,128)(2,1)S(1)}, bf16[64,2048]{1,0:T(8,128)(2,1)S(1)}, u32[]{:S(2)}, u32[]{:S(2)}) collective-permute-start(bf16[64,2048]{1,0:T(8,128)(2,1)S(1)} %collective-permute-done.9.refs_2_), channel_id=1, source_target_pairs={{8,0},{16,8},{24,16},{28,24},{20,28},{12,20},{4,12},{0,4},{9,1},{1... | collective-permute-start | bytes 786440 | tf_op jit(solution)/shard_map/ppermute | solution.py:213
  128.2 17.8 %collective-permute-start.22 = (bf16[64,2048]{1,0:T(8,128)(2,1)S(1)}, bf16[64,2048]{1,0:T(8,128)(2,1)S(1)}, u32[]{:S(2)}, u32[]{:S(2)}) collective-permute-start(bf16[64,2048]{1,0:T(8,128)(2,1)S(1)} %collective-permute-done.17.refs_3_), channel_id=1, source_target_pairs={{8,0},{16,8},{24,16},{28,24},{20,28},{12,20},{4,12},{0,4},{9,1},{1... | collective-permute-start | bytes 786440 | tf_op jit(solution)/shard_map/ppermute | solution.py:216
  133.2 14.1 %collective-permute-start.21 = (bf16[64,2048]{1,0:T(8,128)(2,1)S(1)}, bf16[64,2048]{1,0:T(8,128)(2,1)S(1)}, u32[]{:S(2)}, u32[]{:S(2)}) collective-permute-start(bf16[64,2048]{1,0:T(8,128)(2,1)S(1)} %collective-permute-done.14.refs_0_), channel_id=1, source_target_pairs={{0,8},{8,16},{16,24},{24,28},{28,20},{20,12},{12,4},{4,0},{1,9},{9... | collective-permute-start | bytes 786440 | tf_op jit(solution)/shard_map/ppermute | solution.py:216
  140.0 12.4 %collective-permute-start.6 = (bf16[3,56,384]{2,1,0:T(8,128)(2,1)S(1)}, bf16[3,56,384]{2,1,0:T(8,128)(2,1)S(1)}, u32[]{:S(2)}, u32[]{:S(2)}) collective-permute-start(bf16[3,56,384]{2,1,0:T(8,128)(2,1)S(1)} %copy-done.28), channel_id=1, source_target_pairs={{0,3},{1,0},{2,1},{3,2},{4,7},{5,4},{6,5},{7,6},{8,11},{9,8},{10,9... | collective-permute-start | bytes 387080 | tf_op jit(solution)/shard_map/ppermute | solution.py:297
  144.6 8.7 %collective-permute-start.11 = (bf16[3,56,256]{2,1,0:T(8,128)(2,1)}, bf16[3,56,256]{2,1,0:T(8,128)(2,1)S(1)}, u32[]{:S(2)}, u32[]{:S(2)}) collective-permute-start(bf16[3,56,256]{2,1,0:T(8,128)(2,1)} %get-tuple-element.31), channel_id=1, source_target_pairs={{0,1},{1,2},{2,3},{3,0},{4,5},{5,6},{6,7},{7,4},{8,9},{9,10},{10,1... | collective-permute-start | bytes 258056 | tf_op jit(solution)/shard_map/ppermute | solution.py:297
  144.9 9.9 %collective-permute-start.12 = (bf16[3,56,256]{2,1,0:T(8,128)(2,1)}, bf16[3,56,256]{2,1,0:T(8,128)(2,1)S(1)}, u32[]{:S(2)}, u32[]{:S(2)}) collective-permute-start(bf16[3,56,256]{2,1,0:T(8,128)(2,1)} %get-tuple-element.32), channel_id=1, source_target_pairs={{0,2},{1,3},{2,0},{3,1},{4,6},{5,7},{6,4},{7,5},{8,10},{9,11},{10,... | collective-permute-start | bytes 258056 | tf_op jit(solution)/shard_map/ppermute | solution.py:297
  146.0 8.8 %collective-permute-start.13 = (bf16[3,56,256]{2,1,0:T(8,128)(2,1)}, bf16[3,56,256]{2,1,0:T(8,128)(2,1)S(1)}, u32[]{:S(2)}, u32[]{:S(2)}) collective-permute-start(bf16[3,56,256]{2,1,0:T(8,128)(2,1)} %get-tuple-element.33), channel_id=1, source_target_pairs={{0,3},{1,0},{2,1},{3,2},{4,7},{5,4},{6,5},{7,6},{8,11},{9,8},{10,9... | collective-permute-start | bytes 258056 | tf_op jit(solution)/shard_map/ppermute | solution.py:297
  147.4 8.7 %collective-permute-start.18 = (bf16[3,56,256]{2,1,0:T(8,128)(2,1)}, bf16[3,56,256]{2,1,0:T(8,128)(2,1)S(1)}, u32[]{:S(2)}, u32[]{:S(2)}) collective-permute-start(bf16[3,56,256]{2,1,0:T(8,128)(2,1)} %get-tuple-element.35), channel_id=1, source_target_pairs={{0,1},{1,2},{2,3},{3,0},{4,5},{5,6},{6,7},{7,4},{8,9},{9,10},{10,1... | collective-permute-start | bytes 258056 | tf_op jit(solution)/shard_map/ppermute | solution.py:297
  152.5 6.6 %collective-permute-start.19 = (bf16[3,56,256]{2,1,0:T(8,128)(2,1)}, bf16[3,56,256]{2,1,0:T(8,128)(2,1)S(1)}, u32[]{:S(2)}, u32[]{:S(2)}) collective-permute-start(bf16[3,56,256]{2,1,0:T(8,128)(2,1)} %get-tuple-element.36), channel_id=1, source_target_pairs={{0,2},{1,3},{2,0},{3,1},{4,6},{5,7},{6,4},{7,5},{8,10},{9,11},{10,... | collective-permute-start | bytes 258056 | tf_op jit(solution)/shard_map/ppermute | solution.py:297
  172.6 7.8 %collective-permute-start.38 = (f32[56,33]{1,0:T(8,128)}, f32[56,33]{1,0:T(8,128)S(1)}, u32[]{:S(2)}, u32[]{:S(2)}) collective-permute-start(f32[56,33]{1,0:T(8,128)} %shard_map.235), channel_id=1, source_target_pairs={{0,0},{1,4},{2,8},{3,12},{4,16},{5,20},{6,24},{7,28},{8,1},{9,5},{... | collective-permute-start | bytes 22184 | tf_op jit(solution)/shard_map/ppermute | solution.py:353
  189.3 13.0 %collective-permute-start.36 = (bf16[3,56,1024]{2,1,0:T(8,128)(2,1)S(1)}, bf16[3,56,1024]{2,1,0:T(8,128)(2,1)S(1)}, u32[]{:S(2)}, u32[]{:S(2)}) collective-permute-start(bf16[3,56,1024]{2,1,0:T(8,128)(2,1)S(1)} %copy-done.20), channel_id=1, source_target_pairs={{0,1},{1,0},{2,3},{3,2},{4,5},{5,4},{6,7},{7,6},{8,9},{9,8},{10,11... | collective-permute-start | bytes 1032200 | tf_op jit(solution)/shard_map/ppermute | solution.py:318
  189.3 11.0 %collective-permute-start.35 = (bf16[3,56,1024]{2,1,0:T(8,128)(2,1)S(1)}, bf16[3,56,1024]{2,1,0:T(8,128)(2,1)S(1)}, u32[]{:S(2)}, u32[]{:S(2)}) collective-permute-start(bf16[3,56,1024]{2,1,0:T(8,128)(2,1)S(1)} %copy-done.20), channel_id=1, source_target_pairs={{0,2},{1,3},{2,0},{3,1},{4,6},{5,7},{6,4},{7,5},{8,10},{9,11},{10,... | collective-permute-start | bytes 1032200 | tf_op jit(solution)/shard_map/ppermute | solution.py:314
  (49 other events, 601.3 us)
where the time goes:
time: 215 us; the launch traced here: 211 us
  waiting for transfers between devices  65.5 us (30%)
  starting transfers between devices  48.9 us (23%)
  local copies, waits for them, and re-layouts  39.4 us (18%)
  Pallas kernels  39.3 us (18%)
  between operations  16.5 us (8%)
    ppermute x8, waiting for transfers between devices, local(): upper.append(lax.ppermute(sent, ('seq', 'ch'), route))  38.9 us
    pallas_call x7, Pallas kernels, call(): pl.pallas_call(kernel, out_shape=outs, in_specs=specs, out_specs=[whole]...  32 us
    unnamed x100, local copies, waits for them, and re-layouts  20.9 us
    ppermute x8, starting transfers between devices, local(): upper.append(lax.ppermute(sent, ('seq', 'ch'), route))  14.9 us
    dynamic_slice x8, local copies, waits for them, and re-layouts, picked(): return jnp.asarray(np.asarray(table, np.int32))[index]  10.1 us
    ppermute x3, waiting for transfers between devices, local(): lax.ppermute(returned, 'seq', [(s, s ^ reach) for s in range(n_seq)])  9.74 us
    ppermute x12, starting transfers between devices, local(): lax.ppermute(sums[d], 'ch', [(h, (h + d) % n_ch) for h in range(n_ch)])  9.49 us
    ppermute x6, starting transfers between devices, ring_gather(): from_behind = tuple((lax.ppermute(a, 'seq', ahead) for a in from_behind))  9.12 us
  transfers between devices with their start and end apart: 42, of which 15 were waited for; matrix products, arithmetic and copies ran while one was open for 17% of the time, Pallas kernels for 7%

commit v1 on v0

--- a/solution.py
+++ b/solution.py
@@ -12,7 +12,7 @@
 
 F32 = jnp.float32
 BF16 = jnp.bfloat16
-VMEM_BYTES = 56 * 1024 * 1024
+MIB = 1024 * 1024
 
 
 def round_up(value, multiple):
@@ -62,7 +62,22 @@
     hs_ref[...] = cos_half * uneven - sin_half * even
 
 
-def project_kernel(starts_ref, weight_ref, *refs, pieces):
+def part_start(index, part, rows):
+    return pl.multiple_of(jnp.minimum(index * part, rows - part), 8)
+
+
+def pack_kernel(place_ref, grad_ref, packed_ref, pieces_ref, poles_ref, *, rows, n_ch):
+    part = poles_ref.shape[0]
+    grad = grad_ref[...].astype(F32)
+    for piece in range(pieces_ref.shape[0]):
+        start = piece // n_ch * rows + min(piece % n_ch * part, rows - part)
+        pieces_ref[piece] = grad[start : start + part].astype(BF16)
+    own = place_ref[0]
+    start = own // n_ch * rows + part_start(own % n_ch, part, rows)
+    poles_ref[...] = packed_ref[pl.ds(pl.multiple_of(start, 8), part), :]
+
+
+def project_kernel(place_ref, weight_ref, *refs, pieces):
     feature_refs = refs[:pieces]
     out_refs = refs[pieces:-2]
     features_ref, sums_ref = refs[-2:]
@@ -78,11 +93,21 @@
             preferred_element_type=F32,
         )
     for step, out_ref in enumerate(out_refs):
-        start = pl.multiple_of(starts_ref[step], 8)
+        start = part_start((place_ref[1] + step) % len(out_refs), part, weight_ref.shape[1])
         out_ref[...] = sums_ref[:, pl.ds(start, part), :].astype(out_ref.dtype)
 
 
-def conv_kernel(slots_ref, *refs, order, group_slots, shares):
+def ring_place(index, count):
+    return jnp.where(index % 2 == 0, index // 2, count - (index + 1) // 2)
+
+
+def ring_slot(index, place, count):
+    ahead = (ring_place(index, count) - place + count) % count
+    near = jnp.where(ahead * 2 < count, 2 * ahead, 2 * (count - ahead) - 1)
+    return jnp.where(ahead * 2 == count, count - 1, near)
+
+
+def conv_kernel(place_ref, *refs, order, group_slots, shares):
     partial_refs = refs[: len(group_slots) * shares]
     (
         gout_ref, poles_ref, hc_ref, hs_ref, cos_ref, sin_ref, twist_ref,
@@ -101,14 +126,17 @@
             proj_ref[slot] = total[:, :, place * block_len : (place + 1) * block_len]
             slot += 1
 
+    place = ring_place(place_ref[0], blocks)
+    slots = [ring_slot(jnp.int32(b), place, blocks) for b in range(blocks)]
+
     def in_order(gate):
-        return jnp.concatenate([proj_ref[slots_ref[b], gate] for b in range(blocks)], 1)
+        return jnp.concatenate([proj_ref[slots[b], gate] for b in range(blocks)], 1)
 
     queries = in_order(0)
     keys = in_order(1)
     values = in_order(2)
     upper = jnp.concatenate(
-        [gout_ref[slots_ref[blocks + b]].astype(F32) for b in range(blocks)], 1
+        [gout_ref[b].astype(F32) for b in range(blocks)], 1
     )
     product = keys * values
     middle = upper * queries
@@ -137,8 +165,8 @@
     grads = (upper * (restored[:rows] + skip * product), mix * values, mix * keys)
     for gate, grad in enumerate(grads):
         for b in range(blocks):
-            place = pl.multiple_of(slots_ref[b] * block_len, block_len)
-            grad_ref[gate, :, pl.ds(place, block_len)] = grad[
+            column = pl.multiple_of(slots[b] * block_len, block_len)
+            grad_ref[gate, :, pl.ds(column, block_len)] = grad[
                 :, b * block_len : (b + 1) * block_len
             ].astype(BF16)
     skip_ref[...] = jnp.sum(product * middle, axis=1, keepdims=True)
@@ -158,7 +186,7 @@
     out_ref[:, 2 * order : 2 * order + 1] = skip_ref[...]
 
 
-def weight_kernel(starts_ref, *refs, shares):
+def weight_kernel(place_ref, *refs, shares):
     grad_refs = refs[:shares]
     feature_ref, out_ref, wide_ref, rows_ref = refs[shares:]
     gates = out_ref.shape[0]
@@ -167,7 +195,9 @@
     @pl.when(pl.program_id(0) == 0)
     def _():
         for share, grad_ref in enumerate(grad_refs):
-            start = pl.multiple_of(starts_ref[share], 8)
+            core, step = share // (shares // 2), 2 * (share % (shares // 2))
+            owner = place_ref[1] + core * (1 - 2 * (place_ref[1] % 2))
+            start = part_start((owner - step + shares) % shares, part, out_ref.shape[1])
             wide_ref[:, pl.ds(start, part), :] = grad_ref[...].astype(F32)
         rows_ref[...] = wide_ref[...].astype(BF16)
 
@@ -179,6 +209,8 @@
     size = sum(a.size * a.dtype.itemsize for a in operands) + sum(
         o.size * o.dtype.itemsize for o in outs
     )
+    scratch_size = sum(math.prod(a.shape) * a.dtype.itemsize for a in scratch)
+    limit = min(56 * MIB, 2 * (size + scratch_size) + 8 * MIB)
     whole = pl.BlockSpec(memory_space=pltpu.VMEM)
     specs = [whole] * len(operands)
     if indexed:
@@ -189,15 +221,11 @@
         in_specs=specs,
         out_specs=[whole] * len(outs),
         scratch_shapes=scratch,
-        compiler_params=pltpu.CompilerParams(vmem_limit_bytes=VMEM_BYTES),
+        compiler_params=pltpu.CompilerParams(vmem_limit_bytes=limit),
         cost_estimate=pl.CostEstimate(
             flops=flops, bytes_accessed=size, transcendentals=transcendentals
         ),
     )(*operands)
-
-
-def picked(table, index):
-    return jnp.asarray(np.asarray(table, np.int32))[index]
 
 
 def ring_gather(features, ring):
@@ -232,34 +260,31 @@
     per_ch = n_seq // n_ch
     cos_table, sin_table, twist = (jnp.asarray(a) for a in wave_tables(tokens))
 
+    place = jnp.stack([seq_index, ch_index]).astype(jnp.int32)
+
     ring = list(range(0, n_seq, 2)) + list(range(n_seq - 1, 0, -2))
-    offsets = [0] + [o for k in range(1, n_seq // 2) for o in (-k, k)] + [n_seq // 2]
-    slot_of = np.zeros((n_seq, n_seq), np.int32)
-    for place, index in enumerate(ring):
-        for slot, offset in enumerate(offsets):
-            slot_of[index, ring[(place + offset) % n_seq]] = slot
     slots = ring_gather(features, ring)
 
-    piece_starts = [(j // n_ch) * rows + starts[j % n_ch] for j in range(n_seq)]
+    first = slots[1]
+    grad_out, residues, log_rates, skip_gain, first = lax.optimization_barrier(
+        (grad_out, residues, log_rates, skip_gain, first)
+    )
+    slots[1] = first
+
     spread = [((q % n_seq) * n_ch + q // n_seq, q) for q in range(n_seq * n_ch)]
     gather_back = [(b, a) for a, b in spread]
-
     packed = jnp.concatenate([residues, log_rates, skip_gain[:, None]], 1)
-    poles = lax.dynamic_slice_in_dim(packed, picked(piece_starts, seq_index), part, 0)
+    upper, poles = call(
+        functools.partial(pack_kernel, rows=rows, n_ch=n_ch),
+        (
+            jax.ShapeDtypeStruct((n_seq, part, block_len), BF16),
+            jax.ShapeDtypeStruct((part, packed.shape[1]), F32),
+        ),
+        0, 0, place, grad_out, packed, indexed=True,
+    )
     poles = lax.ppermute(poles, ("seq", "ch"), spread)
-
-    upper = []
-    for k in range(n_seq):
-        route = [
-            (((q % n_seq + k) % n_seq) * n_ch + q // n_seq, q) for q in range(n_seq * n_ch)
-        ]
-        begin = picked([piece_starts[(s - k) % n_seq] for s in range(n_seq)], seq_index)
-        sent = lax.dynamic_slice_in_dim(grad_out, begin, part, 0)
-        upper.append(lax.ppermute(sent, ("seq", "ch"), route))
-    upper = jnp.stack(upper)
-    own_piece = (seq_index * n_ch + ch_index) % n_seq
-    upper_slots = (jnp.arange(n_seq, dtype=jnp.int32) - own_piece) % n_seq
-    conv_slots = jnp.concatenate([picked(slot_of, seq_index), upper_slots.astype(jnp.int32)])
+    upper = lax.all_to_all(upper, "seq", split_axis=0, concat_axis=0, tiled=True)
+    upper = lax.ppermute(upper, ("seq", "ch"), spread)
 
     square = part * tokens * tokens
     spectrum = jax.ShapeDtypeStruct((part, tokens), F32)
@@ -269,13 +294,7 @@
     )
 
     weight = qkv_weight.transpose(1, 0, 2)
-    ahead_starts = picked(
-        [[starts[(h + d) % n_ch] for d in range(n_ch)] for h in range(n_ch)], ch_index
-    )
-    behind_starts = picked(
-        [[starts[(h - d) % n_ch] for d in range(n_ch)] for h in range(n_ch)], ch_index
-    )
-    groups = [slots[:3]] + [slots[i : i + 2] for i in range(3, n_seq, 2)]
+    groups = [slots[:3]] + [slots[i : i + 4] for i in range(3, n_seq - 1, 4)] + [slots[n_seq - 1 :]]
     group_slots = [len(group) for group in groups]
     partials = []
     for group in groups:
@@ -287,7 +306,7 @@
                 jax.ShapeDtypeStruct((gates, part, span), F32 if d == 0 else BF16)
                 for d in range(n_ch)
             ],
-            2 * gates * rows * width * span, 0, ahead_starts, weight, *pieces,
+            2 * gates * rows * width * span, 0, place, weight, *pieces,
             scratch=[pltpu.VMEM((span, width), BF16), pltpu.VMEM((gates, rows, span), F32)],
             indexed=True,
         )
@@ -305,27 +324,26 @@
             spectrum,
             jax.ShapeDtypeStruct((part, 1), F32),
         ),
-        32 * square, 0, conv_slots, *partials, upper, poles, hc, hs,
+        32 * square, 0, place, *partials, upper, poles, hc, hs,
         cos_table, sin_table, twist,
         scratch=[pltpu.VMEM((n_seq, gates, part, block_len), F32)], indexed=True,
     )
 
-    held = [grads] + [
+    swap = [(h, h ^ 1) for h in range(n_ch)]
+    across = [
         lax.ppermute(grads, "ch", [(h, (h + d) % n_ch) for h in range(n_ch)])
         for d in range(2, n_ch, 2)
     ]
-    swap = [(h, h ^ 1) for h in range(n_ch)]
-    held += [lax.ppermute(a, "ch", swap) for a in held]
-    order_of = [
-        [starts[((h ^ core) - d) % n_ch] for core in (0, 1) for d in range(0, n_ch, 2)]
-        for h in range(n_ch)
-    ]
-
+    swapped = lax.ppermute(grads, "ch", swap)
+    tgc, swapped = lax.optimization_barrier((tgc, swapped))
     (pole_sums,) = call(
         functools.partial(pole_kernel, order=order),
         (jax.ShapeDtypeStruct((part, 2 * order + 1), F32),),
         8 * square, part * tokens * order, poles, tgc, tgs, cos_table, sin_table, skip_sum,
     )
+
+    pole_sums, across = lax.optimization_barrier((pole_sums, across))
+    held = [grads] + across + [swapped] + [lax.ppermute(a, "ch", swap) for a in across]
 
     every_feature = jnp.concatenate([piece for slot in slots for piece in slot], 0)
     tile = min(512, width)
@@ -341,22 +359,20 @@
             pltpu.VMEM((gates, rows, tokens), F32),
             pltpu.VMEM((gates, rows, tokens), BF16),
         ],
-        compiler_params=pltpu.CompilerParams(vmem_limit_bytes=VMEM_BYTES),
+        compiler_params=pltpu.CompilerParams(
+            vmem_limit_bytes=min(56 * MIB, 16 * MIB + 12 * gates * rows * tokens + 4 * tokens * tile)
+        ),
         cost_estimate=pl.CostEstimate(
             flops=2 * gates * rows * width * tokens,
             bytes_accessed=4 * gates * rows * width + 2 * tokens * (width + gates * rows),
             transcendentals=0,
         ),
-    )(picked(order_of, ch_index), *held, every_feature)
+    )(place, *held, every_feature)
     weight_grad = weight_grad.transpose(1, 0, 2)
 
-    returned = lax.ppermute(pole_sums, ("seq", "ch"), gather_back)[None]
-    reach = 1
-    while reach < n_seq:
-        other = lax.ppermute(returned, "seq", [(s, s ^ reach) for s in range(n_seq)])
-        returned = jnp.concatenate([returned, other], 0)
-        reach *= 2
-    returned = returned[jnp.arange(n_seq) ^ seq_index]
+    returned = lax.ppermute(pole_sums, ("seq", "ch"), gather_back)
+    returned = jnp.broadcast_to(returned[None], (n_seq,) + returned.shape)
+    returned = lax.all_to_all(returned, "seq", split_axis=0, concat_axis=0, tiled=True)
     pieces = []
     for block in range(per_ch):
         filled = 0

time: 215 us -> 145 us (0.67)
  the two profiles are of different devices: /device:TPU:4 before, /device:TPU:0 now
where the time goes in v1:
time: 145 us; the launch traced here: 144 us
  starting transfers between devices  50.8 us (35%)
  local copies, waits for them, and re-layouts  35 us (24%)
  waiting for transfers between devices  31.1 us (21%)
  Pallas kernels  22.8 us (16%)
  other arithmetic  2.81 us (2%)
    unnamed x63, local copies, waits for them, and re-layouts  29.3 us
    pallas_call x7, Pallas kernels, call(): pl.pallas_call(kernel, out_shape=outs, in_specs=specs, out_specs=[whole]...  15.9 us
    ppermute x6, starting transfers between devices, ring_gather(): from_behind = tuple((lax.ppermute(a, 'seq', ahead) for a in from_behind))  14.6 us
    all_to_all x1, starting transfers between devices, local(): lax.all_to_all(returned, 'seq', split_axis=0, concat_axis=0, tiled=True)  11.2 us
    ppermute x9, starting transfers between devices, local(): lax.ppermute(sums[d], 'ch', [(h, (h + d) % n_ch) for h in range(n_ch)])  9.78 us
    ppermute x6, waiting for transfers between devices, ring_gather(): from_behind = tuple((lax.ppermute(a, 'seq', ahead) for a in from_behind))  8.62 us
    ppermute x6, waiting for transfers between devices, ring_gather(): from_ahead = tuple((lax.ppermute(a, 'seq', behind) for a in from_ahead))  8.45 us
    pallas_call x1, Pallas kernels, local(): pl.pallas_call(functools.partial(weight_kernel, shares=n_ch), out_shape=j...  6.9 us
  transfers between devices with their start and end apart: 31, of which 10 were waited for; matrix products, arithmetic and copies ran while one was open for 15% of the time, Pallas kernels for 9%

profile of v1, /device:TPU:0, one launch (start us, length us, event | category | flops | bytes accessed | tf_op | source)
XLA Modules:
  0.0 143.6 jit_solution(12807231544236989168)
XLA Ops:
  0.6 2.0 %fusion = (bf16[64,2048]{1,0:T(8,128)(2,1)}, bf16[64,2048]{1,0:T(8,128)(2,1)}) fusion(bf16[128,2048]{1,0:T(8,128)(2,1)} %param.9), kind=kLoop, calls=%fused_computation.25 | loop fusion | bytes 1048576 | tf_op jit(solution)/shard_map/slice | solution.py:236
  2.7 3.0 %collective-permute-start = (bf16[64,2048]{1,0:T(8,128)(2,1)}, bf16[64,2048]{1,0:T(8,128)(2,1)S(1)}, u32[]{:S(2)}, u32[]{:S(2)}) collective-permute-start(bf16[64,2048]{1,0:T(8,128)(2,1)} %get-tuple-element.65.refs_0_), channel_id=1, source_target_pairs={{0,8},{8,16},{16,24},{24,28},{28,20},{20,12},{12,4},{4,0},{1,9},{9... | collective-permute-start | bytes 786440 | tf_op jit(solution)/shard_map/ppermute | solution.py:240
  5.7 2.0 %collective-permute-start.1 = (bf16[64,2048]{1,0:T(8,128)(2,1)}, bf16[64,2048]{1,0:T(8,128)(2,1)}, u32[]{:S(2)}, u32[]{:S(2)}) collective-permute-start(bf16[64,2048]{1,0:T(8,128)(2,1)} %get-tuple-element.64.refs_1_), channel_id=1, source_target_pairs={{0,8},{8,16},{16,24},{24,28},{28,20},{20,12},{12,4},{4,0},{1,9},{9... | collective-permute-start | bytes 786440 | tf_op jit(solution)/shard_map/ppermute | solution.py:240
  8.3 1.9 %constant_dynamic-update-slice_fusion.14 = bf16[1024,2048]{1,0:T(8,128)(2,1)} fusion(bf16[128,2048]{1,0:T(8,128)(2,1)} %param.9), kind=kLoop, calls=%fused_computation.15 | loop fusion | bytes 1048576
  10.2 2.7 %collective-permute-done.refs_2_ = bf16[64,2048]{1,0:T(8,128)(2,1)S(1)} collective-permute-done((bf16[64,2048]{1,0:T(8,128)(2,1)}, bf16[64,2048]{1,0:T(8,128)(2,1)S(1)}, u32[]{:S(2)}, u32[]{:S(2)}) %collective-permute-start) | collective-permute-done | bytes 262176 | tf_op jit(solution)/shard_map/ppermute | solution.py:240
  12.9 4.9 %collective-permute-done.1.refs_3_ = bf16[64,2048]{1,0:T(8,128)(2,1)} collective-permute-done((bf16[64,2048]{1,0:T(8,128)(2,1)}, bf16[64,2048]{1,0:T(8,128)(2,1)}, u32[]{:S(2)}, u32[]{:S(2)}) %collective-permute-start.1) | collective-permute-done | bytes 262176 | tf_op jit(solution)/shard_map/ppermute | solution.py:240
  23.7 6.2 %all-to-all-start = ((bf16[8,56,128]{2,1,0:T(8,128)(2,1)}), bf16[8,56,128]{2,1,0:T(8,128)(2,1)}, u32[]{:S(2)}, u32[]{:S(2)}) async-start(bf16[8,56,128]{2,1,0:T(8,128)(2,1)} %copy-done.6), calls=%async_computation | async-start | bytes 229376 | tf_op jit(solution)/shard_map/all_to_all | solution.py:286
  29.9 1.9 %collective-permute-start.24 = (f32[56,33]{1,0:T(8,128)}, f32[56,33]{1,0:T(8,128)S(1)}, u32[]{:S(2)}, u32[]{:S(2)}) collective-permute-start(f32[56,33]{1,0:T(8,128)} %copy-done.20), channel_id=1, source_target_pairs={{0,0},{4,1},{8,2},{12,3},{16,4},{20,5},{24,6},{28,7},{1,8},{5,9},{... | collective-permute-start | bytes 22184 | tf_op jit(solution)/shard_map/ppermute | solution.py:285
  32.5 3.2 %collective-permute-start.7 = (bf16[64,2048]{1,0:T(8,128)(2,1)S(1)}, bf16[64,2048]{1,0:T(8,128)(2,1)S(1)}, u32[]{:S(2)}, u32[]{:S(2)}) collective-permute-start(bf16[64,2048]{1,0:T(8,128)(2,1)S(1)} %collective-permute-done.refs_2_), channel_id=1, source_target_pairs={{0,8},{8,16},{16,24},{24,28},{28,20},{20,12},{12,4},{4,0},{1,9},{9... | collective-permute-start | bytes 786440 | tf_op jit(solution)/shard_map/ppermute | solution.py:240
  35.8 1.9 %collective-permute-start.8 = (bf16[64,2048]{1,0:T(8,128)(2,1)}, bf16[64,2048]{1,0:T(8,128)(2,1)S(1)}, u32[]{:S(2)}, u32[]{:S(2)}) collective-permute-start(bf16[64,2048]{1,0:T(8,128)(2,1)} %collective-permute-done.1.refs_3_), channel_id=1, source_target_pairs={{0,8},{8,16},{16,24},{24,28},{28,20},{20,12},{12,4},{4,0},{1,9},{9... | collective-permute-start | bytes 786440 | tf_op jit(solution)/shard_map/ppermute | solution.py:240
  37.8 1.7 %constant_dynamic-update-slice_fusion.12 = bf16[1024,2048]{1,0:T(8,128)(2,1)} fusion(bf16[1024,2048]{1,0:T(8,128)(2,1)} %constant_dynamic-update-slice_fusion.13, bf16[64,2048]{1,0:T(8,128)(2,1)} %collective-permute-done.1.refs_3_), kind=kLoop, calls=%fused_computation.13 | loop fusion | bytes 524288
  41.6 3.6 %shard_map.120 = (f32[3,56,384]{2,1,0:T(8,128)S(1)}, bf16[3,56,384]{2,1,0:T(8,128)(2,1)}, bf16[3,56,384]{2,1,0:T(8,128)(2,1)}, bf16[3,56,384]{2,1,0:T(8,128)(2,1)}) custom-call(s32[2]{0:T(128)S(1)} %copy-done.10, bf16[3,208,2048]{2,1,0:T(8,128)(2,1)S(1)} %bitcast.25, bf16[64,2048]{1,0:T(8,128)(2,1)} %get-tuple-element.65.refs_0_, ...), custom_call_target="tpu_custom_call" | custom-call | flops 981467136 | bytes 4773896 | tf_op jit(solution)/shard_map/pallas_call | solution.py:218
  46.9 2.4 %collective-permute-start.11 = (bf16[64,2048]{1,0:T(8,128)(2,1)S(1)}, bf16[64,2048]{1,0:T(8,128)(2,1)}, u32[]{:S(2)}, u32[]{:S(2)}) collective-permute-start(bf16[64,2048]{1,0:T(8,128)(2,1)S(1)} %collective-permute-done.7.refs_0_), channel_id=1, source_target_pairs={{0,8},{8,16},{16,24},{24,28},{28,20},{20,12},{12,4},{4,0},{1,9},{9... | collective-permute-start | bytes 786440 | tf_op jit(solution)/shard_map/ppermute | solution.py:240
  49.3 2.0 %collective-permute-start.12 = (bf16[64,2048]{1,0:T(8,128)(2,1)S(1)}, bf16[64,2048]{1,0:T(8,128)(2,1)S(1)}, u32[]{:S(2)}, u32[]{:S(2)}) collective-permute-start(bf16[64,2048]{1,0:T(8,128)(2,1)S(1)} %collective-permute-done.8.refs_1_), channel_id=1, source_target_pairs={{0,8},{8,16},{16,24},{24,28},{28,20},{20,12},{12,4},{4,0},{1,9},{9... | collective-permute-start | bytes 786440 | tf_op jit(solution)/shard_map/ppermute | solution.py:240
  55.2 2.6 %collective-permute-start.18 = (bf16[64,2048]{1,0:T(8,128)(2,1)}, bf16[64,2048]{1,0:T(8,128)(2,1)S(1)}, u32[]{:S(2)}, u32[]{:S(2)}) collective-permute-start(bf16[64,2048]{1,0:T(8,128)(2,1)} %collective-permute-done.11.refs_4_), channel_id=1, source_target_pairs={{0,8},{8,16},{16,24},{24,28},{28,20},{20,12},{12,4},{4,0},{1,9},{9... | collective-permute-start | bytes 786440 | tf_op jit(solution)/shard_map/ppermute | solution.py:244
  57.8 8.0 %collective-permute-done.14.refs_7_ = bf16[64,2048]{1,0:T(8,128)(2,1)} collective-permute-done((bf16[64,2048]{1,0:T(8,128)(2,1)S(1)}, bf16[64,2048]{1,0:T(8,128)(2,1)}, u32[]{:S(2)}, u32[]{:S(2)}) %collective-permute-start.14) | collective-permute-done | bytes 262176 | tf_op jit(solution)/shard_map/ppermute | solution.py:241
  66.7 1.9 %collective-permute-start.5 = (bf16[3,56,384]{2,1,0:T(8,128)(2,1)}, bf16[3,56,384]{2,1,0:T(8,128)(2,1)}, u32[]{:S(2)}, u32[]{:S(2)}) collective-permute-start(bf16[3,56,384]{2,1,0:T(8,128)(2,1)} %get-tuple-element.38), channel_id=1, source_target_pairs={{0,2},{1,3},{2,0},{3,1},{4,6},{5,7},{6,4},{7,5},{8,10},{9,11},{10,... | collective-permute-start | bytes 387080 | tf_op jit(solution)/shard_map/ppermute | solution.py:316
  68.7 3.2 %shard_map.121 = (f32[3,56,512]{2,1,0:T(8,128)S(1)}, bf16[3,56,512]{2,1,0:T(8,128)(2,1)S(1)}, bf16[3,56,512]{2,1,0:T(8,128)(2,1)S(1)}, bf16[3,56,512]{2,1,0:T(8,128)(2,1)S(1)}) custom-call(s32[2]{0:T(128)S(1)} %copy-done.11, bf16[3,208,2048]{2,1,0:T(8,128)(2,1)S(1)} %bitcast.26, bf16[64,2048]{1,0:T(8,128)(2,1)S(1)} %collective-permute-done.7.refs_0_, ...), custom_call_target="tpu_custom_call" | custom-call | flops 1308622848 | bytes 5513224 | tf_op jit(solution)/shard_map/pallas_call | solution.py:218
  76.2 1.8 %collective-permute-start.15 = (bf16[3,56,512]{2,1,0:T(8,128)(2,1)}, bf16[3,56,512]{2,1,0:T(8,128)(2,1)S(1)}, u32[]{:S(2)}, u32[]{:S(2)}) collective-permute-start(bf16[3,56,512]{2,1,0:T(8,128)(2,1)} %copy-done.19), channel_id=1, source_target_pairs={{0,1},{1,2},{2,3},{3,0},{4,5},{5,6},{6,7},{7,4},{8,9},{9,10},{10,1... | collective-permute-start | bytes 516104 | tf_op jit(solution)/shard_map/ppermute | solution.py:316
  78.0 1.7 %constant_dynamic-update-slice_fusion.5 = bf16[1024,2048]{1,0:T(8,128)(2,1)} fusion(bf16[1024,2048]{1,0:T(8,128)(2,1)} %constant_dynamic-update-slice_fusion.6, bf16[64,2048]{1,0:T(8,128)(2,1)} %collective-permute-done.11.refs_4_), kind=kLoop, calls=%fused_computation.6 | loop fusion | bytes 524288
  81.0 2.6 %collective-permute-start.16 = (bf16[3,56,512]{2,1,0:T(8,128)(2,1)}, bf16[3,56,512]{2,1,0:T(8,128)(2,1)S(1)}, u32[]{:S(2)}, u32[]{:S(2)}) collective-permute-start(bf16[3,56,512]{2,1,0:T(8,128)(2,1)} %copy-done.18), channel_id=1, source_target_pairs={{0,2},{1,3},{2,0},{3,1},{4,6},{5,7},{6,4},{7,5},{8,10},{9,11},{10,... | collective-permute-start | bytes 516104 | tf_op jit(solution)/shard_map/ppermute | solution.py:316
  87.1 1.7 %constant_dynamic-update-slice_fusion.4 = bf16[1024,2048]{1,0:T(8,128)(2,1)} fusion(bf16[1024,2048]{1,0:T(8,128)(2,1)} %constant_dynamic-update-slice_fusion.5, bf16[64,2048]{1,0:T(8,128)(2,1)} %copy-done.5), kind=kLoop, calls=%fused_computation.5 | loop fusion | bytes 524288
  88.8 2.0 %collective-permute-done.17.refs_7_ = bf16[3,56,512]{2,1,0:T(8,128)(2,1)S(1)} collective-permute-done((bf16[3,56,512]{2,1,0:T(8,128)(2,1)S(1)}, bf16[3,56,512]{2,1,0:T(8,128)(2,1)S(1)}, u32[]{:S(2)}, u32[]{:S(2)}) %collective-permute-start.17) | collective-permute-done | bytes 172064 | tf_op jit(solution)/shard_map/ppermute | solution.py:316
  92.3 1.6 %copy-done.2 = bf16[1024,1024]{1,0:T(8,128)(2,1)S(1)} copy-done((bf16[1024,1024]{1,0:T(8,128)(2,1)S(1)}, bf16[1024,1024]{1,0:T(8,128)(2,1)}, u32[]{:S(2)}) %copy-start.2) | copy-done | bytes 2097176
  93.9 1.6 %copy-done.4 = bf16[1024,1024]{1,0:T(8,128)(2,1)S(1)} copy-done((bf16[1024,1024]{1,0:T(8,128)(2,1)S(1)}, bf16[1024,1024]{1,0:T(8,128)(2,1)}, u32[]{:S(2)}) %copy-start.4) | copy-done | bytes 2097176
  99.3 3.7 %shard_map.125 = (bf16[3,56,1024]{2,1,0:T(8,128)(2,1)S(1)}, f32[56,1024]{1,0:T(8,128)S(1)}, f32[56,1024]{1,0:T(8,128)S(1)}, f32[56,1]{1,0:T(8,128)S(1)}) custom-call(s32[2]{0:T(128)S(1)} %copy-done.11, f32[3,56,384]{2,1,0:T(8,128)S(1)} %copy-done.13, bf16[3,56,384]{2,1,0:T(8,128)(2,1)} %collective-permute-done.4.refs_1_, ...), custom_call_target="tpu_custom_call" | custom-call | flops 1879048192 | bytes 7306696 | tf_op jit(solution)/shard_map/pallas_call | solution.py:218
  105.4 1.7 %constant_dynamic-update-slice_fusion.2 = bf16[1024,2048]{1,0:T(8,128)(2,1)} fusion(bf16[1024,2048]{1,0:T(8,128)(2,1)} %constant_dynamic-update-slice_fusion.3, bf16[64,2048]{1,0:T(8,128)(2,1)} %collective-permute-done.14.refs_7_), kind=kLoop, calls=%fused_computation.3 | loop fusion | bytes 524288
  107.1 2.0 %shard_map.126 = f32[56,33]{1,0:T(8,128)S(1)} custom-call(f32[56,33]{1,0:T(8,128)S(1)} %collective-permute-done.24.poles_ref.refs_13_, f32[56,1024]{1,0:T(8,128)S(1)} %get-tuple-element.58.tgc_ref, f32[56,1024]{1,0:T(8,128)S(1)} %get-tuple-element.59.tgs_ref, bf16[1024,1024]{1,0:T(8,128)(2,1)S(1)} %copy-done.2, bf16[1024,1024]{1,0:T(8,128)(2,1)S(1)} %copy-done.4, ...), custom_call_target="tpu_custom_call" | custom-call | flops 469762048 | bytes 4668064 | tf_op jit(solution)/shard_map/pallas_call | solution.py:218
  109.1 4.3 %collective-permute-done.26.refs_1_ = bf16[3,56,1024]{2,1,0:T(8,128)(2,1)S(1)} collective-permute-done((bf16[3,56,1024]{2,1,0:T(8,128)(2,1)S(1)}, bf16[3,56,1024]{2,1,0:T(8,128)(2,1)S(1)}, u32[]{:S(2)}, u32[]{:S(2)}) %collective-permute-start.26) | collective-permute-done | bytes 344096 | tf_op jit(solution)/shard_map/ppermute | solution.py:334
  115.8 11.2 %all-to-all-start.1 = ((f32[8,1,1848]{2,1,0:T(1,128)}), f32[8,1,1848]{2,1,0:T(1,128)S(1)}, u32[]{:S(2)}, u32[]{:S(2)}) async-start(f32[8,1,1848]{2,1,0:T(1,128)} %reshape.9), calls=%async_computation.1 | async-start | bytes 122880 | tf_op jit(solution)/shard_map/all_to_all | solution.py:375
  127.7 6.1 %all-to-all-done.1 = f32[8,1,1848]{2,1,0:T(1,128)S(1)} async-done(((f32[8,1,1848]{2,1,0:T(1,128)}), f32[8,1,1848]{2,1,0:T(1,128)S(1)}, u32[]{:S(2)}, u32[]{:S(2)}) %all-to-all-start.1) | async-done | bytes 59168 | tf_op jit(solution)/shard_map/all_to_all | solution.py:375
  136.7 6.9 %shard_map.127 = f32[3,208,2048]{2,1,0:T(8,128)} custom-call(s32[2]{0:T(128)S(1)} %copy-done.11, bf16[3,56,1024]{2,1,0:T(8,128)(2,1)S(1)} %get-tuple-element.56.refs_0_, bf16[3,56,1024]{2,1,0:T(8,128)(2,1)S(1)} %collective-permute-done.26.refs_1_, bf16[3,56,1024]{2,1,0:T(8,128)(2,1)S(1)} %collective-permute-done.25.refs_2_, ...), custom_call_target="tpu_custom_call" | custom-call | flops 2617245696 | bytes 10584064 | tf_op jit(solution)/shard_map/pallas_call | solution.py:350
  (114 shorter events, 38.7 us)
Async XLA Ops:
  0.6 40.4 %copy-start = (bf16[208,3,2048]{2,0,1:T(8,128)(2,1)S(1)}, bf16[208,3,2048]{2,0,1:T(8,128)(2,1)}, u32[]{:S(2)}) copy-start(bf16[208,3,2048]{2,0,1:T(8,128)(2,1)} %param.10) | copy-start | bytes 7667716
  2.7 10.3 %collective-permute-start = (bf16[64,2048]{1,0:T(8,128)(2,1)}, bf16[64,2048]{1,0:T(8,128)(2,1)S(1)}, u32[]{:S(2)}, u32[]{:S(2)}) collective-permute-start(bf16[64,2048]{1,0:T(8,128)(2,1)} %get-tuple-element.65.refs_0_), channel_id=1, source_target_pairs={{0,8},{8,16},{16,24},{24,28},{28,20},{20,12},{12,4},{4,0},{1,9},{9... | collective-permute-start | bytes 786440 | tf_op jit(solution)/shard_map/ppermute | solution.py:240
  5.7 32.0 %collective-permute-start.2 = (bf16[64,2048]{1,0:T(8,128)(2,1)}, bf16[64,2048]{1,0:T(8,128)(2,1)S(1)}, u32[]{:S(2)}, u32[]{:S(2)}) collective-permute-start(bf16[64,2048]{1,0:T(8,128)(2,1)} %get-tuple-element.65.refs_0_), channel_id=1, source_target_pairs={{8,0},{16,8},{24,16},{28,24},{20,28},{12,20},{4,12},{0,4},{9,1},{1... | collective-permute-start | bytes 786440 | tf_op jit(solution)/shard_map/ppermute | solution.py:241
  5.7 12.1 %collective-permute-start.1 = (bf16[64,2048]{1,0:T(8,128)(2,1)}, bf16[64,2048]{1,0:T(8,128)(2,1)}, u32[]{:S(2)}, u32[]{:S(2)}) collective-permute-start(bf16[64,2048]{1,0:T(8,128)(2,1)} %get-tuple-element.64.refs_1_), channel_id=1, source_target_pairs={{0,8},{8,16},{16,24},{24,28},{28,20},{20,12},{12,4},{4,0},{1,9},{9... | collective-permute-start | bytes 786440 | tf_op jit(solution)/shard_map/ppermute | solution.py:240
  7.7 31.8 %collective-permute-start.3 = (bf16[64,2048]{1,0:T(8,128)(2,1)}, bf16[64,2048]{1,0:T(8,128)(2,1)S(1)}, u32[]{:S(2)}, u32[]{:S(2)}) collective-permute-start(bf16[64,2048]{1,0:T(8,128)(2,1)} %get-tuple-element.64.refs_1_), channel_id=1, source_target_pairs={{8,0},{16,8},{24,16},{28,24},{20,28},{12,20},{4,12},{0,4},{9,1},{1... | collective-permute-start | bytes 786440 | tf_op jit(solution)/shard_map/ppermute | solution.py:241
  23.7 51.0 %all-to-all-start = ((bf16[8,56,128]{2,1,0:T(8,128)(2,1)}), bf16[8,56,128]{2,1,0:T(8,128)(2,1)}, u32[]{:S(2)}, u32[]{:S(2)}) async-start(bf16[8,56,128]{2,1,0:T(8,128)(2,1)} %copy-done.6), calls=%async_computation | async-start | bytes 229376 | tf_op jit(solution)/shard_map/all_to_all | solution.py:286
  29.9 15.3 %collective-permute-start.24 = (f32[56,33]{1,0:T(8,128)}, f32[56,33]{1,0:T(8,128)S(1)}, u32[]{:S(2)}, u32[]{:S(2)}) collective-permute-start(f32[56,33]{1,0:T(8,128)} %copy-done.20), channel_id=1, source_target_pairs={{0,0},{4,1},{8,2},{12,3},{16,4},{20,5},{24,6},{28,7},{1,8},{5,9},{... | collective-permute-start | bytes 22184 | tf_op jit(solution)/shard_map/ppermute | solution.py:285
  32.5 14.3 %collective-permute-start.7 = (bf16[64,2048]{1,0:T(8,128)(2,1)S(1)}, bf16[64,2048]{1,0:T(8,128)(2,1)S(1)}, u32[]{:S(2)}, u32[]{:S(2)}) collective-permute-start(bf16[64,2048]{1,0:T(8,128)(2,1)S(1)} %collective-permute-done.refs_2_), channel_id=1, source_target_pairs={{0,8},{8,16},{16,24},{24,28},{28,20},{20,12},{12,4},{4,0},{1,9},{9... | collective-permute-start | bytes 786440 | tf_op jit(solution)/shard_map/ppermute | solution.py:240
  35.8 13.5 %collective-permute-start.8 = (bf16[64,2048]{1,0:T(8,128)(2,1)}, bf16[64,2048]{1,0:T(8,128)(2,1)S(1)}, u32[]{:S(2)}, u32[]{:S(2)}) collective-permute-start(bf16[64,2048]{1,0:T(8,128)(2,1)} %collective-permute-done.1.refs_3_), channel_id=1, source_target_pairs={{0,8},{8,16},{16,24},{24,28},{28,20},{20,12},{12,4},{4,0},{1,9},{9... | collective-permute-start | bytes 786440 | tf_op jit(solution)/shard_map/ppermute | solution.py:240
  37.7 13.6 %collective-permute-start.9 = (bf16[64,2048]{1,0:T(8,128)(2,1)S(1)}, bf16[64,2048]{1,0:T(8,128)(2,1)S(1)}, u32[]{:S(2)}, u32[]{:S(2)}) collective-permute-start(bf16[64,2048]{1,0:T(8,128)(2,1)S(1)} %collective-permute-done.2.refs_4_), channel_id=1, source_target_pairs={{8,0},{16,8},{24,16},{28,24},{20,28},{12,20},{4,12},{0,4},{9,1},{1... | collective-permute-start | bytes 786440 | tf_op jit(solution)/shard_map/ppermute | solution.py:241
  39.5 12.3 %collective-permute-start.10 = (bf16[64,2048]{1,0:T(8,128)(2,1)S(1)}, bf16[64,2048]{1,0:T(8,128)(2,1)S(1)}, u32[]{:S(2)}, u32[]{:S(2)}) collective-permute-start(bf16[64,2048]{1,0:T(8,128)(2,1)S(1)} %collective-permute-done.3.refs_5_), channel_id=1, source_target_pairs={{8,0},{16,8},{24,16},{28,24},{20,28},{12,20},{4,12},{0,4},{9,1},{1... | collective-permute-start | bytes 786440 | tf_op jit(solution)/shard_map/ppermute | solution.py:241
  45.2 35.8 %collective-permute-start.4 = (bf16[3,56,384]{2,1,0:T(8,128)(2,1)}, bf16[3,56,384]{2,1,0:T(8,128)(2,1)}, u32[]{:S(2)}, u32[]{:S(2)}) collective-permute-start(bf16[3,56,384]{2,1,0:T(8,128)(2,1)} %get-tuple-element.37), channel_id=1, source_target_pairs={{0,1},{1,2},{2,3},{3,0},{4,5},{5,6},{6,7},{7,4},{8,9},{9,10},{10,1... | collective-permute-start | bytes 387080 | tf_op jit(solution)/shard_map/ppermute | solution.py:316
  46.9 8.3 %collective-permute-start.11 = (bf16[64,2048]{1,0:T(8,128)(2,1)S(1)}, bf16[64,2048]{1,0:T(8,128)(2,1)}, u32[]{:S(2)}, u32[]{:S(2)}) collective-permute-start(bf16[64,2048]{1,0:T(8,128)(2,1)S(1)} %collective-permute-done.7.refs_0_), channel_id=1, source_target_pairs={{0,8},{8,16},{16,24},{24,28},{28,20},{20,12},{12,4},{4,0},{1,9},{9... | collective-permute-start | bytes 786440 | tf_op jit(solution)/shard_map/ppermute | solution.py:240
  49.3 17.4 %collective-permute-start.12 = (bf16[64,2048]{1,0:T(8,128)(2,1)S(1)}, bf16[64,2048]{1,0:T(8,128)(2,1)S(1)}, u32[]{:S(2)}, u32[]{:S(2)}) collective-permute-start(bf16[64,2048]{1,0:T(8,128)(2,1)S(1)} %collective-permute-done.8.refs_1_), channel_id=1, source_target_pairs={{0,8},{8,16},{16,24},{24,28},{28,20},{20,12},{12,4},{4,0},{1,9},{9... | collective-permute-start | bytes 786440 | tf_op jit(solution)/shard_map/ppermute | solution.py:240
  51.3 17.3 %collective-permute-start.13 = (bf16[64,2048]{1,0:T(8,128)(2,1)S(1)}, bf16[64,2048]{1,0:T(8,128)(2,1)S(1)}, u32[]{:S(2)}, u32[]{:S(2)}) collective-permute-start(bf16[64,2048]{1,0:T(8,128)(2,1)S(1)} %collective-permute-done.9.refs_2_), channel_id=1, source_target_pairs={{8,0},{16,8},{24,16},{28,24},{20,28},{12,20},{4,12},{0,4},{9,1},{1... | collective-permute-start | bytes 786440 | tf_op jit(solution)/shard_map/ppermute | solution.py:241
  51.8 14.0 %collective-permute-start.14 = (bf16[64,2048]{1,0:T(8,128)(2,1)S(1)}, bf16[64,2048]{1,0:T(8,128)(2,1)}, u32[]{:S(2)}, u32[]{:S(2)}) collective-permute-start(bf16[64,2048]{1,0:T(8,128)(2,1)S(1)} %collective-permute-done.10.refs_3_), channel_id=1, source_target_pairs={{8,0},{16,8},{24,16},{28,24},{20,28},{12,20},{4,12},{0,4},{9,1},{1... | collective-permute-start | bytes 786440 | tf_op jit(solution)/shard_map/ppermute | solution.py:241
  55.2 19.5 %collective-permute-start.18 = (bf16[64,2048]{1,0:T(8,128)(2,1)}, bf16[64,2048]{1,0:T(8,128)(2,1)S(1)}, u32[]{:S(2)}, u32[]{:S(2)}) collective-permute-start(bf16[64,2048]{1,0:T(8,128)(2,1)} %collective-permute-done.11.refs_4_), channel_id=1, source_target_pairs={{0,8},{8,16},{16,24},{24,28},{28,20},{20,12},{12,4},{4,0},{1,9},{9... | collective-permute-start | bytes 786440 | tf_op jit(solution)/shard_map/ppermute | solution.py:244
  65.8 10.4 %collective-permute-start.19 = (bf16[64,2048]{1,0:T(8,128)(2,1)}, bf16[64,2048]{1,0:T(8,128)(2,1)S(1)}, u32[]{:S(2)}, u32[]{:S(2)}) collective-permute-start(bf16[64,2048]{1,0:T(8,128)(2,1)} %collective-permute-done.14.refs_7_), channel_id=1, source_target_pairs={{8,0},{16,8},{24,16},{28,24},{20,28},{12,20},{4,12},{0,4},{9,1},{1... | collective-permute-start | bytes 786440 | tf_op jit(solution)/shard_map/ppermute | solution.py:244
  66.7 16.9 %collective-permute-start.5 = (bf16[3,56,384]{2,1,0:T(8,128)(2,1)}, bf16[3,56,384]{2,1,0:T(8,128)(2,1)}, u32[]{:S(2)}, u32[]{:S(2)}) collective-permute-start(bf16[3,56,384]{2,1,0:T(8,128)(2,1)} %get-tuple-element.38), channel_id=1, source_target_pairs={{0,2},{1,3},{2,0},{3,1},{4,6},{5,7},{6,4},{7,5},{8,10},{9,11},{10,... | collective-permute-start | bytes 387080 | tf_op jit(solution)/shard_map/ppermute | solution.py:316
  68.6 16.5 %collective-permute-start.6 = (bf16[3,56,384]{2,1,0:T(8,128)(2,1)}, bf16[3,56,384]{2,1,0:T(8,128)(2,1)}, u32[]{:S(2)}, u32[]{:S(2)}) collective-permute-start(bf16[3,56,384]{2,1,0:T(8,128)(2,1)} %get-tuple-element.39), channel_id=1, source_target_pairs={{0,3},{1,0},{2,1},{3,2},{4,7},{5,4},{6,5},{7,6},{8,11},{9,8},{10,9... | collective-permute-start | bytes 387080 | tf_op jit(solution)/shard_map/ppermute | solution.py:316
  74.7 10.4 %collective-permute-start.23 = (bf16[8,56,128]{2,1,0:T(8,128)(2,1)}, bf16[8,56,128]{2,1,0:T(8,128)(2,1)S(1)}, u32[]{:S(2)}, u32[]{:S(2)}) collective-permute-start(bf16[8,56,128]{2,1,0:T(8,128)(2,1)} %all-to-all-done), channel_id=1, source_target_pairs={{0,0},{4,1},{8,2},{12,3},{16,4},{20,5},{24,6},{28,7},{1,8},{5,9},{... | collective-permute-start | bytes 344072 | tf_op jit(solution)/shard_map/ppermute | solution.py:287
  76.2 9.3 %collective-permute-start.15 = (bf16[3,56,512]{2,1,0:T(8,128)(2,1)}, bf16[3,56,512]{2,1,0:T(8,128)(2,1)S(1)}, u32[]{:S(2)}, u32[]{:S(2)}) collective-permute-start(bf16[3,56,512]{2,1,0:T(8,128)(2,1)} %copy-done.19), channel_id=1, source_target_pairs={{0,1},{1,2},{2,3},{3,0},{4,5},{5,6},{6,7},{7,4},{8,9},{9,10},{10,1... | collective-permute-start | bytes 516104 | tf_op jit(solution)/shard_map/ppermute | solution.py:316
  81.0 7.7 %collective-permute-start.16 = (bf16[3,56,512]{2,1,0:T(8,128)(2,1)}, bf16[3,56,512]{2,1,0:T(8,128)(2,1)S(1)}, u32[]{:S(2)}, u32[]{:S(2)}) collective-permute-start(bf16[3,56,512]{2,1,0:T(8,128)(2,1)} %copy-done.18), channel_id=1, source_target_pairs={{0,2},{1,3},{2,0},{3,1},{4,6},{5,7},{6,4},{7,5},{8,10},{9,11},{10,... | collective-permute-start | bytes 516104 | tf_op jit(solution)/shard_map/ppermute | solution.py:316
  83.6 7.2 %collective-permute-start.17 = (bf16[3,56,512]{2,1,0:T(8,128)(2,1)S(1)}, bf16[3,56,512]{2,1,0:T(8,128)(2,1)S(1)}, u32[]{:S(2)}, u32[]{:S(2)}) collective-permute-start(bf16[3,56,512]{2,1,0:T(8,128)(2,1)S(1)} %get-tuple-element.43), channel_id=1, source_target_pairs={{0,3},{1,0},{2,1},{3,2},{4,7},{5,4},{6,5},{7,6},{8,11},{9,8},{10,9... | collective-permute-start | bytes 516104 | tf_op jit(solution)/shard_map/ppermute | solution.py:316
  85.1 6.1 %collective-permute-start.20 = (bf16[3,56,128]{2,1,0:T(8,128)(2,1)S(1)}, bf16[3,56,128]{2,1,0:T(8,128)(2,1)S(1)}, u32[]{:S(2)}, u32[]{:S(2)}) collective-permute-start(bf16[3,56,128]{2,1,0:T(8,128)(2,1)S(1)} %get-tuple-element.45), channel_id=1, source_target_pairs={{0,1},{1,2},{2,3},{3,0},{4,5},{5,6},{6,7},{7,4},{8,9},{9,10},{10,1... | collective-permute-start | bytes 129032 | tf_op jit(solution)/shard_map/ppermute | solution.py:316
  85.1 7.2 %collective-permute-start.21 = (bf16[3,56,128]{2,1,0:T(8,128)(2,1)S(1)}, bf16[3,56,128]{2,1,0:T(8,128)(2,1)S(1)}, u32[]{:S(2)}, u32[]{:S(2)}) collective-permute-start(bf16[3,56,128]{2,1,0:T(8,128)(2,1)S(1)} %get-tuple-element.46), channel_id=1, source_target_pairs={{0,2},{1,3},{2,0},{3,1},{4,6},{5,7},{6,4},{7,5},{8,10},{9,11},{10,... | collective-permute-start | bytes 129032 | tf_op jit(solution)/shard_map/ppermute | solution.py:316
  85.5 6.8 %collective-permute-start.22 = (bf16[3,56,128]{2,1,0:T(8,128)(2,1)S(1)}, bf16[3,56,128]{2,1,0:T(8,128)(2,1)S(1)}, u32[]{:S(2)}, u32[]{:S(2)}) collective-permute-start(bf16[3,56,128]{2,1,0:T(8,128)(2,1)S(1)} %get-tuple-element.47), channel_id=1, source_target_pairs={{0,3},{1,0},{2,1},{3,2},{4,7},{5,4},{6,5},{7,6},{8,11},{9,8},{10,9... | collective-permute-start | bytes 129032 | tf_op jit(solution)/shard_map/ppermute | solution.py:316
  103.0 4.2 %collective-permute-start.25 = (bf16[3,56,1024]{2,1,0:T(8,128)(2,1)S(1)}, bf16[3,56,1024]{2,1,0:T(8,128)(2,1)S(1)}, u32[]{:S(2)}, u32[]{:S(2)}) collective-permute-start(bf16[3,56,1024]{2,1,0:T(8,128)(2,1)S(1)} %get-tuple-element.56.refs_0_), channel_id=1, source_target_pairs={{0,1},{1,0},{2,3},{3,2},{4,5},{5,4},{6,7},{7,6},{8,9},{9,8},{10,11... | collective-permute-start | bytes 1032200 | tf_op jit(solution)/shard_map/ppermute | solution.py:337
  103.3 10.2 %collective-permute-start.26 = (bf16[3,56,1024]{2,1,0:T(8,128)(2,1)S(1)}, bf16[3,56,1024]{2,1,0:T(8,128)(2,1)S(1)}, u32[]{:S(2)}, u32[]{:S(2)}) collective-permute-start(bf16[3,56,1024]{2,1,0:T(8,128)(2,1)S(1)} %get-tuple-element.56.refs_0_), channel_id=1, source_target_pairs={{0,2},{1,3},{2,0},{3,1},{4,6},{5,7},{6,4},{7,5},{8,10},{9,11},{10,... | collective-permute-start | bytes 1032200 | tf_op jit(solution)/shard_map/ppermute | solution.py:334
  113.5 1.4 collective-permute-start.28
  115.8 18.0 %all-to-all-start.1 = ((f32[8,1,1848]{2,1,0:T(1,128)}), f32[8,1,1848]{2,1,0:T(1,128)S(1)}, u32[]{:S(2)}, u32[]{:S(2)}) async-start(f32[8,1,1848]{2,1,0:T(1,128)} %reshape.9), calls=%async_computation.1 | async-start | bytes 122880 | tf_op jit(solution)/shard_map/all_to_all | solution.py:375
  127.7 9.0 %collective-permute-start.27 = (bf16[3,56,1024]{2,1,0:T(8,128)(2,1)S(1)}, bf16[3,56,1024]{2,1,0:T(8,128)(2,1)S(1)}, u32[]{:S(2)}, u32[]{:S(2)}) collective-permute-start(bf16[3,56,1024]{2,1,0:T(8,128)(2,1)S(1)} %collective-permute-done.26.refs_1_), channel_id=1, source_target_pairs={{0,1},{1,0},{2,3},{3,2},{4,5},{5,4},{6,7},{7,6},{8,9},{9,8},{10,11... | collective-permute-start | bytes 1032200 | tf_op jit(solution)/shard_map/ppermute | solution.py:346
  (22 other events, 156.0 us)

commit v2 on v1

--- a/solution.py
+++ b/solution.py
@@ -66,27 +66,43 @@
     return pl.multiple_of(jnp.minimum(index * part, rows - part), 8)
 
 
-def pack_kernel(place_ref, grad_ref, packed_ref, pieces_ref, poles_ref, *, rows, n_ch):
-    part = poles_ref.shape[0]
+def pieces_kernel(grad_ref, pieces_ref, *, rows, n_ch):
+    part = pieces_ref.shape[1]
     grad = grad_ref[...].astype(F32)
     for piece in range(pieces_ref.shape[0]):
         start = piece // n_ch * rows + min(piece % n_ch * part, rows - part)
         pieces_ref[piece] = grad[start : start + part].astype(BF16)
+
+
+def poles_kernel(place_ref, packed_ref, poles_ref, *, rows, n_ch):
+    part = poles_ref.shape[0]
     own = place_ref[0]
     start = own // n_ch * rows + part_start(own % n_ch, part, rows)
     poles_ref[...] = packed_ref[pl.ds(pl.multiple_of(start, 8), part), :]
 
 
+def fetch(sources, targets, semaphores):
+    copies = [
+        pltpu.make_async_copy(source, target, semaphores.at[i])
+        for i, (source, target) in enumerate(zip(sources, targets))
+    ]
+    for copy in copies:
+        copy.start()
+    for copy in copies:
+        copy.wait()
+
+
 def project_kernel(place_ref, weight_ref, *refs, pieces):
     feature_refs = refs[:pieces]
-    out_refs = refs[pieces:-2]
-    features_ref, sums_ref = refs[-2:]
+    out_refs = refs[pieces:-3]
+    features_ref, sums_ref, semaphores = refs[-3:]
     gates, _, _ = weight_ref.shape
     part = out_refs[0].shape[1]
-    row = 0
+    targets, row = [], 0
     for feature_ref in feature_refs:
-        features_ref[row : row + feature_ref.shape[0], :] = feature_ref[...]
+        targets.append(features_ref.at[pl.ds(row, feature_ref.shape[0]), :])
         row += feature_ref.shape[0]
+    fetch(feature_refs, targets, semaphores)
     for gate in range(gates):
         sums_ref[gate] = lax.dot_general(
             weight_ref[gate], features_ref[...], (((1,), (1,)), ((), ())),
@@ -111,13 +127,15 @@
     partial_refs = refs[: len(group_slots) * shares]
     (
         gout_ref, poles_ref, hc_ref, hs_ref, cos_ref, sin_ref, twist_ref,
-        grad_ref, tgc_ref, tgs_ref, skip_ref, proj_ref,
+        grad_ref, tgc_ref, tgs_ref, skip_ref, proj_ref, *scratch_refs,
     ) = refs[len(group_slots) * shares :]
+    *held_refs, semaphores = scratch_refs
+    fetch(partial_refs, held_refs, semaphores)
     rows, tokens = hc_ref.shape
     blocks, _, _, block_len = proj_ref.shape
     slot = 0
     for group, count in enumerate(group_slots):
-        own_ref, *other_refs = partial_refs[group * shares : (group + 1) * shares]
+        own_ref, *other_refs = held_refs[group * shares : (group + 1) * shares]
         total = own_ref[...]
         for other_ref in other_refs:
             total = total + other_ref[...].astype(F32)
@@ -188,7 +206,7 @@
 
 def weight_kernel(place_ref, *refs, shares):
     grad_refs = refs[:shares]
-    feature_ref, out_ref, wide_ref, rows_ref = refs[shares:]
+    *feature_refs, out_ref, wide_ref, rows_ref, features_ref = refs[shares:]
     gates = out_ref.shape[0]
     part = grad_refs[0].shape[1]
 
@@ -201,20 +219,28 @@
             wide_ref[:, pl.ds(start, part), :] = grad_ref[...].astype(F32)
         rows_ref[...] = wide_ref[...].astype(BF16)
 
+    row = 0
+    for feature_ref in feature_refs:
+        features_ref[row : row + feature_ref.shape[0], :] = feature_ref[...]
+        row += feature_ref.shape[0]
     for gate in range(gates):
-        out_ref[gate] = dot(rows_ref[gate], feature_ref[...])
-
-
-def call(kernel, outs, flops, transcendentals, *operands, scratch=(), indexed=False):
+        out_ref[gate] = dot(rows_ref[gate], features_ref[...])
+
+
+def call(kernel, outs, flops, transcendentals, *operands, scratch=(), indexed=False, late=()):
     size = sum(a.size * a.dtype.itemsize for a in operands) + sum(
         o.size * o.dtype.itemsize for o in outs
     )
     scratch_size = sum(math.prod(a.shape) * a.dtype.itemsize for a in scratch)
+    if late:
+        scratch = [*scratch, pltpu.SemaphoreType.DMA((len(late),))]
     limit = min(56 * MIB, 2 * (size + scratch_size) + 8 * MIB)
     whole = pl.BlockSpec(memory_space=pltpu.VMEM)
     specs = [whole] * len(operands)
     if indexed:
         specs[0] = pl.BlockSpec(memory_space=pltpu.SMEM)
+    for operand in late:
+        specs[operand] = pl.BlockSpec(memory_space=pltpu.HBM)
     return pl.pallas_call(
         kernel,
         out_shape=outs,
@@ -228,22 +254,9 @@
     )(*operands)
 
 
-def ring_gather(features, ring):
-    count = len(ring)
-    half = features.shape[0] // 2
-    ahead = [(ring[i], ring[(i + 1) % count]) for i in range(count)]
-    behind = [(b, a) for a, b in ahead]
-    own = (features[:half], features[half:])
-    slots = [own]
-    from_behind, from_ahead = own, own
-    for _ in range(count // 2 - 1):
-        from_behind = tuple(lax.ppermute(a, "seq", ahead) for a in from_behind)
-        from_ahead = tuple(lax.ppermute(a, "seq", behind) for a in from_ahead)
-        slots += [from_behind, from_ahead]
-    slots.append(
-        (lax.ppermute(from_behind[0], "seq", ahead), lax.ppermute(from_ahead[1], "seq", behind))
-    )
-    return slots
+def ring_routes(ring):
+    ahead = [(a, ring[(i + 1) % len(ring)]) for i, a in enumerate(ring)]
+    return ahead, [(b, a) for a, b in ahead]
 
 
 def local(features, qkv_weight, grad_out, residues, log_rates, skip_gain):
@@ -263,44 +276,18 @@
     place = jnp.stack([seq_index, ch_index]).astype(jnp.int32)
 
     ring = list(range(0, n_seq, 2)) + list(range(n_seq - 1, 0, -2))
-    slots = ring_gather(features, ring)
-
-    first = slots[1]
-    grad_out, residues, log_rates, skip_gain, first = lax.optimization_barrier(
-        (grad_out, residues, log_rates, skip_gain, first)
-    )
-    slots[1] = first
-
-    spread = [((q % n_seq) * n_ch + q // n_seq, q) for q in range(n_seq * n_ch)]
-    gather_back = [(b, a) for a, b in spread]
-    packed = jnp.concatenate([residues, log_rates, skip_gain[:, None]], 1)
-    upper, poles = call(
-        functools.partial(pack_kernel, rows=rows, n_ch=n_ch),
-        (
-            jax.ShapeDtypeStruct((n_seq, part, block_len), BF16),
-            jax.ShapeDtypeStruct((part, packed.shape[1]), F32),
-        ),
-        0, 0, place, grad_out, packed, indexed=True,
-    )
-    poles = lax.ppermute(poles, ("seq", "ch"), spread)
-    upper = lax.all_to_all(upper, "seq", split_axis=0, concat_axis=0, tiled=True)
-    upper = lax.ppermute(upper, ("seq", "ch"), spread)
+    ahead, behind = ring_routes(ring)
+
+    def send_on(pair):
+        return lax.ppermute(pair[0], "seq", ahead), lax.ppermute(pair[1], "seq", behind)
 
     square = part * tokens * tokens
     spectrum = jax.ShapeDtypeStruct((part, tokens), F32)
-    hc, hs = call(
-        functools.partial(taps_kernel, order=order), (spectrum, spectrum),
-        8 * square, part * tokens * order, poles, cos_table, sin_table, twist,
-    )
-
     weight = qkv_weight.transpose(1, 0, 2)
-    groups = [slots[:3]] + [slots[i : i + 4] for i in range(3, n_seq - 1, 4)] + [slots[n_seq - 1 :]]
-    group_slots = [len(group) for group in groups]
-    partials = []
-    for group in groups:
-        pieces = [piece for slot in group for piece in slot]
-        span = len(group) * block_len
-        sums = call(
+
+    def project(pieces):
+        span = sum(piece.shape[0] for piece in pieces)
+        return call(
             functools.partial(project_kernel, pieces=len(pieces)),
             [
                 jax.ShapeDtypeStruct((gates, part, span), F32 if d == 0 else BF16)
@@ -308,13 +295,58 @@
             ],
             2 * gates * rows * width * span, 0, place, weight, *pieces,
             scratch=[pltpu.VMEM((span, width), BF16), pltpu.VMEM((gates, rows, span), F32)],
-            indexed=True,
+            indexed=True, late=range(2, 2 + len(pieces)),
         )
-        partials.append(sums[0])
-        for d in range(1, n_ch):
-            partials.append(
-                lax.ppermute(sums[d], "ch", [(h, (h + d) % n_ch) for h in range(n_ch)])
-            )
+
+    def to_owners(sums):
+        return [sums[0]] + [
+            lax.ppermute(sums[d], "ch", [(h, (h + d) % n_ch) for h in range(n_ch)])
+            for d in range(1, n_ch)
+        ]
+
+    pair = send_on((features, features))
+    pieces = [features, *pair]
+    sums = list(project(pieces))
+    grad_out, residues, log_rates, skip_gain, sums[0] = lax.optimization_barrier(
+        (grad_out, residues, log_rates, skip_gain, sums[0])
+    )
+    (upper,) = call(
+        functools.partial(pieces_kernel, rows=rows, n_ch=n_ch),
+        (jax.ShapeDtypeStruct((n_seq, part, block_len), BF16),), 0, 0, grad_out,
+    )
+    upper = lax.all_to_all(upper, "seq", split_axis=0, concat_axis=0, tiled=True)
+    group_slots = [3]
+    partials = to_owners(sums)
+    later = []
+    for step in range(2, n_seq // 2):
+        pair = send_on(pair)
+        if step == 2:
+            pair, upper = lax.optimization_barrier((pair, upper))
+        pieces += pair
+        later += pair
+        if step % 2 == 1 or step == n_seq // 2 - 1:
+            partials += to_owners(project(later))
+            group_slots.append(len(later))
+            later = []
+    half = block_len // 2
+    pair = send_on((pair[0][:half], pair[1][half:]))
+    pieces += pair
+    partials += to_owners(project(list(pair)))
+    group_slots.append(1)
+
+    spread = [((q % n_seq) * n_ch + q // n_seq, q) for q in range(n_seq * n_ch)]
+    gather_back = [(b, a) for a, b in spread]
+    upper = lax.ppermute(upper, ("seq", "ch"), spread)
+    packed = jnp.concatenate([residues, log_rates, skip_gain[:, None]], 1)
+    (poles,) = call(
+        functools.partial(poles_kernel, rows=rows, n_ch=n_ch),
+        (jax.ShapeDtypeStruct((part, packed.shape[1]), F32),), 0, 0, place, packed, indexed=True,
+    )
+    poles = lax.ppermute(poles, ("seq", "ch"), spread)
+    hc, hs = call(
+        functools.partial(taps_kernel, order=order), (spectrum, spectrum),
+        8 * square, part * tokens * order, poles, cos_table, sin_table, twist,
+    )
 
     grads, tgc, tgs, skip_sum = call(
         functools.partial(conv_kernel, order=order, group_slots=group_slots, shares=n_ch),
@@ -326,7 +358,9 @@
         ),
         32 * square, 0, place, *partials, upper, poles, hc, hs,
         cos_table, sin_table, twist,
-        scratch=[pltpu.VMEM((n_seq, gates, part, block_len), F32)], indexed=True,
+        scratch=[pltpu.VMEM((n_seq, gates, part, block_len), F32)]
+        + [pltpu.VMEM(a.shape, a.dtype) for a in partials],
+        indexed=True, late=range(1, 1 + len(partials)),
     )
 
     swap = [(h, h ^ 1) for h in range(n_ch)]
@@ -342,10 +376,8 @@
         8 * square, part * tokens * order, poles, tgc, tgs, cos_table, sin_table, skip_sum,
     )
 
-    pole_sums, across = lax.optimization_barrier((pole_sums, across))
     held = [grads] + across + [swapped] + [lax.ppermute(a, "ch", swap) for a in across]
 
-    every_feature = jnp.concatenate([piece for slot in slots for piece in slot], 0)
     tile = min(512, width)
     weight_grad = pl.pallas_call(
         functools.partial(weight_kernel, shares=n_ch),
@@ -353,11 +385,12 @@
         grid=(width // tile,),
         in_specs=[pl.BlockSpec(memory_space=pltpu.SMEM)]
         + [pl.BlockSpec((gates, part, tokens), lambda i: (0, 0, 0))] * n_ch
-        + [pl.BlockSpec((tokens, tile), lambda i: (0, i))],
+        + [pl.BlockSpec((piece.shape[0], tile), lambda i: (0, i)) for piece in pieces],
         out_specs=pl.BlockSpec((gates, rows, tile), lambda i: (0, 0, i)),
         scratch_shapes=[
             pltpu.VMEM((gates, rows, tokens), F32),
             pltpu.VMEM((gates, rows, tokens), BF16),
+            pltpu.VMEM((tokens, tile), BF16),
         ],
         compiler_params=pltpu.CompilerParams(
             vmem_limit_bytes=min(56 * MIB, 16 * MIB + 12 * gates * rows * tokens + 4 * tokens * tile)
@@ -367,7 +400,7 @@
             bytes_accessed=4 * gates * rows * width + 2 * tokens * (width + gates * rows),
             transcendentals=0,
         ),
-    )(place, *held, every_feature)
+    )(place, *held, *pieces)
     weight_grad = weight_grad.transpose(1, 0, 2)
 
     returned = lax.ppermute(pole_sums, ("seq", "ch"), gather_back)

time: 145 us -> 127 us (0.88)
  local copies, waits for them, and re-layouts: 35 us -> 13.8 us
  blocking collectives: 0 us -> 13.6 us
  starting transfers between devices: 50.8 us -> 40 us
  Pallas kernels: 22.8 us -> 26.8 us
  waiting for transfers between devices: 31.1 us -> 29.2 us
    unnamed x63 -> x59, local copies, waits for them, and re-layouts: 29.3 us -> 9.31 us
    all_to_all x0 -> x1, blocking collectives: none -> 13.6 us  [local(): lax.all_to_all(upper, 'seq', split_axis=0, concat_axis=0, tiled=True)]
    all_to_all x1 -> x0, starting transfers between devices: 6.19 us -> none  [local(): lax.all_to_all(upper, 'seq', split_axis=0, concat_axis=0, tiled=True)]
    ppermute x23 -> x17, starting transfers between devices: 27.6 us -> 22.6 us  [the longest x9 13.4 us: to_owners(): lax.ppermute(sums[d], 'ch', [(h, (h + d) % n_ch) for h in range(n_ch)])]
    ppermute x1, waiting for transfers between devices: 4.35 us -> 0.01 us  [local(): lax.ppermute(grads, 'ch', [(h, (h + d) % n_ch) for h in range(n_ch)])]
    pallas_call x7 -> x8, Pallas kernels: 15.9 us -> 19.9 us  [call(): pl.pallas_call(kernel, out_shape=outs, in_specs=specs, out_specs=[whole]...]
    all_to_all x1, starting transfers between devices: 11.2 us -> 13.2 us  [local(): lax.all_to_all(returned, 'seq', split_axis=0, concat_axis=0, tiled=True)]
    ppermute x1, starting transfers between devices: 0.34 us -> 1.91 us  [local(): swapped = lax.ppermute(grads, 'ch', swap)]
  transfers between devices with their start and end apart: 31 -> 24, of which waited for: 10 -> 6; matrix products, arithmetic and copies ran while one was open for 15% -> 5% of each run, Pallas kernels for 9% -> 11%
where the time goes in v2:
time: 127 us; the launch traced here: 126 us
  starting transfers between devices  40 us (31%)
  waiting for transfers between devices  29.2 us (23%)
  Pallas kernels  26.8 us (21%)
  local copies, waits for them, and re-layouts  13.8 us (11%)
  blocking collectives  13.6 us (11%)
  other arithmetic  1.51 us (1%)
    pallas_call x8, Pallas kernels, call(): pl.pallas_call(kernel, out_shape=outs, in_specs=specs, out_specs=[whole]...  19.9 us
    all_to_all x1, blocking collectives, local(): lax.all_to_all(upper, 'seq', split_axis=0, concat_axis=0, tiled=True)  13.6 us
    ppermute x9, starting transfers between devices, to_owners(): lax.ppermute(sums[d], 'ch', [(h, (h + d) % n_ch) for h in range(n_ch)])  13.4 us
    all_to_all x1, starting transfers between devices, local(): lax.all_to_all(returned, 'seq', split_axis=0, concat_axis=0, tiled=True)  13.2 us
    ppermute x4, waiting for transfers between devices, send_on(): lax.ppermute(pair[1], 'seq', behind)  12.1 us
    unnamed x59, local copies, waits for them, and re-layouts  9.31 us
    ppermute x4, waiting for transfers between devices, send_on(): lax.ppermute(pair[0], 'seq', ahead)  8.78 us
    ppermute x4, starting transfers between devices, send_on(): lax.ppermute(pair[1], 'seq', behind)  8.56 us
  transfers between devices with their start and end apart: 24, of which 6 were waited for; matrix products, arithmetic and copies ran while one was open for 5% of the time, Pallas kernels for 11%

profile of v2, /device:TPU:0, one launch (start us, length us, event | category | flops | bytes accessed | tf_op | source)
XLA Modules:
  0.0 125.9 jit_solution(5166257128403919704)
XLA Ops:
  0.6 3.0 %collective-permute-start.1 = (bf16[128,2048]{1,0:T(8,128)(2,1)}, bf16[128,2048]{1,0:T(8,128)(2,1)S(1)}, u32[]{:S(2)}, u32[]{:S(2)}) collective-permute-start(bf16[128,2048]{1,0:T(8,128)(2,1)} %refs_4_.1), channel_id=1, source_target_pairs={{8,0},{16,8},{24,16},{28,24},{20,28},{12,20},{4,12},{0,4},{9,1},{1... | collective-permute-start | bytes 1572872 | tf_op jit(solution)/shard_map/ppermute | solution.py:282
  3.8 12.1 %collective-permute-done.1.refs_2_.refs_6_ = bf16[128,2048]{1,0:T(8,128)(2,1)S(1)} collective-permute-done((bf16[128,2048]{1,0:T(8,128)(2,1)}, bf16[128,2048]{1,0:T(8,128)(2,1)S(1)}, u32[]{:S(2)}, u32[]{:S(2)}) %collective-permute-start.1) | collective-permute-done | bytes 524320 | tf_op jit(solution)/shard_map/ppermute | solution.py:282
  15.8 1.7 %collective-permute-start.6 = (bf16[128,2048]{1,0:T(8,128)(2,1)S(1)}, bf16[128,2048]{1,0:T(8,128)(2,1)}, u32[]{:S(2)}, u32[]{:S(2)}) collective-permute-start(bf16[128,2048]{1,0:T(8,128)(2,1)S(1)} %collective-permute-done.1.refs_2_.refs_6_), channel_id=1, source_target_pairs={{8,0},{16,8},{24,16},{28,24},{20,28},{12,20},{4,12},{0,4},{9,1},{1... | collective-permute-start | bytes 1572872 | tf_op jit(solution)/shard_map/ppermute | solution.py:282
  18.0 1.7 %copy-done = bf16[208,3,2048]{2,0,1:T(8,128)(2,1)S(1)} copy-done((bf16[208,3,2048]{2,0,1:T(8,128)(2,1)S(1)}, bf16[208,3,2048]{2,0,1:T(8,128)(2,1)}, u32[]{:S(2)}) %copy-start) | copy-done | bytes 2555928
  19.7 1.0 copy-done.4
  20.7 3.6 %shard_map.120 = (f32[3,56,384]{2,1,0:T(8,128)S(1)}, bf16[3,56,384]{2,1,0:T(8,128)(2,1)S(1)}, bf16[3,56,384]{2,1,0:T(8,128)(2,1)S(1)}, bf16[3,56,384]{2,1,0:T(8,128)(2,1)S(1)}) custom-call(s32[2]{0:T(128)S(1)} %pad_add_fusion.place_ref, bf16[3,208,2048]{2,1,0:T(8,128)(2,1)S(1)} %bitcast.25, bf16[128,2048]{1,0:T(8,128)(2,1)S(1)} %copy-done.4, ...), custom_call_target="tpu_custom_call" | custom-call | flops 981467136 | bytes 4773896 | tf_op jit(solution)/shard_map/pallas_call | solution.py:244
  25.1 13.6 %all_to_all.10 = bf16[8,56,128]{2,1,0:T(8,128)(2,1)} all-to-all(bf16[8,56,128]{2,1,0:T(8,128)(2,1)S(1)} %shard_map.121), channel_id=1, replica_groups=mesh['seq'=8,'ch'=4] {'seq'}, dimensions={0} | all-to-all | bytes 229376 | tf_op jit(solution)/shard_map/all_to_all | solution.py:317
  38.7 2.0 %collective-permute-start.8 = (bf16[128,2048]{1,0:T(8,128)(2,1)}, bf16[128,2048]{1,0:T(8,128)(2,1)S(1)}, u32[]{:S(2)}, u32[]{:S(2)}) collective-permute-start(bf16[128,2048]{1,0:T(8,128)(2,1)} %collective-permute-done.6.refs_1_.refs_8_), channel_id=1, source_target_pairs={{8,0},{16,8},{24,16},{28,24},{20,28},{12,20},{4,12},{0,4},{9,1},{1... | collective-permute-start | bytes 1572872 | tf_op jit(solution)/shard_map/ppermute | solution.py:282
  40.7 8.8 %collective-permute-done.7.refs_2_.refs_9_ = bf16[128,2048]{1,0:T(8,128)(2,1)S(1)} collective-permute-done((bf16[128,2048]{1,0:T(8,128)(2,1)}, bf16[128,2048]{1,0:T(8,128)(2,1)S(1)}, u32[]{:S(2)}, u32[]{:S(2)}) %collective-permute-start.7) | collective-permute-done | bytes 524320 | tf_op jit(solution)/shard_map/ppermute | solution.py:282
  50.2 0.8 copy-done.6
  52.6 1.9 %collective-permute-start.13 = (bf16[64,2048]{1,0:T(8,128)(2,1)}, bf16[64,2048]{1,0:T(8,128)(2,1)}, u32[]{:S(2)}, u32[]{:S(2)}) collective-permute-start(bf16[64,2048]{1,0:T(8,128)(2,1)} %slice.53), channel_id=1, source_target_pairs={{8,0},{16,8},{24,16},{28,24},{20,28},{12,20},{4,12},{0,4},{9,1},{1... | collective-permute-start | bytes 786440 | tf_op jit(solution)/shard_map/ppermute | solution.py:282
  55.2 1.0 copy.20.packed_ref
  58.1 1.5 %collective-permute-start.2 = (bf16[3,56,384]{2,1,0:T(8,128)(2,1)}, bf16[3,56,384]{2,1,0:T(8,128)(2,1)S(1)}, u32[]{:S(2)}, u32[]{:S(2)}) collective-permute-start(bf16[3,56,384]{2,1,0:T(8,128)(2,1)} %copy-done.23), channel_id=1, source_target_pairs={{0,1},{1,2},{2,3},{3,0},{4,5},{5,6},{6,7},{7,4},{8,9},{9,10},{10,1... | collective-permute-start | bytes 387080 | tf_op jit(solution)/shard_map/ppermute | solution.py:303
  59.6 1.7 %collective-permute-start.3 = (bf16[3,56,384]{2,1,0:T(8,128)(2,1)}, bf16[3,56,384]{2,1,0:T(8,128)(2,1)S(1)}, u32[]{:S(2)}, u32[]{:S(2)}) collective-permute-start(bf16[3,56,384]{2,1,0:T(8,128)(2,1)} %copy-done.22), channel_id=1, source_target_pairs={{0,2},{1,3},{2,0},{3,1},{4,6},{5,7},{6,4},{7,5},{8,10},{9,11},{10,... | collective-permute-start | bytes 387080 | tf_op jit(solution)/shard_map/ppermute | solution.py:303
  61.3 1.0 copy-done.7
  62.4 1.0 copy-done.10
  64.0 4.1 %shard_map.122 = (f32[3,56,512]{2,1,0:T(8,128)S(1)}, bf16[3,56,512]{2,1,0:T(8,128)(2,1)S(1)}, bf16[3,56,512]{2,1,0:T(8,128)(2,1)S(1)}, bf16[3,56,512]{2,1,0:T(8,128)(2,1)S(1)}) custom-call(s32[2]{0:T(128)S(1)} %copy-done.16, bf16[3,208,2048]{2,1,0:T(8,128)(2,1)S(1)} %bitcast.26, bf16[128,2048]{1,0:T(8,128)(2,1)} %collective-permute-done.5.refs_0_.refs_7_, ...), custom_call_target="tpu_custom_call" | custom-call | flops 1308622848 | bytes 5513224 | tf_op jit(solution)/shard_map/pallas_call | solution.py:244
  68.3 1.7 %collective-permute-start.4 = (bf16[3,56,384]{2,1,0:T(8,128)(2,1)S(1)}, bf16[3,56,384]{2,1,0:T(8,128)(2,1)S(1)}, u32[]{:S(2)}, u32[]{:S(2)}) collective-permute-start(bf16[3,56,384]{2,1,0:T(8,128)(2,1)S(1)} %copy-done.21), channel_id=1, source_target_pairs={{0,3},{1,0},{2,1},{3,2},{4,7},{5,4},{6,5},{7,6},{8,11},{9,8},{10,9... | collective-permute-start | bytes 387080 | tf_op jit(solution)/shard_map/ppermute | solution.py:303
  71.0 2.4 %shard_map.123 = (f32[3,56,128]{2,1,0:T(8,128)S(1)}, bf16[3,56,128]{2,1,0:T(8,128)(2,1)S(1)}, bf16[3,56,128]{2,1,0:T(8,128)(2,1)S(1)}, bf16[3,56,128]{2,1,0:T(8,128)(2,1)S(1)}) custom-call(s32[2]{0:T(128)S(1)} %copy-done.16, bf16[3,208,2048]{2,1,0:T(8,128)(2,1)S(1)} %bitcast.27, bf16[64,2048]{1,0:T(8,128)(2,1)S(1)} %collective-permute-done.12.refs_0_.refs_11_, ...), custom_call_target="tpu_custom_call" | custom-call | flops 327155712 | bytes 3295240 | tf_op jit(solution)/shard_map/pallas_call | solution.py:244
  73.9 3.7 %collective-permute-start.14 = (bf16[3,56,128]{2,1,0:T(8,128)(2,1)S(1)}, bf16[3,56,128]{2,1,0:T(8,128)(2,1)S(1)}, u32[]{:S(2)}, u32[]{:S(2)}) collective-permute-start(bf16[3,56,128]{2,1,0:T(8,128)(2,1)S(1)} %get-tuple-element.45), channel_id=1, source_target_pairs={{0,1},{1,2},{2,3},{3,0},{4,5},{5,6},{6,7},{7,4},{8,9},{9,10},{10,1... | collective-permute-start | bytes 129032 | tf_op jit(solution)/shard_map/ppermute | solution.py:303
  77.6 3.4 %collective-permute-start.15 = (bf16[3,56,128]{2,1,0:T(8,128)(2,1)S(1)}, bf16[3,56,128]{2,1,0:T(8,128)(2,1)S(1)}, u32[]{:S(2)}, u32[]{:S(2)}) collective-permute-start(bf16[3,56,128]{2,1,0:T(8,128)(2,1)S(1)} %get-tuple-element.46), channel_id=1, source_target_pairs={{0,2},{1,3},{2,0},{3,1},{4,6},{5,7},{6,4},{7,5},{8,10},{9,11},{10,... | collective-permute-start | bytes 129032 | tf_op jit(solution)/shard_map/ppermute | solution.py:303
  80.9 1.0 collective-permute-start.16
  81.9 1.6 %shard_map.125 = (f32[56,1024]{1,0:T(8,128)S(1)}, f32[56,1024]{1,0:T(8,128)S(1)}) custom-call(f32[56,33]{1,0:T(8,128)S(1)} %collective-permute-done.18.poles_ref.refs_13_, bf16[1024,1024]{1,0:T(8,128)(2,1)S(1)} %copy-done.3, bf16[1024,1024]{1,0:T(8,128)(2,1)S(1)} %copy-done.2, f32[2,1024]{1,0:T(2,128)S(1)} %copy-done.13), custom_call_target="tpu_custom_call" | custom-call | flops 469762048 | bytes 4668640 | tf_op jit(solution)/shard_map/pallas_call | solution.py:244
  83.6 5.6 %shard_map.126 = (bf16[3,56,1024]{2,1,0:T(8,128)(2,1)S(1)}, f32[56,1024]{1,0:T(8,128)S(1)}, f32[56,1024]{1,0:T(8,128)S(1)}, f32[56,1]{1,0:T(8,128)S(1)}) custom-call(s32[2]{0:T(128)S(1)} %copy-done.16, f32[3,56,384]{2,1,0:T(8,128)S(1)} %copy-done.19, bf16[3,56,384]{2,1,0:T(8,128)(2,1)S(1)} %collective-permute-done.2.refs_1_, ...), custom_call_target="tpu_custom_call" | custom-call | flops 1879048192 | bytes 7306696 | tf_op jit(solution)/shard_map/pallas_call | solution.py:244
  89.2 1.9 %collective-permute-start.20 = (bf16[3,56,1024]{2,1,0:T(8,128)(2,1)S(1)}, bf16[3,56,1024]{2,1,0:T(8,128)(2,1)S(1)}, u32[]{:S(2)}, u32[]{:S(2)}) collective-permute-start(bf16[3,56,1024]{2,1,0:T(8,128)(2,1)S(1)} %get-tuple-element.54.refs_0_), channel_id=1, source_target_pairs={{0,1},{1,0},{2,3},{3,2},{4,5},{5,4},{6,7},{7,6},{8,9},{9,8},{10,11... | collective-permute-start | bytes 1032200 | tf_op jit(solution)/shard_map/ppermute | solution.py:371
  91.4 1.0 collective-permute-done.20.refs_2_
  92.4 2.0 %shard_map.128 = f32[56,33]{1,0:T(8,128)S(1)} custom-call(f32[56,33]{1,0:T(8,128)S(1)} %collective-permute-done.18.poles_ref.refs_13_, f32[56,1024]{1,0:T(8,128)S(1)} %get-tuple-element.57.tgc_ref, f32[56,1024]{1,0:T(8,128)S(1)} %get-tuple-element.58.tgs_ref, bf16[1024,1024]{1,0:T(8,128)(2,1)S(1)} %copy-done.3, bf16[1024,1024]{1,0:T(8,128)(2,1)S(1)} %copy-done.2, ...), custom_call_target="tpu_custom_call" | custom-call | flops 469762048 | bytes 4668064 | tf_op jit(solution)/shard_map/pallas_call | solution.py:244
  95.3 0.8 reshape.9
  96.1 13.2 %all-to-all-start.1 = ((f32[8,1,1848]{2,1,0:T(1,128)}), f32[8,1,1848]{2,1,0:T(1,128)S(1)}, u32[]{:S(2)}, u32[]{:S(2)}) async-start(f32[8,1,1848]{2,1,0:T(1,128)} %reshape.9), calls=%async_computation.1 | async-start | bytes 122880 | tf_op jit(solution)/shard_map/all_to_all | solution.py:408
  109.3 6.8 %all-to-all-done.1 = f32[8,1,1848]{2,1,0:T(1,128)S(1)} async-done(((f32[8,1,1848]{2,1,0:T(1,128)}), f32[8,1,1848]{2,1,0:T(1,128)S(1)}, u32[]{:S(2)}, u32[]{:S(2)}) %all-to-all-start.1) | async-done | bytes 59168 | tf_op jit(solution)/shard_map/all_to_all | solution.py:408
  116.6 0.8 reduce
  119.0 6.9 %shard_map.127 = f32[3,208,2048]{2,1,0:T(8,128)} custom-call(s32[2]{0:T(128)S(1)} %copy-done.17, bf16[3,56,1024]{2,1,0:T(8,128)(2,1)S(1)} %get-tuple-element.54.refs_0_, bf16[3,56,1024]{2,1,0:T(8,128)(2,1)} %collective-permute-done.19.refs_1_, bf16[3,56,1024]{2,1,0:T(8,128)(2,1)S(1)} %collective-permute-done.20.refs_2_, ...), custom_call_target="tpu_custom_call" | custom-call | flops 2617245696 | bytes 10584064 | tf_op jit(solution)/shard_map/pallas_call | solution.py:382
  (98 shorter events, 11.6 us)
Async XLA Ops:
  0.6 15.2 %collective-permute-start.1 = (bf16[128,2048]{1,0:T(8,128)(2,1)}, bf16[128,2048]{1,0:T(8,128)(2,1)S(1)}, u32[]{:S(2)}, u32[]{:S(2)}) collective-permute-start(bf16[128,2048]{1,0:T(8,128)(2,1)} %refs_4_.1), channel_id=1, source_target_pairs={{8,0},{16,8},{24,16},{28,24},{20,28},{12,20},{4,12},{0,4},{9,1},{1... | collective-permute-start | bytes 1572872 | tf_op jit(solution)/shard_map/ppermute | solution.py:282
  3.6 13.9 %collective-permute-start = (bf16[128,2048]{1,0:T(8,128)(2,1)}, bf16[128,2048]{1,0:T(8,128)(2,1)}, u32[]{:S(2)}, u32[]{:S(2)}) collective-permute-start(bf16[128,2048]{1,0:T(8,128)(2,1)} %refs_4_.1), channel_id=1, source_target_pairs={{0,8},{8,16},{16,24},{24,28},{28,20},{20,12},{12,4},{4,0},{1,9},{9... | collective-permute-start | bytes 1572872 | tf_op jit(solution)/shard_map/ppermute | solution.py:282
  15.8 22.8 %collective-permute-start.6 = (bf16[128,2048]{1,0:T(8,128)(2,1)S(1)}, bf16[128,2048]{1,0:T(8,128)(2,1)}, u32[]{:S(2)}, u32[]{:S(2)}) collective-permute-start(bf16[128,2048]{1,0:T(8,128)(2,1)S(1)} %collective-permute-done.1.refs_2_.refs_6_), channel_id=1, source_target_pairs={{8,0},{16,8},{24,16},{28,24},{20,28},{12,20},{4,12},{0,4},{9,1},{1... | collective-permute-start | bytes 1572872 | tf_op jit(solution)/shard_map/ppermute | solution.py:282
  17.5 21.2 %collective-permute-start.5 = (bf16[128,2048]{1,0:T(8,128)(2,1)}, bf16[128,2048]{1,0:T(8,128)(2,1)}, u32[]{:S(2)}, u32[]{:S(2)}) collective-permute-start(bf16[128,2048]{1,0:T(8,128)(2,1)} %collective-permute-done.refs_1_.refs_5_), channel_id=1, source_target_pairs={{0,8},{8,16},{16,24},{24,28},{28,20},{20,12},{12,4},{4,0},{1,9},{9... | collective-permute-start | bytes 1572872 | tf_op jit(solution)/shard_map/ppermute | solution.py:282
  17.9 33.9 %copy-start.14 = (s32[2]{0:T(128)}, s32[2]{0:T(128)S(1)}, u32[]{:S(2)}) copy-start(s32[2]{0:T(128)S(1)} %pad_add_fusion.place_ref) | copy-start | bytes 28
  20.7 33.8 %copy-start.25 = (f32[416,16]{0,1:T(8,128)S(1)}, f32[416,16]{0,1:T(8,128)}, u32[]{:S(2)}) copy-start(f32[416,16]{0,1:T(8,128)} %param.13) | copy-start | bytes 79876
  20.7 33.8 %copy-start.26 = (f32[416,16]{0,1:T(8,128)S(1)}, f32[416,16]{0,1:T(8,128)}, u32[]{:S(2)}) copy-start(f32[416,16]{0,1:T(8,128)} %param.12) | copy-start | bytes 79876
  20.7 33.8 %copy-start.27 = (f32[416]{0:T(512)S(1)}, f32[416]{0:T(512)}, u32[]{:S(2)}) copy-start(f32[416]{0:T(512)} %param.14) | copy-start | bytes 4996
  20.7 40.6 %copy-start.1 = (bf16[208,3,2048]{2,0,1:T(8,128)(2,1)S(1)}, bf16[208,3,2048]{2,0,1:T(8,128)(2,1)}, u32[]{:S(2)}) copy-start(bf16[208,3,2048]{2,0,1:T(8,128)(2,1)} %param.10) | copy-start | bytes 7667716
  25.0 29.5 %copy-start.18 = (f32[3,56,384]{2,1,0:T(8,128)}, f32[3,56,384]{2,1,0:T(8,128)S(1)}, u32[]{:S(2)}) copy-start(f32[3,56,384]{2,1,0:T(8,128)S(1)} %get-tuple-element.33.refs_0_) | copy-start | bytes 774148
  25.0 29.5 %copy-start.20 = (bf16[3,56,384]{2,1,0:T(8,128)(2,1)}, bf16[3,56,384]{2,1,0:T(8,128)(2,1)S(1)}, u32[]{:S(2)}) copy-start(bf16[3,56,384]{2,1,0:T(8,128)(2,1)S(1)} %get-tuple-element.36) | copy-start | bytes 387076
  25.0 29.5 %copy-start.22 = (bf16[3,56,384]{2,1,0:T(8,128)(2,1)}, bf16[3,56,384]{2,1,0:T(8,128)(2,1)S(1)}, u32[]{:S(2)}) copy-start(bf16[3,56,384]{2,1,0:T(8,128)(2,1)S(1)} %get-tuple-element.35) | copy-start | bytes 387076
  38.7 10.8 %collective-permute-start.7 = (bf16[128,2048]{1,0:T(8,128)(2,1)}, bf16[128,2048]{1,0:T(8,128)(2,1)S(1)}, u32[]{:S(2)}, u32[]{:S(2)}) collective-permute-start(bf16[128,2048]{1,0:T(8,128)(2,1)} %collective-permute-done.5.refs_0_.refs_7_), channel_id=1, source_target_pairs={{0,8},{8,16},{16,24},{24,28},{28,20},{20,12},{12,4},{4,0},{1,9},{9... | collective-permute-start | bytes 1572872 | tf_op jit(solution)/shard_map/ppermute | solution.py:282
  38.7 12.4 %collective-permute-start.8 = (bf16[128,2048]{1,0:T(8,128)(2,1)}, bf16[128,2048]{1,0:T(8,128)(2,1)S(1)}, u32[]{:S(2)}, u32[]{:S(2)}) collective-permute-start(bf16[128,2048]{1,0:T(8,128)(2,1)} %collective-permute-done.6.refs_1_.refs_8_), channel_id=1, source_target_pairs={{8,0},{16,8},{24,16},{28,24},{20,28},{12,20},{4,12},{0,4},{9,1},{1... | collective-permute-start | bytes 1572872 | tf_op jit(solution)/shard_map/ppermute | solution.py:282
  51.0 19.3 %collective-permute-start.12 = (bf16[64,2048]{1,0:T(8,128)(2,1)}, bf16[64,2048]{1,0:T(8,128)(2,1)S(1)}, u32[]{:S(2)}, u32[]{:S(2)}) collective-permute-start(bf16[64,2048]{1,0:T(8,128)(2,1)} %slice.52), channel_id=1, source_target_pairs={{0,8},{8,16},{16,24},{24,28},{28,20},{20,12},{12,4},{4,0},{1,9},{9... | collective-permute-start | bytes 786440 | tf_op jit(solution)/shard_map/ppermute | solution.py:282
  52.6 17.7 %collective-permute-start.13 = (bf16[64,2048]{1,0:T(8,128)(2,1)}, bf16[64,2048]{1,0:T(8,128)(2,1)}, u32[]{:S(2)}, u32[]{:S(2)}) collective-permute-start(bf16[64,2048]{1,0:T(8,128)(2,1)} %slice.53), channel_id=1, source_target_pairs={{8,0},{16,8},{24,16},{28,24},{20,28},{12,20},{4,12},{0,4},{9,1},{1... | collective-permute-start | bytes 786440 | tf_op jit(solution)/shard_map/ppermute | solution.py:282
  57.4 10.8 %collective-permute-start.18 = (f32[56,33]{1,0:T(8,128)S(1)}, f32[56,33]{1,0:T(8,128)S(1)}, u32[]{:S(2)}, u32[]{:S(2)}) collective-permute-start(f32[56,33]{1,0:T(8,128)S(1)} %shard_map.124), channel_id=1, source_target_pairs={{0,0},{4,1},{8,2},{12,3},{16,4},{20,5},{24,6},{28,7},{1,8},{5,9},{... | collective-permute-start | bytes 22184 | tf_op jit(solution)/shard_map/ppermute | solution.py:345
  58.1 10.2 %collective-permute-start.2 = (bf16[3,56,384]{2,1,0:T(8,128)(2,1)}, bf16[3,56,384]{2,1,0:T(8,128)(2,1)S(1)}, u32[]{:S(2)}, u32[]{:S(2)}) collective-permute-start(bf16[3,56,384]{2,1,0:T(8,128)(2,1)} %copy-done.23), channel_id=1, source_target_pairs={{0,1},{1,2},{2,3},{3,0},{4,5},{5,6},{6,7},{7,4},{8,9},{9,10},{10,1... | collective-permute-start | bytes 387080 | tf_op jit(solution)/shard_map/ppermute | solution.py:303
  59.6 10.4 %collective-permute-start.3 = (bf16[3,56,384]{2,1,0:T(8,128)(2,1)}, bf16[3,56,384]{2,1,0:T(8,128)(2,1)S(1)}, u32[]{:S(2)}, u32[]{:S(2)}) collective-permute-start(bf16[3,56,384]{2,1,0:T(8,128)(2,1)} %copy-done.22), channel_id=1, source_target_pairs={{0,2},{1,3},{2,0},{3,1},{4,6},{5,7},{6,4},{7,5},{8,10},{9,11},{10,... | collective-permute-start | bytes 387080 | tf_op jit(solution)/shard_map/ppermute | solution.py:303
  68.2 12.8 %collective-permute-start.9 = (bf16[3,56,512]{2,1,0:T(8,128)(2,1)S(1)}, bf16[3,56,512]{2,1,0:T(8,128)(2,1)S(1)}, u32[]{:S(2)}, u32[]{:S(2)}) collective-permute-start(bf16[3,56,512]{2,1,0:T(8,128)(2,1)S(1)} %get-tuple-element.41), channel_id=1, source_target_pairs={{0,1},{1,2},{2,3},{3,0},{4,5},{5,6},{6,7},{7,4},{8,9},{9,10},{10,1... | collective-permute-start | bytes 516104 | tf_op jit(solution)/shard_map/ppermute | solution.py:303
  68.3 5.6 %collective-permute-start.4 = (bf16[3,56,384]{2,1,0:T(8,128)(2,1)S(1)}, bf16[3,56,384]{2,1,0:T(8,128)(2,1)S(1)}, u32[]{:S(2)}, u32[]{:S(2)}) collective-permute-start(bf16[3,56,384]{2,1,0:T(8,128)(2,1)S(1)} %copy-done.21), channel_id=1, source_target_pairs={{0,3},{1,0},{2,1},{3,2},{4,7},{5,4},{6,5},{7,6},{8,11},{9,8},{10,9... | collective-permute-start | bytes 387080 | tf_op jit(solution)/shard_map/ppermute | solution.py:303
  70.0 13.5 %collective-permute-start.10 = (bf16[3,56,512]{2,1,0:T(8,128)(2,1)S(1)}, bf16[3,56,512]{2,1,0:T(8,128)(2,1)S(1)}, u32[]{:S(2)}, u32[]{:S(2)}) collective-permute-start(bf16[3,56,512]{2,1,0:T(8,128)(2,1)S(1)} %get-tuple-element.42), channel_id=1, source_target_pairs={{0,2},{1,3},{2,0},{3,1},{4,6},{5,7},{6,4},{7,5},{8,10},{9,11},{10,... | collective-permute-start | bytes 516104 | tf_op jit(solution)/shard_map/ppermute | solution.py:303
  70.3 13.2 %collective-permute-start.11 = (bf16[3,56,512]{2,1,0:T(8,128)(2,1)S(1)}, bf16[3,56,512]{2,1,0:T(8,128)(2,1)S(1)}, u32[]{:S(2)}, u32[]{:S(2)}) collective-permute-start(bf16[3,56,512]{2,1,0:T(8,128)(2,1)S(1)} %get-tuple-element.43), channel_id=1, source_target_pairs={{0,3},{1,0},{2,1},{3,2},{4,7},{5,4},{6,5},{7,6},{8,11},{9,8},{10,9... | collective-permute-start | bytes 516104 | tf_op jit(solution)/shard_map/ppermute | solution.py:303
  70.3 7.3 %collective-permute-start.17 = (bf16[8,56,128]{2,1,0:T(8,128)(2,1)S(1)}, bf16[8,56,128]{2,1,0:T(8,128)(2,1)S(1)}, u32[]{:S(2)}, u32[]{:S(2)}) collective-permute-start(bf16[8,56,128]{2,1,0:T(8,128)(2,1)S(1)} %copy-done.24), channel_id=1, source_target_pairs={{0,0},{4,1},{8,2},{12,3},{16,4},{20,5},{24,6},{28,7},{1,8},{5,9},{... | collective-permute-start | bytes 344072 | tf_op jit(solution)/shard_map/ppermute | solution.py:339
  73.9 9.6 %collective-permute-start.14 = (bf16[3,56,128]{2,1,0:T(8,128)(2,1)S(1)}, bf16[3,56,128]{2,1,0:T(8,128)(2,1)S(1)}, u32[]{:S(2)}, u32[]{:S(2)}) collective-permute-start(bf16[3,56,128]{2,1,0:T(8,128)(2,1)S(1)} %get-tuple-element.45), channel_id=1, source_target_pairs={{0,1},{1,2},{2,3},{3,0},{4,5},{5,6},{6,7},{7,4},{8,9},{9,10},{10,1... | collective-permute-start | bytes 129032 | tf_op jit(solution)/shard_map/ppermute | solution.py:303
  77.6 5.9 %collective-permute-start.15 = (bf16[3,56,128]{2,1,0:T(8,128)(2,1)S(1)}, bf16[3,56,128]{2,1,0:T(8,128)(2,1)S(1)}, u32[]{:S(2)}, u32[]{:S(2)}) collective-permute-start(bf16[3,56,128]{2,1,0:T(8,128)(2,1)S(1)} %get-tuple-element.46), channel_id=1, source_target_pairs={{0,2},{1,3},{2,0},{3,1},{4,6},{5,7},{6,4},{7,5},{8,10},{9,11},{10,... | collective-permute-start | bytes 129032 | tf_op jit(solution)/shard_map/ppermute | solution.py:303
  80.9 2.7 %collective-permute-start.16 = (bf16[3,56,128]{2,1,0:T(8,128)(2,1)S(1)}, bf16[3,56,128]{2,1,0:T(8,128)(2,1)S(1)}, u32[]{:S(2)}, u32[]{:S(2)}) collective-permute-start(bf16[3,56,128]{2,1,0:T(8,128)(2,1)S(1)} %get-tuple-element.47), channel_id=1, source_target_pairs={{0,3},{1,0},{2,1},{3,2},{4,7},{5,4},{6,5},{7,6},{8,11},{9,8},{10,9... | collective-permute-start | bytes 129032 | tf_op jit(solution)/shard_map/ppermute | solution.py:303
  89.2 3.2 %collective-permute-start.20 = (bf16[3,56,1024]{2,1,0:T(8,128)(2,1)S(1)}, bf16[3,56,1024]{2,1,0:T(8,128)(2,1)S(1)}, u32[]{:S(2)}, u32[]{:S(2)}) collective-permute-start(bf16[3,56,1024]{2,1,0:T(8,128)(2,1)S(1)} %get-tuple-element.54.refs_0_), channel_id=1, source_target_pairs={{0,1},{1,0},{2,3},{3,2},{4,5},{5,4},{6,7},{7,6},{8,9},{9,8},{10,11... | collective-permute-start | bytes 1032200 | tf_op jit(solution)/shard_map/ppermute | solution.py:371
  91.1 18.1 %collective-permute-start.19 = (bf16[3,56,1024]{2,1,0:T(8,128)(2,1)S(1)}, bf16[3,56,1024]{2,1,0:T(8,128)(2,1)}, u32[]{:S(2)}, u32[]{:S(2)}) collective-permute-start(bf16[3,56,1024]{2,1,0:T(8,128)(2,1)S(1)} %get-tuple-element.54.refs_0_), channel_id=1, source_target_pairs={{0,2},{1,3},{2,0},{3,1},{4,6},{5,7},{6,4},{7,5},{8,10},{9,11},{10,... | collective-permute-start | bytes 1032200 | tf_op jit(solution)/shard_map/ppermute | solution.py:368
  94.5 0.7 collective-permute-start.22
  96.1 20.0 %all-to-all-start.1 = ((f32[8,1,1848]{2,1,0:T(1,128)}), f32[8,1,1848]{2,1,0:T(1,128)S(1)}, u32[]{:S(2)}, u32[]{:S(2)}) async-start(f32[8,1,1848]{2,1,0:T(1,128)} %reshape.9), calls=%async_computation.1 | async-start | bytes 122880 | tf_op jit(solution)/shard_map/all_to_all | solution.py:408
  109.2 9.7 %collective-permute-start.21 = (bf16[3,56,1024]{2,1,0:T(8,128)(2,1)}, bf16[3,56,1024]{2,1,0:T(8,128)(2,1)}, u32[]{:S(2)}, u32[]{:S(2)}) collective-permute-start(bf16[3,56,1024]{2,1,0:T(8,128)(2,1)} %collective-permute-done.19.refs_1_), channel_id=1, source_target_pairs={{0,1},{1,0},{2,3},{3,2},{4,5},{5,4},{6,7},{7,6},{8,9},{9,8},{10,11... | collective-permute-start | bytes 1032200 | tf_op jit(solution)/shard_map/ppermute | solution.py:379
  (20 other events, 199.4 us)

commit v3 on v2

--- a/solution.py
+++ b/solution.py
@@ -66,12 +66,18 @@
     return pl.multiple_of(jnp.minimum(index * part, rows - part), 8)
 
 
-def pieces_kernel(grad_ref, pieces_ref, *, rows, n_ch):
-    part = pieces_ref.shape[1]
-    grad = grad_ref[...].astype(F32)
-    for piece in range(pieces_ref.shape[0]):
-        start = piece // n_ch * rows + min(piece % n_ch * part, rows - part)
-        pieces_ref[piece] = grad[start : start + part].astype(BF16)
+def pieces_kernel(place_ref, grad_ref, *refs, rows, n_ch):
+    *out_refs, wide_ref = refs
+    count = sum(out_ref.shape[0] for out_ref in out_refs)
+    part = out_refs[0].shape[1]
+    wide_ref[...] = grad_ref[...].astype(F32)
+    slot = 0
+    for out_ref in out_refs:
+        for place in range(out_ref.shape[0]):
+            piece = place_ref[0] ^ slot
+            start = piece // n_ch * rows + part_start(piece % n_ch, part, rows)
+            out_ref[place] = wide_ref[pl.ds(pl.multiple_of(start, 8), part), :].astype(BF16)
+            slot += 1
 
 
 def poles_kernel(place_ref, packed_ref, poles_ref, *, rows, n_ch):
@@ -97,7 +103,7 @@
     out_refs = refs[pieces:-3]
     features_ref, sums_ref, semaphores = refs[-3:]
     gates, _, _ = weight_ref.shape
-    part = out_refs[0].shape[1]
+    part = out_refs[0].shape[-2]
     targets, row = [], 0
     for feature_ref in feature_refs:
         targets.append(features_ref.at[pl.ds(row, feature_ref.shape[0]), :])
@@ -108,8 +114,14 @@
             weight_ref[gate], features_ref[...], (((1,), (1,)), ((), ())),
             preferred_element_type=F32,
         )
+    rows = weight_ref.shape[1]
+    if len(out_refs) == 1:
+        for owner in range(out_refs[0].shape[0]):
+            start = min(owner * part, rows - part)
+            out_refs[0][owner] = sums_ref[:, start : start + part, :].astype(BF16)
+        return
     for step, out_ref in enumerate(out_refs):
-        start = part_start((place_ref[1] + step) % len(out_refs), part, weight_ref.shape[1])
+        start = part_start((place_ref[1] + step) % len(out_refs), part, rows)
         out_ref[...] = sums_ref[:, pl.ds(start, part), :].astype(out_ref.dtype)
 
 
@@ -123,20 +135,22 @@
     return jnp.where(ahead * 2 == count, count - 1, near)
 
 
-def conv_kernel(place_ref, *refs, order, group_slots, shares):
-    partial_refs = refs[: len(group_slots) * shares]
+def conv_kernel(place_ref, *refs, order, n_ch, group_slots, group_shares):
+    shares = sum(group_shares)
+    partial_refs = refs[:shares]
     (
         gout_ref, poles_ref, hc_ref, hs_ref, cos_ref, sin_ref, twist_ref,
         grad_ref, tgc_ref, tgs_ref, skip_ref, proj_ref, *scratch_refs,
-    ) = refs[len(group_slots) * shares :]
+    ) = refs[shares:]
     *held_refs, semaphores = scratch_refs
     fetch(partial_refs, held_refs, semaphores)
     rows, tokens = hc_ref.shape
     blocks, _, _, block_len = proj_ref.shape
     slot = 0
-    for group, count in enumerate(group_slots):
-        own_ref, *other_refs = held_refs[group * shares : (group + 1) * shares]
-        total = own_ref[...]
+    for count, share in zip(group_slots, group_shares):
+        own_ref, *other_refs = held_refs[:share]
+        held_refs = held_refs[share:]
+        total = own_ref[...].astype(F32)
         for other_ref in other_refs:
             total = total + other_ref[...].astype(F32)
         total = total.astype(BF16).astype(F32)
@@ -153,8 +167,9 @@
     queries = in_order(0)
     keys = in_order(1)
     values = in_order(2)
+    piece = (place_ref[0] * n_ch + place_ref[1]) % blocks
     upper = jnp.concatenate(
-        [gout_ref[b].astype(F32) for b in range(blocks)], 1
+        [gout_ref[b ^ piece].astype(F32) for b in range(blocks)], 1
     )
     product = keys * values
     middle = upper * queries
@@ -227,6 +242,13 @@
         out_ref[gate] = dot(rows_ref[gate], features_ref[...])
 
 
+def assemble_kernel(place_ref, held_ref, out_ref, *, rows, n_ch):
+    count, part, _ = held_ref.shape
+    for piece in range(count):
+        start = piece // n_ch * rows + min(piece % n_ch * part, rows - part)
+        out_ref[start : start + part, :] = held_ref[piece ^ place_ref[0]]
+
+
 def call(kernel, outs, flops, transcendentals, *operands, scratch=(), indexed=False, late=()):
     size = sum(a.size * a.dtype.itemsize for a in operands) + sum(
         o.size * o.dtype.itemsize for o in outs
@@ -269,8 +291,6 @@
     tokens = n_seq * block_len
     order = residues.shape[1]
     part = round_up(-(-rows // n_ch), 8)
-    starts = [min(h * part, rows - part) for h in range(n_ch)]
-    per_ch = n_seq // n_ch
     cos_table, sin_table, twist = (jnp.asarray(a) for a in wave_tables(tokens))
 
     place = jnp.stack([seq_index, ch_index]).astype(jnp.int32)
@@ -285,58 +305,30 @@
     spectrum = jax.ShapeDtypeStruct((part, tokens), F32)
     weight = qkv_weight.transpose(1, 0, 2)
 
-    def project(pieces):
+    def project(pieces, outs):
         span = sum(piece.shape[0] for piece in pieces)
         return call(
-            functools.partial(project_kernel, pieces=len(pieces)),
-            [
-                jax.ShapeDtypeStruct((gates, part, span), F32 if d == 0 else BF16)
-                for d in range(n_ch)
-            ],
+            functools.partial(project_kernel, pieces=len(pieces)), outs,
             2 * gates * rows * width * span, 0, place, weight, *pieces,
             scratch=[pltpu.VMEM((span, width), BF16), pltpu.VMEM((gates, rows, span), F32)],
             indexed=True, late=range(2, 2 + len(pieces)),
         )
 
+    def early(pieces):
+        span = sum(piece.shape[0] for piece in pieces)
+        (sums,) = project(pieces, [jax.ShapeDtypeStruct((n_ch, gates, part, span), BF16)])
+        return sums
+
     def to_owners(sums):
-        return [sums[0]] + [
-            lax.ppermute(sums[d], "ch", [(h, (h + d) % n_ch) for h in range(n_ch)])
-            for d in range(1, n_ch)
-        ]
+        return lax.psum_scatter(sums, "ch", scatter_dimension=0, tiled=False)
+
+    def trade(array, reach):
+        return lax.ppermute(array, "seq", [(d, d ^ reach) for d in range(n_seq)])
 
     pair = send_on((features, features))
-    pieces = [features, *pair]
-    sums = list(project(pieces))
-    grad_out, residues, log_rates, skip_gain, sums[0] = lax.optimization_barrier(
-        (grad_out, residues, log_rates, skip_gain, sums[0])
-    )
-    (upper,) = call(
-        functools.partial(pieces_kernel, rows=rows, n_ch=n_ch),
-        (jax.ShapeDtypeStruct((n_seq, part, block_len), BF16),), 0, 0, grad_out,
-    )
-    upper = lax.all_to_all(upper, "seq", split_axis=0, concat_axis=0, tiled=True)
-    group_slots = [3]
-    partials = to_owners(sums)
-    later = []
-    for step in range(2, n_seq // 2):
-        pair = send_on(pair)
-        if step == 2:
-            pair, upper = lax.optimization_barrier((pair, upper))
-        pieces += pair
-        later += pair
-        if step % 2 == 1 or step == n_seq // 2 - 1:
-            partials += to_owners(project(later))
-            group_slots.append(len(later))
-            later = []
-    half = block_len // 2
-    pair = send_on((pair[0][:half], pair[1][half:]))
-    pieces += pair
-    partials += to_owners(project(list(pair)))
-    group_slots.append(1)
 
     spread = [((q % n_seq) * n_ch + q // n_seq, q) for q in range(n_seq * n_ch)]
     gather_back = [(b, a) for a, b in spread]
-    upper = lax.ppermute(upper, ("seq", "ch"), spread)
     packed = jnp.concatenate([residues, log_rates, skip_gain[:, None]], 1)
     (poles,) = call(
         functools.partial(poles_kernel, rows=rows, n_ch=n_ch),
@@ -348,8 +340,60 @@
         8 * square, part * tokens * order, poles, cos_table, sin_table, twist,
     )
 
+    low, high = call(
+        functools.partial(pieces_kernel, rows=rows, n_ch=n_ch),
+        [jax.ShapeDtypeStruct((n_seq // 2, part, block_len), BF16)] * 2, 0, 0, place, grad_out,
+        scratch=[pltpu.VMEM(grad_out.shape, F32)], indexed=True,
+    )
+    high = trade(high, n_seq // 2)
+    pair, hc, high = lax.optimization_barrier((pair, hc, high))
+    upper = jnp.concatenate([low, high], 0)
+
+    pieces = [features, *pair]
+    group_slots = [3]
+    next_pair = send_on(pair)
+    sums = early(pieces)
+    partials = [to_owners(sums)]
+    reach = n_seq // 4
+    while reach:
+        shaped = upper.reshape(-1, 2, reach, part, block_len)
+        moved = trade(shaped[:, 1], reach)
+        upper = jnp.stack([shaped[:, 0], moved], 1).reshape(n_seq, part, block_len)
+        reach //= 2
+    for step in range(2, n_seq // 2):
+        pair = next_pair
+        if step == 2:
+            pair, upper, sums = lax.optimization_barrier((pair, upper, sums))
+            upper = lax.ppermute(upper, ("seq", "ch"), spread)
+        pieces += pair
+        if step < n_seq // 2 - 1:
+            next_pair = send_on(pair)
+        else:
+            half = block_len // 2
+            halves, pair = lax.optimization_barrier(((pair[0][:half], pair[1][half:]), pair))
+            next_pair = send_on(halves)
+        partials.append(to_owners(early(list(pair))))
+        group_slots.append(2)
+    pair = next_pair
+    pieces += pair
+    last = project(
+        list(pair),
+        [
+            jax.ShapeDtypeStruct((gates, part, block_len), F32 if d == 0 else BF16)
+            for d in range(n_ch)
+        ],
+    )
+    group_slots.append(1)
+    group_shares = [1] * len(partials) + [n_ch]
+    partials += [last[0]] + [
+        lax.ppermute(last[d], "ch", [(h, (h + d) % n_ch) for h in range(n_ch)])
+        for d in range(1, n_ch)
+    ]
+
     grads, tgc, tgs, skip_sum = call(
-        functools.partial(conv_kernel, order=order, group_slots=group_slots, shares=n_ch),
+        functools.partial(
+            conv_kernel, order=order, n_ch=n_ch, group_slots=group_slots, group_shares=group_shares
+        ),
         (
             jax.ShapeDtypeStruct((gates, part, tokens), BF16),
             spectrum,
@@ -403,17 +447,16 @@
     )(place, *held, *pieces)
     weight_grad = weight_grad.transpose(1, 0, 2)
 
-    returned = lax.ppermute(pole_sums, ("seq", "ch"), gather_back)
-    returned = jnp.broadcast_to(returned[None], (n_seq,) + returned.shape)
-    returned = lax.all_to_all(returned, "seq", split_axis=0, concat_axis=0, tiled=True)
-    pieces = []
-    for block in range(per_ch):
-        filled = 0
-        for h, begin in enumerate(starts):
-            if begin + part > filled:
-                pieces.append(returned[block * n_ch + h, filled - begin :])
-                filled = begin + part
-    sums = jnp.concatenate(pieces, 0)
+    returned = lax.ppermute(pole_sums, ("seq", "ch"), gather_back)[None]
+    reach = 1
+    while reach < n_seq:
+        returned = jnp.concatenate([returned, trade(returned, reach)], 0)
+        reach *= 2
+    (sums,) = call(
+        functools.partial(assemble_kernel, rows=rows, n_ch=n_ch),
+        [jax.ShapeDtypeStruct((residues.shape[0], 2 * order + 1), F32)], 0, 0, place, returned,
+        indexed=True,
+    )
     return (weight_grad, sums[:, :order], sums[:, order : 2 * order], sums[:, 2 * order])
 
 

time: 127 us -> 170 us (1.34)
  waiting for transfers between devices: 29.2 us -> 52 us
  local copies, waits for them, and re-layouts: 13.8 us -> 31.2 us
  blocking collectives: 13.6 us -> 0 us
  between operations: 0.99 us -> 14.1 us
  starting transfers between devices: 40 us -> 44.2 us
    ppermute x10, waiting for transfers between devices: 0.61 us -> 20.5 us  [the longest x6 18.5 us: trade(): return lax.ppermute(array, 'seq', [(d, d ^ reach) for d in range(n_seq)])]
    unnamed x59 -> x75, local copies, waits for them, and re-layouts: 9.31 us -> 27.1 us
    ppermute x10, starting transfers between devices: 14 us -> 30.8 us  [the longest x6 27.5 us: trade(): return lax.ppermute(array, 'seq', [(d, d ^ reach) for d in range(n_seq)])]
    all_to_all x1 -> x0, blocking collectives: 13.6 us -> none  [local(): lax.all_to_all(upper, 'seq', split_axis=0, concat_axis=0, tiled=True)]
    all_to_all x1 -> x0, starting transfers between devices: 13.2 us -> none  [local(): lax.all_to_all(returned, 'seq', split_axis=0, concat_axis=0, tiled=True)]
    reduce_scatter x0 -> x2, waiting for transfers between devices: none -> 12.3 us  [to_owners(): return lax.psum_scatter(sums, 'ch', scatter_dimension=0, tiled=False)]
    ppermute x4, waiting for transfers between devices: 12.1 us -> 0.07 us  [send_on(): lax.ppermute(pair[1], 'seq', behind)]
    ppermute x4, waiting for transfers between devices: 8.78 us -> 17.7 us  [send_on(): lax.ppermute(pair[0], 'seq', ahead)]
  transfers between devices with their start and end apart: 24 -> 26, of which waited for: 6 -> 12; matrix products, arithmetic and copies ran while one was open for 5% -> 5% of each run, Pallas kernels for 11% -> 7%
where the time goes in v3:
time: 170 us; the launch traced here: 169 us
  waiting for transfers between devices  52 us (31%)
  starting transfers between devices  44.2 us (26%)
  local copies, waits for them, and re-layouts  31.2 us (18%)
  Pallas kernels  25.7 us (15%)
  between operations  14.1 us (8%)
  other arithmetic  2.23 us (1%)
    ppermute x6, starting transfers between devices, trade(): return lax.ppermute(array, 'seq', [(d, d ^ reach) for d in range(n_seq)])  27.5 us
    unnamed x75, local copies, waits for them, and re-layouts  27.1 us
    pallas_call x10, Pallas kernels, call(): pl.pallas_call(kernel, out_shape=outs, in_specs=specs, out_specs=[whole]...  19.4 us
    ppermute x6, waiting for transfers between devices, trade(): return lax.ppermute(array, 'seq', [(d, d ^ reach) for d in range(n_seq)])  18.5 us
    ppermute x4, waiting for transfers between devices, send_on(): lax.ppermute(pair[0], 'seq', ahead)  17.7 us
    reduce_scatter x2, waiting for transfers between devices, to_owners(): return lax.psum_scatter(sums, 'ch', scatter_dimension=0, tiled=False)  12.3 us
    ppermute x4, starting transfers between devices, send_on(): lax.ppermute(pair[1], 'seq', behind)  9.29 us
    pallas_call x1, Pallas kernels, local(): pl.pallas_call(functools.partial(weight_kernel, shares=n_ch), out_shape=j...  6.28 us
  transfers between devices with their start and end apart: 26, of which 12 were waited for; matrix products, arithmetic and copies ran while one was open for 5% of the time, Pallas kernels for 7%

profile of v3, /device:TPU:0, one launch (start us, length us, event | category | flops | bytes accessed | tf_op | source)
XLA Modules:
  0.0 169.4 jit_solution(8127282174206715747)
XLA Ops:
  7.2 3.0 %collective-permute-start.1 = (bf16[128,2048]{1,0:T(8,128)(2,1)}, bf16[128,2048]{1,0:T(8,128)(2,1)S(1)}, u32[]{:S(2)}, u32[]{:S(2)}) collective-permute-start(bf16[128,2048]{1,0:T(8,128)(2,1)} %refs_4_.1), channel_id=1, source_target_pairs={{8,0},{16,8},{24,16},{28,24},{20,28},{12,20},{4,12},{0,4},{9,1},{1... | collective-permute-start | bytes 1572872 | tf_op jit(solution)/shard_map/ppermute | solution.py:302
  11.9 3.0 %collective-permute-start.3 = (bf16[4,56,128]{2,1,0:T(8,128)(2,1)S(1)}, bf16[4,56,128]{2,1,0:T(8,128)(2,1)S(1)}, u32[]{:S(2)}, u32[]{:S(2)}) collective-permute-start(bf16[4,56,128]{2,1,0:T(8,128)(2,1)S(1)} %get-tuple-element.30), channel_id=1, source_target_pairs={{0,16},{4,20},{8,24},{12,28},{16,0},{20,4},{24,8},{28,12},{1,17},{... | collective-permute-start | bytes 172040 | tf_op jit(solution)/shard_map/ppermute | solution.py:326
  18.7 1.6 copy-done.1
  20.3 1.6 copy-done.3
  22.6 1.5 shard_map.121
  24.8 1.6 collective-permute-done.3
  26.4 3.3 %shard_map.123 = bf16[4,3,56,384]{3,2,1,0:T(8,128)(2,1)S(1)} custom-call(s32[2]{0:T(128)S(1)} %pad_add_fusion.place_ref, bf16[3,208,2048]{2,1,0:T(8,128)(2,1)S(1)} %bitcast.23, bf16[128,2048]{1,0:T(8,128)(2,1)S(1)} %copy-done.7, bf16[128,2048]{1,0:T(8,128)(2,1)} %collective-permute-done.refs_1_.refs_5_, ...), custom_call_target="tpu_custom_call" | custom-call | flops 981467136 | bytes 4644872 | tf_op jit(solution)/shard_map/pallas_call | solution.py:266
  30.6 5.0 %collective-permute-start.6 = (bf16[2,2,56,128]{3,2,1,0:T(8,128)(2,1)S(1)}, bf16[2,2,56,128]{3,2,1,0:T(8,128)(2,1)S(1)}, u32[]{:S(2)}, u32[]{:S(2)}) collective-permute-start(bf16[2,2,56,128]{3,2,1,0:T(8,128)(2,1)S(1)} %get-tuple-element.71), channel_id=1, source_target_pairs={{0,8},{4,12},{8,0},{12,4},{16,24},{20,28},{24,16},{28,20},{1,9},{5... | collective-permute-start | bytes 172040 | tf_op jit(solution)/shard_map/ppermute | solution.py:326
  35.7 3.1 %collective-permute-start.5 = (bf16[128,2048]{1,0:T(8,128)(2,1)S(1)}, bf16[128,2048]{1,0:T(8,128)(2,1)S(1)}, u32[]{:S(2)}, u32[]{:S(2)}) collective-permute-start(bf16[128,2048]{1,0:T(8,128)(2,1)S(1)} %collective-permute-done.1.refs_2_.refs_6_), channel_id=1, source_target_pairs={{8,0},{16,8},{24,16},{28,24},{20,28},{12,20},{4,12},{0,4},{9,1},{1... | collective-permute-start | bytes 1572872 | tf_op jit(solution)/shard_map/ppermute | solution.py:302
  38.8 4.1 %collective-permute-start.7 = (bf16[4,1,56,128]{3,2,0,1:T(8,128)(2,1)S(1)}, bf16[4,1,56,128]{3,2,0,1:T(8,128)(2,1)S(1)}, u32[]{:S(2)}, u32[]{:S(2)}) collective-permute-start(bf16[4,1,56,128]{3,2,0,1:T(8,128)(2,1)S(1)} %get-tuple-element.69), channel_id=1, source_target_pairs={{0,4},{4,0},{8,12},{12,8},{16,20},{20,16},{24,28},{28,24},{1,5},{5... | collective-permute-start | bytes 172040 | tf_op jit(solution)/shard_map/ppermute | solution.py:326
  42.9 8.9 %collective-permute-done.7 = bf16[4,1,56,128]{3,2,0,1:T(8,128)(2,1)S(1)} collective-permute-done((bf16[4,1,56,128]{3,2,0,1:T(8,128)(2,1)S(1)}, bf16[4,1,56,128]{3,2,0,1:T(8,128)(2,1)S(1)}, u32[]{:S(2)}, u32[]{:S(2)}) %collective-permute-start.7) | collective-permute-done | bytes 57376 | tf_op jit(solution)/shard_map/ppermute | solution.py:326
  52.4 2.5 %shard_map.124 = bf16[4,3,56,256]{3,2,1,0:T(8,128)(2,1)} custom-call(s32[2]{0:T(128)S(1)} %pad_add_fusion.place_ref, bf16[3,208,2048]{2,1,0:T(8,128)(2,1)S(1)} %bitcast.24, bf16[128,2048]{1,0:T(8,128)(2,1)S(1)} %collective-permute-done.4.refs_0_.refs_7_, bf16[128,2048]{1,0:T(8,128)(2,1)S(1)} %collective-permute-done.5.refs_1_.refs_8_), custom_call_target="tpu_custom_call" | custom-call | flops 654311424 | bytes 3948552 | tf_op jit(solution)/shard_map/pallas_call | solution.py:266
  58.9 12.8 %collective-permute-done.8.refs_0_.refs_9_ = bf16[128,2048]{1,0:T(8,128)(2,1)S(1)} collective-permute-done((bf16[128,2048]{1,0:T(8,128)(2,1)}, bf16[128,2048]{1,0:T(8,128)(2,1)S(1)}, u32[]{:S(2)}, u32[]{:S(2)}) %collective-permute-start.8) | collective-permute-done | bytes 524320 | tf_op jit(solution)/shard_map/ppermute | solution.py:302
  73.4 2.5 %shard_map.125 = bf16[4,3,56,256]{3,2,1,0:T(8,128)(2,1)} custom-call(s32[2]{0:T(128)S(1)} %pad_add_fusion.place_ref, bf16[3,208,2048]{2,1,0:T(8,128)(2,1)S(1)} %bitcast.25, bf16[128,2048]{1,0:T(8,128)(2,1)S(1)} %collective-permute-done.8.refs_0_.refs_9_, bf16[128,2048]{1,0:T(8,128)(2,1)S(1)} %collective-permute-done.9.refs_1_.refs_10_), custom_call_target="tpu_custom_call" | custom-call | flops 654311424 | bytes 3948552 | tf_op jit(solution)/shard_map/pallas_call | solution.py:266
  76.1 1.9 %collective-permute-start.11 = (bf16[64,2048]{1,0:T(8,128)(2,1)}, bf16[64,2048]{1,0:T(8,128)(2,1)S(1)}, u32[]{:S(2)}, u32[]{:S(2)}) collective-permute-start(bf16[64,2048]{1,0:T(8,128)(2,1)} %slice.41), channel_id=1, source_target_pairs={{8,0},{16,8},{24,16},{28,24},{20,28},{12,20},{4,12},{0,4},{9,1},{1... | collective-permute-start | bytes 786440 | tf_op jit(solution)/shard_map/ppermute | solution.py:302
  78.0 1.5 collective-permute-start.15
  79.6 4.9 %collective-permute-done.10.refs_0_.refs_11_ = bf16[64,2048]{1,0:T(8,128)(2,1)S(1)} collective-permute-done((bf16[64,2048]{1,0:T(8,128)(2,1)}, bf16[64,2048]{1,0:T(8,128)(2,1)S(1)}, u32[]{:S(2)}, u32[]{:S(2)}) %collective-permute-start.10) | collective-permute-done | bytes 262176 | tf_op jit(solution)/shard_map/ppermute | solution.py:302
  84.5 2.1 %shard_map.126 = (f32[3,56,128]{2,1,0:T(8,128)S(1)}, bf16[3,56,128]{2,1,0:T(8,128)(2,1)}, bf16[3,56,128]{2,1,0:T(8,128)(2,1)}, bf16[3,56,128]{2,1,0:T(8,128)(2,1)}) custom-call(s32[2]{0:T(128)S(1)} %pad_add_fusion.place_ref, bf16[3,208,2048]{2,1,0:T(8,128)(2,1)S(1)} %bitcast.26, bf16[64,2048]{1,0:T(8,128)(2,1)S(1)} %collective-permute-done.10.refs_0_.refs_11_, ...), custom_call_target="tpu_custom_call" | custom-call | flops 327155712 | bytes 3295240 | tf_op jit(solution)/shard_map/pallas_call | solution.py:266
  88.3 1.4 collective-permute-start.14
  91.8 12.3 %reduce-scatter.8.cloned.1.call-done = bf16[1,3,56,256]{3,2,1,0:T(8,128)(2,1)} async-done(((bf16[4,3,56,256]{3,2,1,0:T(8,128)(2,1)}), bf16[1,3,56,256]{3,2,1,0:T(8,128)(2,1)}) %reduce-scatter.8.cloned.1.call-update) | async-done | bytes 86032 | tf_op jit(solution)/shard_map/reduce_scatter | solution.py:323
  104.1 1.6 copy-done.2
  105.7 1.6 copy-done.4
  112.8 3.8 %shard_map.127 = (bf16[3,56,1024]{2,1,0:T(8,128)(2,1)S(1)}, f32[56,1024]{1,0:T(8,128)S(1)}, f32[56,1024]{1,0:T(8,128)S(1)}, f32[56,1]{1,0:T(8,128)S(1)}) custom-call(s32[2]{0:T(128)S(1)} %pad_add_fusion.place_ref, bf16[3,56,384]{2,1,0:T(8,128)(2,1)S(1)} %bitcast.27, bf16[3,56,256]{2,1,0:T(8,128)(2,1)S(1)} %bitcast.28, bf16[3,56,256]{2,1,0:T(8,128)(2,1)S(1)} %bitcast.29, ...), custom_call_target="tpu_custom_call" | custom-call | flops 1879048192 | bytes 6102472 | tf_op jit(solution)/shard_map/pallas_call | solution.py:266
  119.0 2.0 %shard_map.129 = f32[56,33]{1,0:T(8,128)S(1)} custom-call(f32[56,33]{1,0:T(8,128)S(1)} %collective-permute-done.2.poles_ref.refs_8_, f32[56,1024]{1,0:T(8,128)S(1)} %get-tuple-element.51.tgc_ref, f32[56,1024]{1,0:T(8,128)S(1)} %get-tuple-element.52.tgs_ref, bf16[1024,1024]{1,0:T(8,128)(2,1)S(1)} %copy-done.4, bf16[1024,1024]{1,0:T(8,128)(2,1)S(1)} %copy-done.2, ...), custom_call_target="tpu_custom_call" | custom-call | flops 469762048 | bytes 4668064 | tf_op jit(solution)/shard_map/pallas_call | solution.py:266
  121.9 6.6 %collective-permute-start.20 = (f32[1,56,33]{2,1,0:T(8,128)S(1)}, f32[1,56,33]{2,1,0:T(8,128)S(1)}, u32[]{:S(2)}, u32[]{:S(2)}) collective-permute-start(f32[1,56,33]{2,1,0:T(8,128)S(1)} %bitcast.33), channel_id=1, source_target_pairs={{0,4},{4,0},{8,12},{12,8},{16,20},{20,16},{24,28},{28,24},{1,5},{5... | collective-permute-start | bytes 22184 | tf_op jit(solution)/shard_map/ppermute | solution.py:326
  128.5 1.8 %collective-permute-done.20 = f32[1,56,33]{2,1,0:T(8,128)S(1)} collective-permute-done((f32[1,56,33]{2,1,0:T(8,128)S(1)}, f32[1,56,33]{2,1,0:T(8,128)S(1)}, u32[]{:S(2)}, u32[]{:S(2)}) %collective-permute-start.20) | collective-permute-done | bytes 7424 | tf_op jit(solution)/shard_map/ppermute | solution.py:326
  130.4 2.9 %collective-permute-start.21 = (f32[2,56,33]{2,1,0:T(8,128)S(1)}, f32[2,56,33]{2,1,0:T(8,128)S(1)}, u32[]{:S(2)}, u32[]{:S(2)}) collective-permute-start(f32[2,56,33]{2,1,0:T(8,128)S(1)} %pad_maximum_fusion.6), channel_id=1, source_target_pairs={{0,8},{4,12},{8,0},{12,4},{16,24},{20,28},{24,16},{28,20},{1,9},{5... | collective-permute-start | bytes 44360 | tf_op jit(solution)/shard_map/ppermute | solution.py:326
  133.3 2.2 %collective-permute-done.21 = f32[2,56,33]{2,1,0:T(8,128)S(1)} collective-permute-done((f32[2,56,33]{2,1,0:T(8,128)S(1)}, f32[2,56,33]{2,1,0:T(8,128)S(1)}, u32[]{:S(2)}, u32[]{:S(2)}) %collective-permute-start.21) | collective-permute-done | bytes 14816 | tf_op jit(solution)/shard_map/ppermute | solution.py:326
  135.5 5.8 %collective-permute-start.22 = (f32[4,56,33]{2,1,0:T(8,128)S(1)}, f32[4,56,33]{2,1,0:T(8,128)S(1)}, u32[]{:S(2)}, u32[]{:S(2)}) collective-permute-start(f32[4,56,33]{2,1,0:T(8,128)S(1)} %pad_maximum_fusion.4), channel_id=1, source_target_pairs={{0,16},{4,20},{8,24},{12,28},{16,0},{20,4},{24,8},{28,12},{1,17},{... | collective-permute-start | bytes 88712 | tf_op jit(solution)/shard_map/ppermute | solution.py:326
  141.3 4.0 %collective-permute-done.22 = f32[4,56,33]{2,1,0:T(8,128)S(1)} collective-permute-done((f32[4,56,33]{2,1,0:T(8,128)S(1)}, f32[4,56,33]{2,1,0:T(8,128)S(1)}, u32[]{:S(2)}, u32[]{:S(2)}) %collective-permute-start.22) | collective-permute-done | bytes 29600 | tf_op jit(solution)/shard_map/ppermute | solution.py:326
  146.7 1.7 copy.33
  156.6 6.3 %shard_map.128 = f32[3,208,2048]{2,1,0:T(8,128)} custom-call(s32[2]{0:T(128)S(1)} %pad_add_fusion.place_ref, bf16[3,56,1024]{2,1,0:T(8,128)(2,1)S(1)} %copy-done.19, bf16[3,56,1024]{2,1,0:T(8,128)(2,1)} %collective-permute-done.16.refs_1_, bf16[3,56,1024]{2,1,0:T(8,128)(2,1)S(1)} %copy-done.21, bf16[3,56,1024]{2,1,0:T(8,128)(2,1)S(1)} %copy-done.23, ...), custom_call_target="tpu_custom_call" | custom-call | flops 2617245696 | bytes 10584064 | tf_op jit(solution)/shard_map/pallas_call | solution.py:426
  (124 shorter events, 36.5 us)
Async XLA Ops:
  7.2 19.2 %copy-start = (bf16[208,3,2048]{2,0,1:T(8,128)(2,1)S(1)}, bf16[208,3,2048]{2,0,1:T(8,128)(2,1)}, u32[]{:S(2)}) copy-start(bf16[208,3,2048]{2,0,1:T(8,128)(2,1)} %param.10) | copy-start | bytes 7667716
  7.2 82.6 %reduce-scatter.10.cloned.1.call-start = ((), (), s32[]{:S(2)}) async-start(), calls=%async_computation.5 | async-start | bytes 645120
  7.2 19.2 %collective-permute-start.1 = (bf16[128,2048]{1,0:T(8,128)(2,1)}, bf16[128,2048]{1,0:T(8,128)(2,1)S(1)}, u32[]{:S(2)}, u32[]{:S(2)}) collective-permute-start(bf16[128,2048]{1,0:T(8,128)(2,1)} %refs_4_.1), channel_id=1, source_target_pairs={{8,0},{16,8},{24,16},{28,24},{20,28},{12,20},{4,12},{0,4},{9,1},{1... | collective-permute-start | bytes 1572872 | tf_op jit(solution)/shard_map/ppermute | solution.py:302
  10.2 16.2 %collective-permute-start = (bf16[128,2048]{1,0:T(8,128)(2,1)}, bf16[128,2048]{1,0:T(8,128)(2,1)}, u32[]{:S(2)}, u32[]{:S(2)}) collective-permute-start(bf16[128,2048]{1,0:T(8,128)(2,1)} %refs_4_.1), channel_id=1, source_target_pairs={{0,8},{8,16},{16,24},{24,28},{28,20},{20,12},{12,4},{4,0},{1,9},{9... | collective-permute-start | bytes 1572872 | tf_op jit(solution)/shard_map/ppermute | solution.py:302
  11.9 14.4 %collective-permute-start.3 = (bf16[4,56,128]{2,1,0:T(8,128)(2,1)S(1)}, bf16[4,56,128]{2,1,0:T(8,128)(2,1)S(1)}, u32[]{:S(2)}, u32[]{:S(2)}) collective-permute-start(bf16[4,56,128]{2,1,0:T(8,128)(2,1)S(1)} %get-tuple-element.30), channel_id=1, source_target_pairs={{0,16},{4,20},{8,24},{12,28},{16,0},{20,4},{24,8},{28,12},{1,17},{... | collective-permute-start | bytes 172040 | tf_op jit(solution)/shard_map/ppermute | solution.py:326
  18.0 0.7 collective-permute-start.2
  30.5 59.3 %reduce-scatter.6.cloned.1.call-start = ((), (), s32[]{:S(2)}) async-start(), calls=%async_computation.3 | async-start | bytes 430080 | tf_op jit(solution)/shard_map/reduce_scatter | solution.py:323
  30.6 8.1 %collective-permute-start.6 = (bf16[2,2,56,128]{3,2,1,0:T(8,128)(2,1)S(1)}, bf16[2,2,56,128]{3,2,1,0:T(8,128)(2,1)S(1)}, u32[]{:S(2)}, u32[]{:S(2)}) collective-permute-start(bf16[2,2,56,128]{3,2,1,0:T(8,128)(2,1)S(1)} %get-tuple-element.71), channel_id=1, source_target_pairs={{0,8},{4,12},{8,0},{12,4},{16,24},{20,28},{24,16},{28,20},{1,9},{5... | collective-permute-start | bytes 172040 | tf_op jit(solution)/shard_map/ppermute | solution.py:326
  35.6 16.8 %collective-permute-start.4 = (bf16[128,2048]{1,0:T(8,128)(2,1)}, bf16[128,2048]{1,0:T(8,128)(2,1)S(1)}, u32[]{:S(2)}, u32[]{:S(2)}) collective-permute-start(bf16[128,2048]{1,0:T(8,128)(2,1)} %collective-permute-done.refs_1_.refs_5_), channel_id=1, source_target_pairs={{0,8},{8,16},{16,24},{24,28},{28,20},{20,12},{12,4},{4,0},{1,9},{9... | collective-permute-start | bytes 1572872 | tf_op jit(solution)/shard_map/ppermute | solution.py:302
  35.7 16.8 %collective-permute-start.5 = (bf16[128,2048]{1,0:T(8,128)(2,1)S(1)}, bf16[128,2048]{1,0:T(8,128)(2,1)S(1)}, u32[]{:S(2)}, u32[]{:S(2)}) collective-permute-start(bf16[128,2048]{1,0:T(8,128)(2,1)S(1)} %collective-permute-done.1.refs_2_.refs_6_), channel_id=1, source_target_pairs={{8,0},{16,8},{24,16},{28,24},{20,28},{12,20},{4,12},{0,4},{9,1},{1... | collective-permute-start | bytes 1572872 | tf_op jit(solution)/shard_map/ppermute | solution.py:302
  38.8 13.0 %collective-permute-start.7 = (bf16[4,1,56,128]{3,2,0,1:T(8,128)(2,1)S(1)}, bf16[4,1,56,128]{3,2,0,1:T(8,128)(2,1)S(1)}, u32[]{:S(2)}, u32[]{:S(2)}) collective-permute-start(bf16[4,1,56,128]{3,2,0,1:T(8,128)(2,1)S(1)} %get-tuple-element.69), channel_id=1, source_target_pairs={{0,4},{4,0},{8,12},{12,8},{16,20},{20,16},{24,28},{28,24},{1,5},{5... | collective-permute-start | bytes 172040 | tf_op jit(solution)/shard_map/ppermute | solution.py:326
  56.5 47.6 %reduce-scatter.8.cloned.1.call-start = ((), (), s32[]{:S(2)}) async-start(), calls=%async_computation.4 | async-start | bytes 430080 | tf_op jit(solution)/shard_map/reduce_scatter | solution.py:323
  56.6 15.2 %collective-permute-start.8 = (bf16[128,2048]{1,0:T(8,128)(2,1)}, bf16[128,2048]{1,0:T(8,128)(2,1)S(1)}, u32[]{:S(2)}, u32[]{:S(2)}) collective-permute-start(bf16[128,2048]{1,0:T(8,128)(2,1)} %copy-done.11), channel_id=1, source_target_pairs={{0,8},{8,16},{16,24},{24,28},{28,20},{20,12},{12,4},{4,0},{1,9},{9... | collective-permute-start | bytes 1572872 | tf_op jit(solution)/shard_map/ppermute | solution.py:302
  57.6 14.9 %collective-permute-start.9 = (bf16[128,2048]{1,0:T(8,128)(2,1)}, bf16[128,2048]{1,0:T(8,128)(2,1)S(1)}, u32[]{:S(2)}, u32[]{:S(2)}) collective-permute-start(bf16[128,2048]{1,0:T(8,128)(2,1)} %copy-done.13), channel_id=1, source_target_pairs={{8,0},{16,8},{24,16},{28,24},{20,28},{12,20},{4,12},{0,4},{9,1},{1... | collective-permute-start | bytes 1572872 | tf_op jit(solution)/shard_map/ppermute | solution.py:302
  75.9 28.2 %copy-start.26 = (f32[2,1024]{1,0:T(2,128)S(1)}, f32[2,1024]{1,0:T(2,128)}, u32[]{:S(2)}) copy-start(f32[2,1024]{1,0:T(2,128)} %constant.17.clone.twist_ref.refs_13_) | copy-start | bytes 24580
  75.9 8.5 %collective-permute-start.10 = (bf16[64,2048]{1,0:T(8,128)(2,1)}, bf16[64,2048]{1,0:T(8,128)(2,1)S(1)}, u32[]{:S(2)}, u32[]{:S(2)}) collective-permute-start(bf16[64,2048]{1,0:T(8,128)(2,1)} %slice.40), channel_id=1, source_target_pairs={{0,8},{8,16},{16,24},{24,28},{28,20},{20,12},{12,4},{4,0},{1,9},{9... | collective-permute-start | bytes 786440 | tf_op jit(solution)/shard_map/ppermute | solution.py:302
  76.1 8.4 %collective-permute-start.11 = (bf16[64,2048]{1,0:T(8,128)(2,1)}, bf16[64,2048]{1,0:T(8,128)(2,1)S(1)}, u32[]{:S(2)}, u32[]{:S(2)}) collective-permute-start(bf16[64,2048]{1,0:T(8,128)(2,1)} %slice.41), channel_id=1, source_target_pairs={{8,0},{16,8},{24,16},{28,24},{20,28},{12,20},{4,12},{0,4},{9,1},{1... | collective-permute-start | bytes 786440 | tf_op jit(solution)/shard_map/ppermute | solution.py:302
  78.0 11.7 %collective-permute-start.15 = (bf16[8,56,128]{2,1,0:T(8,128)(2,1)}, bf16[8,56,128]{2,1,0:T(8,128)(2,1)S(1)}, u32[]{:S(2)}, u32[]{:S(2)}) collective-permute-start(bf16[8,56,128]{2,1,0:T(8,128)(2,1)} %bitcast.37), channel_id=1, source_target_pairs={{0,0},{4,1},{8,2},{12,3},{16,4},{20,5},{24,6},{28,7},{1,8},{5,9},{... | collective-permute-start | bytes 344072 | tf_op jit(solution)/shard_map/ppermute | solution.py:367
  87.2 3.7 %collective-permute-start.12 = (bf16[3,56,128]{2,1,0:T(8,128)(2,1)}, bf16[3,56,128]{2,1,0:T(8,128)(2,1)S(1)}, u32[]{:S(2)}, u32[]{:S(2)}) collective-permute-start(bf16[3,56,128]{2,1,0:T(8,128)(2,1)} %get-tuple-element.42), channel_id=1, source_target_pairs={{0,1},{1,2},{2,3},{3,0},{4,5},{5,6},{6,7},{7,4},{8,9},{9,10},{10,1... | collective-permute-start | bytes 129032 | tf_op jit(solution)/shard_map/ppermute | solution.py:389
  87.2 4.5 %collective-permute-start.13 = (bf16[3,56,128]{2,1,0:T(8,128)(2,1)}, bf16[3,56,128]{2,1,0:T(8,128)(2,1)S(1)}, u32[]{:S(2)}, u32[]{:S(2)}) collective-permute-start(bf16[3,56,128]{2,1,0:T(8,128)(2,1)} %get-tuple-element.43), channel_id=1, source_target_pairs={{0,2},{1,3},{2,0},{3,1},{4,6},{5,7},{6,4},{7,5},{8,10},{9,11},{10,... | collective-permute-start | bytes 129032 | tf_op jit(solution)/shard_map/ppermute | solution.py:389
  88.3 3.5 %collective-permute-start.14 = (bf16[3,56,128]{2,1,0:T(8,128)(2,1)}, bf16[3,56,128]{2,1,0:T(8,128)(2,1)S(1)}, u32[]{:S(2)}, u32[]{:S(2)}) collective-permute-start(bf16[3,56,128]{2,1,0:T(8,128)(2,1)} %get-tuple-element.44), channel_id=1, source_target_pairs={{0,3},{1,0},{2,1},{3,2},{4,7},{5,4},{6,5},{7,6},{8,11},{9,8},{10,9... | collective-permute-start | bytes 129032 | tf_op jit(solution)/shard_map/ppermute | solution.py:389
  116.6 28.8 %copy-start.18 = (bf16[3,56,1024]{2,1,0:T(8,128)(2,1)}, bf16[3,56,1024]{2,1,0:T(8,128)(2,1)S(1)}, u32[]{:S(2)}) copy-start(bf16[3,56,1024]{2,1,0:T(8,128)(2,1)S(1)} %get-tuple-element.48.refs_0_) | copy-start | bytes 1032196
  116.6 1.7 %collective-permute-start.17 = (bf16[3,56,1024]{2,1,0:T(8,128)(2,1)S(1)}, bf16[3,56,1024]{2,1,0:T(8,128)(2,1)S(1)}, u32[]{:S(2)}, u32[]{:S(2)}) collective-permute-start(bf16[3,56,1024]{2,1,0:T(8,128)(2,1)S(1)} %get-tuple-element.48.refs_0_), channel_id=1, source_target_pairs={{0,1},{1,0},{2,3},{3,2},{4,5},{5,4},{6,7},{7,6},{8,9},{9,8},{10,11... | collective-permute-start | bytes 1032200 | tf_op jit(solution)/shard_map/ppermute | solution.py:415
  116.6 24.6 %collective-permute-start.16 = (bf16[3,56,1024]{2,1,0:T(8,128)(2,1)S(1)}, bf16[3,56,1024]{2,1,0:T(8,128)(2,1)}, u32[]{:S(2)}, u32[]{:S(2)}) collective-permute-start(bf16[3,56,1024]{2,1,0:T(8,128)(2,1)S(1)} %get-tuple-element.48.refs_0_), channel_id=1, source_target_pairs={{0,2},{1,3},{2,0},{3,1},{4,6},{5,7},{6,4},{7,5},{8,10},{9,11},{10,... | collective-permute-start | bytes 1032200 | tf_op jit(solution)/shard_map/ppermute | solution.py:412
  121.1 29.6 %copy-start.6 = (bf16[128,2048]{1,0:T(8,128)(2,1)S(1)}, bf16[128,2048]{1,0:T(8,128)(2,1)}, u32[]{:S(2)}) copy-start(bf16[128,2048]{1,0:T(8,128)(2,1)} %copy-done.5) | copy-start | bytes 1572868
  121.1 29.5 %copy-start.8 = (bf16[128,2048]{1,0:T(8,128)(2,1)S(1)}, bf16[128,2048]{1,0:T(8,128)(2,1)}, u32[]{:S(2)}) copy-start(bf16[128,2048]{1,0:T(8,128)(2,1)} %refs_4_.1) | copy-start | bytes 1572868
  121.1 29.5 %copy-start.10 = (bf16[128,2048]{1,0:T(8,128)(2,1)S(1)}, bf16[128,2048]{1,0:T(8,128)(2,1)}, u32[]{:S(2)}) copy-start(bf16[128,2048]{1,0:T(8,128)(2,1)} %copy-done.9) | copy-start | bytes 1572868
  121.1 0.8 collective-permute-start.19
  121.9 8.5 %collective-permute-start.20 = (f32[1,56,33]{2,1,0:T(8,128)S(1)}, f32[1,56,33]{2,1,0:T(8,128)S(1)}, u32[]{:S(2)}, u32[]{:S(2)}) collective-permute-start(f32[1,56,33]{2,1,0:T(8,128)S(1)} %bitcast.33), channel_id=1, source_target_pairs={{0,4},{4,0},{8,12},{12,8},{16,20},{20,16},{24,28},{28,24},{1,5},{5... | collective-permute-start | bytes 22184 | tf_op jit(solution)/shard_map/ppermute | solution.py:326
  130.4 5.1 %collective-permute-start.21 = (f32[2,56,33]{2,1,0:T(8,128)S(1)}, f32[2,56,33]{2,1,0:T(8,128)S(1)}, u32[]{:S(2)}, u32[]{:S(2)}) collective-permute-start(f32[2,56,33]{2,1,0:T(8,128)S(1)} %pad_maximum_fusion.6), channel_id=1, source_target_pairs={{0,8},{4,12},{8,0},{12,4},{16,24},{20,28},{24,16},{28,20},{1,9},{5... | collective-permute-start | bytes 44360 | tf_op jit(solution)/shard_map/ppermute | solution.py:326
  135.5 9.8 %collective-permute-start.22 = (f32[4,56,33]{2,1,0:T(8,128)S(1)}, f32[4,56,33]{2,1,0:T(8,128)S(1)}, u32[]{:S(2)}, u32[]{:S(2)}) collective-permute-start(f32[4,56,33]{2,1,0:T(8,128)S(1)} %pad_maximum_fusion.4), channel_id=1, source_target_pairs={{0,16},{4,20},{8,24},{12,28},{16,0},{20,4},{24,8},{28,12},{1,17},{... | collective-permute-start | bytes 88712 | tf_op jit(solution)/shard_map/ppermute | solution.py:326
  141.3 8.6 %collective-permute-start.18 = (bf16[3,56,1024]{2,1,0:T(8,128)(2,1)}, bf16[3,56,1024]{2,1,0:T(8,128)(2,1)S(1)}, u32[]{:S(2)}, u32[]{:S(2)}) collective-permute-start(bf16[3,56,1024]{2,1,0:T(8,128)(2,1)} %collective-permute-done.16.refs_1_), channel_id=1, source_target_pairs={{0,1},{1,0},{2,3},{3,2},{4,5},{5,4},{6,7},{7,6},{8,9},{9,8},{10,11... | collective-permute-start | bytes 1032200 | tf_op jit(solution)/shard_map/ppermute | solution.py:423
  (30 other events, 46.4 us)
Sparse Core Ops, SparseCore 0:
  30.6 27.1 reduce-scatter.9
  60.3 20.5 reduce-scatter.5
  83.6 20.4 reduce-scatter.7

commit v4 on v2

--- a/solution.py
+++ b/solution.py
@@ -97,7 +97,7 @@
     out_refs = refs[pieces:-3]
     features_ref, sums_ref, semaphores = refs[-3:]
     gates, _, _ = weight_ref.shape
-    part = out_refs[0].shape[1]
+    part = out_refs[0].shape[-2]
     targets, row = [], 0
     for feature_ref in feature_refs:
         targets.append(features_ref.at[pl.ds(row, feature_ref.shape[0]), :])
@@ -108,8 +108,9 @@
             weight_ref[gate], features_ref[...], (((1,), (1,)), ((), ())),
             preferred_element_type=F32,
         )
+    rows = weight_ref.shape[1]
     for step, out_ref in enumerate(out_refs):
-        start = part_start((place_ref[1] + step) % len(out_refs), part, weight_ref.shape[1])
+        start = part_start((place_ref[1] + step) % len(out_refs), part, rows)
         out_ref[...] = sums_ref[:, pl.ds(start, part), :].astype(out_ref.dtype)
 
 
@@ -124,11 +125,12 @@
 
 
 def conv_kernel(place_ref, *refs, order, group_slots, shares):
-    partial_refs = refs[: len(group_slots) * shares]
+    count = len(group_slots) * shares
+    partial_refs = refs[:count]
     (
         gout_ref, poles_ref, hc_ref, hs_ref, cos_ref, sin_ref, twist_ref,
         grad_ref, tgc_ref, tgs_ref, skip_ref, proj_ref, *scratch_refs,
-    ) = refs[len(group_slots) * shares :]
+    ) = refs[count:]
     *held_refs, semaphores = scratch_refs
     fetch(partial_refs, held_refs, semaphores)
     rows, tokens = hc_ref.shape
@@ -153,9 +155,7 @@
     queries = in_order(0)
     keys = in_order(1)
     values = in_order(2)
-    upper = jnp.concatenate(
-        [gout_ref[b].astype(F32) for b in range(blocks)], 1
-    )
+    upper = jnp.concatenate([gout_ref[b].astype(F32) for b in range(blocks)], 1)
     product = keys * values
     middle = upper * queries
     signals = jnp.concatenate([product, middle], 0)
@@ -204,6 +204,12 @@
     out_ref[:, 2 * order : 2 * order + 1] = skip_ref[...]
 
 
+def share_start(own, share, shares, part, rows):
+    core, step = share // (shares // 2), 2 * (share % (shares // 2))
+    owner = own + core * (1 - 2 * (own % 2))
+    return part_start((owner - step + shares) % shares, part, rows)
+
+
 def weight_kernel(place_ref, *refs, shares):
     grad_refs = refs[:shares]
     *feature_refs, out_ref, wide_ref, rows_ref, features_ref = refs[shares:]
@@ -213,9 +219,7 @@
     @pl.when(pl.program_id(0) == 0)
     def _():
         for share, grad_ref in enumerate(grad_refs):
-            core, step = share // (shares // 2), 2 * (share % (shares // 2))
-            owner = place_ref[1] + core * (1 - 2 * (place_ref[1] % 2))
-            start = part_start((owner - step + shares) % shares, part, out_ref.shape[1])
+            start = share_start(place_ref[1], share, shares, part, out_ref.shape[1])
             wide_ref[:, pl.ds(start, part), :] = grad_ref[...].astype(F32)
         rows_ref[...] = wide_ref[...].astype(BF16)
 
@@ -227,14 +231,36 @@
         out_ref[gate] = dot(rows_ref[gate], features_ref[...])
 
 
-def call(kernel, outs, flops, transcendentals, *operands, scratch=(), indexed=False, late=()):
+def assemble_kernel(place_ref, *refs, rows, order):
+    *block_refs, residue_ref, rate_ref, skip_ref, sums_ref = refs
+    count = len(block_refs)
+    sums_ref[...] = jnp.zeros_like(sums_ref)
+    width = block_refs[0].shape[1]
+    for turn, block_ref in enumerate(block_refs):
+        block = (place_ref[0] + turn) % count
+        sums_ref[pl.ds(pl.multiple_of(block * rows, 8), rows), :width] = block_ref[...]
+    turned = sums_ref[...].T
+    channels = residue_ref.shape[1]
+    residue_ref[...] = turned[:order, :channels]
+    rate_ref[...] = turned[order : 2 * order, :channels]
+    skip_ref[...] = turned[2 * order : 2 * order + 1, :channels]
+
+
+def gather_kernel(place_ref, *refs):
+    *held_refs, out_ref = refs
+    for share, held_ref in enumerate(held_refs):
+        start = share_start(place_ref[1], share, len(held_refs), held_ref.shape[0], out_ref.shape[0])
+        out_ref[pl.ds(start, held_ref.shape[0]), :] = held_ref[...]
+
+
+def call(kernel, outs, flops, transcendentals, *operands, scratch=(), indexed=False, late=(), grant=0):
     size = sum(a.size * a.dtype.itemsize for a in operands) + sum(
         o.size * o.dtype.itemsize for o in outs
     )
     scratch_size = sum(math.prod(a.shape) * a.dtype.itemsize for a in scratch)
     if late:
         scratch = [*scratch, pltpu.SemaphoreType.DMA((len(late),))]
-    limit = min(56 * MIB, 2 * (size + scratch_size) + 8 * MIB)
+    limit = max(grant, min(56 * MIB, 2 * (size + scratch_size) + 8 * MIB))
     whole = pl.BlockSpec(memory_space=pltpu.VMEM)
     specs = [whole] * len(operands)
     if indexed:
@@ -269,8 +295,6 @@
     tokens = n_seq * block_len
     order = residues.shape[1]
     part = round_up(-(-rows // n_ch), 8)
-    starts = [min(h * part, rows - part) for h in range(n_ch)]
-    per_ch = n_seq // n_ch
     cos_table, sin_table, twist = (jnp.asarray(a) for a in wave_tables(tokens))
 
     place = jnp.stack([seq_index, ch_index]).astype(jnp.int32)
@@ -287,7 +311,7 @@
 
     def project(pieces):
         span = sum(piece.shape[0] for piece in pieces)
-        return call(
+        sums = call(
             functools.partial(project_kernel, pieces=len(pieces)),
             [
                 jax.ShapeDtypeStruct((gates, part, span), F32 if d == 0 else BF16)
@@ -297,6 +321,7 @@
             scratch=[pltpu.VMEM((span, width), BF16), pltpu.VMEM((gates, rows, span), F32)],
             indexed=True, late=range(2, 2 + len(pieces)),
         )
+        return list(sums)
 
     def to_owners(sums):
         return [sums[0]] + [
@@ -305,44 +330,51 @@
         ]
 
     pair = send_on((features, features))
-    pieces = [features, *pair]
-    sums = list(project(pieces))
-    grad_out, residues, log_rates, skip_gain, sums[0] = lax.optimization_barrier(
-        (grad_out, residues, log_rates, skip_gain, sums[0])
-    )
+
+    spread = [((q % n_seq) * n_ch + q // n_seq, q) for q in range(n_seq * n_ch)]
     (upper,) = call(
         functools.partial(pieces_kernel, rows=rows, n_ch=n_ch),
         (jax.ShapeDtypeStruct((n_seq, part, block_len), BF16),), 0, 0, grad_out,
     )
     upper = lax.all_to_all(upper, "seq", split_axis=0, concat_axis=0, tiled=True)
-    group_slots = [3]
-    partials = to_owners(sums)
-    later = []
-    for step in range(2, n_seq // 2):
-        pair = send_on(pair)
-        if step == 2:
-            pair, upper = lax.optimization_barrier((pair, upper))
-        pieces += pair
-        later += pair
-        if step % 2 == 1 or step == n_seq // 2 - 1:
-            partials += to_owners(project(later))
-            group_slots.append(len(later))
-            later = []
-    half = block_len // 2
-    pair = send_on((pair[0][:half], pair[1][half:]))
-    pieces += pair
-    partials += to_owners(project(list(pair)))
-    group_slots.append(1)
-
-    spread = [((q % n_seq) * n_ch + q // n_seq, q) for q in range(n_seq * n_ch)]
-    gather_back = [(b, a) for a, b in spread]
-    upper = lax.ppermute(upper, ("seq", "ch"), spread)
+    pair, upper, residues, log_rates, skip_gain = lax.optimization_barrier(
+        (pair, upper, residues, log_rates, skip_gain)
+    )
     packed = jnp.concatenate([residues, log_rates, skip_gain[:, None]], 1)
     (poles,) = call(
         functools.partial(poles_kernel, rows=rows, n_ch=n_ch),
         (jax.ShapeDtypeStruct((part, packed.shape[1]), F32),), 0, 0, place, packed, indexed=True,
     )
-    poles = lax.ppermute(poles, ("seq", "ch"), spread)
+
+    pieces = [features, *pair]
+    group_slots = [3]
+    next_pair = send_on(pair)
+    sums = project(pieces)
+    partials = to_owners(sums)
+    for step in range(2, n_seq // 2):
+        pair = next_pair
+        if step == 2:
+            pair, poles, upper, sums[0] = lax.optimization_barrier((pair, poles, upper, sums[0]))
+            partials[0] = sums[0]
+        pieces += pair
+        if step < n_seq // 2 - 1:
+            next_pair = send_on(pair)
+        else:
+            half = block_len // 2
+            pair, poles, upper, partials[: n_ch + 1] = lax.optimization_barrier(
+                (pair, poles, upper, partials[: n_ch + 1])
+            )
+            halves, pair = lax.optimization_barrier(((pair[0][:half], pair[1][half:]), pair))
+            next_pair = send_on(halves)
+        if step == 2:
+            poles = lax.ppermute(poles, ("seq", "ch"), spread)
+            upper = lax.ppermute(upper, ("seq", "ch"), spread)
+        partials += to_owners(project(list(pair)))
+        group_slots.append(2)
+    pair = next_pair
+    pieces += pair
+    partials += to_owners(project(list(pair)))
+    group_slots.append(1)
     hc, hs = call(
         functools.partial(taps_kernel, order=order), (spectrum, spectrum),
         8 * square, part * tokens * order, poles, cos_table, sin_table, twist,
@@ -360,14 +392,18 @@
         cos_table, sin_table, twist,
         scratch=[pltpu.VMEM((n_seq, gates, part, block_len), F32)]
         + [pltpu.VMEM(a.shape, a.dtype) for a in partials],
-        indexed=True, late=range(1, 1 + len(partials)),
+        indexed=True, late=range(1, 1 + len(partials)), grant=60 * MIB,
     )
 
     swap = [(h, h ^ 1) for h in range(n_ch)]
-    across = [
-        lax.ppermute(grads, "ch", [(h, (h + d) % n_ch) for h in range(n_ch)])
-        for d in range(2, n_ch, 2)
-    ]
+
+    def chips(array):
+        return [
+            lax.ppermute(array, "ch", [(h, (h + d) % n_ch) for h in range(n_ch)])
+            for d in range(2, n_ch, 2)
+        ]
+
+    across = chips(grads)
     swapped = lax.ppermute(grads, "ch", swap)
     tgc, swapped = lax.optimization_barrier((tgc, swapped))
     (pole_sums,) = call(
@@ -377,6 +413,22 @@
     )
 
     held = [grads] + across + [swapped] + [lax.ppermute(a, "ch", swap) for a in across]
+
+    sums = [pole_sums] + chips(pole_sums)
+    sums += [lax.ppermute(a, "ch", swap) for a in sums]
+    (block_sums,) = call(
+        gather_kernel, [jax.ShapeDtypeStruct((rows, 2 * order + 1), F32)], 0, 0, place, *sums,
+        indexed=True,
+    )
+    turns = n_seq // n_ch
+    blocks = []
+    for turn in range(turns):
+        route = [
+            ((h * turns + (s + turn) % turns) * n_ch + s // turns, s * n_ch + h)
+            for s in range(n_seq)
+            for h in range(n_ch)
+        ]
+        blocks.append(lax.ppermute(block_sums, ("seq", "ch"), route))
 
     tile = min(512, width)
     weight_grad = pl.pallas_call(
@@ -393,7 +445,7 @@
             pltpu.VMEM((tokens, tile), BF16),
         ],
         compiler_params=pltpu.CompilerParams(
-            vmem_limit_bytes=min(56 * MIB, 16 * MIB + 12 * gates * rows * tokens + 4 * tokens * tile)
+            vmem_limit_bytes=60 * MIB
         ),
         cost_estimate=pl.CostEstimate(
             flops=2 * gates * rows * width * tokens,
@@ -403,18 +455,14 @@
     )(place, *held, *pieces)
     weight_grad = weight_grad.transpose(1, 0, 2)
 
-    returned = lax.ppermute(pole_sums, ("seq", "ch"), gather_back)
-    returned = jnp.broadcast_to(returned[None], (n_seq,) + returned.shape)
-    returned = lax.all_to_all(returned, "seq", split_axis=0, concat_axis=0, tiled=True)
-    pieces = []
-    for block in range(per_ch):
-        filled = 0
-        for h, begin in enumerate(starts):
-            if begin + part > filled:
-                pieces.append(returned[block * n_ch + h, filled - begin :])
-                filled = begin + part
-    sums = jnp.concatenate(pieces, 0)
-    return (weight_grad, sums[:, :order], sums[:, order : 2 * order], sums[:, 2 * order])
+    channels = residues.shape[0]
+    by_pole = jax.ShapeDtypeStruct((order, channels), F32)
+    residue_grad, rate_grad, skip_grad = call(
+        functools.partial(assemble_kernel, rows=rows, order=order),
+        [by_pole, by_pole, jax.ShapeDtypeStruct((1, channels), F32)], 0, 0, place, *blocks,
+        scratch=[pltpu.VMEM((round_up(channels, 128), 128), F32)], indexed=True,
+    )
+    return (weight_grad, residue_grad.T, rate_grad.T, skip_grad.reshape(channels))
 
 
 def solution(mesh):

time: 127 us -> 123 us (0.969)
  the two profiles are of different devices: /device:TPU:0 before, /device:TPU:4 now
where the time goes in v4:
time: 123 us; the launch traced here: 122 us
  starting transfers between devices  33.8 us (27%)
  waiting for transfers between devices  29.3 us (24%)
  Pallas kernels  28.6 us (23%)
  blocking collectives  16.9 us (14%)
  local copies, waits for them, and re-layouts  11.6 us (9%)
  between operations  1.3 us (1%)
    pallas_call x11, Pallas kernels, call(): pl.pallas_call(kernel, out_shape=outs, in_specs=specs, out_specs=[whole]...  21 us
    all_to_all x1, blocking collectives, local(): lax.all_to_all(upper, 'seq', split_axis=0, concat_axis=0, tiled=True)  16.9 us
    ppermute x2, waiting for transfers between devices, chips(): lax.ppermute(array, 'ch', [(h, (h + d) % n_ch) for h in range(n_ch)])  12.1 us
    unnamed x92, local copies, waits for them, and re-layouts  11.5 us
    ppermute x12, starting transfers between devices, to_owners(): lax.ppermute(sums[d], 'ch', [(h, (h + d) % n_ch) for h in range(n_ch)])  8.44 us
    ppermute x4, starting transfers between devices, send_on(): lax.ppermute(pair[1], 'seq', behind)  7.66 us
    pallas_call x1, Pallas kernels, local(): pl.pallas_call(functools.partial(weight_kernel, shares=n_ch), out_shape=j...  7.61 us
    ppermute x2, waiting for transfers between devices, local(): blocks.append(lax.ppermute(block_sums, ('seq', 'ch'), route))  7.51 us
  transfers between devices with their start and end apart: 30, of which 9 were waited for; matrix products, arithmetic and copies ran while one was open for 1% of the time, Pallas kernels for 11%

profile of v4, /device:TPU:4, one launch (start us, length us, event | category | flops | bytes accessed | tf_op | source)
XLA Modules:
  0.0 122.5 jit_solution(3926815005271190393)
XLA Ops:
  0.6 1.5 %collective-permute-start.1 = (bf16[128,2048]{1,0:T(8,128)(2,1)}, bf16[128,2048]{1,0:T(8,128)(2,1)S(1)}, u32[]{:S(2)}, u32[]{:S(2)}) collective-permute-start(bf16[128,2048]{1,0:T(8,128)(2,1)} %refs_4_.1), channel_id=1, source_target_pairs={{8,0},{16,8},{24,16},{28,24},{20,28},{12,20},{4,12},{0,4},{9,1},{1... | collective-permute-start | bytes 1572872 | tf_op jit(solution)/shard_map/ppermute | solution.py:306
  3.6 16.9 %all_to_all.5 = bf16[8,56,128]{2,1,0:T(8,128)(2,1)S(1)} all-to-all(bf16[8,56,128]{2,1,0:T(8,128)(2,1)S(1)} %shard_map.120), channel_id=1, replica_groups=mesh['seq'=8,'ch'=4] {'seq'}, dimensions={0} | all-to-all | bytes 229376 | tf_op jit(solution)/shard_map/all_to_all | solution.py:339
  20.6 2.0 %collective-permute-start.3 = (bf16[128,2048]{1,0:T(8,128)(2,1)S(1)}, bf16[128,2048]{1,0:T(8,128)(2,1)S(1)}, u32[]{:S(2)}, u32[]{:S(2)}) collective-permute-start(bf16[128,2048]{1,0:T(8,128)(2,1)S(1)} %collective-permute-done.1.refs_2_.refs_6_), channel_id=1, source_target_pairs={{8,0},{16,8},{24,16},{28,24},{20,28},{12,20},{4,12},{0,4},{9,1},{1... | collective-permute-start | bytes 1572872 | tf_op jit(solution)/shard_map/ppermute | solution.py:306
  24.2 1.7 %copy-done = bf16[208,3,2048]{2,0,1:T(8,128)(2,1)S(1)} copy-done((bf16[208,3,2048]{2,0,1:T(8,128)(2,1)S(1)}, bf16[208,3,2048]{2,0,1:T(8,128)(2,1)}, u32[]{:S(2)}) %copy-start) | copy-done | bytes 2555928
  25.9 1.0 copy-done.8
  26.9 2.4 %shard_map.122 = (f32[3,56,384]{2,1,0:T(8,128)S(1)}, bf16[3,56,384]{2,1,0:T(8,128)(2,1)S(1)}, bf16[3,56,384]{2,1,0:T(8,128)(2,1)S(1)}, bf16[3,56,384]{2,1,0:T(8,128)(2,1)S(1)}) custom-call(s32[2]{0:T(128)S(1)} %pad_add_fusion.place_ref, bf16[3,208,2048]{2,1,0:T(8,128)(2,1)S(1)} %bitcast.8, bf16[128,2048]{1,0:T(8,128)(2,1)S(1)} %copy-done.8, ...), custom_call_target="tpu_custom_call" | custom-call | flops 981467136 | bytes 4773896 | tf_op jit(solution)/shard_map/pallas_call | solution.py:270
  29.4 3.2 %collective-permute-done.2.refs_0_.refs_7_ = bf16[128,2048]{1,0:T(8,128)(2,1)S(1)} collective-permute-done((bf16[128,2048]{1,0:T(8,128)(2,1)S(1)}, bf16[128,2048]{1,0:T(8,128)(2,1)S(1)}, u32[]{:S(2)}, u32[]{:S(2)}) %collective-permute-start.2) | collective-permute-done | bytes 524320 | tf_op jit(solution)/shard_map/ppermute | solution.py:306
  33.4 1.3 %collective-permute-start.5 = (bf16[128,2048]{1,0:T(8,128)(2,1)S(1)}, bf16[128,2048]{1,0:T(8,128)(2,1)S(1)}, u32[]{:S(2)}, u32[]{:S(2)}) collective-permute-start(bf16[128,2048]{1,0:T(8,128)(2,1)S(1)} %collective-permute-done.3.refs_1_.refs_8_), channel_id=1, source_target_pairs={{8,0},{16,8},{24,16},{28,24},{20,28},{12,20},{4,12},{0,4},{9,1},{1... | collective-permute-start | bytes 1572872 | tf_op jit(solution)/shard_map/ppermute | solution.py:306
  35.2 1.4 %collective-permute-start.10 = (bf16[3,56,384]{2,1,0:T(8,128)(2,1)S(1)}, bf16[3,56,384]{2,1,0:T(8,128)(2,1)S(1)}, u32[]{:S(2)}, u32[]{:S(2)}) collective-permute-start(bf16[3,56,384]{2,1,0:T(8,128)(2,1)S(1)} %get-tuple-element.69), channel_id=1, source_target_pairs={{0,3},{1,0},{2,1},{3,2},{4,7},{5,4},{6,5},{7,6},{8,11},{9,8},{10,9... | collective-permute-start | bytes 387080 | tf_op jit(solution)/shard_map/ppermute | solution.py:328
  36.7 3.2 %collective-permute-done.8.refs_1_ = bf16[3,56,384]{2,1,0:T(8,128)(2,1)S(1)} collective-permute-done((bf16[3,56,384]{2,1,0:T(8,128)(2,1)S(1)}, bf16[3,56,384]{2,1,0:T(8,128)(2,1)S(1)}, u32[]{:S(2)}, u32[]{:S(2)}) %collective-permute-start.8) | collective-permute-done | bytes 129056 | tf_op jit(solution)/shard_map/ppermute | solution.py:328
  39.9 2.5 %collective-permute-start.7 = (bf16[8,56,128]{2,1,0:T(8,128)(2,1)S(1)}, bf16[8,56,128]{2,1,0:T(8,128)(2,1)S(1)}, u32[]{:S(2)}, u32[]{:S(2)}) collective-permute-start(bf16[8,56,128]{2,1,0:T(8,128)(2,1)S(1)} %all_to_all.5), channel_id=1, source_target_pairs={{0,0},{4,1},{8,2},{12,3},{16,4},{20,5},{24,6},{28,7},{1,8},{5,9},{... | collective-permute-start | bytes 344072 | tf_op jit(solution)/shard_map/ppermute | solution.py:371
  42.4 5.3 %collective-permute-start.6 = (f32[56,33]{1,0:T(8,128)S(1)}, f32[56,33]{1,0:T(8,128)S(1)}, u32[]{:S(2)}, u32[]{:S(2)}) collective-permute-start(f32[56,33]{1,0:T(8,128)S(1)} %shard_map.121), channel_id=1, source_target_pairs={{0,0},{4,1},{8,2},{12,3},{16,4},{20,5},{24,6},{28,7},{1,8},{5,9},{... | collective-permute-start | bytes 22184 | tf_op jit(solution)/shard_map/ppermute | solution.py:370
  47.7 1.8 %shard_map.123 = (f32[3,56,256]{2,1,0:T(8,128)S(1)}, bf16[3,56,256]{2,1,0:T(8,128)(2,1)S(1)}, bf16[3,56,256]{2,1,0:T(8,128)(2,1)S(1)}, bf16[3,56,256]{2,1,0:T(8,128)(2,1)S(1)}) custom-call(s32[2]{0:T(128)S(1)} %pad_add_fusion.place_ref, bf16[3,208,2048]{2,1,0:T(8,128)(2,1)S(1)} %bitcast.9, bf16[128,2048]{1,0:T(8,128)(2,1)S(1)} %collective-permute-done.2.refs_0_.refs_7_, ...), custom_call_target="tpu_custom_call" | custom-call | flops 654311424 | bytes 4034568 | tf_op jit(solution)/shard_map/pallas_call | solution.py:270
  50.3 2.8 %collective-permute-start.18 = (bf16[64,2048]{1,0:T(8,128)(2,1)S(1)}, bf16[64,2048]{1,0:T(8,128)(2,1)S(1)}, u32[]{:S(2)}, u32[]{:S(2)}) collective-permute-start(bf16[64,2048]{1,0:T(8,128)(2,1)S(1)} %slice.7), channel_id=1, source_target_pairs={{8,0},{16,8},{24,16},{28,24},{20,28},{12,20},{4,12},{0,4},{9,1},{1... | collective-permute-start | bytes 786440 | tf_op jit(solution)/shard_map/ppermute | solution.py:306
  54.5 1.5 %collective-permute-start.13 = (bf16[3,56,256]{2,1,0:T(8,128)(2,1)S(1)}, bf16[3,56,256]{2,1,0:T(8,128)(2,1)S(1)}, u32[]{:S(2)}, u32[]{:S(2)}) collective-permute-start(bf16[3,56,256]{2,1,0:T(8,128)(2,1)S(1)} %get-tuple-element.78), channel_id=1, source_target_pairs={{0,3},{1,0},{2,1},{3,2},{4,7},{5,4},{6,5},{7,6},{8,11},{9,8},{10,9... | collective-permute-start | bytes 258056 | tf_op jit(solution)/shard_map/ppermute | solution.py:328
  56.0 1.8 %shard_map.124 = (f32[3,56,256]{2,1,0:T(8,128)S(1)}, bf16[3,56,256]{2,1,0:T(8,128)(2,1)S(1)}, bf16[3,56,256]{2,1,0:T(8,128)(2,1)S(1)}, bf16[3,56,256]{2,1,0:T(8,128)(2,1)S(1)}) custom-call(s32[2]{0:T(128)S(1)} %pad_add_fusion.place_ref, bf16[3,208,2048]{2,1,0:T(8,128)(2,1)S(1)} %bitcast.10, bf16[128,2048]{1,0:T(8,128)(2,1)S(1)} %collective-permute-done.4.refs_0_.refs_9_, ...), custom_call_target="tpu_custom_call" | custom-call | flops 654311424 | bytes 4034568 | tf_op jit(solution)/shard_map/pallas_call | solution.py:270
  57.9 1.9 %collective-permute-done.17.refs_0_.refs_11_ = bf16[64,2048]{1,0:T(8,128)(2,1)S(1)} collective-permute-done((bf16[64,2048]{1,0:T(8,128)(2,1)S(1)}, bf16[64,2048]{1,0:T(8,128)(2,1)S(1)}, u32[]{:S(2)}, u32[]{:S(2)}) %collective-permute-start.17) | collective-permute-done | bytes 262176 | tf_op jit(solution)/shard_map/ppermute | solution.py:306
  59.9 1.5 %collective-permute-start.16 = (bf16[3,56,256]{2,1,0:T(8,128)(2,1)S(1)}, bf16[3,56,256]{2,1,0:T(8,128)(2,1)S(1)}, u32[]{:S(2)}, u32[]{:S(2)}) collective-permute-start(bf16[3,56,256]{2,1,0:T(8,128)(2,1)S(1)} %get-tuple-element.86), channel_id=1, source_target_pairs={{0,3},{1,0},{2,1},{3,2},{4,7},{5,4},{6,5},{7,6},{8,11},{9,8},{10,9... | collective-permute-start | bytes 258056 | tf_op jit(solution)/shard_map/ppermute | solution.py:328
  61.4 1.4 %shard_map.125 = (f32[3,56,128]{2,1,0:T(8,128)S(1)}, bf16[3,56,128]{2,1,0:T(8,128)(2,1)S(1)}, bf16[3,56,128]{2,1,0:T(8,128)(2,1)S(1)}, bf16[3,56,128]{2,1,0:T(8,128)(2,1)S(1)}) custom-call(s32[2]{0:T(128)S(1)} %pad_add_fusion.place_ref, bf16[3,208,2048]{2,1,0:T(8,128)(2,1)S(1)} %bitcast.11, bf16[64,2048]{1,0:T(8,128)(2,1)S(1)} %collective-permute-done.17.refs_0_.refs_11_, ...), custom_call_target="tpu_custom_call" | custom-call | flops 327155712 | bytes 3295240 | tf_op jit(solution)/shard_map/pallas_call | solution.py:270
  65.0 1.5 %shard_map.126 = (f32[56,1024]{1,0:T(8,128)S(1)}, f32[56,1024]{1,0:T(8,128)S(1)}) custom-call(f32[56,33]{1,0:T(8,128)S(1)} %collective-permute-done.6.poles_ref.refs_17_, bf16[1024,1024]{1,0:T(8,128)(2,1)S(1)} %copy-done.4, bf16[1024,1024]{1,0:T(8,128)(2,1)S(1)} %copy-done.2, f32[2,1024]{1,0:T(2,128)S(1)} %copy-done.23), custom_call_target="tpu_custom_call" | custom-call | flops 469762048 | bytes 4668640 | tf_op jit(solution)/shard_map/pallas_call | solution.py:270
  68.7 7.6 %shard_map.127 = (bf16[3,56,1024]{2,1,0:T(8,128)(2,1)}, f32[56,1024]{1,0:T(8,128)}, f32[56,1024]{1,0:T(8,128)}, f32[56,1]{1,0:T(8,128)}) custom-call(s32[2]{0:T(128)} %copy-done.20, f32[3,56,384]{2,1,0:T(8,128)} %copy-done.24, bf16[3,56,384]{2,1,0:T(8,128)(2,1)} %copy-done.33, bf16[3,56,384]{2,1,0:T(8,128)(2,1)} %copy-done.34, ...), custom_call_target="tpu_custom_call" | custom-call | flops 1879048192 | bytes 7306696 | tf_op jit(solution)/shard_map/pallas_call | solution.py:270
  76.3 1.5 %collective-permute-start.22 = (bf16[3,56,1024]{2,1,0:T(8,128)(2,1)}, bf16[3,56,1024]{2,1,0:T(8,128)(2,1)S(1)}, u32[]{:S(2)}, u32[]{:S(2)}) collective-permute-start(bf16[3,56,1024]{2,1,0:T(8,128)(2,1)} %get-tuple-element.97.refs_0_), channel_id=1, source_target_pairs={{0,2},{1,3},{2,0},{3,1},{4,6},{5,7},{6,4},{7,5},{8,10},{9,11},{10,... | collective-permute-start | bytes 1032200 | tf_op jit(solution)/shard_map/ppermute | solution.py:402
  77.8 8.9 %collective-permute-done.22.refs_1_ = bf16[3,56,1024]{2,1,0:T(8,128)(2,1)S(1)} collective-permute-done((bf16[3,56,1024]{2,1,0:T(8,128)(2,1)}, bf16[3,56,1024]{2,1,0:T(8,128)(2,1)S(1)}, u32[]{:S(2)}, u32[]{:S(2)}) %collective-permute-start.22) | collective-permute-done | bytes 344096 | tf_op jit(solution)/shard_map/ppermute | solution.py:402
  86.8 1.8 %copy-done.5 = bf16[1024,1024]{1,0:T(8,128)(2,1)S(1)} copy-done((bf16[1024,1024]{1,0:T(8,128)(2,1)S(1)}, bf16[1024,1024]{1,0:T(8,128)(2,1)}, u32[]{:S(2)}) %copy-start.5) | copy-done | bytes 2097176
  91.2 2.0 %shard_map.129.refs_0_ = f32[56,33]{1,0:T(8,128)S(1)} custom-call(f32[56,33]{1,0:T(8,128)S(1)} %copy-done.18, f32[56,1024]{1,0:T(8,128)S(1)} %copy-done.15, f32[56,1024]{1,0:T(8,128)S(1)} %copy-done.16, bf16[1024,1024]{1,0:T(8,128)(2,1)S(1)} %copy-done.5, bf16[1024,1024]{1,0:T(8,128)(2,1)S(1)} %copy-done.3, f32[56,1]{1,0:T(8,128)S(1)} %copy-done.22), custom_call_target="tpu_custom_call" | custom-call | flops 469762048 | bytes 4668064 | tf_op jit(solution)/shard_map/pallas_call | solution.py:270
  94.0 3.2 %collective-permute-done.25.refs_1_ = f32[56,33]{1,0:T(8,128)S(1)} collective-permute-done((f32[56,33]{1,0:T(8,128)S(1)}, f32[56,33]{1,0:T(8,128)S(1)}, u32[]{:S(2)}, u32[]{:S(2)}) %collective-permute-start.25) | collective-permute-done | bytes 7424 | tf_op jit(solution)/shard_map/ppermute | solution.py:402
  97.2 1.2 collective-permute-done.27.refs_3_
  99.9 5.4 %collective-permute-start.28 = (f32[208,33]{1,0:T(8,128)S(1)}, f32[208,33]{1,0:T(8,128)S(1)}, u32[]{:S(2)}, u32[]{:S(2)}) collective-permute-start(f32[208,33]{1,0:T(8,128)S(1)} %shard_map.130), channel_id=1, source_target_pairs={{0,0},{8,1},{16,2},{24,3},{4,4},{12,5},{20,6},{28,7},{1,8},{9,9},{... | collective-permute-start | bytes 82376 | tf_op jit(solution)/shard_map/ppermute | solution.py:431
  105.3 5.8 %collective-permute-done.29.refs_1_ = f32[208,33]{1,0:T(8,128)S(1)} collective-permute-done((f32[208,33]{1,0:T(8,128)S(1)}, f32[208,33]{1,0:T(8,128)S(1)}, u32[]{:S(2)}, u32[]{:S(2)}) %collective-permute-start.29) | collective-permute-done | bytes 27488 | tf_op jit(solution)/shard_map/ppermute | solution.py:431
  111.1 1.7 %collective-permute-done.28.refs_0_ = f32[208,33]{1,0:T(8,128)S(1)} collective-permute-done((f32[208,33]{1,0:T(8,128)S(1)}, f32[208,33]{1,0:T(8,128)S(1)}, u32[]{:S(2)}, u32[]{:S(2)}) %collective-permute-start.28) | collective-permute-done | bytes 27488 | tf_op jit(solution)/shard_map/ppermute | solution.py:431
  112.8 1.3 %shard_map.131 = (f32[16,416]{1,0:T(8,128)}, f32[16,416]{1,0:T(8,128)}, f32[1,416]{1,0:T(1,128)}) custom-call(s32[2]{0:T(128)S(1)} %copy-done.21, f32[208,33]{1,0:T(8,128)S(1)} %collective-permute-done.28.refs_0_, f32[208,33]{1,0:T(8,128)S(1)} %collective-permute-done.29.refs_1_), custom_call_target="tpu_custom_call" | custom-call | bytes 109832 | tf_op jit(solution)/shard_map/pallas_call | solution.py:270
  114.9 7.6 %shard_map.128 = f32[3,208,2048]{2,1,0:T(8,128)} custom-call(s32[2]{0:T(128)} %copy-done.20, bf16[3,56,1024]{2,1,0:T(8,128)(2,1)} %get-tuple-element.97.refs_0_, bf16[3,56,1024]{2,1,0:T(8,128)(2,1)} %copy-done.30, bf16[3,56,1024]{2,1,0:T(8,128)(2,1)} %copy-done.31, bf16[3,56,1024]{2,1,0:T(8,128)(2,1)} %copy-done.32, bf16[128,2048]{1,0:T(8,128)(2,1)} %refs_4_.1, ...), custom_call_target="tpu_custom_call" | custom-call | flops 2617245696 | bytes 10584064 | tf_op jit(solution)/shard_map/pallas_call | solution.py:434
  (138 shorter events, 16.3 us)
Async XLA Ops:
  0.6 19.9 %collective-permute-start.1 = (bf16[128,2048]{1,0:T(8,128)(2,1)}, bf16[128,2048]{1,0:T(8,128)(2,1)S(1)}, u32[]{:S(2)}, u32[]{:S(2)}) collective-permute-start(bf16[128,2048]{1,0:T(8,128)(2,1)} %refs_4_.1), channel_id=1, source_target_pairs={{8,0},{16,8},{24,16},{28,24},{20,28},{12,20},{4,12},{0,4},{9,1},{1... | collective-permute-start | bytes 1572872 | tf_op jit(solution)/shard_map/ppermute | solution.py:306
  2.2 18.3 %collective-permute-start = (bf16[128,2048]{1,0:T(8,128)(2,1)}, bf16[128,2048]{1,0:T(8,128)(2,1)S(1)}, u32[]{:S(2)}, u32[]{:S(2)}) collective-permute-start(bf16[128,2048]{1,0:T(8,128)(2,1)} %refs_4_.1), channel_id=1, source_target_pairs={{0,8},{8,16},{16,24},{24,28},{28,20},{20,12},{12,4},{4,0},{1,9},{9... | collective-permute-start | bytes 1572872 | tf_op jit(solution)/shard_map/ppermute | solution.py:306
  20.5 12.1 %collective-permute-start.2 = (bf16[128,2048]{1,0:T(8,128)(2,1)S(1)}, bf16[128,2048]{1,0:T(8,128)(2,1)S(1)}, u32[]{:S(2)}, u32[]{:S(2)}) collective-permute-start(bf16[128,2048]{1,0:T(8,128)(2,1)S(1)} %collective-permute-done.refs_1_.refs_5_), channel_id=1, source_target_pairs={{0,8},{8,16},{16,24},{24,28},{28,20},{20,12},{12,4},{4,0},{1,9},{9... | collective-permute-start | bytes 1572872 | tf_op jit(solution)/shard_map/ppermute | solution.py:306
  20.6 12.1 %collective-permute-start.3 = (bf16[128,2048]{1,0:T(8,128)(2,1)S(1)}, bf16[128,2048]{1,0:T(8,128)(2,1)S(1)}, u32[]{:S(2)}, u32[]{:S(2)}) collective-permute-start(bf16[128,2048]{1,0:T(8,128)(2,1)S(1)} %collective-permute-done.1.refs_2_.refs_6_), channel_id=1, source_target_pairs={{8,0},{16,8},{24,16},{28,24},{20,28},{12,20},{4,12},{0,4},{9,1},{1... | collective-permute-start | bytes 1572872 | tf_op jit(solution)/shard_map/ppermute | solution.py:306
  22.7 38.7 %copy-start.20 = (s32[2]{0:T(128)}, s32[2]{0:T(128)S(1)}, u32[]{:S(2)}) copy-start(s32[2]{0:T(128)S(1)} %pad_add_fusion.place_ref) | copy-start | bytes 28
  32.7 33.9 %copy-start.12 = (bf16[128,2048]{1,0:T(8,128)(2,1)}, bf16[128,2048]{1,0:T(8,128)(2,1)S(1)}, u32[]{:S(2)}) copy-start(bf16[128,2048]{1,0:T(8,128)(2,1)S(1)} %collective-permute-done.3.refs_1_.refs_8_) | copy-start | bytes 1572868
  32.7 17.0 %collective-permute-start.4 = (bf16[128,2048]{1,0:T(8,128)(2,1)S(1)}, bf16[128,2048]{1,0:T(8,128)(2,1)S(1)}, u32[]{:S(2)}, u32[]{:S(2)}) collective-permute-start(bf16[128,2048]{1,0:T(8,128)(2,1)S(1)} %collective-permute-done.2.refs_0_.refs_7_), channel_id=1, source_target_pairs={{0,8},{8,16},{16,24},{24,28},{28,20},{20,12},{12,4},{4,0},{1,9},{9... | collective-permute-start | bytes 1572872 | tf_op jit(solution)/shard_map/ppermute | solution.py:306
  33.4 16.3 %collective-permute-start.5 = (bf16[128,2048]{1,0:T(8,128)(2,1)S(1)}, bf16[128,2048]{1,0:T(8,128)(2,1)S(1)}, u32[]{:S(2)}, u32[]{:S(2)}) collective-permute-start(bf16[128,2048]{1,0:T(8,128)(2,1)S(1)} %collective-permute-done.3.refs_1_.refs_8_), channel_id=1, source_target_pairs={{8,0},{16,8},{24,16},{28,24},{20,28},{12,20},{4,12},{0,4},{9,1},{1... | collective-permute-start | bytes 1572872 | tf_op jit(solution)/shard_map/ppermute | solution.py:306
  34.7 5.2 %collective-permute-start.8 = (bf16[3,56,384]{2,1,0:T(8,128)(2,1)S(1)}, bf16[3,56,384]{2,1,0:T(8,128)(2,1)S(1)}, u32[]{:S(2)}, u32[]{:S(2)}) collective-permute-start(bf16[3,56,384]{2,1,0:T(8,128)(2,1)S(1)} %get-tuple-element.67), channel_id=1, source_target_pairs={{0,1},{1,2},{2,3},{3,0},{4,5},{5,6},{6,7},{7,4},{8,9},{9,10},{10,1... | collective-permute-start | bytes 387080 | tf_op jit(solution)/shard_map/ppermute | solution.py:328
  34.7 7.7 %collective-permute-start.9 = (bf16[3,56,384]{2,1,0:T(8,128)(2,1)S(1)}, bf16[3,56,384]{2,1,0:T(8,128)(2,1)S(1)}, u32[]{:S(2)}, u32[]{:S(2)}) collective-permute-start(bf16[3,56,384]{2,1,0:T(8,128)(2,1)S(1)} %get-tuple-element.68), channel_id=1, source_target_pairs={{0,2},{1,3},{2,0},{3,1},{4,6},{5,7},{6,4},{7,5},{8,10},{9,11},{10,... | collective-permute-start | bytes 387080 | tf_op jit(solution)/shard_map/ppermute | solution.py:328
  35.2 14.4 %collective-permute-start.10 = (bf16[3,56,384]{2,1,0:T(8,128)(2,1)S(1)}, bf16[3,56,384]{2,1,0:T(8,128)(2,1)S(1)}, u32[]{:S(2)}, u32[]{:S(2)}) collective-permute-start(bf16[3,56,384]{2,1,0:T(8,128)(2,1)S(1)} %get-tuple-element.69), channel_id=1, source_target_pairs={{0,3},{1,0},{2,1},{3,2},{4,7},{5,4},{6,5},{7,6},{8,11},{9,8},{10,9... | collective-permute-start | bytes 387080 | tf_op jit(solution)/shard_map/ppermute | solution.py:328
  39.9 9.7 %collective-permute-start.7 = (bf16[8,56,128]{2,1,0:T(8,128)(2,1)S(1)}, bf16[8,56,128]{2,1,0:T(8,128)(2,1)S(1)}, u32[]{:S(2)}, u32[]{:S(2)}) collective-permute-start(bf16[8,56,128]{2,1,0:T(8,128)(2,1)S(1)} %all_to_all.5), channel_id=1, source_target_pairs={{0,0},{4,1},{8,2},{12,3},{16,4},{20,5},{24,6},{28,7},{1,8},{5,9},{... | collective-permute-start | bytes 344072 | tf_op jit(solution)/shard_map/ppermute | solution.py:371
  42.4 7.2 %collective-permute-start.6 = (f32[56,33]{1,0:T(8,128)S(1)}, f32[56,33]{1,0:T(8,128)S(1)}, u32[]{:S(2)}, u32[]{:S(2)}) collective-permute-start(f32[56,33]{1,0:T(8,128)S(1)} %shard_map.121), channel_id=1, source_target_pairs={{0,0},{4,1},{8,2},{12,3},{16,4},{20,5},{24,6},{28,7},{1,8},{5,9},{... | collective-permute-start | bytes 22184 | tf_op jit(solution)/shard_map/ppermute | solution.py:370
  50.3 9.6 %collective-permute-start.17 = (bf16[64,2048]{1,0:T(8,128)(2,1)S(1)}, bf16[64,2048]{1,0:T(8,128)(2,1)S(1)}, u32[]{:S(2)}, u32[]{:S(2)}) collective-permute-start(bf16[64,2048]{1,0:T(8,128)(2,1)S(1)} %slice.6), channel_id=1, source_target_pairs={{0,8},{8,16},{16,24},{24,28},{28,20},{20,12},{12,4},{4,0},{1,9},{9... | collective-permute-start | bytes 786440 | tf_op jit(solution)/shard_map/ppermute | solution.py:306
  50.3 9.6 %collective-permute-start.18 = (bf16[64,2048]{1,0:T(8,128)(2,1)S(1)}, bf16[64,2048]{1,0:T(8,128)(2,1)S(1)}, u32[]{:S(2)}, u32[]{:S(2)}) collective-permute-start(bf16[64,2048]{1,0:T(8,128)(2,1)S(1)} %slice.7), channel_id=1, source_target_pairs={{8,0},{16,8},{24,16},{28,24},{20,28},{12,20},{4,12},{0,4},{9,1},{1... | collective-permute-start | bytes 786440 | tf_op jit(solution)/shard_map/ppermute | solution.py:306
  53.1 4.8 %collective-permute-start.11 = (bf16[3,56,256]{2,1,0:T(8,128)(2,1)S(1)}, bf16[3,56,256]{2,1,0:T(8,128)(2,1)S(1)}, u32[]{:S(2)}, u32[]{:S(2)}) collective-permute-start(bf16[3,56,256]{2,1,0:T(8,128)(2,1)S(1)} %get-tuple-element.76), channel_id=1, source_target_pairs={{0,1},{1,2},{2,3},{3,0},{4,5},{5,6},{6,7},{7,4},{8,9},{9,10},{10,1... | collective-permute-start | bytes 258056 | tf_op jit(solution)/shard_map/ppermute | solution.py:328
  53.8 9.1 %collective-permute-start.12 = (bf16[3,56,256]{2,1,0:T(8,128)(2,1)S(1)}, bf16[3,56,256]{2,1,0:T(8,128)(2,1)S(1)}, u32[]{:S(2)}, u32[]{:S(2)}) collective-permute-start(bf16[3,56,256]{2,1,0:T(8,128)(2,1)S(1)} %get-tuple-element.77), channel_id=1, source_target_pairs={{0,2},{1,3},{2,0},{3,1},{4,6},{5,7},{6,4},{7,5},{8,10},{9,11},{10,... | collective-permute-start | bytes 258056 | tf_op jit(solution)/shard_map/ppermute | solution.py:328
  54.5 8.5 %collective-permute-start.13 = (bf16[3,56,256]{2,1,0:T(8,128)(2,1)S(1)}, bf16[3,56,256]{2,1,0:T(8,128)(2,1)S(1)}, u32[]{:S(2)}, u32[]{:S(2)}) collective-permute-start(bf16[3,56,256]{2,1,0:T(8,128)(2,1)S(1)} %get-tuple-element.78), channel_id=1, source_target_pairs={{0,3},{1,0},{2,1},{3,2},{4,7},{5,4},{6,5},{7,6},{8,11},{9,8},{10,9... | collective-permute-start | bytes 258056 | tf_op jit(solution)/shard_map/ppermute | solution.py:328
  57.9 6.1 %collective-permute-start.14 = (bf16[3,56,256]{2,1,0:T(8,128)(2,1)S(1)}, bf16[3,56,256]{2,1,0:T(8,128)(2,1)S(1)}, u32[]{:S(2)}, u32[]{:S(2)}) collective-permute-start(bf16[3,56,256]{2,1,0:T(8,128)(2,1)S(1)} %get-tuple-element.84), channel_id=1, source_target_pairs={{0,1},{1,2},{2,3},{3,0},{4,5},{5,6},{6,7},{7,4},{8,9},{9,10},{10,1... | collective-permute-start | bytes 258056 | tf_op jit(solution)/shard_map/ppermute | solution.py:328
  59.9 8.1 %collective-permute-start.15 = (bf16[3,56,256]{2,1,0:T(8,128)(2,1)S(1)}, bf16[3,56,256]{2,1,0:T(8,128)(2,1)S(1)}, u32[]{:S(2)}, u32[]{:S(2)}) collective-permute-start(bf16[3,56,256]{2,1,0:T(8,128)(2,1)S(1)} %get-tuple-element.85), channel_id=1, source_target_pairs={{0,2},{1,3},{2,0},{3,1},{4,6},{5,7},{6,4},{7,5},{8,10},{9,11},{10,... | collective-permute-start | bytes 258056 | tf_op jit(solution)/shard_map/ppermute | solution.py:328
  59.9 8.1 %collective-permute-start.16 = (bf16[3,56,256]{2,1,0:T(8,128)(2,1)S(1)}, bf16[3,56,256]{2,1,0:T(8,128)(2,1)S(1)}, u32[]{:S(2)}, u32[]{:S(2)}) collective-permute-start(bf16[3,56,256]{2,1,0:T(8,128)(2,1)S(1)} %get-tuple-element.86), channel_id=1, source_target_pairs={{0,3},{1,0},{2,1},{3,2},{4,7},{5,4},{6,5},{7,6},{8,11},{9,8},{10,9... | collective-permute-start | bytes 258056 | tf_op jit(solution)/shard_map/ppermute | solution.py:328
  62.9 5.1 %collective-permute-start.19 = (bf16[3,56,128]{2,1,0:T(8,128)(2,1)S(1)}, bf16[3,56,128]{2,1,0:T(8,128)(2,1)S(1)}, u32[]{:S(2)}, u32[]{:S(2)}) collective-permute-start(bf16[3,56,128]{2,1,0:T(8,128)(2,1)S(1)} %get-tuple-element.90), channel_id=1, source_target_pairs={{0,1},{1,2},{2,3},{3,0},{4,5},{5,6},{6,7},{7,4},{8,9},{9,10},{10,1... | collective-permute-start | bytes 129032 | tf_op jit(solution)/shard_map/ppermute | solution.py:328
  63.0 5.1 %collective-permute-start.20 = (bf16[3,56,128]{2,1,0:T(8,128)(2,1)S(1)}, bf16[3,56,128]{2,1,0:T(8,128)(2,1)S(1)}, u32[]{:S(2)}, u32[]{:S(2)}) collective-permute-start(bf16[3,56,128]{2,1,0:T(8,128)(2,1)S(1)} %get-tuple-element.91), channel_id=1, source_target_pairs={{0,2},{1,3},{2,0},{3,1},{4,6},{5,7},{6,4},{7,5},{8,10},{9,11},{10,... | collective-permute-start | bytes 129032 | tf_op jit(solution)/shard_map/ppermute | solution.py:328
  64.0 4.0 %collective-permute-start.21 = (bf16[3,56,128]{2,1,0:T(8,128)(2,1)S(1)}, bf16[3,56,128]{2,1,0:T(8,128)(2,1)S(1)}, u32[]{:S(2)}, u32[]{:S(2)}) collective-permute-start(bf16[3,56,128]{2,1,0:T(8,128)(2,1)S(1)} %get-tuple-element.92), channel_id=1, source_target_pairs={{0,3},{1,0},{2,1},{3,2},{4,7},{5,4},{6,5},{7,6},{8,11},{9,8},{10,9... | collective-permute-start | bytes 129032 | tf_op jit(solution)/shard_map/ppermute | solution.py:328
  76.3 10.4 %collective-permute-start.22 = (bf16[3,56,1024]{2,1,0:T(8,128)(2,1)}, bf16[3,56,1024]{2,1,0:T(8,128)(2,1)S(1)}, u32[]{:S(2)}, u32[]{:S(2)}) collective-permute-start(bf16[3,56,1024]{2,1,0:T(8,128)(2,1)} %get-tuple-element.97.refs_0_), channel_id=1, source_target_pairs={{0,2},{1,3},{2,0},{3,1},{4,6},{5,7},{6,4},{7,5},{8,10},{9,11},{10,... | collective-permute-start | bytes 1032200 | tf_op jit(solution)/shard_map/ppermute | solution.py:402
  77.8 8.9 %collective-permute-start.23 = (bf16[3,56,1024]{2,1,0:T(8,128)(2,1)}, bf16[3,56,1024]{2,1,0:T(8,128)(2,1)S(1)}, u32[]{:S(2)}, u32[]{:S(2)}) collective-permute-start(bf16[3,56,1024]{2,1,0:T(8,128)(2,1)} %get-tuple-element.97.refs_0_), channel_id=1, source_target_pairs={{0,1},{1,0},{2,3},{3,2},{4,5},{5,4},{6,7},{7,6},{8,9},{9,8},{10,11... | collective-permute-start | bytes 1032200 | tf_op jit(solution)/shard_map/ppermute | solution.py:407
  86.7 27.4 %collective-permute-start.24 = (bf16[3,56,1024]{2,1,0:T(8,128)(2,1)S(1)}, bf16[3,56,1024]{2,1,0:T(8,128)(2,1)S(1)}, u32[]{:S(2)}, u32[]{:S(2)}) collective-permute-start(bf16[3,56,1024]{2,1,0:T(8,128)(2,1)S(1)} %collective-permute-done.22.refs_1_), channel_id=1, source_target_pairs={{0,1},{1,0},{2,3},{3,2},{4,5},{5,4},{6,7},{7,6},{8,9},{9,8},{10,11... | collective-permute-start | bytes 1032200 | tf_op jit(solution)/shard_map/ppermute | solution.py:415
  93.2 4.0 %collective-permute-start.25 = (f32[56,33]{1,0:T(8,128)S(1)}, f32[56,33]{1,0:T(8,128)S(1)}, u32[]{:S(2)}, u32[]{:S(2)}) collective-permute-start(f32[56,33]{1,0:T(8,128)S(1)} %shard_map.129.refs_0_), channel_id=1, source_target_pairs={{0,2},{1,3},{2,0},{3,1},{4,6},{5,7},{6,4},{7,5},{8,10},{9,11},{10,... | collective-permute-start | bytes 22184 | tf_op jit(solution)/shard_map/ppermute | solution.py:402
  93.9 3.3 %collective-permute-start.26 = (f32[56,33]{1,0:T(8,128)S(1)}, f32[56,33]{1,0:T(8,128)S(1)}, u32[]{:S(2)}, u32[]{:S(2)}) collective-permute-start(f32[56,33]{1,0:T(8,128)S(1)} %shard_map.129.refs_0_), channel_id=1, source_target_pairs={{0,1},{1,0},{2,3},{3,2},{4,5},{5,4},{6,7},{7,6},{8,9},{9,8},{10,11... | collective-permute-start | bytes 22184 | tf_op jit(solution)/shard_map/ppermute | solution.py:418
  97.2 1.2 collective-permute-start.27
  99.0 12.1 %collective-permute-start.29 = (f32[208,33]{1,0:T(8,128)S(1)}, f32[208,33]{1,0:T(8,128)S(1)}, u32[]{:S(2)}, u32[]{:S(2)}) collective-permute-start(f32[208,33]{1,0:T(8,128)S(1)} %shard_map.130), channel_id=1, source_target_pairs={{4,0},{12,1},{20,2},{28,3},{0,4},{8,5},{16,6},{24,7},{5,8},{13,9},... | collective-permute-start | bytes 82376 | tf_op jit(solution)/shard_map/ppermute | solution.py:431
  99.9 12.9 %collective-permute-start.28 = (f32[208,33]{1,0:T(8,128)S(1)}, f32[208,33]{1,0:T(8,128)S(1)}, u32[]{:S(2)}, u32[]{:S(2)}) collective-permute-start(f32[208,33]{1,0:T(8,128)S(1)} %shard_map.130), channel_id=1, source_target_pairs={{0,0},{8,1},{16,2},{24,3},{4,4},{12,5},{20,6},{28,7},{1,8},{9,9},{... | collective-permute-start | bytes 82376 | tf_op jit(solution)/shard_map/ppermute | solution.py:431
  (44 other events, 439.9 us)

commit v5 on v4

--- a/solution.py
+++ b/solution.py
@@ -88,6 +88,10 @@
     ]
     for copy in copies:
         copy.start()
+    return copies
+
+
+def finish(copies):
     for copy in copies:
         copy.wait()
 
@@ -102,7 +106,7 @@
     for feature_ref in feature_refs:
         targets.append(features_ref.at[pl.ds(row, feature_ref.shape[0]), :])
         row += feature_ref.shape[0]
-    fetch(feature_refs, targets, semaphores)
+    finish(fetch(feature_refs, targets, semaphores))
     for gate in range(gates):
         sums_ref[gate] = lax.dot_general(
             weight_ref[gate], features_ref[...], (((1,), (1,)), ((), ())),
@@ -128,21 +132,26 @@
     count = len(group_slots) * shares
     partial_refs = refs[:count]
     (
-        gout_ref, poles_ref, hc_ref, hs_ref, cos_ref, sin_ref, twist_ref,
-        grad_ref, tgc_ref, tgs_ref, skip_ref, proj_ref, *scratch_refs,
+        poles_ref, twist_ref, gout_from, hc_from, hs_from, cos_from, sin_from, grad_ref,
+        tgc_ref, tgs_ref, skip_ref, proj_ref, *scratch_refs,
     ) = refs[count:]
-    *held_refs, semaphores = scratch_refs
-    fetch(partial_refs, held_refs, semaphores)
+    *held_refs, gout_ref, hc_ref, hs_ref, cos_ref, sin_ref, semaphores = scratch_refs
+    copies = fetch(
+        (*partial_refs, gout_from, cos_from, sin_from, hc_from, hs_from),
+        (*held_refs, gout_ref, cos_ref, sin_ref, hc_ref, hs_ref),
+        semaphores,
+    )
+    finish(copies[: count + 1])
     rows, tokens = hc_ref.shape
     blocks, _, _, block_len = proj_ref.shape
     slot = 0
-    for group, count in enumerate(group_slots):
+    for group, span in enumerate(group_slots):
         own_ref, *other_refs = held_refs[group * shares : (group + 1) * shares]
         total = own_ref[...]
         for other_ref in other_refs:
             total = total + other_ref[...].astype(F32)
         total = total.astype(BF16).astype(F32)
-        for place in range(count):
+        for place in range(span):
             proj_ref[slot] = total[:, :, place * block_len : (place + 1) * block_len]
             slot += 1
 
@@ -160,6 +169,7 @@
     middle = upper * queries
     signals = jnp.concatenate([product, middle], 0)
     parts = two_parts(signals)
+    finish(copies[count + 1 :])
     even = dot(parts, cos_ref[...])
     uneven = dot(parts, sin_ref[...])
     even = even[: 2 * rows] + even[2 * rows :]
@@ -266,7 +276,7 @@
     if indexed:
         specs[0] = pl.BlockSpec(memory_space=pltpu.SMEM)
     for operand in late:
-        specs[operand] = pl.BlockSpec(memory_space=pltpu.HBM)
+        specs[operand] = pl.BlockSpec(memory_space=pl.ANY)
     return pl.pallas_call(
         kernel,
         out_shape=outs,
@@ -332,45 +342,43 @@
     pair = send_on((features, features))
 
     spread = [((q % n_seq) * n_ch + q // n_seq, q) for q in range(n_seq * n_ch)]
-    (upper,) = call(
-        functools.partial(pieces_kernel, rows=rows, n_ch=n_ch),
-        (jax.ShapeDtypeStruct((n_seq, part, block_len), BF16),), 0, 0, grad_out,
-    )
-    upper = lax.all_to_all(upper, "seq", split_axis=0, concat_axis=0, tiled=True)
-    pair, upper, residues, log_rates, skip_gain = lax.optimization_barrier(
-        (pair, upper, residues, log_rates, skip_gain)
-    )
     packed = jnp.concatenate([residues, log_rates, skip_gain[:, None]], 1)
     (poles,) = call(
         functools.partial(poles_kernel, rows=rows, n_ch=n_ch),
         (jax.ShapeDtypeStruct((part, packed.shape[1]), F32),), 0, 0, place, packed, indexed=True,
     )
-
-    pieces = [features, *pair]
-    group_slots = [3]
+    grad_out, poles = lax.optimization_barrier((grad_out, poles))
+    poles = lax.ppermute(poles, ("seq", "ch"), spread)
+    (upper,) = call(
+        functools.partial(pieces_kernel, rows=rows, n_ch=n_ch),
+        (jax.ShapeDtypeStruct((n_seq, part, block_len), BF16),), 0, 0, grad_out,
+    )
+    upper = lax.all_to_all(upper, "seq", split_axis=0, concat_axis=0, tiled=True)
+    pair, upper, poles = lax.optimization_barrier((pair, upper, poles))
+    upper = lax.ppermute(upper, ("seq", "ch"), spread)
+
+    pieces, group_slots, partials = [features, *pair], [], []
+    waiting = list(pieces)
     next_pair = send_on(pair)
-    sums = project(pieces)
-    partials = to_owners(sums)
     for step in range(2, n_seq // 2):
         pair = next_pair
         if step == 2:
-            pair, poles, upper, sums[0] = lax.optimization_barrier((pair, poles, upper, sums[0]))
-            partials[0] = sums[0]
+            pair, upper = lax.optimization_barrier((pair, upper))
+        else:
+            pair, sums[0] = lax.optimization_barrier((pair, sums[0]))
+            partials[-n_ch] = sums[0]
         pieces += pair
+        waiting += pair
         if step < n_seq // 2 - 1:
             next_pair = send_on(pair)
         else:
             half = block_len // 2
-            pair, poles, upper, partials[: n_ch + 1] = lax.optimization_barrier(
-                (pair, poles, upper, partials[: n_ch + 1])
-            )
-            halves, pair = lax.optimization_barrier(((pair[0][:half], pair[1][half:]), pair))
+            halves, waiting = lax.optimization_barrier(((pair[0][:half], pair[1][half:]), waiting))
             next_pair = send_on(halves)
-        if step == 2:
-            poles = lax.ppermute(poles, ("seq", "ch"), spread)
-            upper = lax.ppermute(upper, ("seq", "ch"), spread)
-        partials += to_owners(project(list(pair)))
-        group_slots.append(2)
+        sums = project(waiting)
+        partials += to_owners(sums)
+        group_slots.append(len(waiting))
+        waiting = []
     pair = next_pair
     pieces += pair
     partials += to_owners(project(list(pair)))
@@ -380,6 +388,7 @@
         8 * square, part * tokens * order, poles, cos_table, sin_table, twist,
     )
 
+    tables = (upper, hc, hs, cos_table, sin_table)
     grads, tgc, tgs, skip_sum = call(
         functools.partial(conv_kernel, order=order, group_slots=group_slots, shares=n_ch),
         (
@@ -388,11 +397,14 @@
             spectrum,
             jax.ShapeDtypeStruct((part, 1), F32),
         ),
-        32 * square, 0, place, *partials, upper, poles, hc, hs,
-        cos_table, sin_table, twist,
+        32 * square, 0, place, *partials, poles, twist, *tables,
         scratch=[pltpu.VMEM((n_seq, gates, part, block_len), F32)]
-        + [pltpu.VMEM(a.shape, a.dtype) for a in partials],
-        indexed=True, late=range(1, 1 + len(partials)), grant=60 * MIB,
+        + [pltpu.VMEM(a.shape, a.dtype) for a in (*partials, *tables)],
+        indexed=True, grant=60 * MIB,
+        late=[
+            *range(1, 1 + len(partials)),
+            *range(3 + len(partials), 3 + len(partials) + len(tables)),
+        ],
     )
 
     swap = [(h, h ^ 1) for h in range(n_ch)]
@@ -405,13 +417,13 @@
 
     across = chips(grads)
     swapped = lax.ppermute(grads, "ch", swap)
-    tgc, swapped = lax.optimization_barrier((tgc, swapped))
     (pole_sums,) = call(
         functools.partial(pole_kernel, order=order),
         (jax.ShapeDtypeStruct((part, 2 * order + 1), F32),),
         8 * square, part * tokens * order, poles, tgc, tgs, cos_table, sin_table, skip_sum,
     )
 
+    across, pole_sums = lax.optimization_barrier((across, pole_sums))
     held = [grads] + across + [swapped] + [lax.ppermute(a, "ch", swap) for a in across]
 
     sums = [pole_sums] + chips(pole_sums)
@@ -453,6 +465,7 @@
             transcendentals=0,
         ),
     )(place, *held, *pieces)
+    weight_grad, blocks = lax.optimization_barrier((weight_grad, blocks))
     weight_grad = weight_grad.transpose(1, 0, 2)
 
     channels = residues.shape[0]

time: 123 us -> 114 us (0.927)
  blocking collectives: 16.9 us -> 0 us
  starting transfers between devices: 33.8 us -> 38.8 us
  waiting for transfers between devices: 29.3 us -> 32.1 us
    all_to_all x1 -> x0, blocking collectives: 16.9 us -> none  [local(): lax.all_to_all(upper, 'seq', split_axis=0, concat_axis=0, tiled=True)]
    ppermute x1, waiting for transfers between devices: 0.01 us -> 9.5 us  [local(): upper = lax.ppermute(upper, ('seq', 'ch'), spread)]
    ppermute x2, waiting for transfers between devices: 7.51 us -> 0.86 us  [local(): blocks.append(lax.ppermute(block_sums, ('seq', 'ch'), route))]
    ppermute x4, starting transfers between devices: 1.34 us -> 7.47 us  [send_on(): lax.ppermute(pair[0], 'seq', ahead)]
    all_to_all x0 -> x1, starting transfers between devices: none -> 5.81 us  [local(): lax.all_to_all(upper, 'seq', split_axis=0, concat_axis=0, tiled=True)]
    ppermute x2, waiting for transfers between devices: 12.1 us -> 6.68 us  [chips(): lax.ppermute(array, 'ch', [(h, (h + d) % n_ch) for h in range(n_ch)])]
    ppermute x4, starting transfers between devices: 7.66 us -> 4.96 us  [send_on(): lax.ppermute(pair[1], 'seq', behind)]
    ppermute x4, waiting for transfers between devices: 0.07 us -> 2.35 us  [send_on(): lax.ppermute(pair[1], 'seq', behind)]
  transfers between devices with their start and end apart: 30 -> 28, of which waited for: 9 -> 11; matrix products, arithmetic and copies ran while one was open for 1% -> 1% of each run, Pallas kernels for 11% -> 18%
where the time goes in v5:
time: 114 us; the launch traced here: 112 us
  starting transfers between devices  38.8 us (34%)
  waiting for transfers between devices  32.1 us (28%)
  Pallas kernels  28 us (25%)
  local copies, waits for them, and re-layouts  11.6 us (10%)
    pallas_call x10, Pallas kernels, call(): pl.pallas_call(kernel, out_shape=outs, in_specs=specs, out_specs=[whole]...  20.4 us
    unnamed x84, local copies, waits for them, and re-layouts  11.4 us
    ppermute x1, waiting for transfers between devices, local(): upper = lax.ppermute(upper, ('seq', 'ch'), spread)  9.5 us
    pallas_call x1, Pallas kernels, local(): pl.pallas_call(functools.partial(weight_kernel, shares=n_ch), out_shape=j...  7.61 us
    ppermute x4, starting transfers between devices, send_on(): lax.ppermute(pair[0], 'seq', ahead)  7.47 us
    ppermute x2, waiting for transfers between devices, chips(): lax.ppermute(array, 'ch', [(h, (h + d) % n_ch) for h in range(n_ch)])  6.68 us
    ppermute x9, starting transfers between devices, to_owners(): lax.ppermute(sums[d], 'ch', [(h, (h + d) % n_ch) for h in range(n_ch)])  6.27 us
    all_to_all x1, starting transfers between devices, local(): lax.all_to_all(upper, 'seq', split_axis=0, concat_axis=0, tiled=True)  5.81 us
  transfers between devices with their start and end apart: 28, of which 11 were waited for; matrix products, arithmetic and copies ran while one was open for 1% of the time, Pallas kernels for 18%

profile of v5, /device:TPU:4, one launch (start us, length us, event | category | flops | bytes accessed | tf_op | source)
XLA Modules:
  0.0 112.4 jit_solution(3565121458756669944)
XLA Ops:
  0.6 1.6 %collective-permute-start = (bf16[128,2048]{1,0:T(8,128)(2,1)}, bf16[128,2048]{1,0:T(8,128)(2,1)S(1)}, u32[]{:S(2)}, u32[]{:S(2)}) collective-permute-start(bf16[128,2048]{1,0:T(8,128)(2,1)} %refs_4_.1), channel_id=1, source_target_pairs={{0,8},{8,16},{16,24},{24,28},{28,20},{20,12},{12,4},{4,0},{1,9},{9... | collective-permute-start | bytes 1572872 | tf_op jit(solution)/shard_map/ppermute | solution.py:316
  5.9 5.8 %all-to-all-start = ((bf16[8,56,128]{2,1,0:T(8,128)(2,1)}), bf16[8,56,128]{2,1,0:T(8,128)(2,1)S(1)}, u32[]{:S(2)}, u32[]{:S(2)}) async-start(bf16[8,56,128]{2,1,0:T(8,128)(2,1)} %shard_map.121), calls=%async_computation | async-start | bytes 229376 | tf_op jit(solution)/shard_map/all_to_all | solution.py:356
  11.7 4.8 %collective-permute-start.2 = (f32[56,33]{1,0:T(8,128)S(1)}, f32[56,33]{1,0:T(8,128)S(1)}, u32[]{:S(2)}, u32[]{:S(2)}) collective-permute-start(f32[56,33]{1,0:T(8,128)S(1)} %shard_map.120), channel_id=1, source_target_pairs={{0,0},{4,1},{8,2},{12,3},{16,4},{20,5},{24,6},{28,7},{1,8},{5,9},{... | collective-permute-start | bytes 22184 | tf_op jit(solution)/shard_map/ppermute | solution.py:351
  16.4 2.2 %collective-permute-done.2.poles_ref.refs_12_ = f32[56,33]{1,0:T(8,128)S(1)} collective-permute-done((f32[56,33]{1,0:T(8,128)S(1)}, f32[56,33]{1,0:T(8,128)S(1)}, u32[]{:S(2)}, u32[]{:S(2)}) %collective-permute-start.2) | collective-permute-done | bytes 7424 | tf_op jit(solution)/shard_map/ppermute | solution.py:351
  20.4 2.8 %collective-permute-start.4 = (bf16[128,2048]{1,0:T(8,128)(2,1)S(1)}, bf16[128,2048]{1,0:T(8,128)(2,1)S(1)}, u32[]{:S(2)}, u32[]{:S(2)}) collective-permute-start(bf16[128,2048]{1,0:T(8,128)(2,1)S(1)} %collective-permute-done.1.refs_2_.refs_6_), channel_id=1, source_target_pairs={{8,0},{16,8},{24,16},{28,24},{20,28},{12,20},{4,12},{0,4},{9,1},{1... | collective-permute-start | bytes 1572872 | tf_op jit(solution)/shard_map/ppermute | solution.py:316
  23.2 2.9 %collective-permute-start.5 = (bf16[8,56,128]{2,1,0:T(8,128)(2,1)S(1)}, bf16[8,56,128]{2,1,0:T(8,128)(2,1)S(1)}, u32[]{:S(2)}, u32[]{:S(2)}) collective-permute-start(bf16[8,56,128]{2,1,0:T(8,128)(2,1)S(1)} %all-to-all-done), channel_id=1, source_target_pairs={{0,0},{4,1},{8,2},{12,3},{16,4},{20,5},{24,6},{28,7},{1,8},{5,9},{... | collective-permute-start | bytes 344072 | tf_op jit(solution)/shard_map/ppermute | solution.py:358
  26.1 9.5 %collective-permute-done.5.refs_14_ = bf16[8,56,128]{2,1,0:T(8,128)(2,1)S(1)} collective-permute-done((bf16[8,56,128]{2,1,0:T(8,128)(2,1)S(1)}, bf16[8,56,128]{2,1,0:T(8,128)(2,1)S(1)}, u32[]{:S(2)}, u32[]{:S(2)}) %collective-permute-start.5) | collective-permute-done | bytes 114720 | tf_op jit(solution)/shard_map/ppermute | solution.py:358
  35.6 3.1 %collective-permute-start.6 = (bf16[128,2048]{1,0:T(8,128)(2,1)S(1)}, bf16[128,2048]{1,0:T(8,128)(2,1)S(1)}, u32[]{:S(2)}, u32[]{:S(2)}) collective-permute-start(bf16[128,2048]{1,0:T(8,128)(2,1)S(1)} %collective-permute-done.3.refs_3_.refs_7_), channel_id=1, source_target_pairs={{0,8},{8,16},{16,24},{24,28},{28,20},{20,12},{12,4},{4,0},{1,9},{9... | collective-permute-start | bytes 1572872 | tf_op jit(solution)/shard_map/ppermute | solution.py:316
  38.7 1.4 %collective-permute-start.7 = (bf16[128,2048]{1,0:T(8,128)(2,1)S(1)}, bf16[128,2048]{1,0:T(8,128)(2,1)S(1)}, u32[]{:S(2)}, u32[]{:S(2)}) collective-permute-start(bf16[128,2048]{1,0:T(8,128)(2,1)S(1)} %collective-permute-done.4.refs_4_.refs_8_), channel_id=1, source_target_pairs={{8,0},{16,8},{24,16},{28,24},{20,28},{12,20},{4,12},{0,4},{9,1},{1... | collective-permute-start | bytes 1572872 | tf_op jit(solution)/shard_map/ppermute | solution.py:316
  40.1 1.7 %copy-done = bf16[208,3,2048]{2,0,1:T(8,128)(2,1)S(1)} copy-done((bf16[208,3,2048]{2,0,1:T(8,128)(2,1)S(1)}, bf16[208,3,2048]{2,0,1:T(8,128)(2,1)}, u32[]{:S(2)}) %copy-start) | copy-done | bytes 2555928
  42.9 3.4 %shard_map.122 = (f32[3,56,640]{2,1,0:T(8,128)S(1)}, bf16[3,56,640]{2,1,0:T(8,128)(2,1)S(1)}, bf16[3,56,640]{2,1,0:T(8,128)(2,1)S(1)}, bf16[3,56,640]{2,1,0:T(8,128)(2,1)S(1)}) custom-call(s32[2]{0:T(128)S(1)} %pad_add_fusion.place_ref, bf16[3,208,2048]{2,1,0:T(8,128)(2,1)S(1)} %bitcast.8, bf16[128,2048]{1,0:T(8,128)(2,1)S(1)} %copy-done.9, ...), custom_call_target="tpu_custom_call" | custom-call | flops 1635778560 | bytes 6252552 | tf_op jit(solution)/shard_map/pallas_call | solution.py:280
  46.4 3.9 %collective-permute-done.6.refs_0_.refs_9_ = bf16[128,2048]{1,0:T(8,128)(2,1)S(1)} collective-permute-done((bf16[128,2048]{1,0:T(8,128)(2,1)S(1)}, bf16[128,2048]{1,0:T(8,128)(2,1)S(1)}, u32[]{:S(2)}, u32[]{:S(2)}) %collective-permute-start.6) | collective-permute-done | bytes 524320 | tf_op jit(solution)/shard_map/ppermute | solution.py:316
  50.4 2.3 %collective-permute-done.7.refs_1_.refs_10_ = bf16[128,2048]{1,0:T(8,128)(2,1)S(1)} collective-permute-done((bf16[128,2048]{1,0:T(8,128)(2,1)S(1)}, bf16[128,2048]{1,0:T(8,128)(2,1)S(1)}, u32[]{:S(2)}, u32[]{:S(2)}) %collective-permute-start.7) | collective-permute-done | bytes 524320 | tf_op jit(solution)/shard_map/ppermute | solution.py:316
  52.8 1.8 %collective-permute-start.14 = (bf16[64,2048]{1,0:T(8,128)(2,1)S(1)}, bf16[64,2048]{1,0:T(8,128)(2,1)S(1)}, u32[]{:S(2)}, u32[]{:S(2)}) collective-permute-start(bf16[64,2048]{1,0:T(8,128)(2,1)S(1)} %slice.6), channel_id=1, source_target_pairs={{0,8},{8,16},{16,24},{24,28},{28,20},{20,12},{12,4},{4,0},{1,9},{9... | collective-permute-start | bytes 786440 | tf_op jit(solution)/shard_map/ppermute | solution.py:316
  55.2 1.5 %collective-permute-start.10 = (bf16[3,56,640]{2,1,0:T(8,128)(2,1)S(1)}, bf16[3,56,640]{2,1,0:T(8,128)(2,1)S(1)}, u32[]{:S(2)}, u32[]{:S(2)}) collective-permute-start(bf16[3,56,640]{2,1,0:T(8,128)(2,1)S(1)} %get-tuple-element.57), channel_id=1, source_target_pairs={{0,3},{1,0},{2,1},{3,2},{4,7},{5,4},{6,5},{7,6},{8,11},{9,8},{10,9... | collective-permute-start | bytes 645128 | tf_op jit(solution)/shard_map/ppermute | solution.py:338
  56.7 1.8 %shard_map.123 = (f32[3,56,256]{2,1,0:T(8,128)S(1)}, bf16[3,56,256]{2,1,0:T(8,128)(2,1)S(1)}, bf16[3,56,256]{2,1,0:T(8,128)(2,1)S(1)}, bf16[3,56,256]{2,1,0:T(8,128)(2,1)S(1)}) custom-call(s32[2]{0:T(128)S(1)} %pad_add_fusion.place_ref, bf16[3,208,2048]{2,1,0:T(8,128)(2,1)S(1)} %bitcast.9, bf16[128,2048]{1,0:T(8,128)(2,1)S(1)} %collective-permute-done.6.refs_0_.refs_9_, ...), custom_call_target="tpu_custom_call" | custom-call | flops 654311424 | bytes 4034568 | tf_op jit(solution)/shard_map/pallas_call | solution.py:280
  58.5 3.4 %collective-permute-done.8.refs_1_ = bf16[3,56,640]{2,1,0:T(8,128)(2,1)S(1)} collective-permute-done((bf16[3,56,640]{2,1,0:T(8,128)(2,1)S(1)}, bf16[3,56,640]{2,1,0:T(8,128)(2,1)S(1)}, u32[]{:S(2)}, u32[]{:S(2)}) %collective-permute-start.8) | collective-permute-done | bytes 215072 | tf_op jit(solution)/shard_map/ppermute | solution.py:338
  62.3 1.5 %collective-permute-start.13 = (bf16[3,56,256]{2,1,0:T(8,128)(2,1)S(1)}, bf16[3,56,256]{2,1,0:T(8,128)(2,1)S(1)}, u32[]{:S(2)}, u32[]{:S(2)}) collective-permute-start(bf16[3,56,256]{2,1,0:T(8,128)(2,1)S(1)} %get-tuple-element.65), channel_id=1, source_target_pairs={{0,3},{1,0},{2,1},{3,2},{4,7},{5,4},{6,5},{7,6},{8,11},{9,8},{10,9... | collective-permute-start | bytes 258056 | tf_op jit(solution)/shard_map/ppermute | solution.py:338
  63.7 1.4 %shard_map.124 = (f32[3,56,128]{2,1,0:T(8,128)S(1)}, bf16[3,56,128]{2,1,0:T(8,128)(2,1)S(1)}, bf16[3,56,128]{2,1,0:T(8,128)(2,1)S(1)}, bf16[3,56,128]{2,1,0:T(8,128)(2,1)S(1)}) custom-call(s32[2]{0:T(128)S(1)} %pad_add_fusion.place_ref, bf16[3,208,2048]{2,1,0:T(8,128)(2,1)S(1)} %bitcast.10, bf16[64,2048]{1,0:T(8,128)(2,1)S(1)} %collective-permute-done.14.refs_0_.refs_11_, ...), custom_call_target="tpu_custom_call" | custom-call | flops 327155712 | bytes 3295240 | tf_op jit(solution)/shard_map/pallas_call | solution.py:280
  65.2 1.1 collective-permute-start.16
  67.1 1.2 %collective-permute-done.11.refs_5_ = bf16[3,56,256]{2,1,0:T(8,128)(2,1)S(1)} collective-permute-done((bf16[3,56,256]{2,1,0:T(8,128)(2,1)S(1)}, bf16[3,56,256]{2,1,0:T(8,128)(2,1)S(1)}, u32[]{:S(2)}, u32[]{:S(2)}) %collective-permute-start.11) | collective-permute-done | bytes 86048 | tf_op jit(solution)/shard_map/ppermute | solution.py:338
  69.1 1.5 %shard_map.125 = (f32[56,1024]{1,0:T(8,128)S(1)}, f32[56,1024]{1,0:T(8,128)S(1)}) custom-call(f32[56,33]{1,0:T(8,128)S(1)} %collective-permute-done.2.poles_ref.refs_12_, bf16[1024,1024]{1,0:T(8,128)(2,1)S(1)} %copy-done.1, bf16[1024,1024]{1,0:T(8,128)(2,1)S(1)} %copy-done.3, f32[2,1024]{1,0:T(2,128)S(1)} %copy-done.23), custom_call_target="tpu_custom_call" | custom-call | flops 469762048 | bytes 4668640 | tf_op jit(solution)/shard_map/pallas_call | solution.py:280
  72.8 7.0 %shard_map.126 = (bf16[3,56,1024]{2,1,0:T(8,128)(2,1)}, f32[56,1024]{1,0:T(8,128)}, f32[56,1024]{1,0:T(8,128)}, f32[56,1]{1,0:T(8,128)}) custom-call(s32[2]{0:T(128)} %copy-done.20, f32[3,56,640]{2,1,0:T(8,128)} %copy-done.28, bf16[3,56,640]{2,1,0:T(8,128)(2,1)} %copy-done.32, bf16[3,56,640]{2,1,0:T(8,128)(2,1)} %copy-done.33, ...), custom_call_target="tpu_custom_call" | custom-call | flops 1879048192 | bytes 7306696 | tf_op jit(solution)/shard_map/pallas_call | solution.py:280
  80.4 1.6 %copy-done.4 = bf16[1024,1024]{1,0:T(8,128)(2,1)S(1)} copy-done((bf16[1024,1024]{1,0:T(8,128)(2,1)S(1)}, bf16[1024,1024]{1,0:T(8,128)(2,1)}, u32[]{:S(2)}) %copy-start.4) | copy-done | bytes 2097176
  84.7 2.1 %shard_map.127.refs_0_ = f32[56,33]{1,0:T(8,128)S(1)} custom-call(f32[56,33]{1,0:T(8,128)S(1)} %copy-done.17, f32[56,1024]{1,0:T(8,128)S(1)} %copy-done.14, f32[56,1024]{1,0:T(8,128)S(1)} %copy-done.15, bf16[1024,1024]{1,0:T(8,128)(2,1)S(1)} %copy-done.2, bf16[1024,1024]{1,0:T(8,128)(2,1)S(1)} %copy-done.4, f32[56,1]{1,0:T(8,128)S(1)} %copy-done.19), custom_call_target="tpu_custom_call" | custom-call | flops 469762048 | bytes 4668064 | tf_op jit(solution)/shard_map/pallas_call | solution.py:280
  86.7 3.6 %collective-permute-done.19.refs_1_ = bf16[3,56,1024]{2,1,0:T(8,128)(2,1)S(1)} collective-permute-done((bf16[3,56,1024]{2,1,0:T(8,128)(2,1)}, bf16[3,56,1024]{2,1,0:T(8,128)(2,1)S(1)}, u32[]{:S(2)}, u32[]{:S(2)}) %collective-permute-start.19) | collective-permute-done | bytes 344096 | tf_op jit(solution)/shard_map/ppermute | solution.py:414
  91.0 3.1 %collective-permute-done.22.refs_1_ = f32[56,33]{1,0:T(8,128)S(1)} collective-permute-done((f32[56,33]{1,0:T(8,128)S(1)}, f32[56,33]{1,0:T(8,128)S(1)}, u32[]{:S(2)}, u32[]{:S(2)}) %collective-permute-start.22) | collective-permute-done | bytes 7424 | tf_op jit(solution)/shard_map/ppermute | solution.py:414
  94.2 1.2 %collective-permute-done.24.refs_3_ = f32[56,33]{1,0:T(8,128)S(1)} collective-permute-done((f32[56,33]{1,0:T(8,128)S(1)}, f32[56,33]{1,0:T(8,128)S(1)}, u32[]{:S(2)}, u32[]{:S(2)}) %collective-permute-start.24) | collective-permute-done | bytes 7424 | tf_op jit(solution)/shard_map/ppermute | solution.py:430
  95.9 3.4 %collective-permute-start.25 = (f32[208,33]{1,0:T(8,128)S(1)}, f32[208,33]{1,0:T(8,128)S(1)}, u32[]{:S(2)}, u32[]{:S(2)}) collective-permute-start(f32[208,33]{1,0:T(8,128)S(1)} %shard_map.129), channel_id=1, source_target_pairs={{0,0},{8,1},{16,2},{24,3},{4,4},{12,5},{20,6},{28,7},{1,8},{9,9},{... | collective-permute-start | bytes 82376 | tf_op jit(solution)/shard_map/ppermute | solution.py:443
  99.3 1.8 %collective-permute-start.26 = (f32[208,33]{1,0:T(8,128)S(1)}, f32[208,33]{1,0:T(8,128)S(1)}, u32[]{:S(2)}, u32[]{:S(2)}) collective-permute-start(f32[208,33]{1,0:T(8,128)S(1)} %shard_map.129), channel_id=1, source_target_pairs={{4,0},{12,1},{20,2},{28,3},{0,4},{8,5},{16,6},{24,7},{5,8},{13,9},... | collective-permute-start | bytes 82376 | tf_op jit(solution)/shard_map/ppermute | solution.py:443
  102.7 7.6 %shard_map.128 = f32[3,208,2048]{2,1,0:T(8,128)} custom-call(s32[2]{0:T(128)} %copy-done.20, bf16[3,56,1024]{2,1,0:T(8,128)(2,1)} %get-tuple-element.76.refs_0_, bf16[3,56,1024]{2,1,0:T(8,128)(2,1)} %copy-done.29, bf16[3,56,1024]{2,1,0:T(8,128)(2,1)} %copy-done.30, bf16[3,56,1024]{2,1,0:T(8,128)(2,1)} %copy-done.31, bf16[128,2048]{1,0:T(8,128)(2,1)} %refs_4_.1, ...), custom_call_target="tpu_custom_call" | custom-call | flops 2617245696 | bytes 10584064 | tf_op jit(solution)/shard_map/pallas_call | solution.py:446
  111.1 1.3 %shard_map.130 = (f32[16,416]{1,0:T(8,128)}, f32[16,416]{1,0:T(8,128)}, f32[1,416]{1,0:T(1,128)}) custom-call(s32[2]{0:T(128)S(1)} %copy-done.22, f32[208,33]{1,0:T(8,128)S(1)} %collective-permute-done.25.refs_0_, f32[208,33]{1,0:T(8,128)S(1)} %collective-permute-done.26.refs_1_), custom_call_target="tpu_custom_call" | custom-call | bytes 109832 | tf_op jit(solution)/shard_map/pallas_call | solution.py:280
  (124 shorter events, 17.9 us)
Async XLA Ops:
  0.6 18.8 %collective-permute-start = (bf16[128,2048]{1,0:T(8,128)(2,1)}, bf16[128,2048]{1,0:T(8,128)(2,1)S(1)}, u32[]{:S(2)}, u32[]{:S(2)}) collective-permute-start(bf16[128,2048]{1,0:T(8,128)(2,1)} %refs_4_.1), channel_id=1, source_target_pairs={{0,8},{8,16},{16,24},{24,28},{28,20},{20,12},{12,4},{4,0},{1,9},{9... | collective-permute-start | bytes 1572872 | tf_op jit(solution)/shard_map/ppermute | solution.py:316
  2.3 17.2 %collective-permute-start.1 = (bf16[128,2048]{1,0:T(8,128)(2,1)}, bf16[128,2048]{1,0:T(8,128)(2,1)S(1)}, u32[]{:S(2)}, u32[]{:S(2)}) collective-permute-start(bf16[128,2048]{1,0:T(8,128)(2,1)} %refs_4_.1), channel_id=1, source_target_pairs={{8,0},{16,8},{24,16},{28,24},{20,28},{12,20},{4,12},{0,4},{9,1},{1... | collective-permute-start | bytes 1572872 | tf_op jit(solution)/shard_map/ppermute | solution.py:316
  3.7 60.0 %copy-start.20 = (s32[2]{0:T(128)}, s32[2]{0:T(128)S(1)}, u32[]{:S(2)}) copy-start(s32[2]{0:T(128)S(1)} %pad_add_fusion.place_ref) | copy-start | bytes 28
  5.9 13.6 %all-to-all-start = ((bf16[8,56,128]{2,1,0:T(8,128)(2,1)}), bf16[8,56,128]{2,1,0:T(8,128)(2,1)S(1)}, u32[]{:S(2)}, u32[]{:S(2)}) async-start(bf16[8,56,128]{2,1,0:T(8,128)(2,1)} %shard_map.121), calls=%async_computation | async-start | bytes 229376 | tf_op jit(solution)/shard_map/all_to_all | solution.py:356
  11.7 6.9 %collective-permute-start.2 = (f32[56,33]{1,0:T(8,128)S(1)}, f32[56,33]{1,0:T(8,128)S(1)}, u32[]{:S(2)}, u32[]{:S(2)}) collective-permute-start(f32[56,33]{1,0:T(8,128)S(1)} %shard_map.120), channel_id=1, source_target_pairs={{0,0},{4,1},{8,2},{12,3},{16,4},{20,5},{24,6},{28,7},{1,8},{5,9},{... | collective-permute-start | bytes 22184 | tf_op jit(solution)/shard_map/ppermute | solution.py:351
  18.6 50.5 %copy-start.16 = (f32[56,33]{1,0:T(8,128)}, f32[56,33]{1,0:T(8,128)S(1)}, u32[]{:S(2)}) copy-start(f32[56,33]{1,0:T(8,128)S(1)} %collective-permute-done.2.poles_ref.refs_12_) | copy-start | bytes 22180
  19.4 26.9 %copy-start.10 = (bf16[128,2048]{1,0:T(8,128)(2,1)}, bf16[128,2048]{1,0:T(8,128)(2,1)S(1)}, u32[]{:S(2)}) copy-start(bf16[128,2048]{1,0:T(8,128)(2,1)S(1)} %collective-permute-done.refs_1_.refs_5_) | copy-start | bytes 1572868
  19.4 26.9 %copy-start.11 = (bf16[128,2048]{1,0:T(8,128)(2,1)}, bf16[128,2048]{1,0:T(8,128)(2,1)S(1)}, u32[]{:S(2)}) copy-start(bf16[128,2048]{1,0:T(8,128)(2,1)S(1)} %collective-permute-done.1.refs_2_.refs_6_) | copy-start | bytes 1572868
  19.4 16.2 %collective-permute-start.3 = (bf16[128,2048]{1,0:T(8,128)(2,1)S(1)}, bf16[128,2048]{1,0:T(8,128)(2,1)S(1)}, u32[]{:S(2)}, u32[]{:S(2)}) collective-permute-start(bf16[128,2048]{1,0:T(8,128)(2,1)S(1)} %collective-permute-done.refs_1_.refs_5_), channel_id=1, source_target_pairs={{0,8},{8,16},{16,24},{24,28},{28,20},{20,12},{12,4},{4,0},{1,9},{9... | collective-permute-start | bytes 1572872 | tf_op jit(solution)/shard_map/ppermute | solution.py:316
  20.4 15.2 %collective-permute-start.4 = (bf16[128,2048]{1,0:T(8,128)(2,1)S(1)}, bf16[128,2048]{1,0:T(8,128)(2,1)S(1)}, u32[]{:S(2)}, u32[]{:S(2)}) collective-permute-start(bf16[128,2048]{1,0:T(8,128)(2,1)S(1)} %collective-permute-done.1.refs_2_.refs_6_), channel_id=1, source_target_pairs={{8,0},{16,8},{24,16},{28,24},{20,28},{12,20},{4,12},{0,4},{9,1},{1... | collective-permute-start | bytes 1572872 | tf_op jit(solution)/shard_map/ppermute | solution.py:316
  23.2 12.4 %collective-permute-start.5 = (bf16[8,56,128]{2,1,0:T(8,128)(2,1)S(1)}, bf16[8,56,128]{2,1,0:T(8,128)(2,1)S(1)}, u32[]{:S(2)}, u32[]{:S(2)}) collective-permute-start(bf16[8,56,128]{2,1,0:T(8,128)(2,1)S(1)} %all-to-all-done), channel_id=1, source_target_pairs={{0,0},{4,1},{8,2},{12,3},{16,4},{20,5},{24,6},{28,7},{1,8},{5,9},{... | collective-permute-start | bytes 344072 | tf_op jit(solution)/shard_map/ppermute | solution.py:358
  35.6 14.7 %collective-permute-start.6 = (bf16[128,2048]{1,0:T(8,128)(2,1)S(1)}, bf16[128,2048]{1,0:T(8,128)(2,1)S(1)}, u32[]{:S(2)}, u32[]{:S(2)}) collective-permute-start(bf16[128,2048]{1,0:T(8,128)(2,1)S(1)} %collective-permute-done.3.refs_3_.refs_7_), channel_id=1, source_target_pairs={{0,8},{8,16},{16,24},{24,28},{28,20},{20,12},{12,4},{4,0},{1,9},{9... | collective-permute-start | bytes 1572872 | tf_op jit(solution)/shard_map/ppermute | solution.py:316
  38.7 13.9 %collective-permute-start.7 = (bf16[128,2048]{1,0:T(8,128)(2,1)S(1)}, bf16[128,2048]{1,0:T(8,128)(2,1)S(1)}, u32[]{:S(2)}, u32[]{:S(2)}) collective-permute-start(bf16[128,2048]{1,0:T(8,128)(2,1)S(1)} %collective-permute-done.4.refs_4_.refs_8_), channel_id=1, source_target_pairs={{8,0},{16,8},{24,16},{28,24},{20,28},{12,20},{4,12},{0,4},{9,1},{1... | collective-permute-start | bytes 1572872 | tf_op jit(solution)/shard_map/ppermute | solution.py:316
  52.8 9.1 %collective-permute-start.14 = (bf16[64,2048]{1,0:T(8,128)(2,1)S(1)}, bf16[64,2048]{1,0:T(8,128)(2,1)S(1)}, u32[]{:S(2)}, u32[]{:S(2)}) collective-permute-start(bf16[64,2048]{1,0:T(8,128)(2,1)S(1)} %slice.6), channel_id=1, source_target_pairs={{0,8},{8,16},{16,24},{24,28},{28,20},{20,12},{12,4},{4,0},{1,9},{9... | collective-permute-start | bytes 786440 | tf_op jit(solution)/shard_map/ppermute | solution.py:316
  54.6 7.7 %collective-permute-start.15 = (bf16[64,2048]{1,0:T(8,128)(2,1)S(1)}, bf16[64,2048]{1,0:T(8,128)(2,1)S(1)}, u32[]{:S(2)}, u32[]{:S(2)}) collective-permute-start(bf16[64,2048]{1,0:T(8,128)(2,1)S(1)} %slice.7), channel_id=1, source_target_pairs={{8,0},{16,8},{24,16},{28,24},{20,28},{12,20},{4,12},{0,4},{9,1},{1... | collective-permute-start | bytes 786440 | tf_op jit(solution)/shard_map/ppermute | solution.py:316
  54.8 7.0 %collective-permute-start.8 = (bf16[3,56,640]{2,1,0:T(8,128)(2,1)S(1)}, bf16[3,56,640]{2,1,0:T(8,128)(2,1)S(1)}, u32[]{:S(2)}, u32[]{:S(2)}) collective-permute-start(bf16[3,56,640]{2,1,0:T(8,128)(2,1)S(1)} %get-tuple-element.55), channel_id=1, source_target_pairs={{0,1},{1,2},{2,3},{3,0},{4,5},{5,6},{6,7},{7,4},{8,9},{9,10},{10,1... | collective-permute-start | bytes 645128 | tf_op jit(solution)/shard_map/ppermute | solution.py:338
  54.8 10.4 %collective-permute-start.9 = (bf16[3,56,640]{2,1,0:T(8,128)(2,1)S(1)}, bf16[3,56,640]{2,1,0:T(8,128)(2,1)S(1)}, u32[]{:S(2)}, u32[]{:S(2)}) collective-permute-start(bf16[3,56,640]{2,1,0:T(8,128)(2,1)S(1)} %get-tuple-element.56), channel_id=1, source_target_pairs={{0,2},{1,3},{2,0},{3,1},{4,6},{5,7},{6,4},{7,5},{8,10},{9,11},{10,... | collective-permute-start | bytes 645128 | tf_op jit(solution)/shard_map/ppermute | solution.py:338
  55.2 11.1 %collective-permute-start.10 = (bf16[3,56,640]{2,1,0:T(8,128)(2,1)S(1)}, bf16[3,56,640]{2,1,0:T(8,128)(2,1)S(1)}, u32[]{:S(2)}, u32[]{:S(2)}) collective-permute-start(bf16[3,56,640]{2,1,0:T(8,128)(2,1)S(1)} %get-tuple-element.57), channel_id=1, source_target_pairs={{0,3},{1,0},{2,1},{3,2},{4,7},{5,4},{6,5},{7,6},{8,11},{9,8},{10,9... | collective-permute-start | bytes 645128 | tf_op jit(solution)/shard_map/ppermute | solution.py:338
  61.9 6.4 %collective-permute-start.11 = (bf16[3,56,256]{2,1,0:T(8,128)(2,1)S(1)}, bf16[3,56,256]{2,1,0:T(8,128)(2,1)S(1)}, u32[]{:S(2)}, u32[]{:S(2)}) collective-permute-start(bf16[3,56,256]{2,1,0:T(8,128)(2,1)S(1)} %get-tuple-element.63), channel_id=1, source_target_pairs={{0,1},{1,2},{2,3},{3,0},{4,5},{5,6},{6,7},{7,4},{8,9},{9,10},{10,1... | collective-permute-start | bytes 258056 | tf_op jit(solution)/shard_map/ppermute | solution.py:338
  61.9 10.2 %collective-permute-start.12 = (bf16[3,56,256]{2,1,0:T(8,128)(2,1)S(1)}, bf16[3,56,256]{2,1,0:T(8,128)(2,1)S(1)}, u32[]{:S(2)}, u32[]{:S(2)}) collective-permute-start(bf16[3,56,256]{2,1,0:T(8,128)(2,1)S(1)} %get-tuple-element.64), channel_id=1, source_target_pairs={{0,2},{1,3},{2,0},{3,1},{4,6},{5,7},{6,4},{7,5},{8,10},{9,11},{10,... | collective-permute-start | bytes 258056 | tf_op jit(solution)/shard_map/ppermute | solution.py:338
  62.3 9.8 %collective-permute-start.13 = (bf16[3,56,256]{2,1,0:T(8,128)(2,1)S(1)}, bf16[3,56,256]{2,1,0:T(8,128)(2,1)S(1)}, u32[]{:S(2)}, u32[]{:S(2)}) collective-permute-start(bf16[3,56,256]{2,1,0:T(8,128)(2,1)S(1)} %get-tuple-element.65), channel_id=1, source_target_pairs={{0,3},{1,0},{2,1},{3,2},{4,7},{5,4},{6,5},{7,6},{8,11},{9,8},{10,9... | collective-permute-start | bytes 258056 | tf_op jit(solution)/shard_map/ppermute | solution.py:338
  65.2 6.9 %collective-permute-start.16 = (bf16[3,56,128]{2,1,0:T(8,128)(2,1)S(1)}, bf16[3,56,128]{2,1,0:T(8,128)(2,1)S(1)}, u32[]{:S(2)}, u32[]{:S(2)}) collective-permute-start(bf16[3,56,128]{2,1,0:T(8,128)(2,1)S(1)} %get-tuple-element.69), channel_id=1, source_target_pairs={{0,1},{1,2},{2,3},{3,0},{4,5},{5,6},{6,7},{7,4},{8,9},{9,10},{10,1... | collective-permute-start | bytes 129032 | tf_op jit(solution)/shard_map/ppermute | solution.py:338
  66.3 5.8 %collective-permute-start.17 = (bf16[3,56,128]{2,1,0:T(8,128)(2,1)S(1)}, bf16[3,56,128]{2,1,0:T(8,128)(2,1)S(1)}, u32[]{:S(2)}, u32[]{:S(2)}) collective-permute-start(bf16[3,56,128]{2,1,0:T(8,128)(2,1)S(1)} %get-tuple-element.70), channel_id=1, source_target_pairs={{0,2},{1,3},{2,0},{3,1},{4,6},{5,7},{6,4},{7,5},{8,10},{9,11},{10,... | collective-permute-start | bytes 129032 | tf_op jit(solution)/shard_map/ppermute | solution.py:338
  68.3 3.8 %collective-permute-start.18 = (bf16[3,56,128]{2,1,0:T(8,128)(2,1)S(1)}, bf16[3,56,128]{2,1,0:T(8,128)(2,1)S(1)}, u32[]{:S(2)}, u32[]{:S(2)}) collective-permute-start(bf16[3,56,128]{2,1,0:T(8,128)(2,1)S(1)} %get-tuple-element.71), channel_id=1, source_target_pairs={{0,3},{1,0},{2,1},{3,2},{4,7},{5,4},{6,5},{7,6},{8,11},{9,8},{10,9... | collective-permute-start | bytes 129032 | tf_op jit(solution)/shard_map/ppermute | solution.py:338
  79.8 10.4 %collective-permute-start.19 = (bf16[3,56,1024]{2,1,0:T(8,128)(2,1)}, bf16[3,56,1024]{2,1,0:T(8,128)(2,1)S(1)}, u32[]{:S(2)}, u32[]{:S(2)}) collective-permute-start(bf16[3,56,1024]{2,1,0:T(8,128)(2,1)} %get-tuple-element.76.refs_0_), channel_id=1, source_target_pairs={{0,2},{1,3},{2,0},{3,1},{4,6},{5,7},{6,4},{7,5},{8,10},{9,11},{10,... | collective-permute-start | bytes 1032200 | tf_op jit(solution)/shard_map/ppermute | solution.py:414
  80.4 20.8 %collective-permute-start.20 = (bf16[3,56,1024]{2,1,0:T(8,128)(2,1)}, bf16[3,56,1024]{2,1,0:T(8,128)(2,1)S(1)}, u32[]{:S(2)}, u32[]{:S(2)}) collective-permute-start(bf16[3,56,1024]{2,1,0:T(8,128)(2,1)} %get-tuple-element.76.refs_0_), channel_id=1, source_target_pairs={{0,1},{1,0},{2,3},{3,2},{4,5},{5,4},{6,7},{7,6},{8,9},{9,8},{10,11... | collective-permute-start | bytes 1032200 | tf_op jit(solution)/shard_map/ppermute | solution.py:419
  90.3 10.9 %collective-permute-start.21 = (bf16[3,56,1024]{2,1,0:T(8,128)(2,1)S(1)}, bf16[3,56,1024]{2,1,0:T(8,128)(2,1)S(1)}, u32[]{:S(2)}, u32[]{:S(2)}) collective-permute-start(bf16[3,56,1024]{2,1,0:T(8,128)(2,1)S(1)} %collective-permute-done.19.refs_1_), channel_id=1, source_target_pairs={{0,1},{1,0},{2,3},{3,2},{4,5},{5,4},{6,7},{7,6},{8,9},{9,8},{10,11... | collective-permute-start | bytes 1032200 | tf_op jit(solution)/shard_map/ppermute | solution.py:427
  90.3 3.9 %collective-permute-start.22 = (f32[56,33]{1,0:T(8,128)S(1)}, f32[56,33]{1,0:T(8,128)S(1)}, u32[]{:S(2)}, u32[]{:S(2)}) collective-permute-start(f32[56,33]{1,0:T(8,128)S(1)} %shard_map.127.refs_0_), channel_id=1, source_target_pairs={{0,2},{1,3},{2,0},{3,1},{4,6},{5,7},{6,4},{7,5},{8,10},{9,11},{10,... | collective-permute-start | bytes 22184 | tf_op jit(solution)/shard_map/ppermute | solution.py:414
  90.8 3.4 %collective-permute-start.23 = (f32[56,33]{1,0:T(8,128)S(1)}, f32[56,33]{1,0:T(8,128)S(1)}, u32[]{:S(2)}, u32[]{:S(2)}) collective-permute-start(f32[56,33]{1,0:T(8,128)S(1)} %shard_map.127.refs_0_), channel_id=1, source_target_pairs={{0,1},{1,0},{2,3},{3,2},{4,5},{5,4},{6,7},{7,6},{8,9},{9,8},{10,11... | collective-permute-start | bytes 22184 | tf_op jit(solution)/shard_map/ppermute | solution.py:430
  94.1 1.2 %collective-permute-start.24 = (f32[56,33]{1,0:T(8,128)S(1)}, f32[56,33]{1,0:T(8,128)S(1)}, u32[]{:S(2)}, u32[]{:S(2)}) collective-permute-start(f32[56,33]{1,0:T(8,128)S(1)} %collective-permute-done.22.refs_1_), channel_id=1, source_target_pairs={{0,1},{1,0},{2,3},{3,2},{4,5},{5,4},{6,7},{7,6},{8,9},{9,8},{10,11... | collective-permute-start | bytes 22184 | tf_op jit(solution)/shard_map/ppermute | solution.py:430
  95.9 14.3 %collective-permute-start.25 = (f32[208,33]{1,0:T(8,128)S(1)}, f32[208,33]{1,0:T(8,128)S(1)}, u32[]{:S(2)}, u32[]{:S(2)}) collective-permute-start(f32[208,33]{1,0:T(8,128)S(1)} %shard_map.129), channel_id=1, source_target_pairs={{0,0},{8,1},{16,2},{24,3},{4,4},{12,5},{20,6},{28,7},{1,8},{9,9},{... | collective-permute-start | bytes 82376 | tf_op jit(solution)/shard_map/ppermute | solution.py:443
  99.3 11.8 %collective-permute-start.26 = (f32[208,33]{1,0:T(8,128)S(1)}, f32[208,33]{1,0:T(8,128)S(1)}, u32[]{:S(2)}, u32[]{:S(2)}) collective-permute-start(f32[208,33]{1,0:T(8,128)S(1)} %shard_map.129), channel_id=1, source_target_pairs={{4,0},{12,1},{20,2},{28,3},{0,4},{8,5},{16,6},{24,7},{5,8},{13,9},... | collective-permute-start | bytes 82376 | tf_op jit(solution)/shard_map/ppermute | solution.py:443
  (38 other events, 241.0 us)

commit v6 on v5

--- a/solution.py
+++ b/solution.py
@@ -66,12 +66,13 @@
     return pl.multiple_of(jnp.minimum(index * part, rows - part), 8)
 
 
-def pieces_kernel(grad_ref, pieces_ref, *, rows, n_ch):
-    part = pieces_ref.shape[1]
+def pieces_kernel(grad_ref, pieces_ref, *, rows):
+    n_ch, blocks, part, _ = pieces_ref.shape
     grad = grad_ref[...].astype(F32)
-    for piece in range(pieces_ref.shape[0]):
-        start = piece // n_ch * rows + min(piece % n_ch * part, rows - part)
-        pieces_ref[piece] = grad[start : start + part].astype(BF16)
+    for owner in range(n_ch):
+        for block in range(blocks):
+            start = block * rows + min(owner * part, rows - part)
+            pieces_ref[owner, block] = grad[start : start + part].astype(BF16)
 
 
 def poles_kernel(place_ref, packed_ref, poles_ref, *, rows, n_ch):
@@ -132,16 +133,11 @@
     count = len(group_slots) * shares
     partial_refs = refs[:count]
     (
-        poles_ref, twist_ref, gout_from, hc_from, hs_from, cos_from, sin_from, grad_ref,
+        gout_ref, poles_ref, hc_ref, hs_ref, cos_ref, sin_ref, twist_ref, grad_ref,
         tgc_ref, tgs_ref, skip_ref, proj_ref, *scratch_refs,
     ) = refs[count:]
-    *held_refs, gout_ref, hc_ref, hs_ref, cos_ref, sin_ref, semaphores = scratch_refs
-    copies = fetch(
-        (*partial_refs, gout_from, cos_from, sin_from, hc_from, hs_from),
-        (*held_refs, gout_ref, cos_ref, sin_ref, hc_ref, hs_ref),
-        semaphores,
-    )
-    finish(copies[: count + 1])
+    *held_refs, semaphores = scratch_refs
+    finish(fetch(partial_refs, held_refs, semaphores))
     rows, tokens = hc_ref.shape
     blocks, _, _, block_len = proj_ref.shape
     slot = 0
@@ -169,7 +165,6 @@
     middle = upper * queries
     signals = jnp.concatenate([product, middle], 0)
     parts = two_parts(signals)
-    finish(copies[count + 1 :])
     even = dot(parts, cos_ref[...])
     uneven = dot(parts, sin_ref[...])
     even = even[: 2 * rows] + even[2 * rows :]
@@ -237,8 +232,13 @@
     for feature_ref in feature_refs:
         features_ref[row : row + feature_ref.shape[0], :] = feature_ref[...]
         row += feature_ref.shape[0]
-    for gate in range(gates):
-        out_ref[gate] = dot(rows_ref[gate], features_ref[...])
+    rows = out_ref.shape[1]
+    if rows % 16 == 0:
+        every = dot(rows_ref[...].reshape(gates * rows, -1), features_ref[...])
+        out_ref[...] = every.reshape(out_ref.shape)
+    else:
+        for gate in range(gates):
+            out_ref[gate] = dot(rows_ref[gate], features_ref[...])
 
 
 def assemble_kernel(place_ref, *refs, rows, order):
@@ -263,20 +263,20 @@
         out_ref[pl.ds(start, held_ref.shape[0]), :] = held_ref[...]
 
 
-def call(kernel, outs, flops, transcendentals, *operands, scratch=(), indexed=False, late=(), grant=0):
+def call(kernel, outs, flops, transcendentals, *operands, scratch=(), indexed=False, late=()):
     size = sum(a.size * a.dtype.itemsize for a in operands) + sum(
         o.size * o.dtype.itemsize for o in outs
     )
     scratch_size = sum(math.prod(a.shape) * a.dtype.itemsize for a in scratch)
     if late:
         scratch = [*scratch, pltpu.SemaphoreType.DMA((len(late),))]
-    limit = max(grant, min(56 * MIB, 2 * (size + scratch_size) + 8 * MIB))
+    limit = min(56 * MIB, 2 * (size + scratch_size) + 8 * MIB)
     whole = pl.BlockSpec(memory_space=pltpu.VMEM)
     specs = [whole] * len(operands)
     if indexed:
         specs[0] = pl.BlockSpec(memory_space=pltpu.SMEM)
     for operand in late:
-        specs[operand] = pl.BlockSpec(memory_space=pl.ANY)
+        specs[operand] = pl.BlockSpec(memory_space=pltpu.HBM)
     return pl.pallas_call(
         kernel,
         out_shape=outs,
@@ -350,12 +350,13 @@
     grad_out, poles = lax.optimization_barrier((grad_out, poles))
     poles = lax.ppermute(poles, ("seq", "ch"), spread)
     (upper,) = call(
-        functools.partial(pieces_kernel, rows=rows, n_ch=n_ch),
-        (jax.ShapeDtypeStruct((n_seq, part, block_len), BF16),), 0, 0, grad_out,
-    )
+        functools.partial(pieces_kernel, rows=rows),
+        (jax.ShapeDtypeStruct((n_ch, n_seq // n_ch, part, block_len), BF16),), 0, 0, grad_out,
+    )
+    upper = lax.all_to_all(upper, "ch", split_axis=0, concat_axis=0, tiled=True)
+    pair, upper, poles = lax.optimization_barrier((pair, upper, poles))
+    upper = upper.reshape(n_seq, part, block_len)
     upper = lax.all_to_all(upper, "seq", split_axis=0, concat_axis=0, tiled=True)
-    pair, upper, poles = lax.optimization_barrier((pair, upper, poles))
-    upper = lax.ppermute(upper, ("seq", "ch"), spread)
 
     pieces, group_slots, partials = [features, *pair], [], []
     waiting = list(pieces)
@@ -388,7 +389,6 @@
         8 * square, part * tokens * order, poles, cos_table, sin_table, twist,
     )
 
-    tables = (upper, hc, hs, cos_table, sin_table)
     grads, tgc, tgs, skip_sum = call(
         functools.partial(conv_kernel, order=order, group_slots=group_slots, shares=n_ch),
         (
@@ -397,14 +397,10 @@
             spectrum,
             jax.ShapeDtypeStruct((part, 1), F32),
         ),
-        32 * square, 0, place, *partials, poles, twist, *tables,
+        32 * square, 0, place, *partials, upper, poles, hc, hs, cos_table, sin_table, twist,
         scratch=[pltpu.VMEM((n_seq, gates, part, block_len), F32)]
-        + [pltpu.VMEM(a.shape, a.dtype) for a in (*partials, *tables)],
-        indexed=True, grant=60 * MIB,
-        late=[
-            *range(1, 1 + len(partials)),
-            *range(3 + len(partials), 3 + len(partials) + len(tables)),
-        ],
+        + [pltpu.VMEM(a.shape, a.dtype) for a in partials],
+        indexed=True, late=range(1, 1 + len(partials)),
     )
 
     swap = [(h, h ^ 1) for h in range(n_ch)]
@@ -423,10 +419,9 @@
         8 * square, part * tokens * order, poles, tgc, tgs, cos_table, sin_table, skip_sum,
     )
 
-    across, pole_sums = lax.optimization_barrier((across, pole_sums))
+    sums = [pole_sums] + chips(pole_sums)
+    across, sums = lax.optimization_barrier((across, sums))
     held = [grads] + across + [swapped] + [lax.ppermute(a, "ch", swap) for a in across]
-
-    sums = [pole_sums] + chips(pole_sums)
     sums += [lax.ppermute(a, "ch", swap) for a in sums]
     (block_sums,) = call(
         gather_kernel, [jax.ShapeDtypeStruct((rows, 2 * order + 1), F32)], 0, 0, place, *sums,
@@ -457,7 +452,7 @@
             pltpu.VMEM((tokens, tile), BF16),
         ],
         compiler_params=pltpu.CompilerParams(
-            vmem_limit_bytes=60 * MIB
+            vmem_limit_bytes=min(56 * MIB, 16 * MIB + 12 * gates * rows * tokens + 4 * tokens * tile)
         ),
         cost_estimate=pl.CostEstimate(
             flops=2 * gates * rows * width * tokens,

time: 114 us -> 105 us (0.921)
  blocking collectives: 0 us -> 14.2 us
  waiting for transfers between devices: 32.1 us -> 20.5 us
  local copies, waits for them, and re-layouts: 11.6 us -> 3.83 us
  Pallas kernels: 28 us -> 24.7 us
    all_to_all x0 -> x1, blocking collectives: none -> 14.2 us  [local(): lax.all_to_all(upper, 'seq', split_axis=0, concat_axis=0, tiled=True)]
    ppermute x1 -> x0, waiting for transfers between devices: 9.5 us -> none  [local(): upper = lax.ppermute(upper, ('seq', 'ch'), spread)]
    unnamed x84 -> x14, local copies, waits for them, and re-layouts: 11.4 us -> 3.67 us
    ppermute x9, starting transfers between devices: 6.27 us -> 12.1 us  [to_owners(): lax.ppermute(sums[d], 'ch', [(h, (h + d) % n_ch) for h in range(n_ch)])]
    ppermute x4, starting transfers between devices: 7.47 us -> 4.3 us  [send_on(): lax.ppermute(pair[0], 'seq', ahead)]
    ppermute x9, waiting for transfers between devices: 4.6 us -> 1.43 us  [to_owners(): lax.ppermute(sums[d], 'ch', [(h, (h + d) % n_ch) for h in range(n_ch)])]
    ppermute x1 -> x0, starting transfers between devices: 2.9 us -> none  [local(): upper = lax.ppermute(upper, ('seq', 'ch'), spread)]
    ppermute x2, waiting for transfers between devices: 0.86 us -> 3.66 us  [local(): blocks.append(lax.ppermute(block_sums, ('seq', 'ch'), route))]
  transfers between devices with their start and end apart: 28 -> 27, of which waited for: 11 -> 10; matrix products, arithmetic and copies ran while one was open for 1% -> 1% of each run, Pallas kernels for 18% -> 17%
where the time goes in v6:
time: 105 us
  starting transfers between devices  39.6 us (38%)
  Pallas kernels  24.7 us (24%)
  waiting for transfers between devices  20.5 us (20%)
  blocking collectives  14.2 us (14%)
  local copies, waits for them, and re-layouts  3.83 us (4%)
    pallas_call x10, Pallas kernels, call(): pl.pallas_call(kernel, out_shape=outs, in_specs=specs, out_specs=[whole]...  18.9 us
    all_to_all x1, blocking collectives, local(): lax.all_to_all(upper, 'seq', split_axis=0, concat_axis=0, tiled=True)  14.2 us
    ppermute x9, starting transfers between devices, to_owners(): lax.ppermute(sums[d], 'ch', [(h, (h + d) % n_ch) for h in range(n_ch)])  12.1 us
    ppermute x2, waiting for transfers between devices, chips(): lax.ppermute(array, 'ch', [(h, (h + d) % n_ch) for h in range(n_ch)])  7.02 us
    ppermute x4, starting transfers between devices, send_on(): lax.ppermute(pair[1], 'seq', behind)  6.48 us
    ppermute x2, starting transfers between devices, local(): blocks.append(lax.ppermute(block_sums, ('seq', 'ch'), route))  6.08 us
    pallas_call x1, Pallas kernels, local(): pl.pallas_call(functools.partial(weight_kernel, shares=n_ch), out_shape=j...  5.75 us
    ppermute x1, starting transfers between devices, local(): poles = lax.ppermute(poles, ('seq', 'ch'), spread)  4.42 us
  transfers between devices with their start and end apart: 27, of which 10 were waited for; matrix products, arithmetic and copies ran while one was open for 1% of the time, Pallas kernels for 17%

profile of v6, /device:TPU:4, one launch (start us, length us, event | category | flops | bytes accessed | tf_op | source)
XLA Modules:
  0.0 104.5 jit_solution(9654706207173643978)
XLA Ops:
  0.6 1.6 %collective-permute-start = (bf16[128,2048]{1,0:T(8,128)(2,1)}, bf16[128,2048]{1,0:T(8,128)(2,1)S(1)}, u32[]{:S(2)}, u32[]{:S(2)}) collective-permute-start(bf16[128,2048]{1,0:T(8,128)(2,1)} %refs_4_.1), channel_id=1, source_target_pairs={{0,8},{8,16},{16,24},{24,28},{28,20},{20,12},{12,4},{4,0},{1,9},{9... | collective-permute-start | bytes 1572872 | tf_op jit(solution)/shard_map/ppermute | solution.py:316
  5.8 3.3 %all-to-all-start = ((bf16[4,2,56,128]{3,2,1,0:T(8,128)(2,1)}), bf16[4,2,56,128]{3,2,1,0:T(8,128)(2,1)S(1)}, u32[]{:S(2)}, u32[]{:S(2)}) async-start(bf16[4,2,56,128]{3,2,1,0:T(8,128)(2,1)} %shard_map.121), calls=%async_computation | async-start | bytes 229376 | tf_op jit(solution)/shard_map/all_to_all | solution.py:356
  9.2 4.4 %collective-permute-start.2 = (f32[56,33]{1,0:T(8,128)S(1)}, f32[56,33]{1,0:T(8,128)S(1)}, u32[]{:S(2)}, u32[]{:S(2)}) collective-permute-start(f32[56,33]{1,0:T(8,128)S(1)} %shard_map.120), channel_id=1, source_target_pairs={{0,0},{4,1},{8,2},{12,3},{16,4},{20,5},{24,6},{28,7},{1,8},{5,9},{... | collective-permute-start | bytes 22184 | tf_op jit(solution)/shard_map/ppermute | solution.py:351
  13.6 2.5 %collective-permute-done.2.poles_ref.refs_13_ = f32[56,33]{1,0:T(8,128)S(1)} collective-permute-done((f32[56,33]{1,0:T(8,128)S(1)}, f32[56,33]{1,0:T(8,128)S(1)}, u32[]{:S(2)}, u32[]{:S(2)}) %collective-permute-start.2) | collective-permute-done | bytes 7424 | tf_op jit(solution)/shard_map/ppermute | solution.py:351
  16.1 1.3 %collective-permute-start.3 = (bf16[128,2048]{1,0:T(8,128)(2,1)S(1)}, bf16[128,2048]{1,0:T(8,128)(2,1)S(1)}, u32[]{:S(2)}, u32[]{:S(2)}) collective-permute-start(bf16[128,2048]{1,0:T(8,128)(2,1)S(1)} %collective-permute-done.refs_1_.refs_5_), channel_id=1, source_target_pairs={{0,8},{8,16},{16,24},{24,28},{28,20},{20,12},{12,4},{4,0},{1,9},{9... | collective-permute-start | bytes 1572872 | tf_op jit(solution)/shard_map/ppermute | solution.py:316
  17.4 3.3 %collective-permute-start.4 = (bf16[128,2048]{1,0:T(8,128)(2,1)S(1)}, bf16[128,2048]{1,0:T(8,128)(2,1)S(1)}, u32[]{:S(2)}, u32[]{:S(2)}) collective-permute-start(bf16[128,2048]{1,0:T(8,128)(2,1)S(1)} %collective-permute-done.1.refs_2_.refs_6_), channel_id=1, source_target_pairs={{8,0},{16,8},{24,16},{28,24},{20,28},{12,20},{4,12},{0,4},{9,1},{1... | collective-permute-start | bytes 1572872 | tf_op jit(solution)/shard_map/ppermute | solution.py:316
  20.7 14.2 %all_to_all.10.refs_12_ = bf16[8,56,128]{2,1,0:T(8,128)(2,1)S(1)} all-to-all(bf16[8,56,128]{2,1,0:T(8,128)(2,1)S(1)} %bitcast.13), channel_id=1, replica_groups=mesh['seq'=8,'ch'=4] {'seq'}, dimensions={0} | all-to-all | bytes 229376 | tf_op jit(solution)/shard_map/all_to_all | solution.py:359
  35.9 1.1 %collective-permute-start.6 = (bf16[128,2048]{1,0:T(8,128)(2,1)S(1)}, bf16[128,2048]{1,0:T(8,128)(2,1)S(1)}, u32[]{:S(2)}, u32[]{:S(2)}) collective-permute-start(bf16[128,2048]{1,0:T(8,128)(2,1)S(1)} %collective-permute-done.4.refs_4_.refs_8_), channel_id=1, source_target_pairs={{8,0},{16,8},{24,16},{28,24},{20,28},{12,20},{4,12},{0,4},{9,1},{1... | collective-permute-start | bytes 1572872 | tf_op jit(solution)/shard_map/ppermute | solution.py:316
  37.0 1.7 %copy-done = bf16[208,3,2048]{2,0,1:T(8,128)(2,1)S(1)} copy-done((bf16[208,3,2048]{2,0,1:T(8,128)(2,1)S(1)}, bf16[208,3,2048]{2,0,1:T(8,128)(2,1)}, u32[]{:S(2)}) %copy-start) | copy-done | bytes 2555928
  39.8 3.4 %shard_map.122 = (f32[3,56,640]{2,1,0:T(8,128)S(1)}, bf16[3,56,640]{2,1,0:T(8,128)(2,1)S(1)}, bf16[3,56,640]{2,1,0:T(8,128)(2,1)S(1)}, bf16[3,56,640]{2,1,0:T(8,128)(2,1)S(1)}) custom-call(s32[2]{0:T(128)S(1)} %pad_add_fusion.place_ref, bf16[3,208,2048]{2,1,0:T(8,128)(2,1)S(1)} %bitcast.9, bf16[128,2048]{1,0:T(8,128)(2,1)S(1)} %copy-done.3, ...), custom_call_target="tpu_custom_call" | custom-call | flops 1635778560 | bytes 6252552 | tf_op jit(solution)/shard_map/pallas_call | solution.py:280
  43.2 4.0 %collective-permute-done.5.refs_0_.refs_9_ = bf16[128,2048]{1,0:T(8,128)(2,1)S(1)} collective-permute-done((bf16[128,2048]{1,0:T(8,128)(2,1)S(1)}, bf16[128,2048]{1,0:T(8,128)(2,1)S(1)}, u32[]{:S(2)}, u32[]{:S(2)}) %collective-permute-start.5) | collective-permute-done | bytes 524320 | tf_op jit(solution)/shard_map/ppermute | solution.py:316
  48.3 1.7 %collective-permute-start.14 = (bf16[64,2048]{1,0:T(8,128)(2,1)S(1)}, bf16[64,2048]{1,0:T(8,128)(2,1)S(1)}, u32[]{:S(2)}, u32[]{:S(2)}) collective-permute-start(bf16[64,2048]{1,0:T(8,128)(2,1)S(1)} %slice.7), channel_id=1, source_target_pairs={{8,0},{16,8},{24,16},{28,24},{20,28},{12,20},{4,12},{0,4},{9,1},{1... | collective-permute-start | bytes 786440 | tf_op jit(solution)/shard_map/ppermute | solution.py:316
  50.0 3.2 %collective-permute-start.8 = (bf16[3,56,640]{2,1,0:T(8,128)(2,1)S(1)}, bf16[3,56,640]{2,1,0:T(8,128)(2,1)S(1)}, u32[]{:S(2)}, u32[]{:S(2)}) collective-permute-start(bf16[3,56,640]{2,1,0:T(8,128)(2,1)S(1)} %get-tuple-element.57), channel_id=1, source_target_pairs={{0,2},{1,3},{2,0},{3,1},{4,6},{5,7},{6,4},{7,5},{8,10},{9,11},{10,... | collective-permute-start | bytes 645128 | tf_op jit(solution)/shard_map/ppermute | solution.py:338
  53.1 1.4 %collective-permute-start.9 = (bf16[3,56,640]{2,1,0:T(8,128)(2,1)S(1)}, bf16[3,56,640]{2,1,0:T(8,128)(2,1)S(1)}, u32[]{:S(2)}, u32[]{:S(2)}) collective-permute-start(bf16[3,56,640]{2,1,0:T(8,128)(2,1)S(1)} %get-tuple-element.58), channel_id=1, source_target_pairs={{0,3},{1,0},{2,1},{3,2},{4,7},{5,4},{6,5},{7,6},{8,11},{9,8},{10,9... | collective-permute-start | bytes 645128 | tf_op jit(solution)/shard_map/ppermute | solution.py:338
  54.6 1.8 %shard_map.123 = (f32[3,56,256]{2,1,0:T(8,128)S(1)}, bf16[3,56,256]{2,1,0:T(8,128)(2,1)S(1)}, bf16[3,56,256]{2,1,0:T(8,128)(2,1)S(1)}, bf16[3,56,256]{2,1,0:T(8,128)(2,1)S(1)}) custom-call(s32[2]{0:T(128)S(1)} %pad_add_fusion.place_ref, bf16[3,208,2048]{2,1,0:T(8,128)(2,1)S(1)} %bitcast.10, bf16[128,2048]{1,0:T(8,128)(2,1)S(1)} %collective-permute-done.5.refs_0_.refs_9_, ...), custom_call_target="tpu_custom_call" | custom-call | flops 654311424 | bytes 4034568 | tf_op jit(solution)/shard_map/pallas_call | solution.py:280
  56.4 1.4 %collective-permute-start.10 = (bf16[3,56,256]{2,1,0:T(8,128)(2,1)S(1)}, bf16[3,56,256]{2,1,0:T(8,128)(2,1)S(1)}, u32[]{:S(2)}, u32[]{:S(2)}) collective-permute-start(bf16[3,56,256]{2,1,0:T(8,128)(2,1)S(1)} %get-tuple-element.64), channel_id=1, source_target_pairs={{0,1},{1,2},{2,3},{3,0},{4,5},{5,6},{6,7},{7,4},{8,9},{9,10},{10,1... | collective-permute-start | bytes 258056 | tf_op jit(solution)/shard_map/ppermute | solution.py:338
  57.8 2.4 %collective-permute-start.11 = (bf16[3,56,256]{2,1,0:T(8,128)(2,1)S(1)}, bf16[3,56,256]{2,1,0:T(8,128)(2,1)S(1)}, u32[]{:S(2)}, u32[]{:S(2)}) collective-permute-start(bf16[3,56,256]{2,1,0:T(8,128)(2,1)S(1)} %get-tuple-element.65), channel_id=1, source_target_pairs={{0,2},{1,3},{2,0},{3,1},{4,6},{5,7},{6,4},{7,5},{8,10},{9,11},{10,... | collective-permute-start | bytes 258056 | tf_op jit(solution)/shard_map/ppermute | solution.py:338
  60.2 1.4 %collective-permute-start.12 = (bf16[3,56,256]{2,1,0:T(8,128)(2,1)S(1)}, bf16[3,56,256]{2,1,0:T(8,128)(2,1)S(1)}, u32[]{:S(2)}, u32[]{:S(2)}) collective-permute-start(bf16[3,56,256]{2,1,0:T(8,128)(2,1)S(1)} %get-tuple-element.66), channel_id=1, source_target_pairs={{0,3},{1,0},{2,1},{3,2},{4,7},{5,4},{6,5},{7,6},{8,11},{9,8},{10,9... | collective-permute-start | bytes 258056 | tf_op jit(solution)/shard_map/ppermute | solution.py:338
  61.6 1.4 %shard_map.124 = (f32[3,56,128]{2,1,0:T(8,128)S(1)}, bf16[3,56,128]{2,1,0:T(8,128)(2,1)S(1)}, bf16[3,56,128]{2,1,0:T(8,128)(2,1)S(1)}, bf16[3,56,128]{2,1,0:T(8,128)(2,1)S(1)}) custom-call(s32[2]{0:T(128)S(1)} %pad_add_fusion.place_ref, bf16[3,208,2048]{2,1,0:T(8,128)(2,1)S(1)} %bitcast.11, bf16[64,2048]{1,0:T(8,128)(2,1)S(1)} %collective-permute-done.13.refs_0_.refs_11_, ...), custom_call_target="tpu_custom_call" | custom-call | flops 327155712 | bytes 3295240 | tf_op jit(solution)/shard_map/pallas_call | solution.py:280
  63.4 1.2 %collective-permute-start.16 = (bf16[3,56,128]{2,1,0:T(8,128)(2,1)S(1)}, bf16[3,56,128]{2,1,0:T(8,128)(2,1)S(1)}, u32[]{:S(2)}, u32[]{:S(2)}) collective-permute-start(bf16[3,56,128]{2,1,0:T(8,128)(2,1)S(1)} %get-tuple-element.71), channel_id=1, source_target_pairs={{0,2},{1,3},{2,0},{3,1},{4,6},{5,7},{6,4},{7,5},{8,10},{9,11},{10,... | collective-permute-start | bytes 129032 | tf_op jit(solution)/shard_map/ppermute | solution.py:338
  65.6 1.5 %shard_map.125 = (f32[56,1024]{1,0:T(8,128)S(1)}, f32[56,1024]{1,0:T(8,128)S(1)}) custom-call(f32[56,33]{1,0:T(8,128)S(1)} %collective-permute-done.2.poles_ref.refs_13_, bf16[1024,1024]{1,0:T(8,128)(2,1)S(1)} %copy-done.1, bf16[1024,1024]{1,0:T(8,128)(2,1)S(1)} %copy-done.2, f32[2,1024]{1,0:T(2,128)S(1)} %copy-done.6), custom_call_target="tpu_custom_call" | custom-call | flops 469762048 | bytes 4668640 | tf_op jit(solution)/shard_map/pallas_call | solution.py:280
  68.3 5.6 %shard_map.126 = (bf16[3,56,1024]{2,1,0:T(8,128)(2,1)S(1)}, f32[56,1024]{1,0:T(8,128)S(1)}, f32[56,1024]{1,0:T(8,128)S(1)}, f32[56,1]{1,0:T(8,128)S(1)}) custom-call(s32[2]{0:T(128)S(1)} %pad_add_fusion.place_ref, f32[3,56,640]{2,1,0:T(8,128)S(1)} %get-tuple-element.55.refs_0_, bf16[3,56,640]{2,1,0:T(8,128)(2,1)S(1)} %collective-permute-done.7.refs_1_, ...), custom_call_target="tpu_custom_call" | custom-call | flops 1879048192 | bytes 7306696 | tf_op jit(solution)/shard_map/pallas_call | solution.py:280
  74.0 2.1 %collective-permute-start.18 = (bf16[3,56,1024]{2,1,0:T(8,128)(2,1)S(1)}, bf16[3,56,1024]{2,1,0:T(8,128)(2,1)S(1)}, u32[]{:S(2)}, u32[]{:S(2)}) collective-permute-start(bf16[3,56,1024]{2,1,0:T(8,128)(2,1)S(1)} %get-tuple-element.77.refs_0_), channel_id=1, source_target_pairs={{0,2},{1,3},{2,0},{3,1},{4,6},{5,7},{6,4},{7,5},{8,10},{9,11},{10,... | collective-permute-start | bytes 1032200 | tf_op jit(solution)/shard_map/ppermute | solution.py:410
  76.1 2.0 %shard_map.127.refs_0_ = f32[56,33]{1,0:T(8,128)S(1)} custom-call(f32[56,33]{1,0:T(8,128)S(1)} %collective-permute-done.2.poles_ref.refs_13_, f32[56,1024]{1,0:T(8,128)S(1)} %get-tuple-element.78.tgc_ref, f32[56,1024]{1,0:T(8,128)S(1)} %get-tuple-element.79.tgs_ref, bf16[1024,1024]{1,0:T(8,128)(2,1)S(1)} %copy-done.1, bf16[1024,1024]{1,0:T(8,128)(2,1)S(1)} %copy-done.2, ...), custom_call_target="tpu_custom_call" | custom-call | flops 469762048 | bytes 4668064 | tf_op jit(solution)/shard_map/pallas_call | solution.py:280
  78.4 7.0 %collective-permute-done.19.refs_1_ = f32[56,33]{1,0:T(8,128)S(1)} collective-permute-done((f32[56,33]{1,0:T(8,128)S(1)}, f32[56,33]{1,0:T(8,128)S(1)}, u32[]{:S(2)}, u32[]{:S(2)}) %collective-permute-start.19) | collective-permute-done | bytes 7424 | tf_op jit(solution)/shard_map/ppermute | solution.py:410
  85.9 1.2 %collective-permute-done.22.refs_2_ = f32[56,33]{1,0:T(8,128)S(1)} collective-permute-done((f32[56,33]{1,0:T(8,128)S(1)}, f32[56,33]{1,0:T(8,128)S(1)}, u32[]{:S(2)}, u32[]{:S(2)}) %collective-permute-start.22) | collective-permute-done | bytes 7424 | tf_op jit(solution)/shard_map/ppermute | solution.py:425
  87.7 3.6 %collective-permute-start.24 = (f32[208,33]{1,0:T(8,128)S(1)}, f32[208,33]{1,0:T(8,128)S(1)}, u32[]{:S(2)}, u32[]{:S(2)}) collective-permute-start(f32[208,33]{1,0:T(8,128)S(1)} %shard_map.129), channel_id=1, source_target_pairs={{0,0},{8,1},{16,2},{24,3},{4,4},{12,5},{20,6},{28,7},{1,8},{9,9},{... | collective-permute-start | bytes 82376 | tf_op jit(solution)/shard_map/ppermute | solution.py:438
  91.3 2.5 %collective-permute-start.25 = (f32[208,33]{1,0:T(8,128)S(1)}, f32[208,33]{1,0:T(8,128)S(1)}, u32[]{:S(2)}, u32[]{:S(2)}) collective-permute-start(f32[208,33]{1,0:T(8,128)S(1)} %shard_map.129), channel_id=1, source_target_pairs={{4,0},{12,1},{20,2},{28,3},{0,4},{8,5},{16,6},{24,7},{5,8},{13,9},... | collective-permute-start | bytes 82376 | tf_op jit(solution)/shard_map/ppermute | solution.py:438
  93.8 5.7 %shard_map.128 = f32[3,208,2048]{2,1,0:T(8,128)} custom-call(s32[2]{0:T(128)S(1)} %pad_add_fusion.place_ref, bf16[3,56,1024]{2,1,0:T(8,128)(2,1)S(1)} %get-tuple-element.77.refs_0_, bf16[3,56,1024]{2,1,0:T(8,128)(2,1)S(1)} %collective-permute-done.18.refs_1_, bf16[3,56,1024]{2,1,0:T(8,128)(2,1)S(1)} %collective-permute-done.20.refs_2_, ...), custom_call_target="tpu_custom_call" | custom-call | flops 2617245696 | bytes 10584064 | tf_op jit(solution)/shard_map/pallas_call | solution.py:441
  99.6 1.4 %collective-permute-done.24.refs_0_ = f32[208,33]{1,0:T(8,128)S(1)} collective-permute-done((f32[208,33]{1,0:T(8,128)S(1)}, f32[208,33]{1,0:T(8,128)S(1)}, u32[]{:S(2)}, u32[]{:S(2)}) %collective-permute-start.24) | collective-permute-done | bytes 27488 | tf_op jit(solution)/shard_map/ppermute | solution.py:438
  100.9 2.3 %collective-permute-done.25.refs_1_ = f32[208,33]{1,0:T(8,128)S(1)} collective-permute-done((f32[208,33]{1,0:T(8,128)S(1)}, f32[208,33]{1,0:T(8,128)S(1)}, u32[]{:S(2)}, u32[]{:S(2)}) %collective-permute-start.25) | collective-permute-done | bytes 27488 | tf_op jit(solution)/shard_map/ppermute | solution.py:438
  103.2 1.3 %shard_map.130 = (f32[16,416]{1,0:T(8,128)}, f32[16,416]{1,0:T(8,128)}, f32[1,416]{1,0:T(1,128)}) custom-call(s32[2]{0:T(128)S(1)} %pad_add_fusion.place_ref, f32[208,33]{1,0:T(8,128)S(1)} %collective-permute-done.24.refs_0_, f32[208,33]{1,0:T(8,128)S(1)} %collective-permute-done.25.refs_1_), custom_call_target="tpu_custom_call" | custom-call | bytes 109832 | tf_op jit(solution)/shard_map/pallas_call | solution.py:280
  (53 shorter events, 10.6 us)
Async XLA Ops:
  0.6 15.5 %collective-permute-start = (bf16[128,2048]{1,0:T(8,128)(2,1)}, bf16[128,2048]{1,0:T(8,128)(2,1)S(1)}, u32[]{:S(2)}, u32[]{:S(2)}) collective-permute-start(bf16[128,2048]{1,0:T(8,128)(2,1)} %refs_4_.1), channel_id=1, source_target_pairs={{0,8},{8,16},{16,24},{24,28},{28,20},{20,12},{12,4},{4,0},{1,9},{9... | collective-permute-start | bytes 1572872 | tf_op jit(solution)/shard_map/ppermute | solution.py:316
  2.3 13.9 %collective-permute-start.1 = (bf16[128,2048]{1,0:T(8,128)(2,1)}, bf16[128,2048]{1,0:T(8,128)(2,1)S(1)}, u32[]{:S(2)}, u32[]{:S(2)}) collective-permute-start(bf16[128,2048]{1,0:T(8,128)(2,1)} %refs_4_.1), channel_id=1, source_target_pairs={{8,0},{16,8},{24,16},{28,24},{20,28},{12,20},{4,12},{0,4},{9,1},{1... | collective-permute-start | bytes 1572872 | tf_op jit(solution)/shard_map/ppermute | solution.py:316
  5.8 10.3 %all-to-all-start = ((bf16[4,2,56,128]{3,2,1,0:T(8,128)(2,1)}), bf16[4,2,56,128]{3,2,1,0:T(8,128)(2,1)S(1)}, u32[]{:S(2)}, u32[]{:S(2)}) async-start(bf16[4,2,56,128]{3,2,1,0:T(8,128)(2,1)} %shard_map.121), calls=%async_computation | async-start | bytes 229376 | tf_op jit(solution)/shard_map/all_to_all | solution.py:356
  9.2 6.9 %collective-permute-start.2 = (f32[56,33]{1,0:T(8,128)S(1)}, f32[56,33]{1,0:T(8,128)S(1)}, u32[]{:S(2)}, u32[]{:S(2)}) collective-permute-start(f32[56,33]{1,0:T(8,128)S(1)} %shard_map.120), channel_id=1, source_target_pairs={{0,0},{4,1},{8,2},{12,3},{16,4},{20,5},{24,6},{28,7},{1,8},{5,9},{... | collective-permute-start | bytes 22184 | tf_op jit(solution)/shard_map/ppermute | solution.py:351
  16.1 18.8 %collective-permute-start.3 = (bf16[128,2048]{1,0:T(8,128)(2,1)S(1)}, bf16[128,2048]{1,0:T(8,128)(2,1)S(1)}, u32[]{:S(2)}, u32[]{:S(2)}) collective-permute-start(bf16[128,2048]{1,0:T(8,128)(2,1)S(1)} %collective-permute-done.refs_1_.refs_5_), channel_id=1, source_target_pairs={{0,8},{8,16},{16,24},{24,28},{28,20},{20,12},{12,4},{4,0},{1,9},{9... | collective-permute-start | bytes 1572872 | tf_op jit(solution)/shard_map/ppermute | solution.py:316
  17.4 17.5 %collective-permute-start.4 = (bf16[128,2048]{1,0:T(8,128)(2,1)S(1)}, bf16[128,2048]{1,0:T(8,128)(2,1)S(1)}, u32[]{:S(2)}, u32[]{:S(2)}) collective-permute-start(bf16[128,2048]{1,0:T(8,128)(2,1)S(1)} %collective-permute-done.1.refs_2_.refs_6_), channel_id=1, source_target_pairs={{8,0},{16,8},{24,16},{28,24},{20,28},{12,20},{4,12},{0,4},{9,1},{1... | collective-permute-start | bytes 1572872 | tf_op jit(solution)/shard_map/ppermute | solution.py:316
  35.0 12.3 %collective-permute-start.5 = (bf16[128,2048]{1,0:T(8,128)(2,1)S(1)}, bf16[128,2048]{1,0:T(8,128)(2,1)S(1)}, u32[]{:S(2)}, u32[]{:S(2)}) collective-permute-start(bf16[128,2048]{1,0:T(8,128)(2,1)S(1)} %collective-permute-done.3.refs_3_.refs_7_), channel_id=1, source_target_pairs={{0,8},{8,16},{16,24},{24,28},{28,20},{20,12},{12,4},{4,0},{1,9},{9... | collective-permute-start | bytes 1572872 | tf_op jit(solution)/shard_map/ppermute | solution.py:316
  35.9 11.9 %collective-permute-start.6 = (bf16[128,2048]{1,0:T(8,128)(2,1)S(1)}, bf16[128,2048]{1,0:T(8,128)(2,1)S(1)}, u32[]{:S(2)}, u32[]{:S(2)}) collective-permute-start(bf16[128,2048]{1,0:T(8,128)(2,1)S(1)} %collective-permute-done.4.refs_4_.refs_8_), channel_id=1, source_target_pairs={{8,0},{16,8},{24,16},{28,24},{20,28},{12,20},{4,12},{0,4},{9,1},{1... | collective-permute-start | bytes 1572872 | tf_op jit(solution)/shard_map/ppermute | solution.py:316
  37.0 1.7 %copy-start = (bf16[208,3,2048]{2,0,1:T(8,128)(2,1)S(1)}, bf16[208,3,2048]{2,0,1:T(8,128)(2,1)}, u32[]{:S(2)}) copy-start(bf16[208,3,2048]{2,0,1:T(8,128)(2,1)} %param.10) | copy-start | bytes 7667716
  47.9 9.9 %collective-permute-start.13 = (bf16[64,2048]{1,0:T(8,128)(2,1)S(1)}, bf16[64,2048]{1,0:T(8,128)(2,1)S(1)}, u32[]{:S(2)}, u32[]{:S(2)}) collective-permute-start(bf16[64,2048]{1,0:T(8,128)(2,1)S(1)} %slice.6), channel_id=1, source_target_pairs={{0,8},{8,16},{16,24},{24,28},{28,20},{20,12},{12,4},{4,0},{1,9},{9... | collective-permute-start | bytes 786440 | tf_op jit(solution)/shard_map/ppermute | solution.py:316
  48.3 11.9 %collective-permute-start.14 = (bf16[64,2048]{1,0:T(8,128)(2,1)S(1)}, bf16[64,2048]{1,0:T(8,128)(2,1)S(1)}, u32[]{:S(2)}, u32[]{:S(2)}) collective-permute-start(bf16[64,2048]{1,0:T(8,128)(2,1)S(1)} %slice.7), channel_id=1, source_target_pairs={{8,0},{16,8},{24,16},{28,24},{20,28},{12,20},{4,12},{0,4},{9,1},{1... | collective-permute-start | bytes 786440 | tf_op jit(solution)/shard_map/ppermute | solution.py:316
  50.0 6.4 %collective-permute-start.7 = (bf16[3,56,640]{2,1,0:T(8,128)(2,1)S(1)}, bf16[3,56,640]{2,1,0:T(8,128)(2,1)S(1)}, u32[]{:S(2)}, u32[]{:S(2)}) collective-permute-start(bf16[3,56,640]{2,1,0:T(8,128)(2,1)S(1)} %get-tuple-element.56), channel_id=1, source_target_pairs={{0,1},{1,2},{2,3},{3,0},{4,5},{5,6},{6,7},{7,4},{8,9},{9,10},{10,1... | collective-permute-start | bytes 645128 | tf_op jit(solution)/shard_map/ppermute | solution.py:338
  50.0 13.1 %collective-permute-start.8 = (bf16[3,56,640]{2,1,0:T(8,128)(2,1)S(1)}, bf16[3,56,640]{2,1,0:T(8,128)(2,1)S(1)}, u32[]{:S(2)}, u32[]{:S(2)}) collective-permute-start(bf16[3,56,640]{2,1,0:T(8,128)(2,1)S(1)} %get-tuple-element.57), channel_id=1, source_target_pairs={{0,2},{1,3},{2,0},{3,1},{4,6},{5,7},{6,4},{7,5},{8,10},{9,11},{10,... | collective-permute-start | bytes 645128 | tf_op jit(solution)/shard_map/ppermute | solution.py:338
  53.1 12.5 %copy-start.1 = (bf16[1024,1024]{1,0:T(8,128)(2,1)S(1)}, bf16[1024,1024]{1,0:T(8,128)(2,1)}, u32[]{:S(2)}) copy-start(bf16[1024,1024]{1,0:T(8,128)(2,1)} %constant.15.clone.cos_ref.refs_16_) | copy-start | bytes 6291460
  53.1 12.5 %copy-start.2 = (bf16[1024,1024]{1,0:T(8,128)(2,1)S(1)}, bf16[1024,1024]{1,0:T(8,128)(2,1)}, u32[]{:S(2)}) copy-start(bf16[1024,1024]{1,0:T(8,128)(2,1)} %constant.16.clone.sin_ref.refs_17_) | copy-start | bytes 6291460
  53.1 12.5 %copy-start.6 = (f32[2,1024]{1,0:T(2,128)S(1)}, f32[2,1024]{1,0:T(2,128)}, u32[]{:S(2)}) copy-start(f32[2,1024]{1,0:T(2,128)} %constant.17.clone.twist_ref.refs_18_) | copy-start | bytes 24580
  53.1 10.2 %collective-permute-start.9 = (bf16[3,56,640]{2,1,0:T(8,128)(2,1)S(1)}, bf16[3,56,640]{2,1,0:T(8,128)(2,1)S(1)}, u32[]{:S(2)}, u32[]{:S(2)}) collective-permute-start(bf16[3,56,640]{2,1,0:T(8,128)(2,1)S(1)} %get-tuple-element.58), channel_id=1, source_target_pairs={{0,3},{1,0},{2,1},{3,2},{4,7},{5,4},{6,5},{7,6},{8,11},{9,8},{10,9... | collective-permute-start | bytes 645128 | tf_op jit(solution)/shard_map/ppermute | solution.py:338
  56.4 8.2 %collective-permute-start.10 = (bf16[3,56,256]{2,1,0:T(8,128)(2,1)S(1)}, bf16[3,56,256]{2,1,0:T(8,128)(2,1)S(1)}, u32[]{:S(2)}, u32[]{:S(2)}) collective-permute-start(bf16[3,56,256]{2,1,0:T(8,128)(2,1)S(1)} %get-tuple-element.64), channel_id=1, source_target_pairs={{0,1},{1,2},{2,3},{3,0},{4,5},{5,6},{6,7},{7,4},{8,9},{9,10},{10,1... | collective-permute-start | bytes 258056 | tf_op jit(solution)/shard_map/ppermute | solution.py:338
  57.8 9.4 %collective-permute-start.11 = (bf16[3,56,256]{2,1,0:T(8,128)(2,1)S(1)}, bf16[3,56,256]{2,1,0:T(8,128)(2,1)S(1)}, u32[]{:S(2)}, u32[]{:S(2)}) collective-permute-start(bf16[3,56,256]{2,1,0:T(8,128)(2,1)S(1)} %get-tuple-element.65), channel_id=1, source_target_pairs={{0,2},{1,3},{2,0},{3,1},{4,6},{5,7},{6,4},{7,5},{8,10},{9,11},{10,... | collective-permute-start | bytes 258056 | tf_op jit(solution)/shard_map/ppermute | solution.py:338
  60.2 7.0 %collective-permute-start.12 = (bf16[3,56,256]{2,1,0:T(8,128)(2,1)S(1)}, bf16[3,56,256]{2,1,0:T(8,128)(2,1)S(1)}, u32[]{:S(2)}, u32[]{:S(2)}) collective-permute-start(bf16[3,56,256]{2,1,0:T(8,128)(2,1)S(1)} %get-tuple-element.66), channel_id=1, source_target_pairs={{0,3},{1,0},{2,1},{3,2},{4,7},{5,4},{6,5},{7,6},{8,11},{9,8},{10,9... | collective-permute-start | bytes 258056 | tf_op jit(solution)/shard_map/ppermute | solution.py:338
  63.1 4.1 %collective-permute-start.15 = (bf16[3,56,128]{2,1,0:T(8,128)(2,1)S(1)}, bf16[3,56,128]{2,1,0:T(8,128)(2,1)S(1)}, u32[]{:S(2)}, u32[]{:S(2)}) collective-permute-start(bf16[3,56,128]{2,1,0:T(8,128)(2,1)S(1)} %get-tuple-element.70), channel_id=1, source_target_pairs={{0,1},{1,2},{2,3},{3,0},{4,5},{5,6},{6,7},{7,4},{8,9},{9,10},{10,1... | collective-permute-start | bytes 129032 | tf_op jit(solution)/shard_map/ppermute | solution.py:338
  63.4 4.5 %collective-permute-start.16 = (bf16[3,56,128]{2,1,0:T(8,128)(2,1)S(1)}, bf16[3,56,128]{2,1,0:T(8,128)(2,1)S(1)}, u32[]{:S(2)}, u32[]{:S(2)}) collective-permute-start(bf16[3,56,128]{2,1,0:T(8,128)(2,1)S(1)} %get-tuple-element.71), channel_id=1, source_target_pairs={{0,2},{1,3},{2,0},{3,1},{4,6},{5,7},{6,4},{7,5},{8,10},{9,11},{10,... | collective-permute-start | bytes 129032 | tf_op jit(solution)/shard_map/ppermute | solution.py:338
  64.6 3.8 %collective-permute-start.17 = (bf16[3,56,128]{2,1,0:T(8,128)(2,1)S(1)}, bf16[3,56,128]{2,1,0:T(8,128)(2,1)S(1)}, u32[]{:S(2)}, u32[]{:S(2)}) collective-permute-start(bf16[3,56,128]{2,1,0:T(8,128)(2,1)S(1)} %get-tuple-element.72), channel_id=1, source_target_pairs={{0,3},{1,0},{2,1},{3,2},{4,7},{5,4},{6,5},{7,6},{8,11},{9,8},{10,9... | collective-permute-start | bytes 129032 | tf_op jit(solution)/shard_map/ppermute | solution.py:338
  74.0 19.9 %copy-start.4 = (bf16[128,2048]{1,0:T(8,128)(2,1)S(1)}, bf16[128,2048]{1,0:T(8,128)(2,1)}, u32[]{:S(2)}) copy-start(bf16[128,2048]{1,0:T(8,128)(2,1)} %refs_4_.1) | copy-start | bytes 1572868
  74.0 11.4 %collective-permute-start.18 = (bf16[3,56,1024]{2,1,0:T(8,128)(2,1)S(1)}, bf16[3,56,1024]{2,1,0:T(8,128)(2,1)S(1)}, u32[]{:S(2)}, u32[]{:S(2)}) collective-permute-start(bf16[3,56,1024]{2,1,0:T(8,128)(2,1)S(1)} %get-tuple-element.77.refs_0_), channel_id=1, source_target_pairs={{0,2},{1,3},{2,0},{3,1},{4,6},{5,7},{6,4},{7,5},{8,10},{9,11},{10,... | collective-permute-start | bytes 1032200 | tf_op jit(solution)/shard_map/ppermute | solution.py:410
  78.1 7.3 %collective-permute-start.19 = (f32[56,33]{1,0:T(8,128)S(1)}, f32[56,33]{1,0:T(8,128)S(1)}, u32[]{:S(2)}, u32[]{:S(2)}) collective-permute-start(f32[56,33]{1,0:T(8,128)S(1)} %shard_map.127.refs_0_), channel_id=1, source_target_pairs={{0,2},{1,3},{2,0},{3,1},{4,6},{5,7},{6,4},{7,5},{8,10},{9,11},{10,... | collective-permute-start | bytes 22184 | tf_op jit(solution)/shard_map/ppermute | solution.py:410
  78.2 15.6 %collective-permute-start.20 = (bf16[3,56,1024]{2,1,0:T(8,128)(2,1)S(1)}, bf16[3,56,1024]{2,1,0:T(8,128)(2,1)S(1)}, u32[]{:S(2)}, u32[]{:S(2)}) collective-permute-start(bf16[3,56,1024]{2,1,0:T(8,128)(2,1)S(1)} %get-tuple-element.77.refs_0_), channel_id=1, source_target_pairs={{0,1},{1,0},{2,3},{3,2},{4,5},{5,4},{6,7},{7,6},{8,9},{9,8},{10,11... | collective-permute-start | bytes 1032200 | tf_op jit(solution)/shard_map/ppermute | solution.py:415
  85.4 8.4 %collective-permute-start.21 = (bf16[3,56,1024]{2,1,0:T(8,128)(2,1)S(1)}, bf16[3,56,1024]{2,1,0:T(8,128)(2,1)S(1)}, u32[]{:S(2)}, u32[]{:S(2)}) collective-permute-start(bf16[3,56,1024]{2,1,0:T(8,128)(2,1)S(1)} %collective-permute-done.18.refs_1_), channel_id=1, source_target_pairs={{0,1},{1,0},{2,3},{3,2},{4,5},{5,4},{6,7},{7,6},{8,9},{9,8},{10,11... | collective-permute-start | bytes 1032200 | tf_op jit(solution)/shard_map/ppermute | solution.py:424
  85.4 1.7 %collective-permute-start.22 = (f32[56,33]{1,0:T(8,128)S(1)}, f32[56,33]{1,0:T(8,128)S(1)}, u32[]{:S(2)}, u32[]{:S(2)}) collective-permute-start(f32[56,33]{1,0:T(8,128)S(1)} %shard_map.127.refs_0_), channel_id=1, source_target_pairs={{0,1},{1,0},{2,3},{3,2},{4,5},{5,4},{6,7},{7,6},{8,9},{9,8},{10,11... | collective-permute-start | bytes 22184 | tf_op jit(solution)/shard_map/ppermute | solution.py:425
  85.9 1.2 %collective-permute-start.23 = (f32[56,33]{1,0:T(8,128)S(1)}, f32[56,33]{1,0:T(8,128)S(1)}, u32[]{:S(2)}, u32[]{:S(2)}) collective-permute-start(f32[56,33]{1,0:T(8,128)S(1)} %collective-permute-done.19.refs_1_), channel_id=1, source_target_pairs={{0,1},{1,0},{2,3},{3,2},{4,5},{5,4},{6,7},{7,6},{8,9},{9,8},{10,11... | collective-permute-start | bytes 22184 | tf_op jit(solution)/shard_map/ppermute | solution.py:425
  87.7 13.2 %collective-permute-start.24 = (f32[208,33]{1,0:T(8,128)S(1)}, f32[208,33]{1,0:T(8,128)S(1)}, u32[]{:S(2)}, u32[]{:S(2)}) collective-permute-start(f32[208,33]{1,0:T(8,128)S(1)} %shard_map.129), channel_id=1, source_target_pairs={{0,0},{8,1},{16,2},{24,3},{4,4},{12,5},{20,6},{28,7},{1,8},{9,9},{... | collective-permute-start | bytes 82376 | tf_op jit(solution)/shard_map/ppermute | solution.py:438
  91.3 11.9 %collective-permute-start.25 = (f32[208,33]{1,0:T(8,128)S(1)}, f32[208,33]{1,0:T(8,128)S(1)}, u32[]{:S(2)}, u32[]{:S(2)}) collective-permute-start(f32[208,33]{1,0:T(8,128)S(1)} %shard_map.129), channel_id=1, source_target_pairs={{4,0},{12,1},{20,2},{28,3},{0,4},{8,5},{16,6},{24,7},{5,8},{13,9},... | collective-permute-start | bytes 82376 | tf_op jit(solution)/shard_map/ppermute | solution.py:438
  (2 other events, 1.9 us)

commit v7 on v6

--- a/solution.py
+++ b/solution.py
@@ -115,7 +115,7 @@
         )
     rows = weight_ref.shape[1]
     for step, out_ref in enumerate(out_refs):
-        start = part_start((place_ref[1] + step) % len(out_refs), part, rows)
+        start = part_start(place_ref[1] ^ step, part, rows)
         out_ref[...] = sums_ref[:, pl.ds(start, part), :].astype(out_ref.dtype)
 
 
@@ -198,6 +198,7 @@
 def pole_kernel(poles_ref, tgc_ref, tgs_ref, cos_ref, sin_ref, skip_ref, out_ref, *, order):
     rows, tokens = tgc_ref.shape
     taps_grad = wide_dot(tgc_ref[...], cos_ref[...]) + wide_dot(tgs_ref[...], sin_ref[...])
+    out_ref[...] = jnp.zeros_like(out_ref)
     steps = lax.broadcasted_iota(jnp.int32, (rows, tokens), 1).astype(F32)
     for pole in range(order):
         residue = poles_ref[:, pole : pole + 1]
@@ -211,8 +212,7 @@
 
 def share_start(own, share, shares, part, rows):
     core, step = share // (shares // 2), 2 * (share % (shares // 2))
-    owner = own + core * (1 - 2 * (own % 2))
-    return part_start((owner - step + shares) % shares, part, rows)
+    return part_start(own ^ core ^ step, part, rows)
 
 
 def weight_kernel(place_ref, *refs, shares):
@@ -241,26 +241,25 @@
             out_ref[gate] = dot(rows_ref[gate], features_ref[...])
 
 
+def split_kernel(place_ref, held_ref, *out_refs):
+    for step, out_ref in enumerate(out_refs):
+        out_ref[...] = held_ref[place_ref[1] ^ step]
+
+
 def assemble_kernel(place_ref, *refs, rows, order):
-    *block_refs, residue_ref, rate_ref, skip_ref, sums_ref = refs
-    count = len(block_refs)
+    *piece_refs, residue_ref, rate_ref, skip_ref, sums_ref = refs
+    blocks, part, _ = piece_refs[0].shape
     sums_ref[...] = jnp.zeros_like(sums_ref)
-    width = block_refs[0].shape[1]
-    for turn, block_ref in enumerate(block_refs):
-        block = (place_ref[0] + turn) % count
-        sums_ref[pl.ds(pl.multiple_of(block * rows, 8), rows), :width] = block_ref[...]
+    for step, piece_ref in enumerate(piece_refs):
+        start = part_start(place_ref[1] ^ step, part, rows)
+        for block in range(blocks):
+            row = pl.multiple_of(block * rows + start, 8)
+            sums_ref[pl.ds(row, part), :] = piece_ref[block]
     turned = sums_ref[...].T
     channels = residue_ref.shape[1]
     residue_ref[...] = turned[:order, :channels]
     rate_ref[...] = turned[order : 2 * order, :channels]
     skip_ref[...] = turned[2 * order : 2 * order + 1, :channels]
-
-
-def gather_kernel(place_ref, *refs):
-    *held_refs, out_ref = refs
-    for share, held_ref in enumerate(held_refs):
-        start = share_start(place_ref[1], share, len(held_refs), held_ref.shape[0], out_ref.shape[0])
-        out_ref[pl.ds(start, held_ref.shape[0]), :] = held_ref[...]
 
 
 def call(kernel, outs, flops, transcendentals, *operands, scratch=(), indexed=False, late=()):
@@ -335,7 +334,7 @@
 
     def to_owners(sums):
         return [sums[0]] + [
-            lax.ppermute(sums[d], "ch", [(h, (h + d) % n_ch) for h in range(n_ch)])
+            lax.ppermute(sums[d], "ch", [(h, h ^ d) for h in range(n_ch)])
             for d in range(1, n_ch)
         ]
 
@@ -366,8 +365,8 @@
         if step == 2:
             pair, upper = lax.optimization_barrier((pair, upper))
         else:
-            pair, sums[0] = lax.optimization_barrier((pair, sums[0]))
-            partials[-n_ch] = sums[0]
+            pair, near = lax.optimization_barrier((pair, partials[1 - n_ch]))
+            partials[1 - n_ch] = near
         pieces += pair
         waiting += pair
         if step < n_seq // 2 - 1:
@@ -407,35 +406,31 @@
 
     def chips(array):
         return [
-            lax.ppermute(array, "ch", [(h, (h + d) % n_ch) for h in range(n_ch)])
+            lax.ppermute(array, "ch", [(h, h ^ d) for h in range(n_ch)])
             for d in range(2, n_ch, 2)
         ]
 
     across = chips(grads)
     swapped = lax.ppermute(grads, "ch", swap)
+    lanes = round_up(2 * order + 1, 128)
     (pole_sums,) = call(
         functools.partial(pole_kernel, order=order),
-        (jax.ShapeDtypeStruct((part, 2 * order + 1), F32),),
+        (jax.ShapeDtypeStruct((part, lanes), F32),),
         8 * square, part * tokens * order, poles, tgc, tgs, cos_table, sin_table, skip_sum,
     )
 
-    sums = [pole_sums] + chips(pole_sums)
-    across, sums = lax.optimization_barrier((across, sums))
+    every = jnp.broadcast_to(pole_sums[None], (n_seq,) + pole_sums.shape)
+    every = lax.all_to_all(every, "seq", split_axis=0, concat_axis=0, tiled=True)
+    every = every.reshape(n_ch, n_seq // n_ch, part, pole_sums.shape[1])
+    sums = call(
+        split_kernel, [jax.ShapeDtypeStruct(every.shape[1:], F32)] * n_ch, 0, 0, place, every,
+        indexed=True,
+    )
+    across, sums = lax.optimization_barrier((across, list(sums)))
     held = [grads] + across + [swapped] + [lax.ppermute(a, "ch", swap) for a in across]
-    sums += [lax.ppermute(a, "ch", swap) for a in sums]
-    (block_sums,) = call(
-        gather_kernel, [jax.ShapeDtypeStruct((rows, 2 * order + 1), F32)], 0, 0, place, *sums,
-        indexed=True,
-    )
-    turns = n_seq // n_ch
-    blocks = []
-    for turn in range(turns):
-        route = [
-            ((h * turns + (s + turn) % turns) * n_ch + s // turns, s * n_ch + h)
-            for s in range(n_seq)
-            for h in range(n_ch)
-        ]
-        blocks.append(lax.ppermute(block_sums, ("seq", "ch"), route))
+    blocks = [sums[0]] + [
+        lax.ppermute(sums[d], "ch", [(h, h ^ d) for h in range(n_ch)]) for d in range(1, n_ch)
+    ]
 
     tile = min(512, width)
     weight_grad = pl.pallas_call(
@@ -468,7 +463,7 @@
     residue_grad, rate_grad, skip_grad = call(
         functools.partial(assemble_kernel, rows=rows, order=order),
         [by_pole, by_pole, jax.ShapeDtypeStruct((1, channels), F32)], 0, 0, place, *blocks,
-        scratch=[pltpu.VMEM((round_up(channels, 128), 128), F32)], indexed=True,
+        scratch=[pltpu.VMEM((round_up(channels, 128), lanes), F32)], indexed=True,
     )
     return (weight_grad, residue_grad.T, rate_grad.T, skip_grad.reshape(channels))
 

time: 105 us -> 106 us (level)
  the two profiles are of different devices: /device:TPU:4 before, /device:TPU:1 now
where the time goes in v7:
time: 106 us; the launch traced here: 105 us
  starting transfers between devices  33.4 us (32%)
  Pallas kernels  25.4 us (24%)
  waiting for transfers between devices  19.8 us (19%)
  blocking collectives  16.8 us (16%)
  local copies, waits for them, and re-layouts  7.59 us (7%)
    pallas_call x10, Pallas kernels, call(): pl.pallas_call(kernel, out_shape=outs, in_specs=specs, out_specs=[whole]...  19.2 us
    all_to_all x1, blocking collectives, local(): lax.all_to_all(upper, 'seq', split_axis=0, concat_axis=0, tiled=True)  16.8 us
    ppermute x9, starting transfers between devices, to_owners(): lax.ppermute(sums[d], 'ch', [(h, h ^ d) for h in range(n_ch)])  9.6 us
    unnamed x26, local copies, waits for them, and re-layouts  6.74 us
    ppermute x9, waiting for transfers between devices, to_owners(): lax.ppermute(sums[d], 'ch', [(h, h ^ d) for h in range(n_ch)])  6.5 us
    all_to_all x1, waiting for transfers between devices, local(): lax.all_to_all(every, 'seq', split_axis=0, concat_axis=0, tiled=True)  6.5 us
    pallas_call x1, Pallas kernels, local(): pl.pallas_call(functools.partial(weight_kernel, shares=n_ch), out_shape=j...  6.24 us
    ppermute x4, starting transfers between devices, send_on(): lax.ppermute(pair[1], 'seq', behind)  5.83 us
  transfers between devices with their start and end apart: 26, of which 10 were waited for; matrix products, arithmetic and copies ran while one was open for 1% of the time, Pallas kernels for 16%

profile of v7, /device:TPU:1, one launch (start us, length us, event | category | flops | bytes accessed | tf_op | source)
XLA Modules:
  0.0 104.8 jit_solution(1704614946776080528)
XLA Ops:
  0.6 2.1 %collective-permute-start.1 = (bf16[128,2048]{1,0:T(8,128)(2,1)}, bf16[128,2048]{1,0:T(8,128)(2,1)S(1)}, u32[]{:S(2)}, u32[]{:S(2)}) collective-permute-start(bf16[128,2048]{1,0:T(8,128)(2,1)} %refs_4_.1), channel_id=1, source_target_pairs={{8,0},{16,8},{24,16},{28,24},{20,28},{12,20},{4,12},{0,4},{9,1},{1... | collective-permute-start | bytes 1572872 | tf_op jit(solution)/shard_map/ppermute | solution.py:315
  6.0 4.2 %all-to-all-start = ((bf16[4,2,56,128]{3,2,1,0:T(8,128)(2,1)}), bf16[4,2,56,128]{3,2,1,0:T(8,128)(2,1)S(1)}, u32[]{:S(2)}, u32[]{:S(2)}) async-start(bf16[4,2,56,128]{3,2,1,0:T(8,128)(2,1)} %shard_map.121), calls=%async_computation | async-start | bytes 229376 | tf_op jit(solution)/shard_map/all_to_all | solution.py:355
  10.3 3.5 %collective-permute-start.2 = (f32[56,33]{1,0:T(8,128)S(1)}, f32[56,33]{1,0:T(8,128)S(1)}, u32[]{:S(2)}, u32[]{:S(2)}) collective-permute-start(f32[56,33]{1,0:T(8,128)S(1)} %shard_map.120), channel_id=1, source_target_pairs={{0,0},{4,1},{8,2},{12,3},{16,4},{20,5},{24,6},{28,7},{1,8},{5,9},{... | collective-permute-start | bytes 22184 | tf_op jit(solution)/shard_map/ppermute | solution.py:350
  13.8 3.1 %collective-permute-done.2.poles_ref.refs_13_ = f32[56,33]{1,0:T(8,128)S(1)} collective-permute-done((f32[56,33]{1,0:T(8,128)S(1)}, f32[56,33]{1,0:T(8,128)S(1)}, u32[]{:S(2)}, u32[]{:S(2)}) %collective-permute-start.2) | collective-permute-done | bytes 7424 | tf_op jit(solution)/shard_map/ppermute | solution.py:350
  17.9 2.0 %collective-permute-start.4 = (bf16[128,2048]{1,0:T(8,128)(2,1)S(1)}, bf16[128,2048]{1,0:T(8,128)(2,1)S(1)}, u32[]{:S(2)}, u32[]{:S(2)}) collective-permute-start(bf16[128,2048]{1,0:T(8,128)(2,1)S(1)} %collective-permute-done.1.refs_2_.refs_6_), channel_id=1, source_target_pairs={{8,0},{16,8},{24,16},{28,24},{20,28},{12,20},{4,12},{0,4},{9,1},{1... | collective-permute-start | bytes 1572872 | tf_op jit(solution)/shard_map/ppermute | solution.py:315
  19.9 16.8 %all_to_all.15.refs_12_ = bf16[8,56,128]{2,1,0:T(8,128)(2,1)S(1)} all-to-all(bf16[8,56,128]{2,1,0:T(8,128)(2,1)S(1)} %bitcast.15), channel_id=1, replica_groups=mesh['seq'=8,'ch'=4] {'seq'}, dimensions={0} | all-to-all | bytes 229376 | tf_op jit(solution)/shard_map/all_to_all | solution.py:358
  38.3 1.7 %copy-done = bf16[208,3,2048]{2,0,1:T(8,128)(2,1)S(1)} copy-done((bf16[208,3,2048]{2,0,1:T(8,128)(2,1)S(1)}, bf16[208,3,2048]{2,0,1:T(8,128)(2,1)}, u32[]{:S(2)}) %copy-start) | copy-done | bytes 2555928
  40.0 1.0 copy-done.3
  41.0 3.5 %shard_map.122 = (f32[3,56,640]{2,1,0:T(8,128)S(1)}, bf16[3,56,640]{2,1,0:T(8,128)(2,1)S(1)}, bf16[3,56,640]{2,1,0:T(8,128)(2,1)S(1)}, bf16[3,56,640]{2,1,0:T(8,128)(2,1)S(1)}) custom-call(s32[2]{0:T(128)S(1)} %pad_add_fusion.place_ref, bf16[3,208,2048]{2,1,0:T(8,128)(2,1)S(1)} %bitcast.10, bf16[128,2048]{1,0:T(8,128)(2,1)S(1)} %copy-done.3, ...), custom_call_target="tpu_custom_call" | custom-call | flops 1635778560 | bytes 6252552 | tf_op jit(solution)/shard_map/pallas_call | solution.py:279
  44.5 2.0 %collective-permute-start.7 = (bf16[3,56,640]{2,1,0:T(8,128)(2,1)S(1)}, bf16[3,56,640]{2,1,0:T(8,128)(2,1)S(1)}, u32[]{:S(2)}, u32[]{:S(2)}) collective-permute-start(bf16[3,56,640]{2,1,0:T(8,128)(2,1)S(1)} %get-tuple-element.63), channel_id=1, source_target_pairs={{0,1},{1,0},{2,3},{3,2},{4,5},{5,4},{6,7},{7,6},{8,9},{9,8},{10,11... | collective-permute-start | bytes 645128 | tf_op jit(solution)/shard_map/ppermute | solution.py:337
  46.5 1.1 %collective-permute-done.7.refs_1_ = bf16[3,56,640]{2,1,0:T(8,128)(2,1)S(1)} collective-permute-done((bf16[3,56,640]{2,1,0:T(8,128)(2,1)S(1)}, bf16[3,56,640]{2,1,0:T(8,128)(2,1)S(1)}, u32[]{:S(2)}, u32[]{:S(2)}) %collective-permute-start.7) | collective-permute-done | bytes 215072 | tf_op jit(solution)/shard_map/ppermute | solution.py:337
  47.6 1.2 %collective-permute-done.5.refs_0_.refs_9_ = bf16[128,2048]{1,0:T(8,128)(2,1)S(1)} collective-permute-done((bf16[128,2048]{1,0:T(8,128)(2,1)S(1)}, bf16[128,2048]{1,0:T(8,128)(2,1)S(1)}, u32[]{:S(2)}, u32[]{:S(2)}) %collective-permute-start.5) | collective-permute-done | bytes 524320 | tf_op jit(solution)/shard_map/ppermute | solution.py:315
  50.2 1.1 %collective-permute-start.14 = (bf16[64,2048]{1,0:T(8,128)(2,1)S(1)}, bf16[64,2048]{1,0:T(8,128)(2,1)S(1)}, u32[]{:S(2)}, u32[]{:S(2)}) collective-permute-start(bf16[64,2048]{1,0:T(8,128)(2,1)S(1)} %slice.7), channel_id=1, source_target_pairs={{8,0},{16,8},{24,16},{28,24},{20,28},{12,20},{4,12},{0,4},{9,1},{1... | collective-permute-start | bytes 786440 | tf_op jit(solution)/shard_map/ppermute | solution.py:315
  51.3 4.5 %collective-permute-start.9 = (bf16[3,56,640]{2,1,0:T(8,128)(2,1)S(1)}, bf16[3,56,640]{2,1,0:T(8,128)(2,1)S(1)}, u32[]{:S(2)}, u32[]{:S(2)}) collective-permute-start(bf16[3,56,640]{2,1,0:T(8,128)(2,1)S(1)} %get-tuple-element.66), channel_id=1, source_target_pairs={{0,3},{1,2},{2,1},{3,0},{4,7},{5,6},{6,5},{7,4},{8,11},{9,10},{10,... | collective-permute-start | bytes 645128 | tf_op jit(solution)/shard_map/ppermute | solution.py:337
  55.8 1.8 %shard_map.123 = (f32[3,56,256]{2,1,0:T(8,128)S(1)}, bf16[3,56,256]{2,1,0:T(8,128)(2,1)S(1)}, bf16[3,56,256]{2,1,0:T(8,128)(2,1)S(1)}, bf16[3,56,256]{2,1,0:T(8,128)(2,1)S(1)}) custom-call(s32[2]{0:T(128)S(1)} %pad_add_fusion.place_ref, bf16[3,208,2048]{2,1,0:T(8,128)(2,1)S(1)} %bitcast.11, bf16[128,2048]{1,0:T(8,128)(2,1)S(1)} %collective-permute-done.5.refs_0_.refs_9_, ...), custom_call_target="tpu_custom_call" | custom-call | flops 654311424 | bytes 4034568 | tf_op jit(solution)/shard_map/pallas_call | solution.py:279
  57.8 2.4 %collective-permute-start.12 = (bf16[3,56,256]{2,1,0:T(8,128)(2,1)S(1)}, bf16[3,56,256]{2,1,0:T(8,128)(2,1)S(1)}, u32[]{:S(2)}, u32[]{:S(2)}) collective-permute-start(bf16[3,56,256]{2,1,0:T(8,128)(2,1)S(1)} %get-tuple-element.74), channel_id=1, source_target_pairs={{0,3},{1,2},{2,1},{3,0},{4,7},{5,6},{6,5},{7,4},{8,11},{9,10},{10,... | collective-permute-start | bytes 258056 | tf_op jit(solution)/shard_map/ppermute | solution.py:337
  60.2 1.5 %shard_map.124 = (f32[3,56,128]{2,1,0:T(8,128)S(1)}, bf16[3,56,128]{2,1,0:T(8,128)(2,1)S(1)}, bf16[3,56,128]{2,1,0:T(8,128)(2,1)S(1)}, bf16[3,56,128]{2,1,0:T(8,128)(2,1)S(1)}) custom-call(s32[2]{0:T(128)S(1)} %pad_add_fusion.place_ref, bf16[3,208,2048]{2,1,0:T(8,128)(2,1)S(1)} %bitcast.12, bf16[64,2048]{1,0:T(8,128)(2,1)S(1)} %collective-permute-done.13.refs_0_.refs_11_, ...), custom_call_target="tpu_custom_call" | custom-call | flops 327155712 | bytes 3295240 | tf_op jit(solution)/shard_map/pallas_call | solution.py:279
  62.2 3.0 %collective-permute-done.9.refs_3_ = bf16[3,56,640]{2,1,0:T(8,128)(2,1)S(1)} collective-permute-done((bf16[3,56,640]{2,1,0:T(8,128)(2,1)S(1)}, bf16[3,56,640]{2,1,0:T(8,128)(2,1)S(1)}, u32[]{:S(2)}, u32[]{:S(2)}) %collective-permute-start.9) | collective-permute-done | bytes 215072 | tf_op jit(solution)/shard_map/ppermute | solution.py:337
  65.3 1.6 %shard_map.125 = (f32[56,1024]{1,0:T(8,128)S(1)}, f32[56,1024]{1,0:T(8,128)S(1)}) custom-call(f32[56,33]{1,0:T(8,128)S(1)} %collective-permute-done.2.poles_ref.refs_13_, bf16[1024,1024]{1,0:T(8,128)(2,1)S(1)} %copy-done.2, bf16[1024,1024]{1,0:T(8,128)(2,1)S(1)} %copy-done.1, f32[2,1024]{1,0:T(2,128)S(1)} %copy-done.12), custom_call_target="tpu_custom_call" | custom-call | flops 469762048 | bytes 4668640 | tf_op jit(solution)/shard_map/pallas_call | solution.py:279
  67.1 1.0 collective-permute-done.16.refs_10_
  68.2 1.1 %collective-permute-done.17.refs_11_ = bf16[3,56,128]{2,1,0:T(8,128)(2,1)S(1)} collective-permute-done((bf16[3,56,128]{2,1,0:T(8,128)(2,1)S(1)}, bf16[3,56,128]{2,1,0:T(8,128)(2,1)S(1)}, u32[]{:S(2)}, u32[]{:S(2)}) %collective-permute-start.17) | collective-permute-done | bytes 43040 | tf_op jit(solution)/shard_map/ppermute | solution.py:337
  69.3 5.7 %shard_map.126 = (bf16[3,56,1024]{2,1,0:T(8,128)(2,1)S(1)}, f32[56,1024]{1,0:T(8,128)S(1)}, f32[56,1024]{1,0:T(8,128)S(1)}, f32[56,1]{1,0:T(8,128)S(1)}) custom-call(s32[2]{0:T(128)S(1)} %pad_add_fusion.place_ref, f32[3,56,640]{2,1,0:T(8,128)S(1)} %get-tuple-element.62.refs_0_, bf16[3,56,640]{2,1,0:T(8,128)(2,1)S(1)} %collective-permute-done.7.refs_1_, ...), custom_call_target="tpu_custom_call" | custom-call | flops 1879048192 | bytes 7306696 | tf_op jit(solution)/shard_map/pallas_call | solution.py:279
  75.0 2.1 %shard_map.127 = f32[56,128]{1,0:T(8,128)S(1)} custom-call(f32[56,33]{1,0:T(8,128)S(1)} %collective-permute-done.2.poles_ref.refs_13_, f32[56,1024]{1,0:T(8,128)S(1)} %get-tuple-element.86.tgc_ref, f32[56,1024]{1,0:T(8,128)S(1)} %get-tuple-element.87.tgs_ref, bf16[1024,1024]{1,0:T(8,128)(2,1)S(1)} %copy-done.2, bf16[1024,1024]{1,0:T(8,128)(2,1)S(1)} %copy-done.1, ...), custom_call_target="tpu_custom_call" | custom-call | flops 469762048 | bytes 4689344 | tf_op jit(solution)/shard_map/pallas_call | solution.py:279
  77.8 3.4 %all-to-all-start.2 = ((f32[8,56,128]{2,1,0:T(8,128)}), f32[8,56,128]{2,1,0:T(8,128)S(1)}, u32[]{:S(2)}, u32[]{:S(2)}) async-start(f32[8,56,128]{2,1,0:T(8,128)} %broadcast_in_dim.10), calls=%async_computation.2 | async-start | bytes 458752 | tf_op jit(solution)/shard_map/all_to_all | solution.py:423
  82.2 6.5 %all-to-all-done.2 = f32[8,56,128]{2,1,0:T(8,128)S(1)} async-done(((f32[8,56,128]{2,1,0:T(8,128)}), f32[8,56,128]{2,1,0:T(8,128)S(1)}, u32[]{:S(2)}, u32[]{:S(2)}) %all-to-all-start.2) | async-done | bytes 229408 | tf_op jit(solution)/shard_map/all_to_all | solution.py:423
  89.2 1.6 %collective-permute-done.18.refs_1_ = bf16[3,56,1024]{2,1,0:T(8,128)(2,1)} collective-permute-done((bf16[3,56,1024]{2,1,0:T(8,128)(2,1)}, bf16[3,56,1024]{2,1,0:T(8,128)(2,1)}, u32[]{:S(2)}, u32[]{:S(2)}) %collective-permute-start.18) | collective-permute-done | bytes 344096 | tf_op jit(solution)/shard_map/ppermute | solution.py:409
  90.8 1.2 %collective-permute-start.20 = (bf16[3,56,1024]{2,1,0:T(8,128)(2,1)}, bf16[3,56,1024]{2,1,0:T(8,128)(2,1)S(1)}, u32[]{:S(2)}, u32[]{:S(2)}) collective-permute-start(bf16[3,56,1024]{2,1,0:T(8,128)(2,1)} %collective-permute-done.18.refs_1_), channel_id=1, source_target_pairs={{0,1},{1,0},{2,3},{3,2},{4,5},{5,4},{6,7},{7,6},{8,9},{9,8},{10,11... | collective-permute-start | bytes 1032200 | tf_op jit(solution)/shard_map/ppermute | solution.py:430
  93.0 1.1 %collective-permute-start.23 = (f32[2,56,128]{2,1,0:T(8,128)S(1)}, f32[2,56,128]{2,1,0:T(8,128)S(1)}, u32[]{:S(2)}, u32[]{:S(2)}) collective-permute-start(f32[2,56,128]{2,1,0:T(8,128)S(1)} %get-tuple-element.97), channel_id=1, source_target_pairs={{0,3},{1,2},{2,1},{3,0},{4,7},{5,6},{6,5},{7,4},{8,11},{9,10},{10,... | collective-permute-start | bytes 172040 | tf_op jit(solution)/shard_map/ppermute | solution.py:432
  94.2 1.0 copy-done.6
  95.2 1.0 copy-done.8
  97.2 6.2 %shard_map.129 = f32[3,208,2048]{2,1,0:T(8,128)} custom-call(s32[2]{0:T(128)S(1)} %pad_add_fusion.place_ref, bf16[3,56,1024]{2,1,0:T(8,128)(2,1)S(1)} %copy-done.10, bf16[3,56,1024]{2,1,0:T(8,128)(2,1)} %collective-permute-done.18.refs_1_, bf16[3,56,1024]{2,1,0:T(8,128)(2,1)} %collective-permute-done.19.refs_2_, ...), custom_call_target="tpu_custom_call" | custom-call | flops 2617245696 | bytes 10584064 | tf_op jit(solution)/shard_map/pallas_call | solution.py:436
  103.5 1.3 %shard_map.130 = (f32[16,416]{1,0:T(8,128)}, f32[16,416]{1,0:T(8,128)}, f32[1,416]{1,0:T(1,128)}) custom-call(s32[2]{0:T(128)S(1)} %pad_add_fusion.place_ref, f32[2,56,128]{2,1,0:T(8,128)S(1)} %get-tuple-element.99.refs_0_, f32[2,56,128]{2,1,0:T(8,128)S(1)} %collective-permute-done.21.refs_1_, f32[2,56,128]{2,1,0:T(8,128)S(1)} %collective-permute-done.22.refs_2_, ...), custom_call_target="tpu_custom_call" | custom-call | bytes 284296 | tf_op jit(solution)/shard_map/pallas_call | solution.py:279
  (64 shorter events, 12.4 us)
Async XLA Ops:
  0.6 16.3 %collective-permute-start.1 = (bf16[128,2048]{1,0:T(8,128)(2,1)}, bf16[128,2048]{1,0:T(8,128)(2,1)S(1)}, u32[]{:S(2)}, u32[]{:S(2)}) collective-permute-start(bf16[128,2048]{1,0:T(8,128)(2,1)} %refs_4_.1), channel_id=1, source_target_pairs={{8,0},{16,8},{24,16},{28,24},{20,28},{12,20},{4,12},{0,4},{9,1},{1... | collective-permute-start | bytes 1572872 | tf_op jit(solution)/shard_map/ppermute | solution.py:315
  2.7 14.2 %collective-permute-start = (bf16[128,2048]{1,0:T(8,128)(2,1)}, bf16[128,2048]{1,0:T(8,128)(2,1)S(1)}, u32[]{:S(2)}, u32[]{:S(2)}) collective-permute-start(bf16[128,2048]{1,0:T(8,128)(2,1)} %refs_4_.1), channel_id=1, source_target_pairs={{0,8},{8,16},{16,24},{24,28},{28,20},{20,12},{12,4},{4,0},{1,9},{9... | collective-permute-start | bytes 1572872 | tf_op jit(solution)/shard_map/ppermute | solution.py:315
  6.0 10.9 %all-to-all-start = ((bf16[4,2,56,128]{3,2,1,0:T(8,128)(2,1)}), bf16[4,2,56,128]{3,2,1,0:T(8,128)(2,1)S(1)}, u32[]{:S(2)}, u32[]{:S(2)}) async-start(bf16[4,2,56,128]{3,2,1,0:T(8,128)(2,1)} %shard_map.121), calls=%async_computation | async-start | bytes 229376 | tf_op jit(solution)/shard_map/all_to_all | solution.py:355
  10.3 6.6 %collective-permute-start.2 = (f32[56,33]{1,0:T(8,128)S(1)}, f32[56,33]{1,0:T(8,128)S(1)}, u32[]{:S(2)}, u32[]{:S(2)}) collective-permute-start(f32[56,33]{1,0:T(8,128)S(1)} %shard_map.120), channel_id=1, source_target_pairs={{0,0},{4,1},{8,2},{12,3},{16,4},{20,5},{24,6},{28,7},{1,8},{5,9},{... | collective-permute-start | bytes 22184 | tf_op jit(solution)/shard_map/ppermute | solution.py:350
  16.9 19.8 %collective-permute-start.3 = (bf16[128,2048]{1,0:T(8,128)(2,1)S(1)}, bf16[128,2048]{1,0:T(8,128)(2,1)S(1)}, u32[]{:S(2)}, u32[]{:S(2)}) collective-permute-start(bf16[128,2048]{1,0:T(8,128)(2,1)S(1)} %collective-permute-done.refs_1_.refs_5_), channel_id=1, source_target_pairs={{0,8},{8,16},{16,24},{24,28},{28,20},{20,12},{12,4},{4,0},{1,9},{9... | collective-permute-start | bytes 1572872 | tf_op jit(solution)/shard_map/ppermute | solution.py:315
  17.9 18.8 %collective-permute-start.4 = (bf16[128,2048]{1,0:T(8,128)(2,1)S(1)}, bf16[128,2048]{1,0:T(8,128)(2,1)S(1)}, u32[]{:S(2)}, u32[]{:S(2)}) collective-permute-start(bf16[128,2048]{1,0:T(8,128)(2,1)S(1)} %collective-permute-done.1.refs_2_.refs_6_), channel_id=1, source_target_pairs={{8,0},{16,8},{24,16},{28,24},{20,28},{12,20},{4,12},{0,4},{9,1},{1... | collective-permute-start | bytes 1572872 | tf_op jit(solution)/shard_map/ppermute | solution.py:315
  36.7 7.8 %copy-start.5 = (bf16[128,2048]{1,0:T(8,128)(2,1)}, bf16[128,2048]{1,0:T(8,128)(2,1)S(1)}, u32[]{:S(2)}) copy-start(bf16[128,2048]{1,0:T(8,128)(2,1)S(1)} %collective-permute-done.3.refs_3_.refs_7_) | copy-start | bytes 1572868
  36.7 7.8 %copy-start.7 = (bf16[128,2048]{1,0:T(8,128)(2,1)}, bf16[128,2048]{1,0:T(8,128)(2,1)S(1)}, u32[]{:S(2)}) copy-start(bf16[128,2048]{1,0:T(8,128)(2,1)S(1)} %collective-permute-done.4.refs_4_.refs_8_) | copy-start | bytes 1572868
  36.7 12.1 %collective-permute-start.5 = (bf16[128,2048]{1,0:T(8,128)(2,1)S(1)}, bf16[128,2048]{1,0:T(8,128)(2,1)S(1)}, u32[]{:S(2)}, u32[]{:S(2)}) collective-permute-start(bf16[128,2048]{1,0:T(8,128)(2,1)S(1)} %collective-permute-done.3.refs_3_.refs_7_), channel_id=1, source_target_pairs={{0,8},{8,16},{16,24},{24,28},{28,20},{20,12},{12,4},{4,0},{1,9},{9... | collective-permute-start | bytes 1572872 | tf_op jit(solution)/shard_map/ppermute | solution.py:315
  37.7 12.1 %collective-permute-start.6 = (bf16[128,2048]{1,0:T(8,128)(2,1)S(1)}, bf16[128,2048]{1,0:T(8,128)(2,1)S(1)}, u32[]{:S(2)}, u32[]{:S(2)}) collective-permute-start(bf16[128,2048]{1,0:T(8,128)(2,1)S(1)} %collective-permute-done.4.refs_4_.refs_8_), channel_id=1, source_target_pairs={{8,0},{16,8},{24,16},{28,24},{20,28},{12,20},{4,12},{0,4},{9,1},{1... | collective-permute-start | bytes 1572872 | tf_op jit(solution)/shard_map/ppermute | solution.py:315
  44.5 3.1 %collective-permute-start.7 = (bf16[3,56,640]{2,1,0:T(8,128)(2,1)S(1)}, bf16[3,56,640]{2,1,0:T(8,128)(2,1)S(1)}, u32[]{:S(2)}, u32[]{:S(2)}) collective-permute-start(bf16[3,56,640]{2,1,0:T(8,128)(2,1)S(1)} %get-tuple-element.63), channel_id=1, source_target_pairs={{0,1},{1,0},{2,3},{3,2},{4,5},{5,4},{6,7},{7,6},{8,9},{9,8},{10,11... | collective-permute-start | bytes 645128 | tf_op jit(solution)/shard_map/ppermute | solution.py:337
  49.8 7.9 %collective-permute-start.13 = (bf16[64,2048]{1,0:T(8,128)(2,1)S(1)}, bf16[64,2048]{1,0:T(8,128)(2,1)S(1)}, u32[]{:S(2)}, u32[]{:S(2)}) collective-permute-start(bf16[64,2048]{1,0:T(8,128)(2,1)S(1)} %slice.6), channel_id=1, source_target_pairs={{0,8},{8,16},{16,24},{24,28},{28,20},{20,12},{12,4},{4,0},{1,9},{9... | collective-permute-start | bytes 786440 | tf_op jit(solution)/shard_map/ppermute | solution.py:315
  50.2 7.7 %collective-permute-start.14 = (bf16[64,2048]{1,0:T(8,128)(2,1)S(1)}, bf16[64,2048]{1,0:T(8,128)(2,1)S(1)}, u32[]{:S(2)}, u32[]{:S(2)}) collective-permute-start(bf16[64,2048]{1,0:T(8,128)(2,1)S(1)} %slice.7), channel_id=1, source_target_pairs={{8,0},{16,8},{24,16},{28,24},{20,28},{12,20},{4,12},{0,4},{9,1},{1... | collective-permute-start | bytes 786440 | tf_op jit(solution)/shard_map/ppermute | solution.py:315
  51.3 10.4 %collective-permute-start.8 = (bf16[3,56,640]{2,1,0:T(8,128)(2,1)S(1)}, bf16[3,56,640]{2,1,0:T(8,128)(2,1)S(1)}, u32[]{:S(2)}, u32[]{:S(2)}) collective-permute-start(bf16[3,56,640]{2,1,0:T(8,128)(2,1)S(1)} %get-tuple-element.65), channel_id=1, source_target_pairs={{0,2},{1,3},{2,0},{3,1},{4,6},{5,7},{6,4},{7,5},{8,10},{9,11},{10,... | collective-permute-start | bytes 645128 | tf_op jit(solution)/shard_map/ppermute | solution.py:337
  51.3 14.0 %copy-start.1 = (bf16[1024,1024]{1,0:T(8,128)(2,1)S(1)}, bf16[1024,1024]{1,0:T(8,128)(2,1)}, u32[]{:S(2)}) copy-start(bf16[1024,1024]{1,0:T(8,128)(2,1)} %constant.16.clone.sin_ref.refs_17_) | copy-start | bytes 6291460
  51.3 14.0 %copy-start.2 = (bf16[1024,1024]{1,0:T(8,128)(2,1)S(1)}, bf16[1024,1024]{1,0:T(8,128)(2,1)}, u32[]{:S(2)}) copy-start(bf16[1024,1024]{1,0:T(8,128)(2,1)} %constant.15.clone.cos_ref.refs_16_) | copy-start | bytes 6291460
  51.3 14.0 %copy-start.12 = (f32[2,1024]{1,0:T(2,128)S(1)}, f32[2,1024]{1,0:T(2,128)}, u32[]{:S(2)}) copy-start(f32[2,1024]{1,0:T(2,128)} %constant.17.clone.twist_ref.refs_18_) | copy-start | bytes 24580
  51.3 14.0 %collective-permute-start.9 = (bf16[3,56,640]{2,1,0:T(8,128)(2,1)S(1)}, bf16[3,56,640]{2,1,0:T(8,128)(2,1)S(1)}, u32[]{:S(2)}, u32[]{:S(2)}) collective-permute-start(bf16[3,56,640]{2,1,0:T(8,128)(2,1)S(1)} %get-tuple-element.66), channel_id=1, source_target_pairs={{0,3},{1,2},{2,1},{3,0},{4,7},{5,6},{6,5},{7,4},{8,11},{9,10},{10,... | collective-permute-start | bytes 645128 | tf_op jit(solution)/shard_map/ppermute | solution.py:337
  57.6 7.7 %collective-permute-start.10 = (bf16[3,56,256]{2,1,0:T(8,128)(2,1)S(1)}, bf16[3,56,256]{2,1,0:T(8,128)(2,1)S(1)}, u32[]{:S(2)}, u32[]{:S(2)}) collective-permute-start(bf16[3,56,256]{2,1,0:T(8,128)(2,1)S(1)} %get-tuple-element.72), channel_id=1, source_target_pairs={{0,1},{1,0},{2,3},{3,2},{4,5},{5,4},{6,7},{7,6},{8,9},{9,8},{10,11... | collective-permute-start | bytes 258056 | tf_op jit(solution)/shard_map/ppermute | solution.py:337
  57.7 9.2 %collective-permute-start.11 = (bf16[3,56,256]{2,1,0:T(8,128)(2,1)S(1)}, bf16[3,56,256]{2,1,0:T(8,128)(2,1)S(1)}, u32[]{:S(2)}, u32[]{:S(2)}) collective-permute-start(bf16[3,56,256]{2,1,0:T(8,128)(2,1)S(1)} %get-tuple-element.73), channel_id=1, source_target_pairs={{0,2},{1,3},{2,0},{3,1},{4,6},{5,7},{6,4},{7,5},{8,10},{9,11},{10,... | collective-permute-start | bytes 258056 | tf_op jit(solution)/shard_map/ppermute | solution.py:337
  57.8 9.3 %collective-permute-start.12 = (bf16[3,56,256]{2,1,0:T(8,128)(2,1)S(1)}, bf16[3,56,256]{2,1,0:T(8,128)(2,1)S(1)}, u32[]{:S(2)}, u32[]{:S(2)}) collective-permute-start(bf16[3,56,256]{2,1,0:T(8,128)(2,1)S(1)} %get-tuple-element.74), channel_id=1, source_target_pairs={{0,3},{1,2},{2,1},{3,0},{4,7},{5,6},{6,5},{7,4},{8,11},{9,10},{10,... | collective-permute-start | bytes 258056 | tf_op jit(solution)/shard_map/ppermute | solution.py:337
  61.7 5.5 %collective-permute-start.15 = (bf16[3,56,128]{2,1,0:T(8,128)(2,1)S(1)}, bf16[3,56,128]{2,1,0:T(8,128)(2,1)S(1)}, u32[]{:S(2)}, u32[]{:S(2)}) collective-permute-start(bf16[3,56,128]{2,1,0:T(8,128)(2,1)S(1)} %get-tuple-element.78), channel_id=1, source_target_pairs={{0,1},{1,0},{2,3},{3,2},{4,5},{5,4},{6,7},{7,6},{8,9},{9,8},{10,11... | collective-permute-start | bytes 129032 | tf_op jit(solution)/shard_map/ppermute | solution.py:337
  65.3 2.9 %collective-permute-start.16 = (bf16[3,56,128]{2,1,0:T(8,128)(2,1)S(1)}, bf16[3,56,128]{2,1,0:T(8,128)(2,1)S(1)}, u32[]{:S(2)}, u32[]{:S(2)}) collective-permute-start(bf16[3,56,128]{2,1,0:T(8,128)(2,1)S(1)} %get-tuple-element.79), channel_id=1, source_target_pairs={{0,2},{1,3},{2,0},{3,1},{4,6},{5,7},{6,4},{7,5},{8,10},{9,11},{10,... | collective-permute-start | bytes 129032 | tf_op jit(solution)/shard_map/ppermute | solution.py:337
  65.3 4.0 %collective-permute-start.17 = (bf16[3,56,128]{2,1,0:T(8,128)(2,1)S(1)}, bf16[3,56,128]{2,1,0:T(8,128)(2,1)S(1)}, u32[]{:S(2)}, u32[]{:S(2)}) collective-permute-start(bf16[3,56,128]{2,1,0:T(8,128)(2,1)S(1)} %get-tuple-element.80), channel_id=1, source_target_pairs={{0,3},{1,2},{2,1},{3,0},{4,7},{5,6},{6,5},{7,4},{8,11},{9,10},{10,... | collective-permute-start | bytes 129032 | tf_op jit(solution)/shard_map/ppermute | solution.py:337
  75.0 19.2 %copy-start.4 = (bf16[128,2048]{1,0:T(8,128)(2,1)S(1)}, bf16[128,2048]{1,0:T(8,128)(2,1)}, u32[]{:S(2)}) copy-start(bf16[128,2048]{1,0:T(8,128)(2,1)} %refs_4_.1) | copy-start | bytes 1572868
  77.8 10.9 %all-to-all-start.2 = ((f32[8,56,128]{2,1,0:T(8,128)}), f32[8,56,128]{2,1,0:T(8,128)S(1)}, u32[]{:S(2)}, u32[]{:S(2)}) async-start(f32[8,56,128]{2,1,0:T(8,128)} %broadcast_in_dim.10), calls=%async_computation.2 | async-start | bytes 458752 | tf_op jit(solution)/shard_map/all_to_all | solution.py:423
  81.2 9.6 %collective-permute-start.18 = (bf16[3,56,1024]{2,1,0:T(8,128)(2,1)}, bf16[3,56,1024]{2,1,0:T(8,128)(2,1)}, u32[]{:S(2)}, u32[]{:S(2)}) collective-permute-start(bf16[3,56,1024]{2,1,0:T(8,128)(2,1)} %copy-done.9), channel_id=1, source_target_pairs={{0,2},{1,3},{2,0},{3,1},{4,6},{5,7},{6,4},{7,5},{8,10},{9,11},{10,... | collective-permute-start | bytes 1032200 | tf_op jit(solution)/shard_map/ppermute | solution.py:409
  82.2 12.0 %collective-permute-start.19 = (bf16[3,56,1024]{2,1,0:T(8,128)(2,1)}, bf16[3,56,1024]{2,1,0:T(8,128)(2,1)}, u32[]{:S(2)}, u32[]{:S(2)}) collective-permute-start(bf16[3,56,1024]{2,1,0:T(8,128)(2,1)} %copy-done.9), channel_id=1, source_target_pairs={{0,1},{1,0},{2,3},{3,2},{4,5},{5,4},{6,7},{7,6},{8,9},{9,8},{10,11... | collective-permute-start | bytes 1032200 | tf_op jit(solution)/shard_map/ppermute | solution.py:414
  90.8 3.4 %collective-permute-start.20 = (bf16[3,56,1024]{2,1,0:T(8,128)(2,1)}, bf16[3,56,1024]{2,1,0:T(8,128)(2,1)S(1)}, u32[]{:S(2)}, u32[]{:S(2)}) collective-permute-start(bf16[3,56,1024]{2,1,0:T(8,128)(2,1)} %collective-permute-done.18.refs_1_), channel_id=1, source_target_pairs={{0,1},{1,0},{2,3},{3,2},{4,5},{5,4},{6,7},{7,6},{8,9},{9,8},{10,11... | collective-permute-start | bytes 1032200 | tf_op jit(solution)/shard_map/ppermute | solution.py:430
  92.0 11.5 %collective-permute-start.21 = (f32[2,56,128]{2,1,0:T(8,128)S(1)}, f32[2,56,128]{2,1,0:T(8,128)S(1)}, u32[]{:S(2)}, u32[]{:S(2)}) collective-permute-start(f32[2,56,128]{2,1,0:T(8,128)S(1)} %get-tuple-element.95), channel_id=1, source_target_pairs={{0,1},{1,0},{2,3},{3,2},{4,5},{5,4},{6,7},{7,6},{8,9},{9,8},{10,11... | collective-permute-start | bytes 172040 | tf_op jit(solution)/shard_map/ppermute | solution.py:432
  92.0 11.5 %collective-permute-start.22 = (f32[2,56,128]{2,1,0:T(8,128)S(1)}, f32[2,56,128]{2,1,0:T(8,128)S(1)}, u32[]{:S(2)}, u32[]{:S(2)}) collective-permute-start(f32[2,56,128]{2,1,0:T(8,128)S(1)} %get-tuple-element.96), channel_id=1, source_target_pairs={{0,2},{1,3},{2,0},{3,1},{4,6},{5,7},{6,4},{7,5},{8,10},{9,11},{10,... | collective-permute-start | bytes 172040 | tf_op jit(solution)/shard_map/ppermute | solution.py:432
  93.0 10.4 %collective-permute-start.23 = (f32[2,56,128]{2,1,0:T(8,128)S(1)}, f32[2,56,128]{2,1,0:T(8,128)S(1)}, u32[]{:S(2)}, u32[]{:S(2)}) collective-permute-start(f32[2,56,128]{2,1,0:T(8,128)S(1)} %get-tuple-element.97), channel_id=1, source_target_pairs={{0,3},{1,2},{2,1},{3,0},{4,7},{5,6},{6,5},{7,4},{8,11},{9,10},{10,... | collective-permute-start | bytes 172040 | tf_op jit(solution)/shard_map/ppermute | solution.py:432
  (7 other events, 8.8 us)

commit v8 on v7

--- a/solution.py
+++ b/solution.py
@@ -73,6 +73,13 @@
         for block in range(blocks):
             start = block * rows + min(owner * part, rows - part)
             pieces_ref[owner, block] = grad[start : start + part].astype(BF16)
+
+
+def turn_kernel(place_ref, held_ref, *out_refs):
+    count = out_refs[0].shape[0]
+    for half, out_ref in enumerate(out_refs):
+        for slot in range(count):
+            out_ref[slot] = held_ref[place_ref[0] ^ (half * count + slot)]
 
 
 def poles_kernel(place_ref, packed_ref, poles_ref, *, rows, n_ch):
@@ -160,7 +167,7 @@
     queries = in_order(0)
     keys = in_order(1)
     values = in_order(2)
-    upper = jnp.concatenate([gout_ref[b].astype(F32) for b in range(blocks)], 1)
+    upper = jnp.concatenate([gout_ref[b ^ place_ref[0]].astype(F32) for b in range(blocks)], 1)
     product = keys * values
     middle = upper * queries
     signals = jnp.concatenate([product, middle], 0)
@@ -217,28 +224,40 @@
 
 def weight_kernel(place_ref, *refs, shares):
     grad_refs = refs[:shares]
-    *feature_refs, out_ref, wide_ref, rows_ref, features_ref = refs[shares:]
+    *feature_refs, out_ref, wide_ref, rows_ref, features_ref, semaphores = refs[shares:]
     gates = out_ref.shape[0]
     part = grad_refs[0].shape[1]
+    tiles, _, width = features_ref.shape
+
+    def copy(tile, piece):
+        row = sum(feature_ref.shape[0] for feature_ref in feature_refs[:piece])
+        feature_ref = feature_refs[piece]
+        return pltpu.make_async_copy(
+            feature_ref.at[:, pl.ds(pl.multiple_of(tile * width, width), width)],
+            features_ref.at[tile, pl.ds(row, feature_ref.shape[0]), :],
+            semaphores.at[tile, piece],
+        )
 
     @pl.when(pl.program_id(0) == 0)
     def _():
+        for tile in range(tiles):
+            for piece in range(len(feature_refs)):
+                copy(tile, piece).start()
         for share, grad_ref in enumerate(grad_refs):
             start = share_start(place_ref[1], share, shares, part, out_ref.shape[1])
             wide_ref[:, pl.ds(start, part), :] = grad_ref[...].astype(F32)
         rows_ref[...] = wide_ref[...].astype(BF16)
 
-    row = 0
-    for feature_ref in feature_refs:
-        features_ref[row : row + feature_ref.shape[0], :] = feature_ref[...]
-        row += feature_ref.shape[0]
+    tile = pl.program_id(0)
+    for piece in range(len(feature_refs)):
+        copy(tile, piece).wait()
     rows = out_ref.shape[1]
     if rows % 16 == 0:
-        every = dot(rows_ref[...].reshape(gates * rows, -1), features_ref[...])
+        every = dot(rows_ref[...].reshape(gates * rows, -1), features_ref[tile])
         out_ref[...] = every.reshape(out_ref.shape)
     else:
         for gate in range(gates):
-            out_ref[gate] = dot(rows_ref[gate], features_ref[...])
+            out_ref[gate] = dot(rows_ref[gate], features_ref[tile])
 
 
 def split_kernel(place_ref, held_ref, *out_refs):
@@ -354,8 +373,23 @@
     )
     upper = lax.all_to_all(upper, "ch", split_axis=0, concat_axis=0, tiled=True)
     pair, upper, poles = lax.optimization_barrier((pair, upper, poles))
-    upper = upper.reshape(n_seq, part, block_len)
-    upper = lax.all_to_all(upper, "seq", split_axis=0, concat_axis=0, tiled=True)
+    low, high = call(
+        turn_kernel, [jax.ShapeDtypeStruct((n_seq // 2, part, block_len), BF16)] * 2, 0, 0,
+        place, upper.reshape(n_seq, part, block_len), indexed=True,
+    )
+
+    def trade(array, reach):
+        return lax.ppermute(array, "seq", [(d, d ^ reach) for d in range(n_seq)])
+
+    def merge(kept, moved):
+        return jnp.stack([kept, moved], 1).reshape(n_seq, part, block_len)
+
+    def cut(array, reach):
+        array = array.reshape(-1, 2, reach, part, block_len)
+        return array[:, 0], array[:, 1]
+
+    reach = n_seq // 2
+    kept, moved = low[None], trade(high, reach)[None]
 
     pieces, group_slots, partials = [features, *pair], [], []
     waiting = list(pieces)
@@ -363,9 +397,9 @@
     for step in range(2, n_seq // 2):
         pair = next_pair
         if step == 2:
-            pair, upper = lax.optimization_barrier((pair, upper))
+            pair, moved = lax.optimization_barrier((pair, moved))
         else:
-            pair, near = lax.optimization_barrier((pair, partials[1 - n_ch]))
+            pair, near, moved = lax.optimization_barrier((pair, partials[1 - n_ch], moved))
             partials[1 - n_ch] = near
         pieces += pair
         waiting += pair
@@ -379,6 +413,15 @@
         partials += to_owners(sums)
         group_slots.append(len(waiting))
         waiting = []
+        if reach > 1:
+            reach //= 2
+            kept, moved = cut(merge(kept, moved), reach)
+            moved = trade(moved, reach)
+    while reach > 1:
+        reach //= 2
+        kept, moved = cut(merge(kept, moved), reach)
+        moved = trade(moved, reach)
+    upper = merge(kept, moved)
     pair = next_pair
     pieces += pair
     partials += to_owners(project(list(pair)))
@@ -412,6 +455,7 @@
 
     across = chips(grads)
     swapped = lax.ppermute(grads, "ch", swap)
+    tgc, swapped = lax.optimization_barrier((tgc, swapped))
     lanes = round_up(2 * order + 1, 128)
     (pole_sums,) = call(
         functools.partial(pole_kernel, order=order),
@@ -439,15 +483,16 @@
         grid=(width // tile,),
         in_specs=[pl.BlockSpec(memory_space=pltpu.SMEM)]
         + [pl.BlockSpec((gates, part, tokens), lambda i: (0, 0, 0))] * n_ch
-        + [pl.BlockSpec((piece.shape[0], tile), lambda i: (0, i)) for piece in pieces],
+        + [pl.BlockSpec(memory_space=pltpu.HBM)] * len(pieces),
         out_specs=pl.BlockSpec((gates, rows, tile), lambda i: (0, 0, i)),
         scratch_shapes=[
             pltpu.VMEM((gates, rows, tokens), F32),
             pltpu.VMEM((gates, rows, tokens), BF16),
-            pltpu.VMEM((tokens, tile), BF16),
+            pltpu.VMEM((width // tile, tokens, tile), BF16),
+            pltpu.SemaphoreType.DMA((width // tile, len(pieces))),
         ],
         compiler_params=pltpu.CompilerParams(
-            vmem_limit_bytes=min(56 * MIB, 16 * MIB + 12 * gates * rows * tokens + 4 * tokens * tile)
+            vmem_limit_bytes=min(56 * MIB, 16 * MIB + 12 * gates * rows * tokens + 2 * tokens * width)
         ),
         cost_estimate=pl.CostEstimate(
             flops=2 * gates * rows * width * tokens,

time: 106 us -> 112 us (1.057)
  blocking collectives: 16.8 us -> 0 us
  waiting for transfers between devices: 19.8 us -> 33.9 us
  starting transfers between devices: 33.4 us -> 39.9 us
    ppermute x0 -> x3, waiting for transfers between devices: none -> 17.1 us  [trade(): return lax.ppermute(array, 'seq', [(d, d ^ reach) for d in range(n_seq)])]
    all_to_all x1 -> x0, blocking collectives: 16.8 us -> none  [local(): lax.all_to_all(upper, 'seq', split_axis=0, concat_axis=0, tiled=True)]
    ppermute x0 -> x3, starting transfers between devices: none -> 3.79 us  [trade(): return lax.ppermute(array, 'seq', [(d, d ^ reach) for d in range(n_seq)])]
    ppermute x9, waiting for transfers between devices: 6.5 us -> 3.45 us  [to_owners(): lax.ppermute(sums[d], 'ch', [(h, h ^ d) for h in range(n_ch)])]
    ppermute x9, starting transfers between devices: 9.6 us -> 11.1 us  [to_owners(): lax.ppermute(sums[d], 'ch', [(h, h ^ d) for h in range(n_ch)])]
    all_to_all x1, starting transfers between devices: 3.4 us -> 4.8 us  [local(): lax.all_to_all(every, 'seq', split_axis=0, concat_axis=0, tiled=True)]
    ppermute x1, waiting for transfers between devices: 0.01 us -> 1.28 us  [local(): swapped = lax.ppermute(grads, 'ch', swap)]
    unnamed x26 -> x30, local copies, waits for them, and re-layouts: 6.74 us -> 7.73 us
  transfers between devices with their start and end apart: 26 -> 29, of which waited for: 10 -> 9; matrix products, arithmetic and copies ran while one was open for 1% -> 1% of each run, Pallas kernels for 16% -> 16%
where the time goes in v8:
time: 112 us; the launch traced here: 111 us
  starting transfers between devices  39.9 us (36%)
  waiting for transfers between devices  33.9 us (30%)
  Pallas kernels  26.5 us (24%)
  local copies, waits for them, and re-layouts  8.62 us (8%)
    pallas_call x11, Pallas kernels, call(): pl.pallas_call(kernel, out_shape=outs, in_specs=specs, out_specs=[whole]...  19.6 us
    ppermute x3, waiting for transfers between devices, trade(): return lax.ppermute(array, 'seq', [(d, d ^ reach) for d in range(n_seq)])  17.1 us
    ppermute x9, starting transfers between devices, to_owners(): lax.ppermute(sums[d], 'ch', [(h, h ^ d) for h in range(n_ch)])  11.1 us
    unnamed x30, local copies, waits for them, and re-layouts  7.73 us
    all_to_all x1, waiting for transfers between devices, local(): lax.all_to_all(every, 'seq', split_axis=0, concat_axis=0, tiled=True)  7.16 us
    pallas_call x1, Pallas kernels, local(): pl.pallas_call(functools.partial(weight_kernel, shares=n_ch), out_shape=j...  6.91 us
    ppermute x4, starting transfers between devices, send_on(): lax.ppermute(pair[1], 'seq', behind)  5.71 us
    all_to_all x1, starting transfers between devices, local(): lax.all_to_all(every, 'seq', split_axis=0, concat_axis=0, tiled=True)  4.8 us
  transfers between devices with their start and end apart: 29, of which 9 were waited for; matrix products, arithmetic and copies ran while one was open for 1% of the time, Pallas kernels for 16%

profile of v8, /device:TPU:1, one launch (start us, length us, event | category | flops | bytes accessed | tf_op | source)
XLA Modules:
  0.0 110.8 jit_solution(14309967708371005152)
XLA Ops:
  0.6 2.1 %collective-permute-start.1 = (bf16[128,2048]{1,0:T(8,128)(2,1)}, bf16[128,2048]{1,0:T(8,128)(2,1)S(1)}, u32[]{:S(2)}, u32[]{:S(2)}) collective-permute-start(bf16[128,2048]{1,0:T(8,128)(2,1)} %refs_4_.1), channel_id=1, source_target_pairs={{8,0},{16,8},{24,16},{28,24},{20,28},{12,20},{4,12},{0,4},{9,1},{1... | collective-permute-start | bytes 1572872 | tf_op jit(solution)/shard_map/ppermute | solution.py:334
  6.0 4.2 %all-to-all-start = ((bf16[4,2,56,128]{3,2,1,0:T(8,128)(2,1)}), bf16[4,2,56,128]{3,2,1,0:T(8,128)(2,1)S(1)}, u32[]{:S(2)}, u32[]{:S(2)}) async-start(bf16[4,2,56,128]{3,2,1,0:T(8,128)(2,1)} %shard_map.121), calls=%async_computation | async-start | bytes 229376 | tf_op jit(solution)/shard_map/all_to_all | solution.py:374
  10.3 3.5 %collective-permute-start.2 = (f32[56,33]{1,0:T(8,128)S(1)}, f32[56,33]{1,0:T(8,128)S(1)}, u32[]{:S(2)}, u32[]{:S(2)}) collective-permute-start(f32[56,33]{1,0:T(8,128)S(1)} %shard_map.120), channel_id=1, source_target_pairs={{0,0},{4,1},{8,2},{12,3},{16,4},{20,5},{24,6},{28,7},{1,8},{5,9},{... | collective-permute-start | bytes 22184 | tf_op jit(solution)/shard_map/ppermute | solution.py:369
  13.8 3.1 %collective-permute-done.2.poles_ref.refs_13_ = f32[56,33]{1,0:T(8,128)S(1)} collective-permute-done((f32[56,33]{1,0:T(8,128)S(1)}, f32[56,33]{1,0:T(8,128)S(1)}, u32[]{:S(2)}, u32[]{:S(2)}) %collective-permute-start.2) | collective-permute-done | bytes 7424 | tf_op jit(solution)/shard_map/ppermute | solution.py:369
  17.9 2.0 %collective-permute-start.4 = (bf16[128,2048]{1,0:T(8,128)(2,1)S(1)}, bf16[128,2048]{1,0:T(8,128)(2,1)S(1)}, u32[]{:S(2)}, u32[]{:S(2)}) collective-permute-start(bf16[128,2048]{1,0:T(8,128)(2,1)S(1)} %collective-permute-done.1.refs_2_.refs_6_), channel_id=1, source_target_pairs={{8,0},{16,8},{24,16},{28,24},{20,28},{12,20},{4,12},{0,4},{9,1},{1... | collective-permute-start | bytes 1572872 | tf_op jit(solution)/shard_map/ppermute | solution.py:334
  20.5 2.7 %collective-permute-start.5 = (bf16[4,56,128]{2,1,0:T(8,128)(2,1)S(1)}, bf16[4,56,128]{2,1,0:T(8,128)(2,1)S(1)}, u32[]{:S(2)}, u32[]{:S(2)}) collective-permute-start(bf16[4,56,128]{2,1,0:T(8,128)(2,1)S(1)} %get-tuple-element.65), channel_id=1, source_target_pairs={{0,16},{4,20},{8,24},{12,28},{16,0},{20,4},{24,8},{28,12},{1,17},{... | collective-permute-start | bytes 172040 | tf_op jit(solution)/shard_map/ppermute | solution.py:382
  23.1 12.8 %collective-permute-done.5 = bf16[4,56,128]{2,1,0:T(8,128)(2,1)S(1)} collective-permute-done((bf16[4,56,128]{2,1,0:T(8,128)(2,1)S(1)}, bf16[4,56,128]{2,1,0:T(8,128)(2,1)S(1)}, u32[]{:S(2)}, u32[]{:S(2)}) %collective-permute-start.5) | collective-permute-done | bytes 57376 | tf_op jit(solution)/shard_map/ppermute | solution.py:382
  36.0 1.4 %collective-permute-start.6 = (bf16[128,2048]{1,0:T(8,128)(2,1)S(1)}, bf16[128,2048]{1,0:T(8,128)(2,1)S(1)}, u32[]{:S(2)}, u32[]{:S(2)}) collective-permute-start(bf16[128,2048]{1,0:T(8,128)(2,1)S(1)} %collective-permute-done.3.refs_3_.refs_7_), channel_id=1, source_target_pairs={{0,8},{8,16},{16,24},{24,28},{28,20},{20,12},{12,4},{4,0},{1,9},{9... | collective-permute-start | bytes 1572872 | tf_op jit(solution)/shard_map/ppermute | solution.py:334
  37.5 1.7 %copy-done = bf16[208,3,2048]{2,0,1:T(8,128)(2,1)S(1)} copy-done((bf16[208,3,2048]{2,0,1:T(8,128)(2,1)S(1)}, bf16[208,3,2048]{2,0,1:T(8,128)(2,1)}, u32[]{:S(2)}) %copy-start) | copy-done | bytes 2555928
  40.3 3.5 %shard_map.123 = (f32[3,56,640]{2,1,0:T(8,128)S(1)}, bf16[3,56,640]{2,1,0:T(8,128)(2,1)S(1)}, bf16[3,56,640]{2,1,0:T(8,128)(2,1)S(1)}, bf16[3,56,640]{2,1,0:T(8,128)(2,1)S(1)}) custom-call(s32[2]{0:T(128)S(1)} %pad_add_fusion.place_ref, bf16[3,208,2048]{2,1,0:T(8,128)(2,1)S(1)} %bitcast.25, bf16[128,2048]{1,0:T(8,128)(2,1)S(1)} %copy-done.3, ...), custom_call_target="tpu_custom_call" | custom-call | flops 1635778560 | bytes 6252552 | tf_op jit(solution)/shard_map/pallas_call | solution.py:298
  43.8 1.6 %collective-permute-start.8 = (bf16[3,56,640]{2,1,0:T(8,128)(2,1)S(1)}, bf16[3,56,640]{2,1,0:T(8,128)(2,1)S(1)}, u32[]{:S(2)}, u32[]{:S(2)}) collective-permute-start(bf16[3,56,640]{2,1,0:T(8,128)(2,1)S(1)} %get-tuple-element.69), channel_id=1, source_target_pairs={{0,1},{1,0},{2,3},{3,2},{4,5},{5,4},{6,7},{7,6},{8,9},{9,8},{10,11... | collective-permute-start | bytes 645128 | tf_op jit(solution)/shard_map/ppermute | solution.py:356
  45.5 1.1 %collective-permute-start.9 = (bf16[2,2,56,128]{3,2,1,0:T(8,128)(2,1)S(1)}, bf16[2,2,56,128]{3,2,1,0:T(8,128)(2,1)S(1)}, u32[]{:S(2)}, u32[]{:S(2)}) collective-permute-start(bf16[2,2,56,128]{3,2,1,0:T(8,128)(2,1)S(1)} %fusion.5), channel_id=1, source_target_pairs={{0,8},{4,12},{8,0},{12,4},{16,24},{20,28},{24,16},{28,20},{1,9},{5... | collective-permute-start | bytes 172040 | tf_op jit(solution)/shard_map/ppermute | solution.py:382
  46.6 4.3 %collective-permute-done.9 = bf16[2,2,56,128]{3,2,1,0:T(8,128)(2,1)S(1)} collective-permute-done((bf16[2,2,56,128]{3,2,1,0:T(8,128)(2,1)S(1)}, bf16[2,2,56,128]{3,2,1,0:T(8,128)(2,1)S(1)}, u32[]{:S(2)}, u32[]{:S(2)}) %collective-permute-start.9) | collective-permute-done | bytes 57376 | tf_op jit(solution)/shard_map/ppermute | solution.py:382
  51.4 1.4 %collective-permute-start.16 = (bf16[64,2048]{1,0:T(8,128)(2,1)S(1)}, bf16[64,2048]{1,0:T(8,128)(2,1)S(1)}, u32[]{:S(2)}, u32[]{:S(2)}) collective-permute-start(bf16[64,2048]{1,0:T(8,128)(2,1)S(1)} %slice.20), channel_id=1, source_target_pairs={{8,0},{16,8},{24,16},{28,24},{20,28},{12,20},{4,12},{0,4},{9,1},{1... | collective-permute-start | bytes 786440 | tf_op jit(solution)/shard_map/ppermute | solution.py:334
  52.8 1.8 %shard_map.124 = (f32[3,56,256]{2,1,0:T(8,128)S(1)}, bf16[3,56,256]{2,1,0:T(8,128)(2,1)S(1)}, bf16[3,56,256]{2,1,0:T(8,128)(2,1)S(1)}, bf16[3,56,256]{2,1,0:T(8,128)(2,1)S(1)}) custom-call(s32[2]{0:T(128)S(1)} %pad_add_fusion.place_ref, bf16[3,208,2048]{2,1,0:T(8,128)(2,1)S(1)} %bitcast.26, bf16[128,2048]{1,0:T(8,128)(2,1)S(1)} %collective-permute-done.6.refs_0_.refs_9_, ...), custom_call_target="tpu_custom_call" | custom-call | flops 654311424 | bytes 4034568 | tf_op jit(solution)/shard_map/pallas_call | solution.py:298
  54.6 2.4 %collective-permute-start.12 = (bf16[3,56,256]{2,1,0:T(8,128)(2,1)S(1)}, bf16[3,56,256]{2,1,0:T(8,128)(2,1)S(1)}, u32[]{:S(2)}, u32[]{:S(2)}) collective-permute-start(bf16[3,56,256]{2,1,0:T(8,128)(2,1)S(1)} %get-tuple-element.80), channel_id=1, source_target_pairs={{0,1},{1,0},{2,3},{3,2},{4,5},{5,4},{6,7},{7,6},{8,9},{9,8},{10,11... | collective-permute-start | bytes 258056 | tf_op jit(solution)/shard_map/ppermute | solution.py:356
  57.3 1.5 %shard_map.126 = (f32[56,1024]{1,0:T(8,128)S(1)}, f32[56,1024]{1,0:T(8,128)S(1)}) custom-call(f32[56,33]{1,0:T(8,128)S(1)} %collective-permute-done.2.poles_ref.refs_13_, bf16[1024,1024]{1,0:T(8,128)(2,1)S(1)} %copy-done.2, bf16[1024,1024]{1,0:T(8,128)(2,1)S(1)} %copy-done.1, f32[2,1024]{1,0:T(2,128)S(1)} %copy-done.14), custom_call_target="tpu_custom_call" | custom-call | flops 469762048 | bytes 4668640 | tf_op jit(solution)/shard_map/pallas_call | solution.py:298
  58.9 4.5 %collective-permute-start.13 = (bf16[3,56,256]{2,1,0:T(8,128)(2,1)S(1)}, bf16[3,56,256]{2,1,0:T(8,128)(2,1)S(1)}, u32[]{:S(2)}, u32[]{:S(2)}) collective-permute-start(bf16[3,56,256]{2,1,0:T(8,128)(2,1)S(1)} %get-tuple-element.81), channel_id=1, source_target_pairs={{0,2},{1,3},{2,0},{3,1},{4,6},{5,7},{6,4},{7,5},{8,10},{9,11},{10,... | collective-permute-start | bytes 258056 | tf_op jit(solution)/shard_map/ppermute | solution.py:356
  63.4 1.5 %shard_map.125 = (f32[3,56,128]{2,1,0:T(8,128)S(1)}, bf16[3,56,128]{2,1,0:T(8,128)(2,1)S(1)}, bf16[3,56,128]{2,1,0:T(8,128)(2,1)S(1)}, bf16[3,56,128]{2,1,0:T(8,128)(2,1)S(1)}) custom-call(s32[2]{0:T(128)S(1)} %pad_add_fusion.place_ref, bf16[3,208,2048]{2,1,0:T(8,128)(2,1)S(1)} %bitcast.27, bf16[64,2048]{1,0:T(8,128)(2,1)S(1)} %collective-permute-done.15.refs_0_.refs_11_, ...), custom_call_target="tpu_custom_call" | custom-call | flops 327155712 | bytes 3295240 | tf_op jit(solution)/shard_map/pallas_call | solution.py:298
  65.3 1.4 %collective-permute-start.18 = (bf16[3,56,128]{2,1,0:T(8,128)(2,1)S(1)}, bf16[3,56,128]{2,1,0:T(8,128)(2,1)S(1)}, u32[]{:S(2)}, u32[]{:S(2)}) collective-permute-start(bf16[3,56,128]{2,1,0:T(8,128)(2,1)S(1)} %get-tuple-element.87), channel_id=1, source_target_pairs={{0,2},{1,3},{2,0},{3,1},{4,6},{5,7},{6,4},{7,5},{8,10},{9,11},{10,... | collective-permute-start | bytes 129032 | tf_op jit(solution)/shard_map/ppermute | solution.py:356
  67.2 2.0 %collective-permute-done.14.refs_7_ = bf16[3,56,256]{2,1,0:T(8,128)(2,1)S(1)} collective-permute-done((bf16[3,56,256]{2,1,0:T(8,128)(2,1)S(1)}, bf16[3,56,256]{2,1,0:T(8,128)(2,1)S(1)}, u32[]{:S(2)}, u32[]{:S(2)}) %collective-permute-start.14) | collective-permute-done | bytes 86048 | tf_op jit(solution)/shard_map/ppermute | solution.py:356
  69.2 1.5 %collective-permute-done.19.refs_11_ = bf16[3,56,128]{2,1,0:T(8,128)(2,1)S(1)} collective-permute-done((bf16[3,56,128]{2,1,0:T(8,128)(2,1)S(1)}, bf16[3,56,128]{2,1,0:T(8,128)(2,1)S(1)}, u32[]{:S(2)}, u32[]{:S(2)}) %collective-permute-start.19) | collective-permute-done | bytes 43040 | tf_op jit(solution)/shard_map/ppermute | solution.py:356
  70.6 5.6 %shard_map.127 = (bf16[3,56,1024]{2,1,0:T(8,128)(2,1)S(1)}, f32[56,1024]{1,0:T(8,128)S(1)}, f32[56,1024]{1,0:T(8,128)S(1)}, f32[56,1]{1,0:T(8,128)S(1)}) custom-call(s32[2]{0:T(128)S(1)} %pad_add_fusion.place_ref, f32[3,56,640]{2,1,0:T(8,128)S(1)} %get-tuple-element.68.refs_0_, bf16[3,56,640]{2,1,0:T(8,128)(2,1)S(1)} %collective-permute-done.8.refs_1_, ...), custom_call_target="tpu_custom_call" | custom-call | flops 1879048192 | bytes 7306696 | tf_op jit(solution)/shard_map/pallas_call | solution.py:298
  76.7 1.3 %collective-permute-done.22.refs_2_ = bf16[3,56,1024]{2,1,0:T(8,128)(2,1)S(1)} collective-permute-done((bf16[3,56,1024]{2,1,0:T(8,128)(2,1)S(1)}, bf16[3,56,1024]{2,1,0:T(8,128)(2,1)S(1)}, u32[]{:S(2)}, u32[]{:S(2)}) %collective-permute-start.22) | collective-permute-done | bytes 344096 | tf_op jit(solution)/shard_map/ppermute | solution.py:457
  78.0 2.0 %shard_map.128 = f32[56,128]{1,0:T(8,128)S(1)} custom-call(f32[56,33]{1,0:T(8,128)S(1)} %collective-permute-done.2.poles_ref.refs_13_, f32[56,1024]{1,0:T(8,128)S(1)} %get-tuple-element.95.tgc_ref, f32[56,1024]{1,0:T(8,128)S(1)} %get-tuple-element.96.tgs_ref, bf16[1024,1024]{1,0:T(8,128)(2,1)S(1)} %copy-done.2, bf16[1024,1024]{1,0:T(8,128)(2,1)S(1)} %copy-done.1, ...), custom_call_target="tpu_custom_call" | custom-call | flops 469762048 | bytes 4689344 | tf_op jit(solution)/shard_map/pallas_call | solution.py:298
  80.8 4.8 %all-to-all-start.1 = ((f32[8,56,128]{2,1,0:T(8,128)}), f32[8,56,128]{2,1,0:T(8,128)S(1)}, u32[]{:S(2)}, u32[]{:S(2)}) async-start(f32[8,56,128]{2,1,0:T(8,128)} %broadcast_in_dim.14), calls=%async_computation.1 | async-start | bytes 458752 | tf_op jit(solution)/shard_map/all_to_all | solution.py:467
  85.7 7.2 %all-to-all-done.1 = f32[8,56,128]{2,1,0:T(8,128)S(1)} async-done(((f32[8,56,128]{2,1,0:T(8,128)}), f32[8,56,128]{2,1,0:T(8,128)S(1)}, u32[]{:S(2)}, u32[]{:S(2)}) %all-to-all-start.1) | async-done | bytes 229408 | tf_op jit(solution)/shard_map/all_to_all | solution.py:467
  93.4 1.4 %collective-permute-done.21.refs_1_ = bf16[3,56,1024]{2,1,0:T(8,128)(2,1)} collective-permute-done((bf16[3,56,1024]{2,1,0:T(8,128)(2,1)}, bf16[3,56,1024]{2,1,0:T(8,128)(2,1)}, u32[]{:S(2)}, u32[]{:S(2)}) %collective-permute-start.21) | collective-permute-done | bytes 344096 | tf_op jit(solution)/shard_map/ppermute | solution.py:452
  94.8 1.5 %collective-permute-start.23 = (bf16[3,56,1024]{2,1,0:T(8,128)(2,1)}, bf16[3,56,1024]{2,1,0:T(8,128)(2,1)S(1)}, u32[]{:S(2)}, u32[]{:S(2)}) collective-permute-start(bf16[3,56,1024]{2,1,0:T(8,128)(2,1)} %collective-permute-done.21.refs_1_), channel_id=1, source_target_pairs={{0,1},{1,0},{2,3},{3,2},{4,5},{5,4},{6,7},{7,6},{8,9},{9,8},{10,11... | collective-permute-start | bytes 1032200 | tf_op jit(solution)/shard_map/ppermute | solution.py:474
  96.5 2.0 %collective-permute-start.26 = (f32[2,56,128]{2,1,0:T(8,128)S(1)}, f32[2,56,128]{2,1,0:T(8,128)S(1)}, u32[]{:S(2)}, u32[]{:S(2)}) collective-permute-start(f32[2,56,128]{2,1,0:T(8,128)S(1)} %get-tuple-element.107), channel_id=1, source_target_pairs={{0,3},{1,2},{2,1},{3,0},{4,7},{5,6},{6,5},{7,4},{8,11},{9,10},{10,... | collective-permute-start | bytes 172040 | tf_op jit(solution)/shard_map/ppermute | solution.py:476
  102.5 6.9 %shard_map.130 = f32[3,208,2048]{2,1,0:T(8,128)} custom-call(s32[2]{0:T(128)S(1)} %pad_add_fusion.place_ref, bf16[3,56,1024]{2,1,0:T(8,128)(2,1)S(1)} %copy-done.10, bf16[3,56,1024]{2,1,0:T(8,128)(2,1)} %collective-permute-done.21.refs_1_, bf16[3,56,1024]{2,1,0:T(8,128)(2,1)S(1)} %copy-done.12, bf16[3,56,1024]{2,1,0:T(8,128)(2,1)S(1)} %collective-permute-done.23.refs_3_, ...), custom_call_target="tpu_custom_call" | custom-call | flops 2617245696 | bytes 10584064 | tf_op jit(solution)/shard_map/pallas_call | solution.py:480
  109.5 1.3 %shard_map.131 = (f32[16,416]{1,0:T(8,128)}, f32[16,416]{1,0:T(8,128)}, f32[1,416]{1,0:T(1,128)}) custom-call(s32[2]{0:T(128)S(1)} %pad_add_fusion.place_ref, f32[2,56,128]{2,1,0:T(8,128)S(1)} %get-tuple-element.109.refs_0_, f32[2,56,128]{2,1,0:T(8,128)S(1)} %collective-permute-done.24.refs_1_, f32[2,56,128]{2,1,0:T(8,128)S(1)} %collective-permute-done.25.refs_2_, ...), custom_call_target="tpu_custom_call" | custom-call | bytes 284296 | tf_op jit(solution)/shard_map/pallas_call | solution.py:298
  (79 shorter events, 13.6 us)
Async XLA Ops:
  0.6 16.3 %collective-permute-start.1 = (bf16[128,2048]{1,0:T(8,128)(2,1)}, bf16[128,2048]{1,0:T(8,128)(2,1)S(1)}, u32[]{:S(2)}, u32[]{:S(2)}) collective-permute-start(bf16[128,2048]{1,0:T(8,128)(2,1)} %refs_4_.1), channel_id=1, source_target_pairs={{8,0},{16,8},{24,16},{28,24},{20,28},{12,20},{4,12},{0,4},{9,1},{1... | collective-permute-start | bytes 1572872 | tf_op jit(solution)/shard_map/ppermute | solution.py:334
  2.7 14.2 %collective-permute-start = (bf16[128,2048]{1,0:T(8,128)(2,1)}, bf16[128,2048]{1,0:T(8,128)(2,1)S(1)}, u32[]{:S(2)}, u32[]{:S(2)}) collective-permute-start(bf16[128,2048]{1,0:T(8,128)(2,1)} %refs_4_.1), channel_id=1, source_target_pairs={{0,8},{8,16},{16,24},{24,28},{28,20},{20,12},{12,4},{4,0},{1,9},{9... | collective-permute-start | bytes 1572872 | tf_op jit(solution)/shard_map/ppermute | solution.py:334
  6.0 10.9 %all-to-all-start = ((bf16[4,2,56,128]{3,2,1,0:T(8,128)(2,1)}), bf16[4,2,56,128]{3,2,1,0:T(8,128)(2,1)S(1)}, u32[]{:S(2)}, u32[]{:S(2)}) async-start(bf16[4,2,56,128]{3,2,1,0:T(8,128)(2,1)} %shard_map.121), calls=%async_computation | async-start | bytes 229376 | tf_op jit(solution)/shard_map/all_to_all | solution.py:374
  10.3 6.6 %collective-permute-start.2 = (f32[56,33]{1,0:T(8,128)S(1)}, f32[56,33]{1,0:T(8,128)S(1)}, u32[]{:S(2)}, u32[]{:S(2)}) collective-permute-start(f32[56,33]{1,0:T(8,128)S(1)} %shard_map.120), channel_id=1, source_target_pairs={{0,0},{4,1},{8,2},{12,3},{16,4},{20,5},{24,6},{28,7},{1,8},{5,9},{... | collective-permute-start | bytes 22184 | tf_op jit(solution)/shard_map/ppermute | solution.py:369
  16.9 19.1 %collective-permute-start.3 = (bf16[128,2048]{1,0:T(8,128)(2,1)S(1)}, bf16[128,2048]{1,0:T(8,128)(2,1)S(1)}, u32[]{:S(2)}, u32[]{:S(2)}) collective-permute-start(bf16[128,2048]{1,0:T(8,128)(2,1)S(1)} %collective-permute-done.refs_1_.refs_5_), channel_id=1, source_target_pairs={{0,8},{8,16},{16,24},{24,28},{28,20},{20,12},{12,4},{4,0},{1,9},{9... | collective-permute-start | bytes 1572872 | tf_op jit(solution)/shard_map/ppermute | solution.py:334
  17.9 18.1 %collective-permute-start.4 = (bf16[128,2048]{1,0:T(8,128)(2,1)S(1)}, bf16[128,2048]{1,0:T(8,128)(2,1)S(1)}, u32[]{:S(2)}, u32[]{:S(2)}) collective-permute-start(bf16[128,2048]{1,0:T(8,128)(2,1)S(1)} %collective-permute-done.1.refs_2_.refs_6_), channel_id=1, source_target_pairs={{8,0},{16,8},{24,16},{28,24},{20,28},{12,20},{4,12},{0,4},{9,1},{1... | collective-permute-start | bytes 1572872 | tf_op jit(solution)/shard_map/ppermute | solution.py:334
  20.5 15.5 %collective-permute-start.5 = (bf16[4,56,128]{2,1,0:T(8,128)(2,1)S(1)}, bf16[4,56,128]{2,1,0:T(8,128)(2,1)S(1)}, u32[]{:S(2)}, u32[]{:S(2)}) collective-permute-start(bf16[4,56,128]{2,1,0:T(8,128)(2,1)S(1)} %get-tuple-element.65), channel_id=1, source_target_pairs={{0,16},{4,20},{8,24},{12,28},{16,0},{20,4},{24,8},{28,12},{1,17},{... | collective-permute-start | bytes 172040 | tf_op jit(solution)/shard_map/ppermute | solution.py:382
  36.0 7.8 %copy-start.5 = (bf16[128,2048]{1,0:T(8,128)(2,1)}, bf16[128,2048]{1,0:T(8,128)(2,1)S(1)}, u32[]{:S(2)}) copy-start(bf16[128,2048]{1,0:T(8,128)(2,1)S(1)} %collective-permute-done.3.refs_3_.refs_7_) | copy-start | bytes 1572868
  36.0 7.8 %copy-start.7 = (bf16[128,2048]{1,0:T(8,128)(2,1)}, bf16[128,2048]{1,0:T(8,128)(2,1)S(1)}, u32[]{:S(2)}) copy-start(bf16[128,2048]{1,0:T(8,128)(2,1)S(1)} %collective-permute-done.4.refs_4_.refs_8_) | copy-start | bytes 1572868
  36.0 15.1 %collective-permute-start.6 = (bf16[128,2048]{1,0:T(8,128)(2,1)S(1)}, bf16[128,2048]{1,0:T(8,128)(2,1)S(1)}, u32[]{:S(2)}, u32[]{:S(2)}) collective-permute-start(bf16[128,2048]{1,0:T(8,128)(2,1)S(1)} %collective-permute-done.3.refs_3_.refs_7_), channel_id=1, source_target_pairs={{0,8},{8,16},{16,24},{24,28},{28,20},{20,12},{12,4},{4,0},{1,9},{9... | collective-permute-start | bytes 1572872 | tf_op jit(solution)/shard_map/ppermute | solution.py:334
  37.4 13.8 %collective-permute-start.7 = (bf16[128,2048]{1,0:T(8,128)(2,1)S(1)}, bf16[128,2048]{1,0:T(8,128)(2,1)S(1)}, u32[]{:S(2)}, u32[]{:S(2)}) collective-permute-start(bf16[128,2048]{1,0:T(8,128)(2,1)S(1)} %collective-permute-done.4.refs_4_.refs_8_), channel_id=1, source_target_pairs={{8,0},{16,8},{24,16},{28,24},{20,28},{12,20},{4,12},{0,4},{9,1},{1... | collective-permute-start | bytes 1572872 | tf_op jit(solution)/shard_map/ppermute | solution.py:334
  43.8 7.3 %collective-permute-start.8 = (bf16[3,56,640]{2,1,0:T(8,128)(2,1)S(1)}, bf16[3,56,640]{2,1,0:T(8,128)(2,1)S(1)}, u32[]{:S(2)}, u32[]{:S(2)}) collective-permute-start(bf16[3,56,640]{2,1,0:T(8,128)(2,1)S(1)} %get-tuple-element.69), channel_id=1, source_target_pairs={{0,1},{1,0},{2,3},{3,2},{4,5},{5,4},{6,7},{7,6},{8,9},{9,8},{10,11... | collective-permute-start | bytes 645128 | tf_op jit(solution)/shard_map/ppermute | solution.py:356
  45.5 5.4 %collective-permute-start.9 = (bf16[2,2,56,128]{3,2,1,0:T(8,128)(2,1)S(1)}, bf16[2,2,56,128]{3,2,1,0:T(8,128)(2,1)S(1)}, u32[]{:S(2)}, u32[]{:S(2)}) collective-permute-start(bf16[2,2,56,128]{3,2,1,0:T(8,128)(2,1)S(1)} %fusion.5), channel_id=1, source_target_pairs={{0,8},{4,12},{8,0},{12,4},{16,24},{20,28},{24,16},{28,20},{1,9},{5... | collective-permute-start | bytes 172040 | tf_op jit(solution)/shard_map/ppermute | solution.py:382
  46.6 18.3 %collective-permute-start.10 = (bf16[3,56,640]{2,1,0:T(8,128)(2,1)S(1)}, bf16[3,56,640]{2,1,0:T(8,128)(2,1)S(1)}, u32[]{:S(2)}, u32[]{:S(2)}) collective-permute-start(bf16[3,56,640]{2,1,0:T(8,128)(2,1)S(1)} %get-tuple-element.73), channel_id=1, source_target_pairs={{0,2},{1,3},{2,0},{3,1},{4,6},{5,7},{6,4},{7,5},{8,10},{9,11},{10,... | collective-permute-start | bytes 645128 | tf_op jit(solution)/shard_map/ppermute | solution.py:356
  50.9 14.1 %collective-permute-start.11 = (bf16[3,56,640]{2,1,0:T(8,128)(2,1)S(1)}, bf16[3,56,640]{2,1,0:T(8,128)(2,1)S(1)}, u32[]{:S(2)}, u32[]{:S(2)}) collective-permute-start(bf16[3,56,640]{2,1,0:T(8,128)(2,1)S(1)} %get-tuple-element.74), channel_id=1, source_target_pairs={{0,3},{1,2},{2,1},{3,0},{4,7},{5,6},{6,5},{7,4},{8,11},{9,10},{10,... | collective-permute-start | bytes 645128 | tf_op jit(solution)/shard_map/ppermute | solution.py:356
  51.3 6.0 %collective-permute-start.15 = (bf16[64,2048]{1,0:T(8,128)(2,1)S(1)}, bf16[64,2048]{1,0:T(8,128)(2,1)S(1)}, u32[]{:S(2)}, u32[]{:S(2)}) collective-permute-start(bf16[64,2048]{1,0:T(8,128)(2,1)S(1)} %slice.19), channel_id=1, source_target_pairs={{0,8},{8,16},{16,24},{24,28},{28,20},{20,12},{12,4},{4,0},{1,9},{9... | collective-permute-start | bytes 786440 | tf_op jit(solution)/shard_map/ppermute | solution.py:334
  51.4 7.5 %collective-permute-start.16 = (bf16[64,2048]{1,0:T(8,128)(2,1)S(1)}, bf16[64,2048]{1,0:T(8,128)(2,1)S(1)}, u32[]{:S(2)}, u32[]{:S(2)}) collective-permute-start(bf16[64,2048]{1,0:T(8,128)(2,1)S(1)} %slice.20), channel_id=1, source_target_pairs={{8,0},{16,8},{24,16},{28,24},{20,28},{12,20},{4,12},{0,4},{9,1},{1... | collective-permute-start | bytes 786440 | tf_op jit(solution)/shard_map/ppermute | solution.py:334
  54.6 12.2 %collective-permute-start.12 = (bf16[3,56,256]{2,1,0:T(8,128)(2,1)S(1)}, bf16[3,56,256]{2,1,0:T(8,128)(2,1)S(1)}, u32[]{:S(2)}, u32[]{:S(2)}) collective-permute-start(bf16[3,56,256]{2,1,0:T(8,128)(2,1)S(1)} %get-tuple-element.80), channel_id=1, source_target_pairs={{0,1},{1,0},{2,3},{3,2},{4,5},{5,4},{6,7},{7,6},{8,9},{9,8},{10,11... | collective-permute-start | bytes 258056 | tf_op jit(solution)/shard_map/ppermute | solution.py:356
  57.3 8.0 %collective-permute-start.20 = (bf16[4,1,56,128]{3,2,0,1:T(8,128)(2,1)S(1)}, bf16[4,1,56,128]{3,2,0,1:T(8,128)(2,1)S(1)}, u32[]{:S(2)}, u32[]{:S(2)}) collective-permute-start(bf16[4,1,56,128]{3,2,0,1:T(8,128)(2,1)S(1)} %get-tuple-element.117), channel_id=1, source_target_pairs={{0,4},{4,0},{8,12},{12,8},{16,20},{20,16},{24,28},{28,24},{1,5},{5... | collective-permute-start | bytes 172040 | tf_op jit(solution)/shard_map/ppermute | solution.py:382
  58.9 8.3 %collective-permute-start.13 = (bf16[3,56,256]{2,1,0:T(8,128)(2,1)S(1)}, bf16[3,56,256]{2,1,0:T(8,128)(2,1)S(1)}, u32[]{:S(2)}, u32[]{:S(2)}) collective-permute-start(bf16[3,56,256]{2,1,0:T(8,128)(2,1)S(1)} %get-tuple-element.81), channel_id=1, source_target_pairs={{0,2},{1,3},{2,0},{3,1},{4,6},{5,7},{6,4},{7,5},{8,10},{9,11},{10,... | collective-permute-start | bytes 258056 | tf_op jit(solution)/shard_map/ppermute | solution.py:356
  64.9 4.3 %collective-permute-start.14 = (bf16[3,56,256]{2,1,0:T(8,128)(2,1)S(1)}, bf16[3,56,256]{2,1,0:T(8,128)(2,1)S(1)}, u32[]{:S(2)}, u32[]{:S(2)}) collective-permute-start(bf16[3,56,256]{2,1,0:T(8,128)(2,1)S(1)} %get-tuple-element.82), channel_id=1, source_target_pairs={{0,3},{1,2},{2,1},{3,0},{4,7},{5,6},{6,5},{7,4},{8,11},{9,10},{10,... | collective-permute-start | bytes 258056 | tf_op jit(solution)/shard_map/ppermute | solution.py:356
  64.9 4.2 %collective-permute-start.17 = (bf16[3,56,128]{2,1,0:T(8,128)(2,1)S(1)}, bf16[3,56,128]{2,1,0:T(8,128)(2,1)S(1)}, u32[]{:S(2)}, u32[]{:S(2)}) collective-permute-start(bf16[3,56,128]{2,1,0:T(8,128)(2,1)S(1)} %get-tuple-element.86), channel_id=1, source_target_pairs={{0,1},{1,0},{2,3},{3,2},{4,5},{5,4},{6,7},{7,6},{8,9},{9,8},{10,11... | collective-permute-start | bytes 129032 | tf_op jit(solution)/shard_map/ppermute | solution.py:356
  65.3 3.8 %collective-permute-start.18 = (bf16[3,56,128]{2,1,0:T(8,128)(2,1)S(1)}, bf16[3,56,128]{2,1,0:T(8,128)(2,1)S(1)}, u32[]{:S(2)}, u32[]{:S(2)}) collective-permute-start(bf16[3,56,128]{2,1,0:T(8,128)(2,1)S(1)} %get-tuple-element.87), channel_id=1, source_target_pairs={{0,2},{1,3},{2,0},{3,1},{4,6},{5,7},{6,4},{7,5},{8,10},{9,11},{10,... | collective-permute-start | bytes 129032 | tf_op jit(solution)/shard_map/ppermute | solution.py:356
  66.8 3.8 %collective-permute-start.19 = (bf16[3,56,128]{2,1,0:T(8,128)(2,1)S(1)}, bf16[3,56,128]{2,1,0:T(8,128)(2,1)S(1)}, u32[]{:S(2)}, u32[]{:S(2)}) collective-permute-start(bf16[3,56,128]{2,1,0:T(8,128)(2,1)S(1)} %get-tuple-element.88), channel_id=1, source_target_pairs={{0,3},{1,2},{2,1},{3,0},{4,7},{5,6},{6,5},{7,4},{8,11},{9,10},{10,... | collective-permute-start | bytes 129032 | tf_op jit(solution)/shard_map/ppermute | solution.py:356
  76.3 1.7 %collective-permute-start.22 = (bf16[3,56,1024]{2,1,0:T(8,128)(2,1)S(1)}, bf16[3,56,1024]{2,1,0:T(8,128)(2,1)S(1)}, u32[]{:S(2)}, u32[]{:S(2)}) collective-permute-start(bf16[3,56,1024]{2,1,0:T(8,128)(2,1)S(1)} %get-tuple-element.93.refs_0_), channel_id=1, source_target_pairs={{0,1},{1,0},{2,3},{3,2},{4,5},{5,4},{6,7},{7,6},{8,9},{9,8},{10,11... | collective-permute-start | bytes 1032200 | tf_op jit(solution)/shard_map/ppermute | solution.py:457
  78.0 20.5 %copy-start.4 = (bf16[128,2048]{1,0:T(8,128)(2,1)S(1)}, bf16[128,2048]{1,0:T(8,128)(2,1)}, u32[]{:S(2)}) copy-start(bf16[128,2048]{1,0:T(8,128)(2,1)} %refs_4_.1) | copy-start | bytes 1572868
  80.8 12.1 %all-to-all-start.1 = ((f32[8,56,128]{2,1,0:T(8,128)}), f32[8,56,128]{2,1,0:T(8,128)S(1)}, u32[]{:S(2)}, u32[]{:S(2)}) async-start(f32[8,56,128]{2,1,0:T(8,128)} %broadcast_in_dim.14), calls=%async_computation.1 | async-start | bytes 458752 | tf_op jit(solution)/shard_map/all_to_all | solution.py:467
  85.6 9.3 %collective-permute-start.21 = (bf16[3,56,1024]{2,1,0:T(8,128)(2,1)}, bf16[3,56,1024]{2,1,0:T(8,128)(2,1)}, u32[]{:S(2)}, u32[]{:S(2)}) collective-permute-start(bf16[3,56,1024]{2,1,0:T(8,128)(2,1)} %copy-done.9), channel_id=1, source_target_pairs={{0,2},{1,3},{2,0},{3,1},{4,6},{5,7},{6,4},{7,5},{8,10},{9,11},{10,... | collective-permute-start | bytes 1032200 | tf_op jit(solution)/shard_map/ppermute | solution.py:452
  94.8 3.7 %collective-permute-start.23 = (bf16[3,56,1024]{2,1,0:T(8,128)(2,1)}, bf16[3,56,1024]{2,1,0:T(8,128)(2,1)S(1)}, u32[]{:S(2)}, u32[]{:S(2)}) collective-permute-start(bf16[3,56,1024]{2,1,0:T(8,128)(2,1)} %collective-permute-done.21.refs_1_), channel_id=1, source_target_pairs={{0,1},{1,0},{2,3},{3,2},{4,5},{5,4},{6,7},{7,6},{8,9},{9,8},{10,11... | collective-permute-start | bytes 1032200 | tf_op jit(solution)/shard_map/ppermute | solution.py:474
  96.3 13.1 %collective-permute-start.24 = (f32[2,56,128]{2,1,0:T(8,128)S(1)}, f32[2,56,128]{2,1,0:T(8,128)S(1)}, u32[]{:S(2)}, u32[]{:S(2)}) collective-permute-start(f32[2,56,128]{2,1,0:T(8,128)S(1)} %get-tuple-element.105), channel_id=1, source_target_pairs={{0,1},{1,0},{2,3},{3,2},{4,5},{5,4},{6,7},{7,6},{8,9},{9,8},{10,11... | collective-permute-start | bytes 172040 | tf_op jit(solution)/shard_map/ppermute | solution.py:476
  96.4 13.1 %collective-permute-start.25 = (f32[2,56,128]{2,1,0:T(8,128)S(1)}, f32[2,56,128]{2,1,0:T(8,128)S(1)}, u32[]{:S(2)}, u32[]{:S(2)}) collective-permute-start(f32[2,56,128]{2,1,0:T(8,128)S(1)} %get-tuple-element.106), channel_id=1, source_target_pairs={{0,2},{1,3},{2,0},{3,1},{4,6},{5,7},{6,4},{7,5},{8,10},{9,11},{10,... | collective-permute-start | bytes 172040 | tf_op jit(solution)/shard_map/ppermute | solution.py:476
  96.5 13.0 %collective-permute-start.26 = (f32[2,56,128]{2,1,0:T(8,128)S(1)}, f32[2,56,128]{2,1,0:T(8,128)S(1)}, u32[]{:S(2)}, u32[]{:S(2)}) collective-permute-start(f32[2,56,128]{2,1,0:T(8,128)S(1)} %get-tuple-element.107), channel_id=1, source_target_pairs={{0,3},{1,2},{2,1},{3,0},{4,7},{5,6},{6,5},{7,4},{8,11},{9,10},{10,... | collective-permute-start | bytes 172040 | tf_op jit(solution)/shard_map/ppermute | solution.py:476
  (12 other events, 32.0 us)

commit v9 on v6

--- a/solution.py
+++ b/solution.py
@@ -115,7 +115,7 @@
         )
     rows = weight_ref.shape[1]
     for step, out_ref in enumerate(out_refs):
-        start = part_start((place_ref[1] + step) % len(out_refs), part, rows)
+        start = part_start(place_ref[1] ^ step, part, rows)
         out_ref[...] = sums_ref[:, pl.ds(start, part), :].astype(out_ref.dtype)
 
 
@@ -211,8 +211,7 @@
 
 def share_start(own, share, shares, part, rows):
     core, step = share // (shares // 2), 2 * (share % (shares // 2))
-    owner = own + core * (1 - 2 * (own % 2))
-    return part_start((owner - step + shares) % shares, part, rows)
+    return part_start(own ^ core ^ step, part, rows)
 
 
 def weight_kernel(place_ref, *refs, shares):
@@ -335,7 +334,7 @@
 
     def to_owners(sums):
         return [sums[0]] + [
-            lax.ppermute(sums[d], "ch", [(h, (h + d) % n_ch) for h in range(n_ch)])
+            lax.ppermute(sums[d], "ch", [(h, h ^ d) for h in range(n_ch)])
             for d in range(1, n_ch)
         ]
 
@@ -366,8 +365,8 @@
         if step == 2:
             pair, upper = lax.optimization_barrier((pair, upper))
         else:
-            pair, sums[0] = lax.optimization_barrier((pair, sums[0]))
-            partials[-n_ch] = sums[0]
+            pair, near = lax.optimization_barrier((pair, partials[1 - n_ch]))
+            partials[1 - n_ch] = near
         pieces += pair
         waiting += pair
         if step < n_seq // 2 - 1:
@@ -407,7 +406,7 @@
 
     def chips(array):
         return [
-            lax.ppermute(array, "ch", [(h, (h + d) % n_ch) for h in range(n_ch)])
+            lax.ppermute(array, "ch", [(h, h ^ d) for h in range(n_ch)])
             for d in range(2, n_ch, 2)
         ]
 

time: 105 us -> 104 us (level)
  starting transfers between devices: 39.6 us -> 36 us
  waiting for transfers between devices: 20.5 us -> 22.9 us
    ppermute x11, waiting for transfers between devices: 8.45 us -> 12.5 us  [the longest x2 7.02 us: chips(): lax.ppermute(array, 'ch', [(h, h ^ d) for h in range(n_ch)])]
    ppermute x11, starting transfers between devices: 14.3 us -> 10.4 us  [the longest x9 8.22 us: to_owners(): lax.ppermute(sums[d], 'ch', [(h, h ^ d) for h in range(n_ch)])]
    ppermute x4, waiting for transfers between devices: 4.04 us -> 2.5 us  [send_on(): lax.ppermute(pair[0], 'seq', ahead)]
  transfers between devices with their start and end apart: 27 -> 27, of which waited for: 10 -> 11; matrix products, arithmetic and copies ran while one was open for 1% -> 1% of each run, Pallas kernels for 17% -> 17%
where the time goes in v9:
time: 104 us; the launch traced here: 103 us
  starting transfers between devices  36 us (35%)
  Pallas kernels  24.6 us (24%)
  waiting for transfers between devices  22.9 us (22%)
  blocking collectives  14.2 us (14%)
  local copies, waits for them, and re-layouts  3.83 us (4%)
    pallas_call x10, Pallas kernels, call(): pl.pallas_call(kernel, out_shape=outs, in_specs=specs, out_specs=[whole]...  18.9 us
    all_to_all x1, blocking collectives, local(): lax.all_to_all(upper, 'seq', split_axis=0, concat_axis=0, tiled=True)  14.2 us
    ppermute x9, starting transfers between devices, to_owners(): lax.ppermute(sums[d], 'ch', [(h, h ^ d) for h in range(n_ch)])  8.22 us
    ppermute x2, waiting for transfers between devices, chips(): lax.ppermute(array, 'ch', [(h, h ^ d) for h in range(n_ch)])  7.02 us
    ppermute x4, starting transfers between devices, send_on(): lax.ppermute(pair[1], 'seq', behind)  6.48 us
    ppermute x2, starting transfers between devices, local(): blocks.append(lax.ppermute(block_sums, ('seq', 'ch'), route))  6.08 us
    pallas_call x1, Pallas kernels, local(): pl.pallas_call(functools.partial(weight_kernel, shares=n_ch), out_shape=j...  5.73 us
    ppermute x9, waiting for transfers between devices, to_owners(): lax.ppermute(sums[d], 'ch', [(h, h ^ d) for h in range(n_ch)])  5.46 us
  transfers between devices with their start and end apart: 27, of which 11 were waited for; matrix products, arithmetic and copies ran while one was open for 1% of the time, Pallas kernels for 17%

profile of v9, /device:TPU:4, one launch (start us, length us, event | category | flops | bytes accessed | tf_op | source)
XLA Modules:
  0.0 103.3 jit_solution(8798203597190084871)
XLA Ops:
  0.6 1.6 %collective-permute-start = (bf16[128,2048]{1,0:T(8,128)(2,1)}, bf16[128,2048]{1,0:T(8,128)(2,1)S(1)}, u32[]{:S(2)}, u32[]{:S(2)}) collective-permute-start(bf16[128,2048]{1,0:T(8,128)(2,1)} %refs_4_.1), channel_id=1, source_target_pairs={{0,8},{8,16},{16,24},{24,28},{28,20},{20,12},{12,4},{4,0},{1,9},{9... | collective-permute-start | bytes 1572872 | tf_op jit(solution)/shard_map/ppermute | solution.py:315
  5.8 3.3 %all-to-all-start = ((bf16[4,2,56,128]{3,2,1,0:T(8,128)(2,1)}), bf16[4,2,56,128]{3,2,1,0:T(8,128)(2,1)S(1)}, u32[]{:S(2)}, u32[]{:S(2)}) async-start(bf16[4,2,56,128]{3,2,1,0:T(8,128)(2,1)} %shard_map.121), calls=%async_computation | async-start | bytes 229376 | tf_op jit(solution)/shard_map/all_to_all | solution.py:355
  9.2 4.4 %collective-permute-start.2 = (f32[56,33]{1,0:T(8,128)S(1)}, f32[56,33]{1,0:T(8,128)S(1)}, u32[]{:S(2)}, u32[]{:S(2)}) collective-permute-start(f32[56,33]{1,0:T(8,128)S(1)} %shard_map.120), channel_id=1, source_target_pairs={{0,0},{4,1},{8,2},{12,3},{16,4},{20,5},{24,6},{28,7},{1,8},{5,9},{... | collective-permute-start | bytes 22184 | tf_op jit(solution)/shard_map/ppermute | solution.py:350
  13.6 2.5 %collective-permute-done.2.poles_ref.refs_13_ = f32[56,33]{1,0:T(8,128)S(1)} collective-permute-done((f32[56,33]{1,0:T(8,128)S(1)}, f32[56,33]{1,0:T(8,128)S(1)}, u32[]{:S(2)}, u32[]{:S(2)}) %collective-permute-start.2) | collective-permute-done | bytes 7424 | tf_op jit(solution)/shard_map/ppermute | solution.py:350
  16.1 1.3 %collective-permute-start.3 = (bf16[128,2048]{1,0:T(8,128)(2,1)S(1)}, bf16[128,2048]{1,0:T(8,128)(2,1)S(1)}, u32[]{:S(2)}, u32[]{:S(2)}) collective-permute-start(bf16[128,2048]{1,0:T(8,128)(2,1)S(1)} %collective-permute-done.refs_1_.refs_5_), channel_id=1, source_target_pairs={{0,8},{8,16},{16,24},{24,28},{28,20},{20,12},{12,4},{4,0},{1,9},{9... | collective-permute-start | bytes 1572872 | tf_op jit(solution)/shard_map/ppermute | solution.py:315
  17.4 3.3 %collective-permute-start.4 = (bf16[128,2048]{1,0:T(8,128)(2,1)S(1)}, bf16[128,2048]{1,0:T(8,128)(2,1)S(1)}, u32[]{:S(2)}, u32[]{:S(2)}) collective-permute-start(bf16[128,2048]{1,0:T(8,128)(2,1)S(1)} %collective-permute-done.1.refs_2_.refs_6_), channel_id=1, source_target_pairs={{8,0},{16,8},{24,16},{28,24},{20,28},{12,20},{4,12},{0,4},{9,1},{1... | collective-permute-start | bytes 1572872 | tf_op jit(solution)/shard_map/ppermute | solution.py:315
  20.7 14.2 %all_to_all.10.refs_12_ = bf16[8,56,128]{2,1,0:T(8,128)(2,1)S(1)} all-to-all(bf16[8,56,128]{2,1,0:T(8,128)(2,1)S(1)} %bitcast.13), channel_id=1, replica_groups=mesh['seq'=8,'ch'=4] {'seq'}, dimensions={0} | all-to-all | bytes 229376 | tf_op jit(solution)/shard_map/all_to_all | solution.py:358
  35.9 1.1 %collective-permute-start.6 = (bf16[128,2048]{1,0:T(8,128)(2,1)S(1)}, bf16[128,2048]{1,0:T(8,128)(2,1)S(1)}, u32[]{:S(2)}, u32[]{:S(2)}) collective-permute-start(bf16[128,2048]{1,0:T(8,128)(2,1)S(1)} %collective-permute-done.4.refs_4_.refs_8_), channel_id=1, source_target_pairs={{8,0},{16,8},{24,16},{28,24},{20,28},{12,20},{4,12},{0,4},{9,1},{1... | collective-permute-start | bytes 1572872 | tf_op jit(solution)/shard_map/ppermute | solution.py:315
  37.0 1.7 %copy-done = bf16[208,3,2048]{2,0,1:T(8,128)(2,1)S(1)} copy-done((bf16[208,3,2048]{2,0,1:T(8,128)(2,1)S(1)}, bf16[208,3,2048]{2,0,1:T(8,128)(2,1)}, u32[]{:S(2)}) %copy-start) | copy-done | bytes 2555928
  38.7 1.0 %copy-done.3 = bf16[128,2048]{1,0:T(8,128)(2,1)S(1)} copy-done((bf16[128,2048]{1,0:T(8,128)(2,1)S(1)}, bf16[128,2048]{1,0:T(8,128)(2,1)}, u32[]{:S(2)}) %copy-start.3) | copy-done | bytes 524312
  39.8 3.4 %shard_map.122 = (f32[3,56,640]{2,1,0:T(8,128)S(1)}, bf16[3,56,640]{2,1,0:T(8,128)(2,1)S(1)}, bf16[3,56,640]{2,1,0:T(8,128)(2,1)S(1)}, bf16[3,56,640]{2,1,0:T(8,128)(2,1)S(1)}) custom-call(s32[2]{0:T(128)S(1)} %pad_add_fusion.place_ref, bf16[3,208,2048]{2,1,0:T(8,128)(2,1)S(1)} %bitcast.9, bf16[128,2048]{1,0:T(8,128)(2,1)S(1)} %copy-done.3, ...), custom_call_target="tpu_custom_call" | custom-call | flops 1635778560 | bytes 6252552 | tf_op jit(solution)/shard_map/pallas_call | solution.py:279
  43.3 1.5 %collective-permute-done.7.refs_1_ = bf16[3,56,640]{2,1,0:T(8,128)(2,1)S(1)} collective-permute-done((bf16[3,56,640]{2,1,0:T(8,128)(2,1)S(1)}, bf16[3,56,640]{2,1,0:T(8,128)(2,1)S(1)}, u32[]{:S(2)}, u32[]{:S(2)}) %collective-permute-start.7) | collective-permute-done | bytes 215072 | tf_op jit(solution)/shard_map/ppermute | solution.py:337
  44.7 2.5 %collective-permute-done.5.refs_0_.refs_9_ = bf16[128,2048]{1,0:T(8,128)(2,1)S(1)} collective-permute-done((bf16[128,2048]{1,0:T(8,128)(2,1)S(1)}, bf16[128,2048]{1,0:T(8,128)(2,1)S(1)}, u32[]{:S(2)}, u32[]{:S(2)}) %collective-permute-start.5) | collective-permute-done | bytes 524320 | tf_op jit(solution)/shard_map/ppermute | solution.py:315
  48.3 1.7 %collective-permute-start.14 = (bf16[64,2048]{1,0:T(8,128)(2,1)S(1)}, bf16[64,2048]{1,0:T(8,128)(2,1)S(1)}, u32[]{:S(2)}, u32[]{:S(2)}) collective-permute-start(bf16[64,2048]{1,0:T(8,128)(2,1)S(1)} %slice.7), channel_id=1, source_target_pairs={{8,0},{16,8},{24,16},{28,24},{20,28},{12,20},{4,12},{0,4},{9,1},{1... | collective-permute-start | bytes 786440 | tf_op jit(solution)/shard_map/ppermute | solution.py:315
  50.0 3.1 %collective-permute-start.8 = (bf16[3,56,640]{2,1,0:T(8,128)(2,1)S(1)}, bf16[3,56,640]{2,1,0:T(8,128)(2,1)S(1)}, u32[]{:S(2)}, u32[]{:S(2)}) collective-permute-start(bf16[3,56,640]{2,1,0:T(8,128)(2,1)S(1)} %get-tuple-element.57), channel_id=1, source_target_pairs={{0,2},{1,3},{2,0},{3,1},{4,6},{5,7},{6,4},{7,5},{8,10},{9,11},{10,... | collective-permute-start | bytes 645128 | tf_op jit(solution)/shard_map/ppermute | solution.py:337
  53.1 1.8 %shard_map.123 = (f32[3,56,256]{2,1,0:T(8,128)S(1)}, bf16[3,56,256]{2,1,0:T(8,128)(2,1)S(1)}, bf16[3,56,256]{2,1,0:T(8,128)(2,1)S(1)}, bf16[3,56,256]{2,1,0:T(8,128)(2,1)S(1)}) custom-call(s32[2]{0:T(128)S(1)} %pad_add_fusion.place_ref, bf16[3,208,2048]{2,1,0:T(8,128)(2,1)S(1)} %bitcast.10, bf16[128,2048]{1,0:T(8,128)(2,1)S(1)} %collective-permute-done.5.refs_0_.refs_9_, ...), custom_call_target="tpu_custom_call" | custom-call | flops 654311424 | bytes 4034568 | tf_op jit(solution)/shard_map/pallas_call | solution.py:279
  55.2 2.3 %collective-permute-start.11 = (bf16[3,56,256]{2,1,0:T(8,128)(2,1)S(1)}, bf16[3,56,256]{2,1,0:T(8,128)(2,1)S(1)}, u32[]{:S(2)}, u32[]{:S(2)}) collective-permute-start(bf16[3,56,256]{2,1,0:T(8,128)(2,1)S(1)} %get-tuple-element.65), channel_id=1, source_target_pairs={{0,2},{1,3},{2,0},{3,1},{4,6},{5,7},{6,4},{7,5},{8,10},{9,11},{10,... | collective-permute-start | bytes 258056 | tf_op jit(solution)/shard_map/ppermute | solution.py:337
  57.5 1.4 %shard_map.124 = (f32[3,56,128]{2,1,0:T(8,128)S(1)}, bf16[3,56,128]{2,1,0:T(8,128)(2,1)S(1)}, bf16[3,56,128]{2,1,0:T(8,128)(2,1)S(1)}, bf16[3,56,128]{2,1,0:T(8,128)(2,1)S(1)}) custom-call(s32[2]{0:T(128)S(1)} %pad_add_fusion.place_ref, bf16[3,208,2048]{2,1,0:T(8,128)(2,1)S(1)} %bitcast.11, bf16[64,2048]{1,0:T(8,128)(2,1)S(1)} %collective-permute-done.13.refs_0_.refs_11_, ...), custom_call_target="tpu_custom_call" | custom-call | flops 327155712 | bytes 3295240 | tf_op jit(solution)/shard_map/pallas_call | solution.py:279
  59.5 3.0 %collective-permute-done.9.refs_3_ = bf16[3,56,640]{2,1,0:T(8,128)(2,1)S(1)} collective-permute-done((bf16[3,56,640]{2,1,0:T(8,128)(2,1)S(1)}, bf16[3,56,640]{2,1,0:T(8,128)(2,1)S(1)}, u32[]{:S(2)}, u32[]{:S(2)}) %collective-permute-start.9) | collective-permute-done | bytes 215072 | tf_op jit(solution)/shard_map/ppermute | solution.py:337
  62.4 1.9 %collective-permute-start.17 = (bf16[3,56,128]{2,1,0:T(8,128)(2,1)S(1)}, bf16[3,56,128]{2,1,0:T(8,128)(2,1)S(1)}, u32[]{:S(2)}, u32[]{:S(2)}) collective-permute-start(bf16[3,56,128]{2,1,0:T(8,128)(2,1)S(1)} %get-tuple-element.72), channel_id=1, source_target_pairs={{0,3},{1,2},{2,1},{3,0},{4,7},{5,6},{6,5},{7,4},{8,11},{9,10},{10,... | collective-permute-start | bytes 129032 | tf_op jit(solution)/shard_map/ppermute | solution.py:337
  64.4 1.5 %shard_map.125 = (f32[56,1024]{1,0:T(8,128)S(1)}, f32[56,1024]{1,0:T(8,128)S(1)}) custom-call(f32[56,33]{1,0:T(8,128)S(1)} %collective-permute-done.2.poles_ref.refs_13_, bf16[1024,1024]{1,0:T(8,128)(2,1)S(1)} %copy-done.1, bf16[1024,1024]{1,0:T(8,128)(2,1)S(1)} %copy-done.2, f32[2,1024]{1,0:T(2,128)S(1)} %copy-done.6), custom_call_target="tpu_custom_call" | custom-call | flops 469762048 | bytes 4668640 | tf_op jit(solution)/shard_map/pallas_call | solution.py:279
  67.0 5.6 %shard_map.126 = (bf16[3,56,1024]{2,1,0:T(8,128)(2,1)S(1)}, f32[56,1024]{1,0:T(8,128)S(1)}, f32[56,1024]{1,0:T(8,128)S(1)}, f32[56,1]{1,0:T(8,128)S(1)}) custom-call(s32[2]{0:T(128)S(1)} %pad_add_fusion.place_ref, f32[3,56,640]{2,1,0:T(8,128)S(1)} %get-tuple-element.54.refs_0_, bf16[3,56,640]{2,1,0:T(8,128)(2,1)S(1)} %collective-permute-done.7.refs_1_, ...), custom_call_target="tpu_custom_call" | custom-call | flops 1879048192 | bytes 7306696 | tf_op jit(solution)/shard_map/pallas_call | solution.py:279
  72.6 1.7 %collective-permute-start.18 = (bf16[3,56,1024]{2,1,0:T(8,128)(2,1)S(1)}, bf16[3,56,1024]{2,1,0:T(8,128)(2,1)S(1)}, u32[]{:S(2)}, u32[]{:S(2)}) collective-permute-start(bf16[3,56,1024]{2,1,0:T(8,128)(2,1)S(1)} %get-tuple-element.77.refs_0_), channel_id=1, source_target_pairs={{0,2},{1,3},{2,0},{3,1},{4,6},{5,7},{6,4},{7,5},{8,10},{9,11},{10,... | collective-permute-start | bytes 1032200 | tf_op jit(solution)/shard_map/ppermute | solution.py:409
  74.3 2.0 %shard_map.127.refs_0_ = f32[56,33]{1,0:T(8,128)S(1)} custom-call(f32[56,33]{1,0:T(8,128)S(1)} %collective-permute-done.2.poles_ref.refs_13_, f32[56,1024]{1,0:T(8,128)S(1)} %get-tuple-element.78.tgc_ref, f32[56,1024]{1,0:T(8,128)S(1)} %get-tuple-element.79.tgs_ref, bf16[1024,1024]{1,0:T(8,128)(2,1)S(1)} %copy-done.1, bf16[1024,1024]{1,0:T(8,128)(2,1)S(1)} %copy-done.2, ...), custom_call_target="tpu_custom_call" | custom-call | flops 469762048 | bytes 4668064 | tf_op jit(solution)/shard_map/pallas_call | solution.py:279
  77.2 7.0 %collective-permute-done.19.refs_1_ = f32[56,33]{1,0:T(8,128)S(1)} collective-permute-done((f32[56,33]{1,0:T(8,128)S(1)}, f32[56,33]{1,0:T(8,128)S(1)}, u32[]{:S(2)}, u32[]{:S(2)}) %collective-permute-start.19) | collective-permute-done | bytes 7424 | tf_op jit(solution)/shard_map/ppermute | solution.py:409
  84.8 1.1 %collective-permute-done.22.refs_2_ = f32[56,33]{1,0:T(8,128)S(1)} collective-permute-done((f32[56,33]{1,0:T(8,128)S(1)}, f32[56,33]{1,0:T(8,128)S(1)}, u32[]{:S(2)}, u32[]{:S(2)}) %collective-permute-start.22) | collective-permute-done | bytes 7424 | tf_op jit(solution)/shard_map/ppermute | solution.py:424
  86.5 2.9 %collective-permute-start.24 = (f32[208,33]{1,0:T(8,128)S(1)}, f32[208,33]{1,0:T(8,128)S(1)}, u32[]{:S(2)}, u32[]{:S(2)}) collective-permute-start(f32[208,33]{1,0:T(8,128)S(1)} %shard_map.129), channel_id=1, source_target_pairs={{0,0},{8,1},{16,2},{24,3},{4,4},{12,5},{20,6},{28,7},{1,8},{9,9},{... | collective-permute-start | bytes 82376 | tf_op jit(solution)/shard_map/ppermute | solution.py:437
  89.4 3.2 %collective-permute-start.25 = (f32[208,33]{1,0:T(8,128)S(1)}, f32[208,33]{1,0:T(8,128)S(1)}, u32[]{:S(2)}, u32[]{:S(2)}) collective-permute-start(f32[208,33]{1,0:T(8,128)S(1)} %shard_map.129), channel_id=1, source_target_pairs={{4,0},{12,1},{20,2},{28,3},{0,4},{8,5},{16,6},{24,7},{5,8},{13,9},... | collective-permute-start | bytes 82376 | tf_op jit(solution)/shard_map/ppermute | solution.py:437
  92.6 5.7 %shard_map.128 = f32[3,208,2048]{2,1,0:T(8,128)} custom-call(s32[2]{0:T(128)S(1)} %pad_add_fusion.place_ref, bf16[3,56,1024]{2,1,0:T(8,128)(2,1)S(1)} %get-tuple-element.77.refs_0_, bf16[3,56,1024]{2,1,0:T(8,128)(2,1)S(1)} %collective-permute-done.18.refs_1_, bf16[3,56,1024]{2,1,0:T(8,128)(2,1)S(1)} %collective-permute-done.20.refs_2_, ...), custom_call_target="tpu_custom_call" | custom-call | flops 2617245696 | bytes 10584064 | tf_op jit(solution)/shard_map/pallas_call | solution.py:440
  98.3 1.4 %collective-permute-done.24.refs_0_ = f32[208,33]{1,0:T(8,128)S(1)} collective-permute-done((f32[208,33]{1,0:T(8,128)S(1)}, f32[208,33]{1,0:T(8,128)S(1)}, u32[]{:S(2)}, u32[]{:S(2)}) %collective-permute-start.24) | collective-permute-done | bytes 27488 | tf_op jit(solution)/shard_map/ppermute | solution.py:437
  99.7 2.3 %collective-permute-done.25.refs_1_ = f32[208,33]{1,0:T(8,128)S(1)} collective-permute-done((f32[208,33]{1,0:T(8,128)S(1)}, f32[208,33]{1,0:T(8,128)S(1)}, u32[]{:S(2)}, u32[]{:S(2)}) %collective-permute-start.25) | collective-permute-done | bytes 27488 | tf_op jit(solution)/shard_map/ppermute | solution.py:437
  102.0 1.3 %shard_map.130 = (f32[16,416]{1,0:T(8,128)}, f32[16,416]{1,0:T(8,128)}, f32[1,416]{1,0:T(1,128)}) custom-call(s32[2]{0:T(128)S(1)} %pad_add_fusion.place_ref, f32[208,33]{1,0:T(8,128)S(1)} %collective-permute-done.24.refs_0_, f32[208,33]{1,0:T(8,128)S(1)} %collective-permute-done.25.refs_1_), custom_call_target="tpu_custom_call" | custom-call | bytes 109832 | tf_op jit(solution)/shard_map/pallas_call | solution.py:279
  (53 shorter events, 9.5 us)
Async XLA Ops:
  0.6 15.5 %collective-permute-start = (bf16[128,2048]{1,0:T(8,128)(2,1)}, bf16[128,2048]{1,0:T(8,128)(2,1)S(1)}, u32[]{:S(2)}, u32[]{:S(2)}) collective-permute-start(bf16[128,2048]{1,0:T(8,128)(2,1)} %refs_4_.1), channel_id=1, source_target_pairs={{0,8},{8,16},{16,24},{24,28},{28,20},{20,12},{12,4},{4,0},{1,9},{9... | collective-permute-start | bytes 1572872 | tf_op jit(solution)/shard_map/ppermute | solution.py:315
  2.3 13.9 %collective-permute-start.1 = (bf16[128,2048]{1,0:T(8,128)(2,1)}, bf16[128,2048]{1,0:T(8,128)(2,1)S(1)}, u32[]{:S(2)}, u32[]{:S(2)}) collective-permute-start(bf16[128,2048]{1,0:T(8,128)(2,1)} %refs_4_.1), channel_id=1, source_target_pairs={{8,0},{16,8},{24,16},{28,24},{20,28},{12,20},{4,12},{0,4},{9,1},{1... | collective-permute-start | bytes 1572872 | tf_op jit(solution)/shard_map/ppermute | solution.py:315
  5.8 10.3 %all-to-all-start = ((bf16[4,2,56,128]{3,2,1,0:T(8,128)(2,1)}), bf16[4,2,56,128]{3,2,1,0:T(8,128)(2,1)S(1)}, u32[]{:S(2)}, u32[]{:S(2)}) async-start(bf16[4,2,56,128]{3,2,1,0:T(8,128)(2,1)} %shard_map.121), calls=%async_computation | async-start | bytes 229376 | tf_op jit(solution)/shard_map/all_to_all | solution.py:355
  9.2 6.9 %collective-permute-start.2 = (f32[56,33]{1,0:T(8,128)S(1)}, f32[56,33]{1,0:T(8,128)S(1)}, u32[]{:S(2)}, u32[]{:S(2)}) collective-permute-start(f32[56,33]{1,0:T(8,128)S(1)} %shard_map.120), channel_id=1, source_target_pairs={{0,0},{4,1},{8,2},{12,3},{16,4},{20,5},{24,6},{28,7},{1,8},{5,9},{... | collective-permute-start | bytes 22184 | tf_op jit(solution)/shard_map/ppermute | solution.py:350
  16.1 18.8 %collective-permute-start.3 = (bf16[128,2048]{1,0:T(8,128)(2,1)S(1)}, bf16[128,2048]{1,0:T(8,128)(2,1)S(1)}, u32[]{:S(2)}, u32[]{:S(2)}) collective-permute-start(bf16[128,2048]{1,0:T(8,128)(2,1)S(1)} %collective-permute-done.refs_1_.refs_5_), channel_id=1, source_target_pairs={{0,8},{8,16},{16,24},{24,28},{28,20},{20,12},{12,4},{4,0},{1,9},{9... | collective-permute-start | bytes 1572872 | tf_op jit(solution)/shard_map/ppermute | solution.py:315
  17.4 17.5 %collective-permute-start.4 = (bf16[128,2048]{1,0:T(8,128)(2,1)S(1)}, bf16[128,2048]{1,0:T(8,128)(2,1)S(1)}, u32[]{:S(2)}, u32[]{:S(2)}) collective-permute-start(bf16[128,2048]{1,0:T(8,128)(2,1)S(1)} %collective-permute-done.1.refs_2_.refs_6_), channel_id=1, source_target_pairs={{8,0},{16,8},{24,16},{28,24},{20,28},{12,20},{4,12},{0,4},{9,1},{1... | collective-permute-start | bytes 1572872 | tf_op jit(solution)/shard_map/ppermute | solution.py:315
  35.0 12.3 %collective-permute-start.5 = (bf16[128,2048]{1,0:T(8,128)(2,1)S(1)}, bf16[128,2048]{1,0:T(8,128)(2,1)S(1)}, u32[]{:S(2)}, u32[]{:S(2)}) collective-permute-start(bf16[128,2048]{1,0:T(8,128)(2,1)S(1)} %collective-permute-done.3.refs_3_.refs_7_), channel_id=1, source_target_pairs={{0,8},{8,16},{16,24},{24,28},{28,20},{20,12},{12,4},{4,0},{1,9},{9... | collective-permute-start | bytes 1572872 | tf_op jit(solution)/shard_map/ppermute | solution.py:315
  35.9 11.9 %collective-permute-start.6 = (bf16[128,2048]{1,0:T(8,128)(2,1)S(1)}, bf16[128,2048]{1,0:T(8,128)(2,1)S(1)}, u32[]{:S(2)}, u32[]{:S(2)}) collective-permute-start(bf16[128,2048]{1,0:T(8,128)(2,1)S(1)} %collective-permute-done.4.refs_4_.refs_8_), channel_id=1, source_target_pairs={{8,0},{16,8},{24,16},{28,24},{20,28},{12,20},{4,12},{0,4},{9,1},{1... | collective-permute-start | bytes 1572872 | tf_op jit(solution)/shard_map/ppermute | solution.py:315
  37.0 1.7 %copy-start = (bf16[208,3,2048]{2,0,1:T(8,128)(2,1)S(1)}, bf16[208,3,2048]{2,0,1:T(8,128)(2,1)}, u32[]{:S(2)}) copy-start(bf16[208,3,2048]{2,0,1:T(8,128)(2,1)} %param.10) | copy-start | bytes 7667716
  43.2 1.5 %collective-permute-start.7 = (bf16[3,56,640]{2,1,0:T(8,128)(2,1)S(1)}, bf16[3,56,640]{2,1,0:T(8,128)(2,1)S(1)}, u32[]{:S(2)}, u32[]{:S(2)}) collective-permute-start(bf16[3,56,640]{2,1,0:T(8,128)(2,1)S(1)} %get-tuple-element.55), channel_id=1, source_target_pairs={{0,1},{1,0},{2,3},{3,2},{4,5},{5,4},{6,7},{7,6},{8,9},{9,8},{10,11... | collective-permute-start | bytes 645128 | tf_op jit(solution)/shard_map/ppermute | solution.py:337
  47.9 7.3 %collective-permute-start.13 = (bf16[64,2048]{1,0:T(8,128)(2,1)S(1)}, bf16[64,2048]{1,0:T(8,128)(2,1)S(1)}, u32[]{:S(2)}, u32[]{:S(2)}) collective-permute-start(bf16[64,2048]{1,0:T(8,128)(2,1)S(1)} %slice.6), channel_id=1, source_target_pairs={{0,8},{8,16},{16,24},{24,28},{28,20},{20,12},{12,4},{4,0},{1,9},{9... | collective-permute-start | bytes 786440 | tf_op jit(solution)/shard_map/ppermute | solution.py:315
  48.3 9.2 %collective-permute-start.14 = (bf16[64,2048]{1,0:T(8,128)(2,1)S(1)}, bf16[64,2048]{1,0:T(8,128)(2,1)S(1)}, u32[]{:S(2)}, u32[]{:S(2)}) collective-permute-start(bf16[64,2048]{1,0:T(8,128)(2,1)S(1)} %slice.7), channel_id=1, source_target_pairs={{8,0},{16,8},{24,16},{28,24},{20,28},{12,20},{4,12},{0,4},{9,1},{1... | collective-permute-start | bytes 786440 | tf_op jit(solution)/shard_map/ppermute | solution.py:315
  50.0 9.0 %collective-permute-start.8 = (bf16[3,56,640]{2,1,0:T(8,128)(2,1)S(1)}, bf16[3,56,640]{2,1,0:T(8,128)(2,1)S(1)}, u32[]{:S(2)}, u32[]{:S(2)}) collective-permute-start(bf16[3,56,640]{2,1,0:T(8,128)(2,1)S(1)} %get-tuple-element.57), channel_id=1, source_target_pairs={{0,2},{1,3},{2,0},{3,1},{4,6},{5,7},{6,4},{7,5},{8,10},{9,11},{10,... | collective-permute-start | bytes 645128 | tf_op jit(solution)/shard_map/ppermute | solution.py:337
  53.1 11.3 %copy-start.1 = (bf16[1024,1024]{1,0:T(8,128)(2,1)S(1)}, bf16[1024,1024]{1,0:T(8,128)(2,1)}, u32[]{:S(2)}) copy-start(bf16[1024,1024]{1,0:T(8,128)(2,1)} %constant.15.clone.cos_ref.refs_16_) | copy-start | bytes 6291460
  53.1 11.3 %copy-start.2 = (bf16[1024,1024]{1,0:T(8,128)(2,1)S(1)}, bf16[1024,1024]{1,0:T(8,128)(2,1)}, u32[]{:S(2)}) copy-start(bf16[1024,1024]{1,0:T(8,128)(2,1)} %constant.16.clone.sin_ref.refs_17_) | copy-start | bytes 6291460
  53.1 11.3 %copy-start.6 = (f32[2,1024]{1,0:T(2,128)S(1)}, f32[2,1024]{1,0:T(2,128)}, u32[]{:S(2)}) copy-start(f32[2,1024]{1,0:T(2,128)} %constant.17.clone.twist_ref.refs_18_) | copy-start | bytes 24580
  53.1 9.3 %collective-permute-start.9 = (bf16[3,56,640]{2,1,0:T(8,128)(2,1)S(1)}, bf16[3,56,640]{2,1,0:T(8,128)(2,1)S(1)}, u32[]{:S(2)}, u32[]{:S(2)}) collective-permute-start(bf16[3,56,640]{2,1,0:T(8,128)(2,1)S(1)} %get-tuple-element.58), channel_id=1, source_target_pairs={{0,3},{1,2},{2,1},{3,0},{4,7},{5,6},{6,5},{7,4},{8,11},{9,10},{10,... | collective-permute-start | bytes 645128 | tf_op jit(solution)/shard_map/ppermute | solution.py:337
  54.9 7.5 %collective-permute-start.10 = (bf16[3,56,256]{2,1,0:T(8,128)(2,1)S(1)}, bf16[3,56,256]{2,1,0:T(8,128)(2,1)S(1)}, u32[]{:S(2)}, u32[]{:S(2)}) collective-permute-start(bf16[3,56,256]{2,1,0:T(8,128)(2,1)S(1)} %get-tuple-element.64), channel_id=1, source_target_pairs={{0,1},{1,0},{2,3},{3,2},{4,5},{5,4},{6,7},{7,6},{8,9},{9,8},{10,11... | collective-permute-start | bytes 258056 | tf_op jit(solution)/shard_map/ppermute | solution.py:337
  55.2 10.7 %collective-permute-start.11 = (bf16[3,56,256]{2,1,0:T(8,128)(2,1)S(1)}, bf16[3,56,256]{2,1,0:T(8,128)(2,1)S(1)}, u32[]{:S(2)}, u32[]{:S(2)}) collective-permute-start(bf16[3,56,256]{2,1,0:T(8,128)(2,1)S(1)} %get-tuple-element.65), channel_id=1, source_target_pairs={{0,2},{1,3},{2,0},{3,1},{4,6},{5,7},{6,4},{7,5},{8,10},{9,11},{10,... | collective-permute-start | bytes 258056 | tf_op jit(solution)/shard_map/ppermute | solution.py:337
  57.5 8.4 %collective-permute-start.12 = (bf16[3,56,256]{2,1,0:T(8,128)(2,1)S(1)}, bf16[3,56,256]{2,1,0:T(8,128)(2,1)S(1)}, u32[]{:S(2)}, u32[]{:S(2)}) collective-permute-start(bf16[3,56,256]{2,1,0:T(8,128)(2,1)S(1)} %get-tuple-element.66), channel_id=1, source_target_pairs={{0,3},{1,2},{2,1},{3,0},{4,7},{5,6},{6,5},{7,4},{8,11},{9,10},{10,... | collective-permute-start | bytes 258056 | tf_op jit(solution)/shard_map/ppermute | solution.py:337
  59.0 7.0 %collective-permute-start.15 = (bf16[3,56,128]{2,1,0:T(8,128)(2,1)S(1)}, bf16[3,56,128]{2,1,0:T(8,128)(2,1)S(1)}, u32[]{:S(2)}, u32[]{:S(2)}) collective-permute-start(bf16[3,56,128]{2,1,0:T(8,128)(2,1)S(1)} %get-tuple-element.70), channel_id=1, source_target_pairs={{0,1},{1,0},{2,3},{3,2},{4,5},{5,4},{6,7},{7,6},{8,9},{9,8},{10,11... | collective-permute-start | bytes 129032 | tf_op jit(solution)/shard_map/ppermute | solution.py:337
  62.4 4.4 %collective-permute-start.16 = (bf16[3,56,128]{2,1,0:T(8,128)(2,1)S(1)}, bf16[3,56,128]{2,1,0:T(8,128)(2,1)S(1)}, u32[]{:S(2)}, u32[]{:S(2)}) collective-permute-start(bf16[3,56,128]{2,1,0:T(8,128)(2,1)S(1)} %get-tuple-element.71), channel_id=1, source_target_pairs={{0,2},{1,3},{2,0},{3,1},{4,6},{5,7},{6,4},{7,5},{8,10},{9,11},{10,... | collective-permute-start | bytes 129032 | tf_op jit(solution)/shard_map/ppermute | solution.py:337
  62.4 4.5 %collective-permute-start.17 = (bf16[3,56,128]{2,1,0:T(8,128)(2,1)S(1)}, bf16[3,56,128]{2,1,0:T(8,128)(2,1)S(1)}, u32[]{:S(2)}, u32[]{:S(2)}) collective-permute-start(bf16[3,56,128]{2,1,0:T(8,128)(2,1)S(1)} %get-tuple-element.72), channel_id=1, source_target_pairs={{0,3},{1,2},{2,1},{3,0},{4,7},{5,6},{6,5},{7,4},{8,11},{9,10},{10,... | collective-permute-start | bytes 129032 | tf_op jit(solution)/shard_map/ppermute | solution.py:337
  72.6 20.0 %copy-start.4 = (bf16[128,2048]{1,0:T(8,128)(2,1)S(1)}, bf16[128,2048]{1,0:T(8,128)(2,1)}, u32[]{:S(2)}) copy-start(bf16[128,2048]{1,0:T(8,128)(2,1)} %refs_4_.1) | copy-start | bytes 1572868
  72.6 11.6 %collective-permute-start.18 = (bf16[3,56,1024]{2,1,0:T(8,128)(2,1)S(1)}, bf16[3,56,1024]{2,1,0:T(8,128)(2,1)S(1)}, u32[]{:S(2)}, u32[]{:S(2)}) collective-permute-start(bf16[3,56,1024]{2,1,0:T(8,128)(2,1)S(1)} %get-tuple-element.77.refs_0_), channel_id=1, source_target_pairs={{0,2},{1,3},{2,0},{3,1},{4,6},{5,7},{6,4},{7,5},{8,10},{9,11},{10,... | collective-permute-start | bytes 1032200 | tf_op jit(solution)/shard_map/ppermute | solution.py:409
  76.3 7.8 %collective-permute-start.19 = (f32[56,33]{1,0:T(8,128)S(1)}, f32[56,33]{1,0:T(8,128)S(1)}, u32[]{:S(2)}, u32[]{:S(2)}) collective-permute-start(f32[56,33]{1,0:T(8,128)S(1)} %shard_map.127.refs_0_), channel_id=1, source_target_pairs={{0,2},{1,3},{2,0},{3,1},{4,6},{5,7},{6,4},{7,5},{8,10},{9,11},{10,... | collective-permute-start | bytes 22184 | tf_op jit(solution)/shard_map/ppermute | solution.py:409
  76.8 15.8 %collective-permute-start.20 = (bf16[3,56,1024]{2,1,0:T(8,128)(2,1)S(1)}, bf16[3,56,1024]{2,1,0:T(8,128)(2,1)S(1)}, u32[]{:S(2)}, u32[]{:S(2)}) collective-permute-start(bf16[3,56,1024]{2,1,0:T(8,128)(2,1)S(1)} %get-tuple-element.77.refs_0_), channel_id=1, source_target_pairs={{0,1},{1,0},{2,3},{3,2},{4,5},{5,4},{6,7},{7,6},{8,9},{9,8},{10,11... | collective-permute-start | bytes 1032200 | tf_op jit(solution)/shard_map/ppermute | solution.py:414
  84.2 8.4 %collective-permute-start.21 = (bf16[3,56,1024]{2,1,0:T(8,128)(2,1)S(1)}, bf16[3,56,1024]{2,1,0:T(8,128)(2,1)S(1)}, u32[]{:S(2)}, u32[]{:S(2)}) collective-permute-start(bf16[3,56,1024]{2,1,0:T(8,128)(2,1)S(1)} %collective-permute-done.18.refs_1_), channel_id=1, source_target_pairs={{0,1},{1,0},{2,3},{3,2},{4,5},{5,4},{6,7},{7,6},{8,9},{9,8},{10,11... | collective-permute-start | bytes 1032200 | tf_op jit(solution)/shard_map/ppermute | solution.py:423
  84.3 1.6 %collective-permute-start.22 = (f32[56,33]{1,0:T(8,128)S(1)}, f32[56,33]{1,0:T(8,128)S(1)}, u32[]{:S(2)}, u32[]{:S(2)}) collective-permute-start(f32[56,33]{1,0:T(8,128)S(1)} %shard_map.127.refs_0_), channel_id=1, source_target_pairs={{0,1},{1,0},{2,3},{3,2},{4,5},{5,4},{6,7},{7,6},{8,9},{9,8},{10,11... | collective-permute-start | bytes 22184 | tf_op jit(solution)/shard_map/ppermute | solution.py:424
  84.7 1.2 %collective-permute-start.23 = (f32[56,33]{1,0:T(8,128)S(1)}, f32[56,33]{1,0:T(8,128)S(1)}, u32[]{:S(2)}, u32[]{:S(2)}) collective-permute-start(f32[56,33]{1,0:T(8,128)S(1)} %collective-permute-done.19.refs_1_), channel_id=1, source_target_pairs={{0,1},{1,0},{2,3},{3,2},{4,5},{5,4},{6,7},{7,6},{8,9},{9,8},{10,11... | collective-permute-start | bytes 22184 | tf_op jit(solution)/shard_map/ppermute | solution.py:424
  86.5 13.2 %collective-permute-start.24 = (f32[208,33]{1,0:T(8,128)S(1)}, f32[208,33]{1,0:T(8,128)S(1)}, u32[]{:S(2)}, u32[]{:S(2)}) collective-permute-start(f32[208,33]{1,0:T(8,128)S(1)} %shard_map.129), channel_id=1, source_target_pairs={{0,0},{8,1},{16,2},{24,3},{4,4},{12,5},{20,6},{28,7},{1,8},{9,9},{... | collective-permute-start | bytes 82376 | tf_op jit(solution)/shard_map/ppermute | solution.py:437
  89.4 12.6 %collective-permute-start.25 = (f32[208,33]{1,0:T(8,128)S(1)}, f32[208,33]{1,0:T(8,128)S(1)}, u32[]{:S(2)}, u32[]{:S(2)}) collective-permute-start(f32[208,33]{1,0:T(8,128)S(1)} %shard_map.129), channel_id=1, source_target_pairs={{4,0},{12,1},{20,2},{28,3},{0,4},{8,5},{16,6},{24,7},{5,8},{13,9},... | collective-permute-start | bytes 82376 | tf_op jit(solution)/shard_map/ppermute | solution.py:437
  (2 other events, 1.9 us)

commit v10 on v9

--- a/solution.py
+++ b/solution.py
@@ -426,16 +426,6 @@
         gather_kernel, [jax.ShapeDtypeStruct((rows, 2 * order + 1), F32)], 0, 0, place, *sums,
         indexed=True,
     )
-    turns = n_seq // n_ch
-    blocks = []
-    for turn in range(turns):
-        route = [
-            ((h * turns + (s + turn) % turns) * n_ch + s // turns, s * n_ch + h)
-            for s in range(n_seq)
-            for h in range(n_ch)
-        ]
-        blocks.append(lax.ppermute(block_sums, ("seq", "ch"), route))
-
     tile = min(512, width)
     weight_grad = pl.pallas_call(
         functools.partial(weight_kernel, shares=n_ch),
@@ -459,7 +449,16 @@
             transcendentals=0,
         ),
     )(place, *held, *pieces)
-    weight_grad, blocks = lax.optimization_barrier((weight_grad, blocks))
+    weight_grad, block_sums = lax.optimization_barrier((weight_grad, block_sums))
+    turns = n_seq // n_ch
+    blocks = []
+    for turn in range(turns):
+        route = [
+            ((h * turns + (s + turn) % turns) * n_ch + s // turns, s * n_ch + h)
+            for s in range(n_seq)
+            for h in range(n_ch)
+        ]
+        blocks.append(lax.ppermute(block_sums, ("seq", "ch"), route))
     weight_grad = weight_grad.transpose(1, 0, 2)
 
     channels = residues.shape[0]

time: 104 us -> 109 us (1.048)
  waiting for transfers between devices: 22.9 us -> 28.6 us
    ppermute x2, waiting for transfers between devices: 3.64 us -> 9.39 us  [local(): blocks.append(lax.ppermute(block_sums, ('seq', 'ch'), route))]
  transfers between devices with their start and end apart: 27 -> 27, of which waited for: 11 -> 11; matrix products, arithmetic and copies ran while one was open for 1% -> 1% of each run, Pallas kernels for 17% -> 11%
where the time goes in v10:
time: 109 us
  starting transfers between devices  36 us (33%)
  waiting for transfers between devices  28.6 us (26%)
  Pallas kernels  24.6 us (23%)
  blocking collectives  14.2 us (13%)
  local copies, waits for them, and re-layouts  3.83 us (4%)
    pallas_call x10, Pallas kernels, call(): pl.pallas_call(kernel, out_shape=outs, in_specs=specs, out_specs=[whole]...  18.9 us
    all_to_all x1, blocking collectives, local(): lax.all_to_all(upper, 'seq', split_axis=0, concat_axis=0, tiled=True)  14.2 us
    ppermute x2, waiting for transfers between devices, local(): blocks.append(lax.ppermute(block_sums, ('seq', 'ch'), route))  9.39 us
    ppermute x9, starting transfers between devices, to_owners(): lax.ppermute(sums[d], 'ch', [(h, h ^ d) for h in range(n_ch)])  8.21 us
    ppermute x2, waiting for transfers between devices, chips(): lax.ppermute(array, 'ch', [(h, h ^ d) for h in range(n_ch)])  7.02 us
    ppermute x4, starting transfers between devices, send_on(): lax.ppermute(pair[1], 'seq', behind)  6.48 us
    ppermute x2, starting transfers between devices, local(): blocks.append(lax.ppermute(block_sums, ('seq', 'ch'), route))  6.07 us
    pallas_call x1, Pallas kernels, local(): pl.pallas_call(functools.partial(weight_kernel, shares=n_ch), out_shape=j...  5.73 us
  transfers between devices with their start and end apart: 27, of which 11 were waited for; matrix products, arithmetic and copies ran while one was open for 1% of the time, Pallas kernels for 11%

profile of v10, /device:TPU:4, one launch (start us, length us, event | category | flops | bytes accessed | tf_op | source)
XLA Modules:
  0.0 109.0 jit_solution(7524700646257126861)
XLA Ops:
  0.6 1.6 %collective-permute-start = (bf16[128,2048]{1,0:T(8,128)(2,1)}, bf16[128,2048]{1,0:T(8,128)(2,1)S(1)}, u32[]{:S(2)}, u32[]{:S(2)}) collective-permute-start(bf16[128,2048]{1,0:T(8,128)(2,1)} %refs_4_.1), channel_id=1, source_target_pairs={{0,8},{8,16},{16,24},{24,28},{28,20},{20,12},{12,4},{4,0},{1,9},{9... | collective-permute-start | bytes 1572872 | tf_op jit(solution)/shard_map/ppermute | solution.py:315
  5.8 3.3 %all-to-all-start = ((bf16[4,2,56,128]{3,2,1,0:T(8,128)(2,1)}), bf16[4,2,56,128]{3,2,1,0:T(8,128)(2,1)S(1)}, u32[]{:S(2)}, u32[]{:S(2)}) async-start(bf16[4,2,56,128]{3,2,1,0:T(8,128)(2,1)} %shard_map.121), calls=%async_computation | async-start | bytes 229376 | tf_op jit(solution)/shard_map/all_to_all | solution.py:355
  9.2 4.4 %collective-permute-start.2 = (f32[56,33]{1,0:T(8,128)S(1)}, f32[56,33]{1,0:T(8,128)S(1)}, u32[]{:S(2)}, u32[]{:S(2)}) collective-permute-start(f32[56,33]{1,0:T(8,128)S(1)} %shard_map.120), channel_id=1, source_target_pairs={{0,0},{4,1},{8,2},{12,3},{16,4},{20,5},{24,6},{28,7},{1,8},{5,9},{... | collective-permute-start | bytes 22184 | tf_op jit(solution)/shard_map/ppermute | solution.py:350
  13.6 2.5 %collective-permute-done.2.poles_ref.refs_13_ = f32[56,33]{1,0:T(8,128)S(1)} collective-permute-done((f32[56,33]{1,0:T(8,128)S(1)}, f32[56,33]{1,0:T(8,128)S(1)}, u32[]{:S(2)}, u32[]{:S(2)}) %collective-permute-start.2) | collective-permute-done | bytes 7424 | tf_op jit(solution)/shard_map/ppermute | solution.py:350
  16.1 1.3 %collective-permute-start.3 = (bf16[128,2048]{1,0:T(8,128)(2,1)S(1)}, bf16[128,2048]{1,0:T(8,128)(2,1)S(1)}, u32[]{:S(2)}, u32[]{:S(2)}) collective-permute-start(bf16[128,2048]{1,0:T(8,128)(2,1)S(1)} %collective-permute-done.refs_1_.refs_5_), channel_id=1, source_target_pairs={{0,8},{8,16},{16,24},{24,28},{28,20},{20,12},{12,4},{4,0},{1,9},{9... | collective-permute-start | bytes 1572872 | tf_op jit(solution)/shard_map/ppermute | solution.py:315
  17.4 3.3 %collective-permute-start.4 = (bf16[128,2048]{1,0:T(8,128)(2,1)S(1)}, bf16[128,2048]{1,0:T(8,128)(2,1)S(1)}, u32[]{:S(2)}, u32[]{:S(2)}) collective-permute-start(bf16[128,2048]{1,0:T(8,128)(2,1)S(1)} %collective-permute-done.1.refs_2_.refs_6_), channel_id=1, source_target_pairs={{8,0},{16,8},{24,16},{28,24},{20,28},{12,20},{4,12},{0,4},{9,1},{1... | collective-permute-start | bytes 1572872 | tf_op jit(solution)/shard_map/ppermute | solution.py:315
  20.7 14.2 %all_to_all.10.refs_12_ = bf16[8,56,128]{2,1,0:T(8,128)(2,1)S(1)} all-to-all(bf16[8,56,128]{2,1,0:T(8,128)(2,1)S(1)} %bitcast.13), channel_id=1, replica_groups=mesh['seq'=8,'ch'=4] {'seq'}, dimensions={0} | all-to-all | bytes 229376 | tf_op jit(solution)/shard_map/all_to_all | solution.py:358
  35.9 1.1 collective-permute-start.6
  37.0 1.7 %copy-done = bf16[208,3,2048]{2,0,1:T(8,128)(2,1)S(1)} copy-done((bf16[208,3,2048]{2,0,1:T(8,128)(2,1)S(1)}, bf16[208,3,2048]{2,0,1:T(8,128)(2,1)}, u32[]{:S(2)}) %copy-start) | copy-done | bytes 2555928
  38.7 1.0 copy-done.3
  39.8 3.4 %shard_map.122 = (f32[3,56,640]{2,1,0:T(8,128)S(1)}, bf16[3,56,640]{2,1,0:T(8,128)(2,1)S(1)}, bf16[3,56,640]{2,1,0:T(8,128)(2,1)S(1)}, bf16[3,56,640]{2,1,0:T(8,128)(2,1)S(1)}) custom-call(s32[2]{0:T(128)S(1)} %pad_add_fusion.place_ref, bf16[3,208,2048]{2,1,0:T(8,128)(2,1)S(1)} %bitcast.9, bf16[128,2048]{1,0:T(8,128)(2,1)S(1)} %copy-done.3, ...), custom_call_target="tpu_custom_call" | custom-call | flops 1635778560 | bytes 6252552 | tf_op jit(solution)/shard_map/pallas_call | solution.py:279
  43.3 1.5 %collective-permute-done.7.refs_1_ = bf16[3,56,640]{2,1,0:T(8,128)(2,1)S(1)} collective-permute-done((bf16[3,56,640]{2,1,0:T(8,128)(2,1)S(1)}, bf16[3,56,640]{2,1,0:T(8,128)(2,1)S(1)}, u32[]{:S(2)}, u32[]{:S(2)}) %collective-permute-start.7) | collective-permute-done | bytes 215072 | tf_op jit(solution)/shard_map/ppermute | solution.py:337
  44.7 2.5 %collective-permute-done.5.refs_0_.refs_9_ = bf16[128,2048]{1,0:T(8,128)(2,1)S(1)} collective-permute-done((bf16[128,2048]{1,0:T(8,128)(2,1)S(1)}, bf16[128,2048]{1,0:T(8,128)(2,1)S(1)}, u32[]{:S(2)}, u32[]{:S(2)}) %collective-permute-start.5) | collective-permute-done | bytes 524320 | tf_op jit(solution)/shard_map/ppermute | solution.py:315
  48.3 1.7 %collective-permute-start.14 = (bf16[64,2048]{1,0:T(8,128)(2,1)S(1)}, bf16[64,2048]{1,0:T(8,128)(2,1)S(1)}, u32[]{:S(2)}, u32[]{:S(2)}) collective-permute-start(bf16[64,2048]{1,0:T(8,128)(2,1)S(1)} %slice.7), channel_id=1, source_target_pairs={{8,0},{16,8},{24,16},{28,24},{20,28},{12,20},{4,12},{0,4},{9,1},{1... | collective-permute-start | bytes 786440 | tf_op jit(solution)/shard_map/ppermute | solution.py:315
  50.0 3.1 %collective-permute-start.8 = (bf16[3,56,640]{2,1,0:T(8,128)(2,1)S(1)}, bf16[3,56,640]{2,1,0:T(8,128)(2,1)S(1)}, u32[]{:S(2)}, u32[]{:S(2)}) collective-permute-start(bf16[3,56,640]{2,1,0:T(8,128)(2,1)S(1)} %get-tuple-element.56), channel_id=1, source_target_pairs={{0,2},{1,3},{2,0},{3,1},{4,6},{5,7},{6,4},{7,5},{8,10},{9,11},{10,... | collective-permute-start | bytes 645128 | tf_op jit(solution)/shard_map/ppermute | solution.py:337
  53.1 1.8 %shard_map.123 = (f32[3,56,256]{2,1,0:T(8,128)S(1)}, bf16[3,56,256]{2,1,0:T(8,128)(2,1)S(1)}, bf16[3,56,256]{2,1,0:T(8,128)(2,1)S(1)}, bf16[3,56,256]{2,1,0:T(8,128)(2,1)S(1)}) custom-call(s32[2]{0:T(128)S(1)} %pad_add_fusion.place_ref, bf16[3,208,2048]{2,1,0:T(8,128)(2,1)S(1)} %bitcast.10, bf16[128,2048]{1,0:T(8,128)(2,1)S(1)} %collective-permute-done.5.refs_0_.refs_9_, ...), custom_call_target="tpu_custom_call" | custom-call | flops 654311424 | bytes 4034568 | tf_op jit(solution)/shard_map/pallas_call | solution.py:279
  55.2 2.3 %collective-permute-start.11 = (bf16[3,56,256]{2,1,0:T(8,128)(2,1)S(1)}, bf16[3,56,256]{2,1,0:T(8,128)(2,1)S(1)}, u32[]{:S(2)}, u32[]{:S(2)}) collective-permute-start(bf16[3,56,256]{2,1,0:T(8,128)(2,1)S(1)} %get-tuple-element.64), channel_id=1, source_target_pairs={{0,2},{1,3},{2,0},{3,1},{4,6},{5,7},{6,4},{7,5},{8,10},{9,11},{10,... | collective-permute-start | bytes 258056 | tf_op jit(solution)/shard_map/ppermute | solution.py:337
  57.5 1.4 %shard_map.124 = (f32[3,56,128]{2,1,0:T(8,128)S(1)}, bf16[3,56,128]{2,1,0:T(8,128)(2,1)S(1)}, bf16[3,56,128]{2,1,0:T(8,128)(2,1)S(1)}, bf16[3,56,128]{2,1,0:T(8,128)(2,1)S(1)}) custom-call(s32[2]{0:T(128)S(1)} %pad_add_fusion.place_ref, bf16[3,208,2048]{2,1,0:T(8,128)(2,1)S(1)} %bitcast.11, bf16[64,2048]{1,0:T(8,128)(2,1)S(1)} %collective-permute-done.13.refs_0_.refs_11_, ...), custom_call_target="tpu_custom_call" | custom-call | flops 327155712 | bytes 3295240 | tf_op jit(solution)/shard_map/pallas_call | solution.py:279
  59.5 3.0 %collective-permute-done.9.refs_3_ = bf16[3,56,640]{2,1,0:T(8,128)(2,1)S(1)} collective-permute-done((bf16[3,56,640]{2,1,0:T(8,128)(2,1)S(1)}, bf16[3,56,640]{2,1,0:T(8,128)(2,1)S(1)}, u32[]{:S(2)}, u32[]{:S(2)}) %collective-permute-start.9) | collective-permute-done | bytes 215072 | tf_op jit(solution)/shard_map/ppermute | solution.py:337
  62.4 1.9 %collective-permute-start.17 = (bf16[3,56,128]{2,1,0:T(8,128)(2,1)S(1)}, bf16[3,56,128]{2,1,0:T(8,128)(2,1)S(1)}, u32[]{:S(2)}, u32[]{:S(2)}) collective-permute-start(bf16[3,56,128]{2,1,0:T(8,128)(2,1)S(1)} %get-tuple-element.71), channel_id=1, source_target_pairs={{0,3},{1,2},{2,1},{3,0},{4,7},{5,6},{6,5},{7,4},{8,11},{9,10},{10,... | collective-permute-start | bytes 129032 | tf_op jit(solution)/shard_map/ppermute | solution.py:337
  64.4 1.5 %shard_map.125 = (f32[56,1024]{1,0:T(8,128)S(1)}, f32[56,1024]{1,0:T(8,128)S(1)}) custom-call(f32[56,33]{1,0:T(8,128)S(1)} %collective-permute-done.2.poles_ref.refs_13_, bf16[1024,1024]{1,0:T(8,128)(2,1)S(1)} %copy-done.1, bf16[1024,1024]{1,0:T(8,128)(2,1)S(1)} %copy-done.2, f32[2,1024]{1,0:T(2,128)S(1)} %copy-done.6), custom_call_target="tpu_custom_call" | custom-call | flops 469762048 | bytes 4668640 | tf_op jit(solution)/shard_map/pallas_call | solution.py:279
  67.0 5.6 %shard_map.126 = (bf16[3,56,1024]{2,1,0:T(8,128)(2,1)S(1)}, f32[56,1024]{1,0:T(8,128)S(1)}, f32[56,1024]{1,0:T(8,128)S(1)}, f32[56,1]{1,0:T(8,128)S(1)}) custom-call(s32[2]{0:T(128)S(1)} %pad_add_fusion.place_ref, f32[3,56,640]{2,1,0:T(8,128)S(1)} %get-tuple-element.53.refs_0_, bf16[3,56,640]{2,1,0:T(8,128)(2,1)S(1)} %collective-permute-done.7.refs_1_, ...), custom_call_target="tpu_custom_call" | custom-call | flops 1879048192 | bytes 7306696 | tf_op jit(solution)/shard_map/pallas_call | solution.py:279
  72.6 1.7 %collective-permute-start.18 = (bf16[3,56,1024]{2,1,0:T(8,128)(2,1)S(1)}, bf16[3,56,1024]{2,1,0:T(8,128)(2,1)S(1)}, u32[]{:S(2)}, u32[]{:S(2)}) collective-permute-start(bf16[3,56,1024]{2,1,0:T(8,128)(2,1)S(1)} %get-tuple-element.76.refs_0_), channel_id=1, source_target_pairs={{0,2},{1,3},{2,0},{3,1},{4,6},{5,7},{6,4},{7,5},{8,10},{9,11},{10,... | collective-permute-start | bytes 1032200 | tf_op jit(solution)/shard_map/ppermute | solution.py:409
  74.3 2.0 %shard_map.127.refs_0_ = f32[56,33]{1,0:T(8,128)S(1)} custom-call(f32[56,33]{1,0:T(8,128)S(1)} %collective-permute-done.2.poles_ref.refs_13_, f32[56,1024]{1,0:T(8,128)S(1)} %get-tuple-element.77.tgc_ref, f32[56,1024]{1,0:T(8,128)S(1)} %get-tuple-element.78.tgs_ref, bf16[1024,1024]{1,0:T(8,128)(2,1)S(1)} %copy-done.1, bf16[1024,1024]{1,0:T(8,128)(2,1)S(1)} %copy-done.2, ...), custom_call_target="tpu_custom_call" | custom-call | flops 469762048 | bytes 4668064 | tf_op jit(solution)/shard_map/pallas_call | solution.py:279
  77.2 7.0 %collective-permute-done.19.refs_1_ = f32[56,33]{1,0:T(8,128)S(1)} collective-permute-done((f32[56,33]{1,0:T(8,128)S(1)}, f32[56,33]{1,0:T(8,128)S(1)}, u32[]{:S(2)}, u32[]{:S(2)}) %collective-permute-start.19) | collective-permute-done | bytes 7424 | tf_op jit(solution)/shard_map/ppermute | solution.py:409
  84.8 1.1 %collective-permute-done.22.refs_2_ = f32[56,33]{1,0:T(8,128)S(1)} collective-permute-done((f32[56,33]{1,0:T(8,128)S(1)}, f32[56,33]{1,0:T(8,128)S(1)}, u32[]{:S(2)}, u32[]{:S(2)}) %collective-permute-start.22) | collective-permute-done | bytes 7424 | tf_op jit(solution)/shard_map/ppermute | solution.py:424
  86.5 5.7 %shard_map.128 = f32[3,208,2048]{2,1,0:T(8,128)} custom-call(s32[2]{0:T(128)S(1)} %pad_add_fusion.place_ref, bf16[3,56,1024]{2,1,0:T(8,128)(2,1)S(1)} %get-tuple-element.76.refs_0_, bf16[3,56,1024]{2,1,0:T(8,128)(2,1)S(1)} %collective-permute-done.18.refs_1_, bf16[3,56,1024]{2,1,0:T(8,128)(2,1)S(1)} %collective-permute-done.20.refs_2_, ...), custom_call_target="tpu_custom_call" | custom-call | flops 2617245696 | bytes 10584064 | tf_op jit(solution)/shard_map/pallas_call | solution.py:430
  92.2 2.9 %collective-permute-start.24 = (f32[208,33]{1,0:T(8,128)S(1)}, f32[208,33]{1,0:T(8,128)S(1)}, u32[]{:S(2)}, u32[]{:S(2)}) collective-permute-start(f32[208,33]{1,0:T(8,128)S(1)} %shard_map.129), channel_id=1, source_target_pairs={{0,0},{8,1},{16,2},{24,3},{4,4},{12,5},{20,6},{28,7},{1,8},{9,9},{... | collective-permute-start | bytes 82376 | tf_op jit(solution)/shard_map/ppermute | solution.py:461
  95.2 3.2 %collective-permute-start.25 = (f32[208,33]{1,0:T(8,128)S(1)}, f32[208,33]{1,0:T(8,128)S(1)}, u32[]{:S(2)}, u32[]{:S(2)}) collective-permute-start(f32[208,33]{1,0:T(8,128)S(1)} %shard_map.129), channel_id=1, source_target_pairs={{4,0},{12,1},{20,2},{28,3},{0,4},{8,5},{16,6},{24,7},{5,8},{13,9},... | collective-permute-start | bytes 82376 | tf_op jit(solution)/shard_map/ppermute | solution.py:461
  98.3 7.1 %collective-permute-done.24.refs_0_ = f32[208,33]{1,0:T(8,128)S(1)} collective-permute-done((f32[208,33]{1,0:T(8,128)S(1)}, f32[208,33]{1,0:T(8,128)S(1)}, u32[]{:S(2)}, u32[]{:S(2)}) %collective-permute-start.24) | collective-permute-done | bytes 27488 | tf_op jit(solution)/shard_map/ppermute | solution.py:461
  105.4 2.3 %collective-permute-done.25.refs_1_ = f32[208,33]{1,0:T(8,128)S(1)} collective-permute-done((f32[208,33]{1,0:T(8,128)S(1)}, f32[208,33]{1,0:T(8,128)S(1)}, u32[]{:S(2)}, u32[]{:S(2)}) %collective-permute-start.25) | collective-permute-done | bytes 27488 | tf_op jit(solution)/shard_map/ppermute | solution.py:461
  107.7 1.3 %shard_map.130 = (f32[16,416]{1,0:T(8,128)}, f32[16,416]{1,0:T(8,128)}, f32[1,416]{1,0:T(1,128)}) custom-call(s32[2]{0:T(128)S(1)} %pad_add_fusion.place_ref, f32[208,33]{1,0:T(8,128)S(1)} %collective-permute-done.24.refs_0_, f32[208,33]{1,0:T(8,128)S(1)} %collective-permute-done.25.refs_1_), custom_call_target="tpu_custom_call" | custom-call | bytes 109832 | tf_op jit(solution)/shard_map/pallas_call | solution.py:279
  (53 shorter events, 9.5 us)
Async XLA Ops:
  0.6 15.5 %collective-permute-start = (bf16[128,2048]{1,0:T(8,128)(2,1)}, bf16[128,2048]{1,0:T(8,128)(2,1)S(1)}, u32[]{:S(2)}, u32[]{:S(2)}) collective-permute-start(bf16[128,2048]{1,0:T(8,128)(2,1)} %refs_4_.1), channel_id=1, source_target_pairs={{0,8},{8,16},{16,24},{24,28},{28,20},{20,12},{12,4},{4,0},{1,9},{9... | collective-permute-start | bytes 1572872 | tf_op jit(solution)/shard_map/ppermute | solution.py:315
  2.3 13.9 %collective-permute-start.1 = (bf16[128,2048]{1,0:T(8,128)(2,1)}, bf16[128,2048]{1,0:T(8,128)(2,1)S(1)}, u32[]{:S(2)}, u32[]{:S(2)}) collective-permute-start(bf16[128,2048]{1,0:T(8,128)(2,1)} %refs_4_.1), channel_id=1, source_target_pairs={{8,0},{16,8},{24,16},{28,24},{20,28},{12,20},{4,12},{0,4},{9,1},{1... | collective-permute-start | bytes 1572872 | tf_op jit(solution)/shard_map/ppermute | solution.py:315
  5.8 10.3 %all-to-all-start = ((bf16[4,2,56,128]{3,2,1,0:T(8,128)(2,1)}), bf16[4,2,56,128]{3,2,1,0:T(8,128)(2,1)S(1)}, u32[]{:S(2)}, u32[]{:S(2)}) async-start(bf16[4,2,56,128]{3,2,1,0:T(8,128)(2,1)} %shard_map.121), calls=%async_computation | async-start | bytes 229376 | tf_op jit(solution)/shard_map/all_to_all | solution.py:355
  9.2 6.9 %collective-permute-start.2 = (f32[56,33]{1,0:T(8,128)S(1)}, f32[56,33]{1,0:T(8,128)S(1)}, u32[]{:S(2)}, u32[]{:S(2)}) collective-permute-start(f32[56,33]{1,0:T(8,128)S(1)} %shard_map.120), channel_id=1, source_target_pairs={{0,0},{4,1},{8,2},{12,3},{16,4},{20,5},{24,6},{28,7},{1,8},{5,9},{... | collective-permute-start | bytes 22184 | tf_op jit(solution)/shard_map/ppermute | solution.py:350
  16.1 18.8 %collective-permute-start.3 = (bf16[128,2048]{1,0:T(8,128)(2,1)S(1)}, bf16[128,2048]{1,0:T(8,128)(2,1)S(1)}, u32[]{:S(2)}, u32[]{:S(2)}) collective-permute-start(bf16[128,2048]{1,0:T(8,128)(2,1)S(1)} %collective-permute-done.refs_1_.refs_5_), channel_id=1, source_target_pairs={{0,8},{8,16},{16,24},{24,28},{28,20},{20,12},{12,4},{4,0},{1,9},{9... | collective-permute-start | bytes 1572872 | tf_op jit(solution)/shard_map/ppermute | solution.py:315
  17.4 17.5 %collective-permute-start.4 = (bf16[128,2048]{1,0:T(8,128)(2,1)S(1)}, bf16[128,2048]{1,0:T(8,128)(2,1)S(1)}, u32[]{:S(2)}, u32[]{:S(2)}) collective-permute-start(bf16[128,2048]{1,0:T(8,128)(2,1)S(1)} %collective-permute-done.1.refs_2_.refs_6_), channel_id=1, source_target_pairs={{8,0},{16,8},{24,16},{28,24},{20,28},{12,20},{4,12},{0,4},{9,1},{1... | collective-permute-start | bytes 1572872 | tf_op jit(solution)/shard_map/ppermute | solution.py:315
  35.0 12.3 %collective-permute-start.5 = (bf16[128,2048]{1,0:T(8,128)(2,1)S(1)}, bf16[128,2048]{1,0:T(8,128)(2,1)S(1)}, u32[]{:S(2)}, u32[]{:S(2)}) collective-permute-start(bf16[128,2048]{1,0:T(8,128)(2,1)S(1)} %collective-permute-done.3.refs_3_.refs_7_), channel_id=1, source_target_pairs={{0,8},{8,16},{16,24},{24,28},{28,20},{20,12},{12,4},{4,0},{1,9},{9... | collective-permute-start | bytes 1572872 | tf_op jit(solution)/shard_map/ppermute | solution.py:315
  35.9 11.9 %collective-permute-start.6 = (bf16[128,2048]{1,0:T(8,128)(2,1)S(1)}, bf16[128,2048]{1,0:T(8,128)(2,1)S(1)}, u32[]{:S(2)}, u32[]{:S(2)}) collective-permute-start(bf16[128,2048]{1,0:T(8,128)(2,1)S(1)} %collective-permute-done.4.refs_4_.refs_8_), channel_id=1, source_target_pairs={{8,0},{16,8},{24,16},{28,24},{20,28},{12,20},{4,12},{0,4},{9,1},{1... | collective-permute-start | bytes 1572872 | tf_op jit(solution)/shard_map/ppermute | solution.py:315
  37.0 1.7 %copy-start = (bf16[208,3,2048]{2,0,1:T(8,128)(2,1)S(1)}, bf16[208,3,2048]{2,0,1:T(8,128)(2,1)}, u32[]{:S(2)}) copy-start(bf16[208,3,2048]{2,0,1:T(8,128)(2,1)} %param.10) | copy-start | bytes 7667716
  43.2 1.5 %collective-permute-start.7 = (bf16[3,56,640]{2,1,0:T(8,128)(2,1)S(1)}, bf16[3,56,640]{2,1,0:T(8,128)(2,1)S(1)}, u32[]{:S(2)}, u32[]{:S(2)}) collective-permute-start(bf16[3,56,640]{2,1,0:T(8,128)(2,1)S(1)} %get-tuple-element.54), channel_id=1, source_target_pairs={{0,1},{1,0},{2,3},{3,2},{4,5},{5,4},{6,7},{7,6},{8,9},{9,8},{10,11... | collective-permute-start | bytes 645128 | tf_op jit(solution)/shard_map/ppermute | solution.py:337
  47.9 7.3 %collective-permute-start.13 = (bf16[64,2048]{1,0:T(8,128)(2,1)S(1)}, bf16[64,2048]{1,0:T(8,128)(2,1)S(1)}, u32[]{:S(2)}, u32[]{:S(2)}) collective-permute-start(bf16[64,2048]{1,0:T(8,128)(2,1)S(1)} %slice.6), channel_id=1, source_target_pairs={{0,8},{8,16},{16,24},{24,28},{28,20},{20,12},{12,4},{4,0},{1,9},{9... | collective-permute-start | bytes 786440 | tf_op jit(solution)/shard_map/ppermute | solution.py:315
  48.3 9.2 %collective-permute-start.14 = (bf16[64,2048]{1,0:T(8,128)(2,1)S(1)}, bf16[64,2048]{1,0:T(8,128)(2,1)S(1)}, u32[]{:S(2)}, u32[]{:S(2)}) collective-permute-start(bf16[64,2048]{1,0:T(8,128)(2,1)S(1)} %slice.7), channel_id=1, source_target_pairs={{8,0},{16,8},{24,16},{28,24},{20,28},{12,20},{4,12},{0,4},{9,1},{1... | collective-permute-start | bytes 786440 | tf_op jit(solution)/shard_map/ppermute | solution.py:315
  50.0 9.0 %collective-permute-start.8 = (bf16[3,56,640]{2,1,0:T(8,128)(2,1)S(1)}, bf16[3,56,640]{2,1,0:T(8,128)(2,1)S(1)}, u32[]{:S(2)}, u32[]{:S(2)}) collective-permute-start(bf16[3,56,640]{2,1,0:T(8,128)(2,1)S(1)} %get-tuple-element.56), channel_id=1, source_target_pairs={{0,2},{1,3},{2,0},{3,1},{4,6},{5,7},{6,4},{7,5},{8,10},{9,11},{10,... | collective-permute-start | bytes 645128 | tf_op jit(solution)/shard_map/ppermute | solution.py:337
  53.1 11.3 %copy-start.1 = (bf16[1024,1024]{1,0:T(8,128)(2,1)S(1)}, bf16[1024,1024]{1,0:T(8,128)(2,1)}, u32[]{:S(2)}) copy-start(bf16[1024,1024]{1,0:T(8,128)(2,1)} %constant.15.clone.cos_ref.refs_16_) | copy-start | bytes 6291460
  53.1 11.3 %copy-start.2 = (bf16[1024,1024]{1,0:T(8,128)(2,1)S(1)}, bf16[1024,1024]{1,0:T(8,128)(2,1)}, u32[]{:S(2)}) copy-start(bf16[1024,1024]{1,0:T(8,128)(2,1)} %constant.16.clone.sin_ref.refs_17_) | copy-start | bytes 6291460
  53.1 11.3 %copy-start.6 = (f32[2,1024]{1,0:T(2,128)S(1)}, f32[2,1024]{1,0:T(2,128)}, u32[]{:S(2)}) copy-start(f32[2,1024]{1,0:T(2,128)} %constant.17.clone.twist_ref.refs_18_) | copy-start | bytes 24580
  53.1 9.3 %collective-permute-start.9 = (bf16[3,56,640]{2,1,0:T(8,128)(2,1)S(1)}, bf16[3,56,640]{2,1,0:T(8,128)(2,1)S(1)}, u32[]{:S(2)}, u32[]{:S(2)}) collective-permute-start(bf16[3,56,640]{2,1,0:T(8,128)(2,1)S(1)} %get-tuple-element.57), channel_id=1, source_target_pairs={{0,3},{1,2},{2,1},{3,0},{4,7},{5,6},{6,5},{7,4},{8,11},{9,10},{10,... | collective-permute-start | bytes 645128 | tf_op jit(solution)/shard_map/ppermute | solution.py:337
  54.9 7.5 %collective-permute-start.10 = (bf16[3,56,256]{2,1,0:T(8,128)(2,1)S(1)}, bf16[3,56,256]{2,1,0:T(8,128)(2,1)S(1)}, u32[]{:S(2)}, u32[]{:S(2)}) collective-permute-start(bf16[3,56,256]{2,1,0:T(8,128)(2,1)S(1)} %get-tuple-element.63), channel_id=1, source_target_pairs={{0,1},{1,0},{2,3},{3,2},{4,5},{5,4},{6,7},{7,6},{8,9},{9,8},{10,11... | collective-permute-start | bytes 258056 | tf_op jit(solution)/shard_map/ppermute | solution.py:337
  55.2 10.7 %collective-permute-start.11 = (bf16[3,56,256]{2,1,0:T(8,128)(2,1)S(1)}, bf16[3,56,256]{2,1,0:T(8,128)(2,1)S(1)}, u32[]{:S(2)}, u32[]{:S(2)}) collective-permute-start(bf16[3,56,256]{2,1,0:T(8,128)(2,1)S(1)} %get-tuple-element.64), channel_id=1, source_target_pairs={{0,2},{1,3},{2,0},{3,1},{4,6},{5,7},{6,4},{7,5},{8,10},{9,11},{10,... | collective-permute-start | bytes 258056 | tf_op jit(solution)/shard_map/ppermute | solution.py:337
  57.5 8.4 %collective-permute-start.12 = (bf16[3,56,256]{2,1,0:T(8,128)(2,1)S(1)}, bf16[3,56,256]{2,1,0:T(8,128)(2,1)S(1)}, u32[]{:S(2)}, u32[]{:S(2)}) collective-permute-start(bf16[3,56,256]{2,1,0:T(8,128)(2,1)S(1)} %get-tuple-element.65), channel_id=1, source_target_pairs={{0,3},{1,2},{2,1},{3,0},{4,7},{5,6},{6,5},{7,4},{8,11},{9,10},{10,... | collective-permute-start | bytes 258056 | tf_op jit(solution)/shard_map/ppermute | solution.py:337
  59.0 7.0 %collective-permute-start.15 = (bf16[3,56,128]{2,1,0:T(8,128)(2,1)S(1)}, bf16[3,56,128]{2,1,0:T(8,128)(2,1)S(1)}, u32[]{:S(2)}, u32[]{:S(2)}) collective-permute-start(bf16[3,56,128]{2,1,0:T(8,128)(2,1)S(1)} %get-tuple-element.69), channel_id=1, source_target_pairs={{0,1},{1,0},{2,3},{3,2},{4,5},{5,4},{6,7},{7,6},{8,9},{9,8},{10,11... | collective-permute-start | bytes 129032 | tf_op jit(solution)/shard_map/ppermute | solution.py:337
  62.4 4.4 %collective-permute-start.16 = (bf16[3,56,128]{2,1,0:T(8,128)(2,1)S(1)}, bf16[3,56,128]{2,1,0:T(8,128)(2,1)S(1)}, u32[]{:S(2)}, u32[]{:S(2)}) collective-permute-start(bf16[3,56,128]{2,1,0:T(8,128)(2,1)S(1)} %get-tuple-element.70), channel_id=1, source_target_pairs={{0,2},{1,3},{2,0},{3,1},{4,6},{5,7},{6,4},{7,5},{8,10},{9,11},{10,... | collective-permute-start | bytes 129032 | tf_op jit(solution)/shard_map/ppermute | solution.py:337
  62.4 4.5 %collective-permute-start.17 = (bf16[3,56,128]{2,1,0:T(8,128)(2,1)S(1)}, bf16[3,56,128]{2,1,0:T(8,128)(2,1)S(1)}, u32[]{:S(2)}, u32[]{:S(2)}) collective-permute-start(bf16[3,56,128]{2,1,0:T(8,128)(2,1)S(1)} %get-tuple-element.71), channel_id=1, source_target_pairs={{0,3},{1,2},{2,1},{3,0},{4,7},{5,6},{6,5},{7,4},{8,11},{9,10},{10,... | collective-permute-start | bytes 129032 | tf_op jit(solution)/shard_map/ppermute | solution.py:337
  72.6 13.9 %copy-start.4 = (bf16[128,2048]{1,0:T(8,128)(2,1)S(1)}, bf16[128,2048]{1,0:T(8,128)(2,1)}, u32[]{:S(2)}) copy-start(bf16[128,2048]{1,0:T(8,128)(2,1)} %refs_4_.1) | copy-start | bytes 1572868
  72.6 11.6 %collective-permute-start.18 = (bf16[3,56,1024]{2,1,0:T(8,128)(2,1)S(1)}, bf16[3,56,1024]{2,1,0:T(8,128)(2,1)S(1)}, u32[]{:S(2)}, u32[]{:S(2)}) collective-permute-start(bf16[3,56,1024]{2,1,0:T(8,128)(2,1)S(1)} %get-tuple-element.76.refs_0_), channel_id=1, source_target_pairs={{0,2},{1,3},{2,0},{3,1},{4,6},{5,7},{6,4},{7,5},{8,10},{9,11},{10,... | collective-permute-start | bytes 1032200 | tf_op jit(solution)/shard_map/ppermute | solution.py:409
  76.3 7.8 %collective-permute-start.19 = (f32[56,33]{1,0:T(8,128)S(1)}, f32[56,33]{1,0:T(8,128)S(1)}, u32[]{:S(2)}, u32[]{:S(2)}) collective-permute-start(f32[56,33]{1,0:T(8,128)S(1)} %shard_map.127.refs_0_), channel_id=1, source_target_pairs={{0,2},{1,3},{2,0},{3,1},{4,6},{5,7},{6,4},{7,5},{8,10},{9,11},{10,... | collective-permute-start | bytes 22184 | tf_op jit(solution)/shard_map/ppermute | solution.py:409
  76.8 9.7 %collective-permute-start.20 = (bf16[3,56,1024]{2,1,0:T(8,128)(2,1)S(1)}, bf16[3,56,1024]{2,1,0:T(8,128)(2,1)S(1)}, u32[]{:S(2)}, u32[]{:S(2)}) collective-permute-start(bf16[3,56,1024]{2,1,0:T(8,128)(2,1)S(1)} %get-tuple-element.76.refs_0_), channel_id=1, source_target_pairs={{0,1},{1,0},{2,3},{3,2},{4,5},{5,4},{6,7},{7,6},{8,9},{9,8},{10,11... | collective-permute-start | bytes 1032200 | tf_op jit(solution)/shard_map/ppermute | solution.py:414
  84.2 2.3 %collective-permute-start.21 = (bf16[3,56,1024]{2,1,0:T(8,128)(2,1)S(1)}, bf16[3,56,1024]{2,1,0:T(8,128)(2,1)S(1)}, u32[]{:S(2)}, u32[]{:S(2)}) collective-permute-start(bf16[3,56,1024]{2,1,0:T(8,128)(2,1)S(1)} %collective-permute-done.18.refs_1_), channel_id=1, source_target_pairs={{0,1},{1,0},{2,3},{3,2},{4,5},{5,4},{6,7},{7,6},{8,9},{9,8},{10,11... | collective-permute-start | bytes 1032200 | tf_op jit(solution)/shard_map/ppermute | solution.py:423
  84.3 1.6 %collective-permute-start.22 = (f32[56,33]{1,0:T(8,128)S(1)}, f32[56,33]{1,0:T(8,128)S(1)}, u32[]{:S(2)}, u32[]{:S(2)}) collective-permute-start(f32[56,33]{1,0:T(8,128)S(1)} %shard_map.127.refs_0_), channel_id=1, source_target_pairs={{0,1},{1,0},{2,3},{3,2},{4,5},{5,4},{6,7},{7,6},{8,9},{9,8},{10,11... | collective-permute-start | bytes 22184 | tf_op jit(solution)/shard_map/ppermute | solution.py:424
  84.7 1.2 %collective-permute-start.23 = (f32[56,33]{1,0:T(8,128)S(1)}, f32[56,33]{1,0:T(8,128)S(1)}, u32[]{:S(2)}, u32[]{:S(2)}) collective-permute-start(f32[56,33]{1,0:T(8,128)S(1)} %collective-permute-done.19.refs_1_), channel_id=1, source_target_pairs={{0,1},{1,0},{2,3},{3,2},{4,5},{5,4},{6,7},{7,6},{8,9},{9,8},{10,11... | collective-permute-start | bytes 22184 | tf_op jit(solution)/shard_map/ppermute | solution.py:424
  92.2 13.2 %collective-permute-start.24 = (f32[208,33]{1,0:T(8,128)S(1)}, f32[208,33]{1,0:T(8,128)S(1)}, u32[]{:S(2)}, u32[]{:S(2)}) collective-permute-start(f32[208,33]{1,0:T(8,128)S(1)} %shard_map.129), channel_id=1, source_target_pairs={{0,0},{8,1},{16,2},{24,3},{4,4},{12,5},{20,6},{28,7},{1,8},{9,9},{... | collective-permute-start | bytes 82376 | tf_op jit(solution)/shard_map/ppermute | solution.py:461
  95.2 12.6 %collective-permute-start.25 = (f32[208,33]{1,0:T(8,128)S(1)}, f32[208,33]{1,0:T(8,128)S(1)}, u32[]{:S(2)}, u32[]{:S(2)}) collective-permute-start(f32[208,33]{1,0:T(8,128)S(1)} %shard_map.129), channel_id=1, source_target_pairs={{4,0},{12,1},{20,2},{28,3},{0,4},{8,5},{16,6},{24,7},{5,8},{13,9},... | collective-permute-start | bytes 82376 | tf_op jit(solution)/shard_map/ppermute | solution.py:461
  (2 other events, 1.9 us)

commit v11 on v9

--- a/solution.py
+++ b/solution.py
@@ -353,7 +353,7 @@
         (jax.ShapeDtypeStruct((n_ch, n_seq // n_ch, part, block_len), BF16),), 0, 0, grad_out,
     )
     upper = lax.all_to_all(upper, "ch", split_axis=0, concat_axis=0, tiled=True)
-    pair, upper, poles = lax.optimization_barrier((pair, upper, poles))
+    pair, poles = lax.optimization_barrier((pair, poles))
     upper = upper.reshape(n_seq, part, block_len)
     upper = lax.all_to_all(upper, "seq", split_axis=0, concat_axis=0, tiled=True)
 

time: 104 us -> 105 us (level)
  starting transfers between devices: 36 us -> 31.3 us
  waiting for transfers between devices: 22.9 us -> 26.9 us
  blocking collectives: 14.2 us -> 16.4 us
    all_to_all x0 -> x1, blocking collectives: none -> 5.89 us  [local(): upper = lax.all_to_all(upper, 'ch', split_axis=0, concat_axis=0, tiled=True)]
    ppermute x1, waiting for transfers between devices: 2.48 us -> 7.37 us  [local(): poles = lax.ppermute(poles, ('seq', 'ch'), spread)]
    all_to_all x1, blocking collectives: 14.2 us -> 10.5 us  [local(): lax.all_to_all(upper, 'seq', split_axis=0, concat_axis=0, tiled=True)]
    all_to_all x1 -> x0, starting transfers between devices: 3.34 us -> none  [local(): upper = lax.all_to_all(upper, 'ch', split_axis=0, concat_axis=0, tiled=True)]
    ppermute x9, starting transfers between devices: 8.22 us -> 6.84 us  [to_owners(): lax.ppermute(sums[d], 'ch', [(h, h ^ d) for h in range(n_ch)])]
  transfers between devices with their start and end apart: 27 -> 26, of which waited for: 11 -> 12; matrix products, arithmetic and copies ran while one was open for 1% -> 1% of each run, Pallas kernels for 17% -> 16%
where the time goes in v11:
time: 105 us; the launch traced here: 104 us
  starting transfers between devices  31.3 us (30%)
  waiting for transfers between devices  26.9 us (26%)
  Pallas kernels  24 us (23%)
  blocking collectives  16.4 us (16%)
  local copies, waits for them, and re-layouts  3.84 us (4%)
    pallas_call x10, Pallas kernels, call(): pl.pallas_call(kernel, out_shape=outs, in_specs=specs, out_specs=[whole]...  18.3 us
    all_to_all x1, blocking collectives, local(): lax.all_to_all(upper, 'seq', split_axis=0, concat_axis=0, tiled=True)  10.5 us
    ppermute x1, waiting for transfers between devices, local(): poles = lax.ppermute(poles, ('seq', 'ch'), spread)  7.37 us
    ppermute x2, waiting for transfers between devices, chips(): lax.ppermute(array, 'ch', [(h, h ^ d) for h in range(n_ch)])  7.01 us
    ppermute x2, starting transfers between devices, local(): blocks.append(lax.ppermute(block_sums, ('seq', 'ch'), route))  6.92 us
    ppermute x9, starting transfers between devices, to_owners(): lax.ppermute(sums[d], 'ch', [(h, h ^ d) for h in range(n_ch)])  6.84 us
    ppermute x4, starting transfers between devices, send_on(): lax.ppermute(pair[1], 'seq', behind)  6.16 us
    all_to_all x1, blocking collectives, local(): upper = lax.all_to_all(upper, 'ch', split_axis=0, concat_axis=0, tiled=True)  5.89 us
  transfers between devices with their start and end apart: 26, of which 12 were waited for; matrix products, arithmetic and copies ran while one was open for 1% of the time, Pallas kernels for 16%

profile of v11, /device:TPU:4, one launch (start us, length us, event | category | flops | bytes accessed | tf_op | source)
XLA Modules:
  0.0 104.3 jit_solution(17007230278066253253)
XLA Ops:
  0.6 1.6 %collective-permute-start = (bf16[128,2048]{1,0:T(8,128)(2,1)}, bf16[128,2048]{1,0:T(8,128)(2,1)S(1)}, u32[]{:S(2)}, u32[]{:S(2)}) collective-permute-start(bf16[128,2048]{1,0:T(8,128)(2,1)} %refs_4_.1), channel_id=1, source_target_pairs={{0,8},{8,16},{16,24},{24,28},{28,20},{20,12},{12,4},{4,0},{1,9},{9... | collective-permute-start | bytes 1572872 | tf_op jit(solution)/shard_map/ppermute | solution.py:315
  4.3 4.4 %collective-permute-start.2 = (f32[56,33]{1,0:T(8,128)S(1)}, f32[56,33]{1,0:T(8,128)S(1)}, u32[]{:S(2)}, u32[]{:S(2)}) collective-permute-start(f32[56,33]{1,0:T(8,128)S(1)} %shard_map.120), channel_id=1, source_target_pairs={{0,0},{4,1},{8,2},{12,3},{16,4},{20,5},{24,6},{28,7},{1,8},{5,9},{... | collective-permute-start | bytes 22184 | tf_op jit(solution)/shard_map/ppermute | solution.py:350
  8.7 7.4 %collective-permute-done.2.poles_ref.refs_13_ = f32[56,33]{1,0:T(8,128)S(1)} collective-permute-done((f32[56,33]{1,0:T(8,128)S(1)}, f32[56,33]{1,0:T(8,128)S(1)}, u32[]{:S(2)}, u32[]{:S(2)}) %collective-permute-start.2) | collective-permute-done | bytes 7424 | tf_op jit(solution)/shard_map/ppermute | solution.py:350
  16.1 1.3 %collective-permute-start.3 = (bf16[128,2048]{1,0:T(8,128)(2,1)S(1)}, bf16[128,2048]{1,0:T(8,128)(2,1)S(1)}, u32[]{:S(2)}, u32[]{:S(2)}) collective-permute-start(bf16[128,2048]{1,0:T(8,128)(2,1)S(1)} %collective-permute-done.refs_1_.refs_5_), channel_id=1, source_target_pairs={{0,8},{8,16},{16,24},{24,28},{28,20},{20,12},{12,4},{4,0},{1,9},{9... | collective-permute-start | bytes 1572872 | tf_op jit(solution)/shard_map/ppermute | solution.py:315
  17.4 2.5 %collective-permute-start.4 = (bf16[128,2048]{1,0:T(8,128)(2,1)S(1)}, bf16[128,2048]{1,0:T(8,128)(2,1)S(1)}, u32[]{:S(2)}, u32[]{:S(2)}) collective-permute-start(bf16[128,2048]{1,0:T(8,128)(2,1)S(1)} %collective-permute-done.1.refs_2_.refs_6_), channel_id=1, source_target_pairs={{8,0},{16,8},{24,16},{28,24},{20,28},{12,20},{4,12},{0,4},{9,1},{1... | collective-permute-start | bytes 1572872 | tf_op jit(solution)/shard_map/ppermute | solution.py:315
  20.9 5.9 %all_to_all.10 = bf16[4,2,56,128]{3,2,1,0:T(8,128)(2,1)S(1)} all-to-all(bf16[4,2,56,128]{3,2,1,0:T(8,128)(2,1)S(1)} %shard_map.121), channel_id=1, replica_groups=mesh['seq'=8,'ch'=4] {'ch'}, dimensions={0} | all-to-all | bytes 229376 | tf_op jit(solution)/shard_map/all_to_all | solution.py:355
  26.8 10.5 %all_to_all.11.refs_12_ = bf16[8,56,128]{2,1,0:T(8,128)(2,1)S(1)} all-to-all(bf16[8,56,128]{2,1,0:T(8,128)(2,1)S(1)} %bitcast.13), channel_id=1, replica_groups=mesh['seq'=8,'ch'=4] {'seq'}, dimensions={0} | all-to-all | bytes 229376 | tf_op jit(solution)/shard_map/all_to_all | solution.py:358
  37.3 2.0 %collective-permute-start.6 = (bf16[128,2048]{1,0:T(8,128)(2,1)S(1)}, bf16[128,2048]{1,0:T(8,128)(2,1)S(1)}, u32[]{:S(2)}, u32[]{:S(2)}) collective-permute-start(bf16[128,2048]{1,0:T(8,128)(2,1)S(1)} %collective-permute-done.4.refs_4_.refs_8_), channel_id=1, source_target_pairs={{8,0},{16,8},{24,16},{28,24},{20,28},{12,20},{4,12},{0,4},{9,1},{1... | collective-permute-start | bytes 1572872 | tf_op jit(solution)/shard_map/ppermute | solution.py:315
  39.3 1.7 %copy-done = bf16[208,3,2048]{2,0,1:T(8,128)(2,1)S(1)} copy-done((bf16[208,3,2048]{2,0,1:T(8,128)(2,1)S(1)}, bf16[208,3,2048]{2,0,1:T(8,128)(2,1)}, u32[]{:S(2)}) %copy-start) | copy-done | bytes 2555928
  41.1 1.0 copy-done.3
  42.1 3.4 %shard_map.122 = (f32[3,56,640]{2,1,0:T(8,128)S(1)}, bf16[3,56,640]{2,1,0:T(8,128)(2,1)S(1)}, bf16[3,56,640]{2,1,0:T(8,128)(2,1)S(1)}, bf16[3,56,640]{2,1,0:T(8,128)(2,1)S(1)}) custom-call(s32[2]{0:T(128)S(1)} %pad_add_fusion.place_ref, bf16[3,208,2048]{2,1,0:T(8,128)(2,1)S(1)} %bitcast.9, bf16[128,2048]{1,0:T(8,128)(2,1)S(1)} %copy-done.3, ...), custom_call_target="tpu_custom_call" | custom-call | flops 1635778560 | bytes 6252552 | tf_op jit(solution)/shard_map/pallas_call | solution.py:279
  45.6 1.5 %collective-permute-done.7.refs_1_ = bf16[3,56,640]{2,1,0:T(8,128)(2,1)S(1)} collective-permute-done((bf16[3,56,640]{2,1,0:T(8,128)(2,1)S(1)}, bf16[3,56,640]{2,1,0:T(8,128)(2,1)S(1)}, u32[]{:S(2)}, u32[]{:S(2)}) %collective-permute-start.7) | collective-permute-done | bytes 215072 | tf_op jit(solution)/shard_map/ppermute | solution.py:337
  47.1 2.6 %collective-permute-done.5.refs_0_.refs_9_ = bf16[128,2048]{1,0:T(8,128)(2,1)S(1)} collective-permute-done((bf16[128,2048]{1,0:T(8,128)(2,1)S(1)}, bf16[128,2048]{1,0:T(8,128)(2,1)S(1)}, u32[]{:S(2)}, u32[]{:S(2)}) %collective-permute-start.5) | collective-permute-done | bytes 524320 | tf_op jit(solution)/shard_map/ppermute | solution.py:315
  50.7 1.2 %collective-permute-start.14 = (bf16[64,2048]{1,0:T(8,128)(2,1)S(1)}, bf16[64,2048]{1,0:T(8,128)(2,1)S(1)}, u32[]{:S(2)}, u32[]{:S(2)}) collective-permute-start(bf16[64,2048]{1,0:T(8,128)(2,1)S(1)} %slice.7), channel_id=1, source_target_pairs={{8,0},{16,8},{24,16},{28,24},{20,28},{12,20},{4,12},{0,4},{9,1},{1... | collective-permute-start | bytes 786440 | tf_op jit(solution)/shard_map/ppermute | solution.py:315
  51.9 1.6 %collective-permute-start.8 = (bf16[3,56,640]{2,1,0:T(8,128)(2,1)S(1)}, bf16[3,56,640]{2,1,0:T(8,128)(2,1)S(1)}, u32[]{:S(2)}, u32[]{:S(2)}) collective-permute-start(bf16[3,56,640]{2,1,0:T(8,128)(2,1)S(1)} %get-tuple-element.55), channel_id=1, source_target_pairs={{0,2},{1,3},{2,0},{3,1},{4,6},{5,7},{6,4},{7,5},{8,10},{9,11},{10,... | collective-permute-start | bytes 645128 | tf_op jit(solution)/shard_map/ppermute | solution.py:337
  53.5 1.8 %shard_map.123 = (f32[3,56,256]{2,1,0:T(8,128)S(1)}, bf16[3,56,256]{2,1,0:T(8,128)(2,1)S(1)}, bf16[3,56,256]{2,1,0:T(8,128)(2,1)S(1)}, bf16[3,56,256]{2,1,0:T(8,128)(2,1)S(1)}) custom-call(s32[2]{0:T(128)S(1)} %pad_add_fusion.place_ref, bf16[3,208,2048]{2,1,0:T(8,128)(2,1)S(1)} %bitcast.10, bf16[128,2048]{1,0:T(8,128)(2,1)S(1)} %collective-permute-done.5.refs_0_.refs_9_, ...), custom_call_target="tpu_custom_call" | custom-call | flops 654311424 | bytes 4034568 | tf_op jit(solution)/shard_map/pallas_call | solution.py:279
  56.2 1.6 %collective-permute-start.11 = (bf16[3,56,256]{2,1,0:T(8,128)(2,1)S(1)}, bf16[3,56,256]{2,1,0:T(8,128)(2,1)S(1)}, u32[]{:S(2)}, u32[]{:S(2)}) collective-permute-start(bf16[3,56,256]{2,1,0:T(8,128)(2,1)S(1)} %get-tuple-element.63), channel_id=1, source_target_pairs={{0,2},{1,3},{2,0},{3,1},{4,6},{5,7},{6,4},{7,5},{8,10},{9,11},{10,... | collective-permute-start | bytes 258056 | tf_op jit(solution)/shard_map/ppermute | solution.py:337
  57.8 1.4 %shard_map.124 = (f32[3,56,128]{2,1,0:T(8,128)S(1)}, bf16[3,56,128]{2,1,0:T(8,128)(2,1)S(1)}, bf16[3,56,128]{2,1,0:T(8,128)(2,1)S(1)}, bf16[3,56,128]{2,1,0:T(8,128)(2,1)S(1)}) custom-call(s32[2]{0:T(128)S(1)} %pad_add_fusion.place_ref, bf16[3,208,2048]{2,1,0:T(8,128)(2,1)S(1)} %bitcast.11, bf16[64,2048]{1,0:T(8,128)(2,1)S(1)} %collective-permute-done.13.refs_0_.refs_11_, ...), custom_call_target="tpu_custom_call" | custom-call | flops 327155712 | bytes 3295240 | tf_op jit(solution)/shard_map/pallas_call | solution.py:279
  60.3 2.9 %collective-permute-done.9.refs_3_ = bf16[3,56,640]{2,1,0:T(8,128)(2,1)S(1)} collective-permute-done((bf16[3,56,640]{2,1,0:T(8,128)(2,1)S(1)}, bf16[3,56,640]{2,1,0:T(8,128)(2,1)S(1)}, u32[]{:S(2)}, u32[]{:S(2)}) %collective-permute-start.9) | collective-permute-done | bytes 215072 | tf_op jit(solution)/shard_map/ppermute | solution.py:337
  63.2 1.9 %collective-permute-start.17 = (bf16[3,56,128]{2,1,0:T(8,128)(2,1)S(1)}, bf16[3,56,128]{2,1,0:T(8,128)(2,1)S(1)}, u32[]{:S(2)}, u32[]{:S(2)}) collective-permute-start(bf16[3,56,128]{2,1,0:T(8,128)(2,1)S(1)} %get-tuple-element.70), channel_id=1, source_target_pairs={{0,3},{1,2},{2,1},{3,0},{4,7},{5,6},{6,5},{7,4},{8,11},{9,10},{10,... | collective-permute-start | bytes 129032 | tf_op jit(solution)/shard_map/ppermute | solution.py:337
  65.1 1.5 %shard_map.125 = (f32[56,1024]{1,0:T(8,128)S(1)}, f32[56,1024]{1,0:T(8,128)S(1)}) custom-call(f32[56,33]{1,0:T(8,128)S(1)} %collective-permute-done.2.poles_ref.refs_13_, bf16[1024,1024]{1,0:T(8,128)(2,1)S(1)} %copy-done.1, bf16[1024,1024]{1,0:T(8,128)(2,1)S(1)} %copy-done.2, f32[2,1024]{1,0:T(2,128)S(1)} %copy-done.6), custom_call_target="tpu_custom_call" | custom-call | flops 469762048 | bytes 4668640 | tf_op jit(solution)/shard_map/pallas_call | solution.py:279
  67.7 5.6 %shard_map.126 = (bf16[3,56,1024]{2,1,0:T(8,128)(2,1)S(1)}, f32[56,1024]{1,0:T(8,128)S(1)}, f32[56,1024]{1,0:T(8,128)S(1)}, f32[56,1]{1,0:T(8,128)S(1)}) custom-call(s32[2]{0:T(128)S(1)} %pad_add_fusion.place_ref, f32[3,56,640]{2,1,0:T(8,128)S(1)} %get-tuple-element.52.refs_0_, bf16[3,56,640]{2,1,0:T(8,128)(2,1)S(1)} %collective-permute-done.7.refs_1_, ...), custom_call_target="tpu_custom_call" | custom-call | flops 1879048192 | bytes 7306696 | tf_op jit(solution)/shard_map/pallas_call | solution.py:279
  73.3 1.7 %collective-permute-start.18 = (bf16[3,56,1024]{2,1,0:T(8,128)(2,1)S(1)}, bf16[3,56,1024]{2,1,0:T(8,128)(2,1)S(1)}, u32[]{:S(2)}, u32[]{:S(2)}) collective-permute-start(bf16[3,56,1024]{2,1,0:T(8,128)(2,1)S(1)} %get-tuple-element.75.refs_0_), channel_id=1, source_target_pairs={{0,2},{1,3},{2,0},{3,1},{4,6},{5,7},{6,4},{7,5},{8,10},{9,11},{10,... | collective-permute-start | bytes 1032200 | tf_op jit(solution)/shard_map/ppermute | solution.py:409
  75.0 2.0 %shard_map.127.refs_0_ = f32[56,33]{1,0:T(8,128)S(1)} custom-call(f32[56,33]{1,0:T(8,128)S(1)} %collective-permute-done.2.poles_ref.refs_13_, f32[56,1024]{1,0:T(8,128)S(1)} %get-tuple-element.76.tgc_ref, f32[56,1024]{1,0:T(8,128)S(1)} %get-tuple-element.77.tgs_ref, bf16[1024,1024]{1,0:T(8,128)(2,1)S(1)} %copy-done.1, bf16[1024,1024]{1,0:T(8,128)(2,1)S(1)} %copy-done.2, ...), custom_call_target="tpu_custom_call" | custom-call | flops 469762048 | bytes 4668064 | tf_op jit(solution)/shard_map/pallas_call | solution.py:279
  77.9 7.0 %collective-permute-done.19.refs_1_ = f32[56,33]{1,0:T(8,128)S(1)} collective-permute-done((f32[56,33]{1,0:T(8,128)S(1)}, f32[56,33]{1,0:T(8,128)S(1)}, u32[]{:S(2)}, u32[]{:S(2)}) %collective-permute-start.19) | collective-permute-done | bytes 7424 | tf_op jit(solution)/shard_map/ppermute | solution.py:409
  85.5 1.1 %collective-permute-done.22.refs_2_ = f32[56,33]{1,0:T(8,128)S(1)} collective-permute-done((f32[56,33]{1,0:T(8,128)S(1)}, f32[56,33]{1,0:T(8,128)S(1)}, u32[]{:S(2)}, u32[]{:S(2)}) %collective-permute-start.22) | collective-permute-done | bytes 7424 | tf_op jit(solution)/shard_map/ppermute | solution.py:424
  87.2 2.9 %collective-permute-start.24 = (f32[208,33]{1,0:T(8,128)S(1)}, f32[208,33]{1,0:T(8,128)S(1)}, u32[]{:S(2)}, u32[]{:S(2)}) collective-permute-start(f32[208,33]{1,0:T(8,128)S(1)} %shard_map.129), channel_id=1, source_target_pairs={{0,0},{8,1},{16,2},{24,3},{4,4},{12,5},{20,6},{28,7},{1,8},{9,9},{... | collective-permute-start | bytes 82376 | tf_op jit(solution)/shard_map/ppermute | solution.py:437
  90.1 4.0 %collective-permute-start.25 = (f32[208,33]{1,0:T(8,128)S(1)}, f32[208,33]{1,0:T(8,128)S(1)}, u32[]{:S(2)}, u32[]{:S(2)}) collective-permute-start(f32[208,33]{1,0:T(8,128)S(1)} %shard_map.129), channel_id=1, source_target_pairs={{4,0},{12,1},{20,2},{28,3},{0,4},{8,5},{16,6},{24,7},{5,8},{13,9},... | collective-permute-start | bytes 82376 | tf_op jit(solution)/shard_map/ppermute | solution.py:437
  94.1 5.7 %shard_map.128 = f32[3,208,2048]{2,1,0:T(8,128)} custom-call(s32[2]{0:T(128)S(1)} %pad_add_fusion.place_ref, bf16[3,56,1024]{2,1,0:T(8,128)(2,1)S(1)} %get-tuple-element.75.refs_0_, bf16[3,56,1024]{2,1,0:T(8,128)(2,1)S(1)} %collective-permute-done.18.refs_1_, bf16[3,56,1024]{2,1,0:T(8,128)(2,1)S(1)} %collective-permute-done.20.refs_2_, ...), custom_call_target="tpu_custom_call" | custom-call | flops 2617245696 | bytes 10584064 | tf_op jit(solution)/shard_map/pallas_call | solution.py:440
  99.9 1.0 collective-permute-done.24.refs_0_
  100.9 2.1 %collective-permute-done.25.refs_1_ = f32[208,33]{1,0:T(8,128)S(1)} collective-permute-done((f32[208,33]{1,0:T(8,128)S(1)}, f32[208,33]{1,0:T(8,128)S(1)}, u32[]{:S(2)}, u32[]{:S(2)}) %collective-permute-start.25) | collective-permute-done | bytes 27488 | tf_op jit(solution)/shard_map/ppermute | solution.py:437
  103.0 1.3 %shard_map.130 = (f32[16,416]{1,0:T(8,128)}, f32[16,416]{1,0:T(8,128)}, f32[1,416]{1,0:T(1,128)}) custom-call(s32[2]{0:T(128)S(1)} %pad_add_fusion.place_ref, f32[208,33]{1,0:T(8,128)S(1)} %collective-permute-done.24.refs_0_, f32[208,33]{1,0:T(8,128)S(1)} %collective-permute-done.25.refs_1_), custom_call_target="tpu_custom_call" | custom-call | bytes 109832 | tf_op jit(solution)/shard_map/pallas_call | solution.py:279
  (52 shorter events, 9.0 us)
Async XLA Ops:
  0.6 15.5 %collective-permute-start = (bf16[128,2048]{1,0:T(8,128)(2,1)}, bf16[128,2048]{1,0:T(8,128)(2,1)S(1)}, u32[]{:S(2)}, u32[]{:S(2)}) collective-permute-start(bf16[128,2048]{1,0:T(8,128)(2,1)} %refs_4_.1), channel_id=1, source_target_pairs={{0,8},{8,16},{16,24},{24,28},{28,20},{20,12},{12,4},{4,0},{1,9},{9... | collective-permute-start | bytes 1572872 | tf_op jit(solution)/shard_map/ppermute | solution.py:315
  2.3 13.9 %collective-permute-start.1 = (bf16[128,2048]{1,0:T(8,128)(2,1)}, bf16[128,2048]{1,0:T(8,128)(2,1)S(1)}, u32[]{:S(2)}, u32[]{:S(2)}) collective-permute-start(bf16[128,2048]{1,0:T(8,128)(2,1)} %refs_4_.1), channel_id=1, source_target_pairs={{8,0},{16,8},{24,16},{28,24},{20,28},{12,20},{4,12},{0,4},{9,1},{1... | collective-permute-start | bytes 1572872 | tf_op jit(solution)/shard_map/ppermute | solution.py:315
  4.3 11.8 %collective-permute-start.2 = (f32[56,33]{1,0:T(8,128)S(1)}, f32[56,33]{1,0:T(8,128)S(1)}, u32[]{:S(2)}, u32[]{:S(2)}) collective-permute-start(f32[56,33]{1,0:T(8,128)S(1)} %shard_map.120), channel_id=1, source_target_pairs={{0,0},{4,1},{8,2},{12,3},{16,4},{20,5},{24,6},{28,7},{1,8},{5,9},{... | collective-permute-start | bytes 22184 | tf_op jit(solution)/shard_map/ppermute | solution.py:350
  16.1 21.2 %collective-permute-start.3 = (bf16[128,2048]{1,0:T(8,128)(2,1)S(1)}, bf16[128,2048]{1,0:T(8,128)(2,1)S(1)}, u32[]{:S(2)}, u32[]{:S(2)}) collective-permute-start(bf16[128,2048]{1,0:T(8,128)(2,1)S(1)} %collective-permute-done.refs_1_.refs_5_), channel_id=1, source_target_pairs={{0,8},{8,16},{16,24},{24,28},{28,20},{20,12},{12,4},{4,0},{1,9},{9... | collective-permute-start | bytes 1572872 | tf_op jit(solution)/shard_map/ppermute | solution.py:315
  17.4 19.9 %collective-permute-start.4 = (bf16[128,2048]{1,0:T(8,128)(2,1)S(1)}, bf16[128,2048]{1,0:T(8,128)(2,1)S(1)}, u32[]{:S(2)}, u32[]{:S(2)}) collective-permute-start(bf16[128,2048]{1,0:T(8,128)(2,1)S(1)} %collective-permute-done.1.refs_2_.refs_6_), channel_id=1, source_target_pairs={{8,0},{16,8},{24,16},{28,24},{20,28},{12,20},{4,12},{0,4},{9,1},{1... | collective-permute-start | bytes 1572872 | tf_op jit(solution)/shard_map/ppermute | solution.py:315
  37.3 12.3 %collective-permute-start.5 = (bf16[128,2048]{1,0:T(8,128)(2,1)S(1)}, bf16[128,2048]{1,0:T(8,128)(2,1)S(1)}, u32[]{:S(2)}, u32[]{:S(2)}) collective-permute-start(bf16[128,2048]{1,0:T(8,128)(2,1)S(1)} %collective-permute-done.3.refs_3_.refs_7_), channel_id=1, source_target_pairs={{0,8},{8,16},{16,24},{24,28},{28,20},{20,12},{12,4},{4,0},{1,9},{9... | collective-permute-start | bytes 1572872 | tf_op jit(solution)/shard_map/ppermute | solution.py:315
  37.3 12.4 %collective-permute-start.6 = (bf16[128,2048]{1,0:T(8,128)(2,1)S(1)}, bf16[128,2048]{1,0:T(8,128)(2,1)S(1)}, u32[]{:S(2)}, u32[]{:S(2)}) collective-permute-start(bf16[128,2048]{1,0:T(8,128)(2,1)S(1)} %collective-permute-done.4.refs_4_.refs_8_), channel_id=1, source_target_pairs={{8,0},{16,8},{24,16},{28,24},{20,28},{12,20},{4,12},{0,4},{9,1},{1... | collective-permute-start | bytes 1572872 | tf_op jit(solution)/shard_map/ppermute | solution.py:315
  39.3 1.7 %copy-start = (bf16[208,3,2048]{2,0,1:T(8,128)(2,1)S(1)}, bf16[208,3,2048]{2,0,1:T(8,128)(2,1)}, u32[]{:S(2)}) copy-start(bf16[208,3,2048]{2,0,1:T(8,128)(2,1)} %param.10) | copy-start | bytes 7667716
  41.1 1.0 copy-start.3
  45.5 1.5 %collective-permute-start.7 = (bf16[3,56,640]{2,1,0:T(8,128)(2,1)S(1)}, bf16[3,56,640]{2,1,0:T(8,128)(2,1)S(1)}, u32[]{:S(2)}, u32[]{:S(2)}) collective-permute-start(bf16[3,56,640]{2,1,0:T(8,128)(2,1)S(1)} %get-tuple-element.53), channel_id=1, source_target_pairs={{0,1},{1,0},{2,3},{3,2},{4,5},{5,4},{6,7},{7,6},{8,9},{9,8},{10,11... | collective-permute-start | bytes 645128 | tf_op jit(solution)/shard_map/ppermute | solution.py:337
  49.8 6.4 %collective-permute-start.13 = (bf16[64,2048]{1,0:T(8,128)(2,1)S(1)}, bf16[64,2048]{1,0:T(8,128)(2,1)S(1)}, u32[]{:S(2)}, u32[]{:S(2)}) collective-permute-start(bf16[64,2048]{1,0:T(8,128)(2,1)S(1)} %slice.6), channel_id=1, source_target_pairs={{0,8},{8,16},{16,24},{24,28},{28,20},{20,12},{12,4},{4,0},{1,9},{9... | collective-permute-start | bytes 786440 | tf_op jit(solution)/shard_map/ppermute | solution.py:315
  50.7 7.1 %collective-permute-start.14 = (bf16[64,2048]{1,0:T(8,128)(2,1)S(1)}, bf16[64,2048]{1,0:T(8,128)(2,1)S(1)}, u32[]{:S(2)}, u32[]{:S(2)}) collective-permute-start(bf16[64,2048]{1,0:T(8,128)(2,1)S(1)} %slice.7), channel_id=1, source_target_pairs={{8,0},{16,8},{24,16},{28,24},{20,28},{12,20},{4,12},{0,4},{9,1},{1... | collective-permute-start | bytes 786440 | tf_op jit(solution)/shard_map/ppermute | solution.py:315
  51.9 7.4 %collective-permute-start.8 = (bf16[3,56,640]{2,1,0:T(8,128)(2,1)S(1)}, bf16[3,56,640]{2,1,0:T(8,128)(2,1)S(1)}, u32[]{:S(2)}, u32[]{:S(2)}) collective-permute-start(bf16[3,56,640]{2,1,0:T(8,128)(2,1)S(1)} %get-tuple-element.55), channel_id=1, source_target_pairs={{0,2},{1,3},{2,0},{3,1},{4,6},{5,7},{6,4},{7,5},{8,10},{9,11},{10,... | collective-permute-start | bytes 645128 | tf_op jit(solution)/shard_map/ppermute | solution.py:337
  53.5 11.6 %copy-start.1 = (bf16[1024,1024]{1,0:T(8,128)(2,1)S(1)}, bf16[1024,1024]{1,0:T(8,128)(2,1)}, u32[]{:S(2)}) copy-start(bf16[1024,1024]{1,0:T(8,128)(2,1)} %constant.15.clone.cos_ref.refs_16_) | copy-start | bytes 6291460
  53.5 11.6 %copy-start.2 = (bf16[1024,1024]{1,0:T(8,128)(2,1)S(1)}, bf16[1024,1024]{1,0:T(8,128)(2,1)}, u32[]{:S(2)}) copy-start(bf16[1024,1024]{1,0:T(8,128)(2,1)} %constant.16.clone.sin_ref.refs_17_) | copy-start | bytes 6291460
  53.5 11.6 %copy-start.6 = (f32[2,1024]{1,0:T(2,128)S(1)}, f32[2,1024]{1,0:T(2,128)}, u32[]{:S(2)}) copy-start(f32[2,1024]{1,0:T(2,128)} %constant.17.clone.twist_ref.refs_18_) | copy-start | bytes 24580
  53.5 9.7 %collective-permute-start.9 = (bf16[3,56,640]{2,1,0:T(8,128)(2,1)S(1)}, bf16[3,56,640]{2,1,0:T(8,128)(2,1)S(1)}, u32[]{:S(2)}, u32[]{:S(2)}) collective-permute-start(bf16[3,56,640]{2,1,0:T(8,128)(2,1)S(1)} %get-tuple-element.56), channel_id=1, source_target_pairs={{0,3},{1,2},{2,1},{3,0},{4,7},{5,6},{6,5},{7,4},{8,11},{9,10},{10,... | collective-permute-start | bytes 645128 | tf_op jit(solution)/shard_map/ppermute | solution.py:337
  55.3 7.8 %collective-permute-start.10 = (bf16[3,56,256]{2,1,0:T(8,128)(2,1)S(1)}, bf16[3,56,256]{2,1,0:T(8,128)(2,1)S(1)}, u32[]{:S(2)}, u32[]{:S(2)}) collective-permute-start(bf16[3,56,256]{2,1,0:T(8,128)(2,1)S(1)} %get-tuple-element.62), channel_id=1, source_target_pairs={{0,1},{1,0},{2,3},{3,2},{4,5},{5,4},{6,7},{7,6},{8,9},{9,8},{10,11... | collective-permute-start | bytes 258056 | tf_op jit(solution)/shard_map/ppermute | solution.py:337
  56.2 10.4 %collective-permute-start.11 = (bf16[3,56,256]{2,1,0:T(8,128)(2,1)S(1)}, bf16[3,56,256]{2,1,0:T(8,128)(2,1)S(1)}, u32[]{:S(2)}, u32[]{:S(2)}) collective-permute-start(bf16[3,56,256]{2,1,0:T(8,128)(2,1)S(1)} %get-tuple-element.63), channel_id=1, source_target_pairs={{0,2},{1,3},{2,0},{3,1},{4,6},{5,7},{6,4},{7,5},{8,10},{9,11},{10,... | collective-permute-start | bytes 258056 | tf_op jit(solution)/shard_map/ppermute | solution.py:337
  57.8 8.8 %collective-permute-start.12 = (bf16[3,56,256]{2,1,0:T(8,128)(2,1)S(1)}, bf16[3,56,256]{2,1,0:T(8,128)(2,1)S(1)}, u32[]{:S(2)}, u32[]{:S(2)}) collective-permute-start(bf16[3,56,256]{2,1,0:T(8,128)(2,1)S(1)} %get-tuple-element.64), channel_id=1, source_target_pairs={{0,3},{1,2},{2,1},{3,0},{4,7},{5,6},{6,5},{7,4},{8,11},{9,10},{10,... | collective-permute-start | bytes 258056 | tf_op jit(solution)/shard_map/ppermute | solution.py:337
  59.3 7.4 %collective-permute-start.15 = (bf16[3,56,128]{2,1,0:T(8,128)(2,1)S(1)}, bf16[3,56,128]{2,1,0:T(8,128)(2,1)S(1)}, u32[]{:S(2)}, u32[]{:S(2)}) collective-permute-start(bf16[3,56,128]{2,1,0:T(8,128)(2,1)S(1)} %get-tuple-element.68), channel_id=1, source_target_pairs={{0,1},{1,0},{2,3},{3,2},{4,5},{5,4},{6,7},{7,6},{8,9},{9,8},{10,11... | collective-permute-start | bytes 129032 | tf_op jit(solution)/shard_map/ppermute | solution.py:337
  63.1 4.4 %collective-permute-start.16 = (bf16[3,56,128]{2,1,0:T(8,128)(2,1)S(1)}, bf16[3,56,128]{2,1,0:T(8,128)(2,1)S(1)}, u32[]{:S(2)}, u32[]{:S(2)}) collective-permute-start(bf16[3,56,128]{2,1,0:T(8,128)(2,1)S(1)} %get-tuple-element.69), channel_id=1, source_target_pairs={{0,2},{1,3},{2,0},{3,1},{4,6},{5,7},{6,4},{7,5},{8,10},{9,11},{10,... | collective-permute-start | bytes 129032 | tf_op jit(solution)/shard_map/ppermute | solution.py:337
  63.2 4.5 %collective-permute-start.17 = (bf16[3,56,128]{2,1,0:T(8,128)(2,1)S(1)}, bf16[3,56,128]{2,1,0:T(8,128)(2,1)S(1)}, u32[]{:S(2)}, u32[]{:S(2)}) collective-permute-start(bf16[3,56,128]{2,1,0:T(8,128)(2,1)S(1)} %get-tuple-element.70), channel_id=1, source_target_pairs={{0,3},{1,2},{2,1},{3,0},{4,7},{5,6},{6,5},{7,4},{8,11},{9,10},{10,... | collective-permute-start | bytes 129032 | tf_op jit(solution)/shard_map/ppermute | solution.py:337
  73.3 20.8 %copy-start.4 = (bf16[128,2048]{1,0:T(8,128)(2,1)S(1)}, bf16[128,2048]{1,0:T(8,128)(2,1)}, u32[]{:S(2)}) copy-start(bf16[128,2048]{1,0:T(8,128)(2,1)} %refs_4_.1) | copy-start | bytes 1572868
  73.3 11.6 %collective-permute-start.18 = (bf16[3,56,1024]{2,1,0:T(8,128)(2,1)S(1)}, bf16[3,56,1024]{2,1,0:T(8,128)(2,1)S(1)}, u32[]{:S(2)}, u32[]{:S(2)}) collective-permute-start(bf16[3,56,1024]{2,1,0:T(8,128)(2,1)S(1)} %get-tuple-element.75.refs_0_), channel_id=1, source_target_pairs={{0,2},{1,3},{2,0},{3,1},{4,6},{5,7},{6,4},{7,5},{8,10},{9,11},{10,... | collective-permute-start | bytes 1032200 | tf_op jit(solution)/shard_map/ppermute | solution.py:409
  77.1 7.8 %collective-permute-start.19 = (f32[56,33]{1,0:T(8,128)S(1)}, f32[56,33]{1,0:T(8,128)S(1)}, u32[]{:S(2)}, u32[]{:S(2)}) collective-permute-start(f32[56,33]{1,0:T(8,128)S(1)} %shard_map.127.refs_0_), channel_id=1, source_target_pairs={{0,2},{1,3},{2,0},{3,1},{4,6},{5,7},{6,4},{7,5},{8,10},{9,11},{10,... | collective-permute-start | bytes 22184 | tf_op jit(solution)/shard_map/ppermute | solution.py:409
  77.5 16.6 %collective-permute-start.20 = (bf16[3,56,1024]{2,1,0:T(8,128)(2,1)S(1)}, bf16[3,56,1024]{2,1,0:T(8,128)(2,1)S(1)}, u32[]{:S(2)}, u32[]{:S(2)}) collective-permute-start(bf16[3,56,1024]{2,1,0:T(8,128)(2,1)S(1)} %get-tuple-element.75.refs_0_), channel_id=1, source_target_pairs={{0,1},{1,0},{2,3},{3,2},{4,5},{5,4},{6,7},{7,6},{8,9},{9,8},{10,11... | collective-permute-start | bytes 1032200 | tf_op jit(solution)/shard_map/ppermute | solution.py:414
  84.9 9.2 %collective-permute-start.21 = (bf16[3,56,1024]{2,1,0:T(8,128)(2,1)S(1)}, bf16[3,56,1024]{2,1,0:T(8,128)(2,1)S(1)}, u32[]{:S(2)}, u32[]{:S(2)}) collective-permute-start(bf16[3,56,1024]{2,1,0:T(8,128)(2,1)S(1)} %collective-permute-done.18.refs_1_), channel_id=1, source_target_pairs={{0,1},{1,0},{2,3},{3,2},{4,5},{5,4},{6,7},{7,6},{8,9},{9,8},{10,11... | collective-permute-start | bytes 1032200 | tf_op jit(solution)/shard_map/ppermute | solution.py:423
  85.0 1.6 %collective-permute-start.22 = (f32[56,33]{1,0:T(8,128)S(1)}, f32[56,33]{1,0:T(8,128)S(1)}, u32[]{:S(2)}, u32[]{:S(2)}) collective-permute-start(f32[56,33]{1,0:T(8,128)S(1)} %shard_map.127.refs_0_), channel_id=1, source_target_pairs={{0,1},{1,0},{2,3},{3,2},{4,5},{5,4},{6,7},{7,6},{8,9},{9,8},{10,11... | collective-permute-start | bytes 22184 | tf_op jit(solution)/shard_map/ppermute | solution.py:424
  85.4 1.2 %collective-permute-start.23 = (f32[56,33]{1,0:T(8,128)S(1)}, f32[56,33]{1,0:T(8,128)S(1)}, u32[]{:S(2)}, u32[]{:S(2)}) collective-permute-start(f32[56,33]{1,0:T(8,128)S(1)} %collective-permute-done.19.refs_1_), channel_id=1, source_target_pairs={{0,1},{1,0},{2,3},{3,2},{4,5},{5,4},{6,7},{7,6},{8,9},{9,8},{10,11... | collective-permute-start | bytes 22184 | tf_op jit(solution)/shard_map/ppermute | solution.py:424
  87.2 13.7 %collective-permute-start.24 = (f32[208,33]{1,0:T(8,128)S(1)}, f32[208,33]{1,0:T(8,128)S(1)}, u32[]{:S(2)}, u32[]{:S(2)}) collective-permute-start(f32[208,33]{1,0:T(8,128)S(1)} %shard_map.129), channel_id=1, source_target_pairs={{0,0},{8,1},{16,2},{24,3},{4,4},{12,5},{20,6},{28,7},{1,8},{9,9},{... | collective-permute-start | bytes 82376 | tf_op jit(solution)/shard_map/ppermute | solution.py:437
  90.1 12.9 %collective-permute-start.25 = (f32[208,33]{1,0:T(8,128)S(1)}, f32[208,33]{1,0:T(8,128)S(1)}, u32[]{:S(2)}, u32[]{:S(2)}) collective-permute-start(f32[208,33]{1,0:T(8,128)S(1)} %shard_map.129), channel_id=1, source_target_pairs={{4,0},{12,1},{20,2},{28,3},{0,4},{8,5},{16,6},{24,7},{5,8},{13,9},... | collective-permute-start | bytes 82376 | tf_op jit(solution)/shard_map/ppermute | solution.py:437
  (1 other events, 0.9 us)

commit v12 on v9

--- a/solution.py
+++ b/solution.py
@@ -375,14 +375,15 @@
             half = block_len // 2
             halves, waiting = lax.optimization_barrier(((pair[0][:half], pair[1][half:]), waiting))
             next_pair = send_on(halves)
+            break
         sums = project(waiting)
         partials += to_owners(sums)
         group_slots.append(len(waiting))
         waiting = []
     pair = next_pair
     pieces += pair
-    partials += to_owners(project(list(pair)))
-    group_slots.append(1)
+    partials += to_owners(project([*waiting, *pair]))
+    group_slots.append(len(waiting) + 1)
     hc, hs = call(
         functools.partial(taps_kernel, order=order), (spectrum, spectrum),
         8 * square, part * tokens * order, poles, cos_table, sin_table, twist,

time: 104 us -> 103 us (level)
  waiting for transfers between devices: 22.9 us -> 24.9 us
  starting transfers between devices: 36 us -> 34.7 us
    ppermute x9 -> x6, starting transfers between devices: 8.22 us -> 6.59 us  [to_owners(): lax.ppermute(sums[d], 'ch', [(h, h ^ d) for h in range(n_ch)])]
    ppermute x4, waiting for transfers between devices: 2.5 us -> 3.68 us  [send_on(): lax.ppermute(pair[0], 'seq', ahead)]
    pallas_call x10 -> x9, Pallas kernels: 18.9 us -> 17.9 us  [call(): pl.pallas_call(kernel, out_shape=outs, in_specs=specs, out_specs=[whole]...]
    ppermute x9 -> x6, waiting for transfers between devices: 5.46 us -> 6.36 us  [to_owners(): lax.ppermute(sums[d], 'ch', [(h, h ^ d) for h in range(n_ch)])]
    unnamed x14 -> x16, local copies, waits for them, and re-layouts: 3.67 us -> 3.68 us
  transfers between devices with their start and end apart: 27 -> 24, of which waited for: 11 -> 12; matrix products, arithmetic and copies ran while one was open for 1% -> 1% of each run, Pallas kernels for 17% -> 16%
where the time goes in v12:
time: 103 us
  starting transfers between devices  34.7 us (34%)
  waiting for transfers between devices  24.9 us (24%)
  Pallas kernels  23.6 us (23%)
  blocking collectives  14.2 us (14%)
  local copies, waits for them, and re-layouts  3.85 us (4%)
    pallas_call x9, Pallas kernels, call(): pl.pallas_call(kernel, out_shape=outs, in_specs=specs, out_specs=[whole]...  17.9 us
    all_to_all x1, blocking collectives, local(): lax.all_to_all(upper, 'seq', split_axis=0, concat_axis=0, tiled=True)  14.2 us
    ppermute x2, starting transfers between devices, local(): blocks.append(lax.ppermute(block_sums, ('seq', 'ch'), route))  6.86 us
    ppermute x6, starting transfers between devices, to_owners(): lax.ppermute(sums[d], 'ch', [(h, h ^ d) for h in range(n_ch)])  6.59 us
    ppermute x2, waiting for transfers between devices, chips(): lax.ppermute(array, 'ch', [(h, h ^ d) for h in range(n_ch)])  6.56 us
    ppermute x4, starting transfers between devices, send_on(): lax.ppermute(pair[1], 'seq', behind)  6.48 us
    ppermute x6, waiting for transfers between devices, to_owners(): lax.ppermute(sums[d], 'ch', [(h, h ^ d) for h in range(n_ch)])  6.36 us
    pallas_call x1, Pallas kernels, local(): pl.pallas_call(functools.partial(weight_kernel, shares=n_ch), out_shape=j...  5.73 us
  transfers between devices with their start and end apart: 24, of which 12 were waited for; matrix products, arithmetic and copies ran while one was open for 1% of the time, Pallas kernels for 16%

profile of v12, /device:TPU:4, one launch (start us, length us, event | category | flops | bytes accessed | tf_op | source)
XLA Modules:
  0.0 103.0 jit_solution(2273860007179020634)
XLA Ops:
  0.6 1.6 %collective-permute-start = (bf16[128,2048]{1,0:T(8,128)(2,1)}, bf16[128,2048]{1,0:T(8,128)(2,1)S(1)}, u32[]{:S(2)}, u32[]{:S(2)}) collective-permute-start(bf16[128,2048]{1,0:T(8,128)(2,1)} %refs_4_.1), channel_id=1, source_target_pairs={{0,8},{8,16},{16,24},{24,28},{28,20},{20,12},{12,4},{4,0},{1,9},{9... | collective-permute-start | bytes 1572872 | tf_op jit(solution)/shard_map/ppermute | solution.py:315
  5.8 3.3 %all-to-all-start = ((bf16[4,2,56,128]{3,2,1,0:T(8,128)(2,1)}), bf16[4,2,56,128]{3,2,1,0:T(8,128)(2,1)S(1)}, u32[]{:S(2)}, u32[]{:S(2)}) async-start(bf16[4,2,56,128]{3,2,1,0:T(8,128)(2,1)} %shard_map.121), calls=%async_computation | async-start | bytes 229376 | tf_op jit(solution)/shard_map/all_to_all | solution.py:355
  9.2 4.4 %collective-permute-start.2 = (f32[56,33]{1,0:T(8,128)S(1)}, f32[56,33]{1,0:T(8,128)S(1)}, u32[]{:S(2)}, u32[]{:S(2)}) collective-permute-start(f32[56,33]{1,0:T(8,128)S(1)} %shard_map.120), channel_id=1, source_target_pairs={{0,0},{4,1},{8,2},{12,3},{16,4},{20,5},{24,6},{28,7},{1,8},{5,9},{... | collective-permute-start | bytes 22184 | tf_op jit(solution)/shard_map/ppermute | solution.py:350
  13.6 2.5 %collective-permute-done.2.poles_ref.refs_9_ = f32[56,33]{1,0:T(8,128)S(1)} collective-permute-done((f32[56,33]{1,0:T(8,128)S(1)}, f32[56,33]{1,0:T(8,128)S(1)}, u32[]{:S(2)}, u32[]{:S(2)}) %collective-permute-start.2) | collective-permute-done | bytes 7424 | tf_op jit(solution)/shard_map/ppermute | solution.py:350
  16.1 1.3 %collective-permute-start.3 = (bf16[128,2048]{1,0:T(8,128)(2,1)S(1)}, bf16[128,2048]{1,0:T(8,128)(2,1)S(1)}, u32[]{:S(2)}, u32[]{:S(2)}) collective-permute-start(bf16[128,2048]{1,0:T(8,128)(2,1)S(1)} %collective-permute-done.refs_1_.refs_5_), channel_id=1, source_target_pairs={{0,8},{8,16},{16,24},{24,28},{28,20},{20,12},{12,4},{4,0},{1,9},{9... | collective-permute-start | bytes 1572872 | tf_op jit(solution)/shard_map/ppermute | solution.py:315
  17.4 3.3 %collective-permute-start.4 = (bf16[128,2048]{1,0:T(8,128)(2,1)S(1)}, bf16[128,2048]{1,0:T(8,128)(2,1)S(1)}, u32[]{:S(2)}, u32[]{:S(2)}) collective-permute-start(bf16[128,2048]{1,0:T(8,128)(2,1)S(1)} %collective-permute-done.1.refs_2_.refs_6_), channel_id=1, source_target_pairs={{8,0},{16,8},{24,16},{28,24},{20,28},{12,20},{4,12},{0,4},{9,1},{1... | collective-permute-start | bytes 1572872 | tf_op jit(solution)/shard_map/ppermute | solution.py:315
  20.7 14.2 %all_to_all.10.refs_8_ = bf16[8,56,128]{2,1,0:T(8,128)(2,1)S(1)} all-to-all(bf16[8,56,128]{2,1,0:T(8,128)(2,1)S(1)} %bitcast.12), channel_id=1, replica_groups=mesh['seq'=8,'ch'=4] {'seq'}, dimensions={0} | all-to-all | bytes 229376 | tf_op jit(solution)/shard_map/all_to_all | solution.py:358
  35.9 1.1 %collective-permute-start.6 = (bf16[128,2048]{1,0:T(8,128)(2,1)S(1)}, bf16[128,2048]{1,0:T(8,128)(2,1)S(1)}, u32[]{:S(2)}, u32[]{:S(2)}) collective-permute-start(bf16[128,2048]{1,0:T(8,128)(2,1)S(1)} %collective-permute-done.4.refs_4_.refs_8_), channel_id=1, source_target_pairs={{8,0},{16,8},{24,16},{28,24},{20,28},{12,20},{4,12},{0,4},{9,1},{1... | collective-permute-start | bytes 1572872 | tf_op jit(solution)/shard_map/ppermute | solution.py:315
  37.0 1.7 %copy-done.2 = bf16[208,3,2048]{2,0,1:T(8,128)(2,1)S(1)} copy-done((bf16[208,3,2048]{2,0,1:T(8,128)(2,1)S(1)}, bf16[208,3,2048]{2,0,1:T(8,128)(2,1)}, u32[]{:S(2)}) %copy-start.2) | copy-done | bytes 2555928
  38.7 1.0 %copy-done.4 = bf16[128,2048]{1,0:T(8,128)(2,1)S(1)} copy-done((bf16[128,2048]{1,0:T(8,128)(2,1)S(1)}, bf16[128,2048]{1,0:T(8,128)(2,1)}, u32[]{:S(2)}) %copy-start.4) | copy-done | bytes 524312
  39.8 3.4 %shard_map.122 = (f32[3,56,640]{2,1,0:T(8,128)S(1)}, bf16[3,56,640]{2,1,0:T(8,128)(2,1)S(1)}, bf16[3,56,640]{2,1,0:T(8,128)(2,1)S(1)}, bf16[3,56,640]{2,1,0:T(8,128)(2,1)S(1)}) custom-call(s32[2]{0:T(128)S(1)} %pad_add_fusion.place_ref, bf16[3,208,2048]{2,1,0:T(8,128)(2,1)S(1)} %bitcast.9, bf16[128,2048]{1,0:T(8,128)(2,1)S(1)} %copy-done.4, ...), custom_call_target="tpu_custom_call" | custom-call | flops 1635778560 | bytes 6252552 | tf_op jit(solution)/shard_map/pallas_call | solution.py:279
  43.3 1.5 %collective-permute-done.7.refs_1_ = bf16[3,56,640]{2,1,0:T(8,128)(2,1)S(1)} collective-permute-done((bf16[3,56,640]{2,1,0:T(8,128)(2,1)S(1)}, bf16[3,56,640]{2,1,0:T(8,128)(2,1)S(1)}, u32[]{:S(2)}, u32[]{:S(2)}) %collective-permute-start.7) | collective-permute-done | bytes 215072 | tf_op jit(solution)/shard_map/ppermute | solution.py:337
  44.8 2.5 %collective-permute-done.5.refs_0_.refs_9_ = bf16[128,2048]{1,0:T(8,128)(2,1)S(1)} collective-permute-done((bf16[128,2048]{1,0:T(8,128)(2,1)S(1)}, bf16[128,2048]{1,0:T(8,128)(2,1)S(1)}, u32[]{:S(2)}, u32[]{:S(2)}) %collective-permute-start.5) | collective-permute-done | bytes 524320 | tf_op jit(solution)/shard_map/ppermute | solution.py:315
  48.3 1.7 %collective-permute-start.11 = (bf16[64,2048]{1,0:T(8,128)(2,1)S(1)}, bf16[64,2048]{1,0:T(8,128)(2,1)S(1)}, u32[]{:S(2)}, u32[]{:S(2)}) collective-permute-start(bf16[64,2048]{1,0:T(8,128)(2,1)S(1)} %slice.7), channel_id=1, source_target_pairs={{8,0},{16,8},{24,16},{28,24},{20,28},{12,20},{4,12},{0,4},{9,1},{1... | collective-permute-start | bytes 786440 | tf_op jit(solution)/shard_map/ppermute | solution.py:315
  50.0 3.1 %collective-permute-start.8 = (bf16[3,56,640]{2,1,0:T(8,128)(2,1)S(1)}, bf16[3,56,640]{2,1,0:T(8,128)(2,1)S(1)}, u32[]{:S(2)}, u32[]{:S(2)}) collective-permute-start(bf16[3,56,640]{2,1,0:T(8,128)(2,1)S(1)} %get-tuple-element.53), channel_id=1, source_target_pairs={{0,2},{1,3},{2,0},{3,1},{4,6},{5,7},{6,4},{7,5},{8,10},{9,11},{10,... | collective-permute-start | bytes 645128 | tf_op jit(solution)/shard_map/ppermute | solution.py:337
  53.1 1.2 %collective-permute-done.10.refs_2_.refs_11_ = bf16[64,2048]{1,0:T(8,128)(2,1)S(1)} collective-permute-done((bf16[64,2048]{1,0:T(8,128)(2,1)S(1)}, bf16[64,2048]{1,0:T(8,128)(2,1)S(1)}, u32[]{:S(2)}, u32[]{:S(2)}) %collective-permute-start.10) | collective-permute-done | bytes 262176 | tf_op jit(solution)/shard_map/ppermute | solution.py:315
  54.6 2.4 %shard_map.123 = (f32[3,56,384]{2,1,0:T(8,128)S(1)}, bf16[3,56,384]{2,1,0:T(8,128)(2,1)S(1)}, bf16[3,56,384]{2,1,0:T(8,128)(2,1)S(1)}, bf16[3,56,384]{2,1,0:T(8,128)(2,1)S(1)}) custom-call(s32[2]{0:T(128)S(1)} %pad_add_fusion.place_ref, bf16[3,208,2048]{2,1,0:T(8,128)(2,1)S(1)} %bitcast.10, bf16[128,2048]{1,0:T(8,128)(2,1)S(1)} %collective-permute-done.5.refs_0_.refs_9_, ...), custom_call_target="tpu_custom_call" | custom-call | flops 981467136 | bytes 4773896 | tf_op jit(solution)/shard_map/pallas_call | solution.py:279
  57.1 3.3 %collective-permute-start.13 = (bf16[3,56,384]{2,1,0:T(8,128)(2,1)S(1)}, bf16[3,56,384]{2,1,0:T(8,128)(2,1)S(1)}, u32[]{:S(2)}, u32[]{:S(2)}) collective-permute-start(bf16[3,56,384]{2,1,0:T(8,128)(2,1)S(1)} %get-tuple-element.63), channel_id=1, source_target_pairs={{0,2},{1,3},{2,0},{3,1},{4,6},{5,7},{6,4},{7,5},{8,10},{9,11},{10,... | collective-permute-start | bytes 387080 | tf_op jit(solution)/shard_map/ppermute | solution.py:337
  60.5 1.5 %shard_map.124 = (f32[56,1024]{1,0:T(8,128)S(1)}, f32[56,1024]{1,0:T(8,128)S(1)}) custom-call(f32[56,33]{1,0:T(8,128)S(1)} %collective-permute-done.2.poles_ref.refs_9_, bf16[1024,1024]{1,0:T(8,128)(2,1)S(1)} %copy-done, bf16[1024,1024]{1,0:T(8,128)(2,1)S(1)} %copy-done.1, f32[2,1024]{1,0:T(2,128)S(1)} %copy-done.7), custom_call_target="tpu_custom_call" | custom-call | flops 469762048 | bytes 4668640 | tf_op jit(solution)/shard_map/pallas_call | solution.py:279
  62.0 2.7 %collective-permute-done.13.refs_6_ = bf16[3,56,384]{2,1,0:T(8,128)(2,1)S(1)} collective-permute-done((bf16[3,56,384]{2,1,0:T(8,128)(2,1)S(1)}, bf16[3,56,384]{2,1,0:T(8,128)(2,1)S(1)}, u32[]{:S(2)}, u32[]{:S(2)}) %collective-permute-start.13) | collective-permute-done | bytes 129056 | tf_op jit(solution)/shard_map/ppermute | solution.py:337
  64.7 2.2 %collective-permute-done.14.refs_7_ = bf16[3,56,384]{2,1,0:T(8,128)(2,1)S(1)} collective-permute-done((bf16[3,56,384]{2,1,0:T(8,128)(2,1)S(1)}, bf16[3,56,384]{2,1,0:T(8,128)(2,1)S(1)}, u32[]{:S(2)}, u32[]{:S(2)}) %collective-permute-start.14) | collective-permute-done | bytes 129056 | tf_op jit(solution)/shard_map/ppermute | solution.py:337
  66.9 5.4 %shard_map.125 = (bf16[3,56,1024]{2,1,0:T(8,128)(2,1)S(1)}, f32[56,1024]{1,0:T(8,128)S(1)}, f32[56,1024]{1,0:T(8,128)S(1)}, f32[56,1]{1,0:T(8,128)S(1)}) custom-call(s32[2]{0:T(128)S(1)} %pad_add_fusion.place_ref, f32[3,56,640]{2,1,0:T(8,128)S(1)} %get-tuple-element.50.refs_0_, bf16[3,56,640]{2,1,0:T(8,128)(2,1)S(1)} %collective-permute-done.7.refs_1_, ...), custom_call_target="tpu_custom_call" | custom-call | flops 1879048192 | bytes 7306696 | tf_op jit(solution)/shard_map/pallas_call | solution.py:279
  72.4 1.6 %collective-permute-start.15 = (bf16[3,56,1024]{2,1,0:T(8,128)(2,1)S(1)}, bf16[3,56,1024]{2,1,0:T(8,128)(2,1)S(1)}, u32[]{:S(2)}, u32[]{:S(2)}) collective-permute-start(bf16[3,56,1024]{2,1,0:T(8,128)(2,1)S(1)} %get-tuple-element.69.refs_0_), channel_id=1, source_target_pairs={{0,2},{1,3},{2,0},{3,1},{4,6},{5,7},{6,4},{7,5},{8,10},{9,11},{10,... | collective-permute-start | bytes 1032200 | tf_op jit(solution)/shard_map/ppermute | solution.py:410
  74.0 2.0 %shard_map.126.refs_0_ = f32[56,33]{1,0:T(8,128)S(1)} custom-call(f32[56,33]{1,0:T(8,128)S(1)} %collective-permute-done.2.poles_ref.refs_9_, f32[56,1024]{1,0:T(8,128)S(1)} %get-tuple-element.70.tgc_ref, f32[56,1024]{1,0:T(8,128)S(1)} %get-tuple-element.71.tgs_ref, bf16[1024,1024]{1,0:T(8,128)(2,1)S(1)} %copy-done, bf16[1024,1024]{1,0:T(8,128)(2,1)S(1)} %copy-done.1, ...), custom_call_target="tpu_custom_call" | custom-call | flops 469762048 | bytes 4668064 | tf_op jit(solution)/shard_map/pallas_call | solution.py:279
  76.6 6.6 %collective-permute-done.16.refs_1_ = f32[56,33]{1,0:T(8,128)S(1)} collective-permute-done((f32[56,33]{1,0:T(8,128)S(1)}, f32[56,33]{1,0:T(8,128)S(1)}, u32[]{:S(2)}, u32[]{:S(2)}) %collective-permute-start.16) | collective-permute-done | bytes 7424 | tf_op jit(solution)/shard_map/ppermute | solution.py:410
  83.7 1.2 %collective-permute-done.19.refs_2_ = f32[56,33]{1,0:T(8,128)S(1)} collective-permute-done((f32[56,33]{1,0:T(8,128)S(1)}, f32[56,33]{1,0:T(8,128)S(1)}, u32[]{:S(2)}, u32[]{:S(2)}) %collective-permute-start.19) | collective-permute-done | bytes 7424 | tf_op jit(solution)/shard_map/ppermute | solution.py:425
  85.4 4.6 %collective-permute-start.21 = (f32[208,33]{1,0:T(8,128)S(1)}, f32[208,33]{1,0:T(8,128)S(1)}, u32[]{:S(2)}, u32[]{:S(2)}) collective-permute-start(f32[208,33]{1,0:T(8,128)S(1)} %shard_map.128), channel_id=1, source_target_pairs={{0,0},{8,1},{16,2},{24,3},{4,4},{12,5},{20,6},{28,7},{1,8},{9,9},{... | collective-permute-start | bytes 82376 | tf_op jit(solution)/shard_map/ppermute | solution.py:438
  90.0 2.3 %collective-permute-start.22 = (f32[208,33]{1,0:T(8,128)S(1)}, f32[208,33]{1,0:T(8,128)S(1)}, u32[]{:S(2)}, u32[]{:S(2)}) collective-permute-start(f32[208,33]{1,0:T(8,128)S(1)} %shard_map.128), channel_id=1, source_target_pairs={{4,0},{12,1},{20,2},{28,3},{0,4},{8,5},{16,6},{24,7},{5,8},{13,9},... | collective-permute-start | bytes 82376 | tf_op jit(solution)/shard_map/ppermute | solution.py:438
  92.3 5.7 %shard_map.127 = f32[3,208,2048]{2,1,0:T(8,128)} custom-call(s32[2]{0:T(128)S(1)} %pad_add_fusion.place_ref, bf16[3,56,1024]{2,1,0:T(8,128)(2,1)S(1)} %get-tuple-element.69.refs_0_, bf16[3,56,1024]{2,1,0:T(8,128)(2,1)S(1)} %collective-permute-done.15.refs_1_, bf16[3,56,1024]{2,1,0:T(8,128)(2,1)S(1)} %collective-permute-done.17.refs_2_, ...), custom_call_target="tpu_custom_call" | custom-call | flops 2617245696 | bytes 10584064 | tf_op jit(solution)/shard_map/pallas_call | solution.py:441
  98.1 1.1 %collective-permute-done.21.refs_0_ = f32[208,33]{1,0:T(8,128)S(1)} collective-permute-done((f32[208,33]{1,0:T(8,128)S(1)}, f32[208,33]{1,0:T(8,128)S(1)}, u32[]{:S(2)}, u32[]{:S(2)}) %collective-permute-start.21) | collective-permute-done | bytes 27488 | tf_op jit(solution)/shard_map/ppermute | solution.py:438
  99.2 2.5 %collective-permute-done.22.refs_1_ = f32[208,33]{1,0:T(8,128)S(1)} collective-permute-done((f32[208,33]{1,0:T(8,128)S(1)}, f32[208,33]{1,0:T(8,128)S(1)}, u32[]{:S(2)}, u32[]{:S(2)}) %collective-permute-start.22) | collective-permute-done | bytes 27488 | tf_op jit(solution)/shard_map/ppermute | solution.py:438
  101.7 1.3 %shard_map.129 = (f32[16,416]{1,0:T(8,128)}, f32[16,416]{1,0:T(8,128)}, f32[1,416]{1,0:T(1,128)}) custom-call(s32[2]{0:T(128)S(1)} %pad_add_fusion.place_ref, f32[208,33]{1,0:T(8,128)S(1)} %collective-permute-done.21.refs_0_, f32[208,33]{1,0:T(8,128)S(1)} %collective-permute-done.22.refs_1_), custom_call_target="tpu_custom_call" | custom-call | bytes 109832 | tf_op jit(solution)/shard_map/pallas_call | solution.py:279
  (48 shorter events, 7.8 us)
Async XLA Ops:
  0.6 15.5 %collective-permute-start = (bf16[128,2048]{1,0:T(8,128)(2,1)}, bf16[128,2048]{1,0:T(8,128)(2,1)S(1)}, u32[]{:S(2)}, u32[]{:S(2)}) collective-permute-start(bf16[128,2048]{1,0:T(8,128)(2,1)} %refs_4_.1), channel_id=1, source_target_pairs={{0,8},{8,16},{16,24},{24,28},{28,20},{20,12},{12,4},{4,0},{1,9},{9... | collective-permute-start | bytes 1572872 | tf_op jit(solution)/shard_map/ppermute | solution.py:315
  2.3 13.9 %collective-permute-start.1 = (bf16[128,2048]{1,0:T(8,128)(2,1)}, bf16[128,2048]{1,0:T(8,128)(2,1)S(1)}, u32[]{:S(2)}, u32[]{:S(2)}) collective-permute-start(bf16[128,2048]{1,0:T(8,128)(2,1)} %refs_4_.1), channel_id=1, source_target_pairs={{8,0},{16,8},{24,16},{28,24},{20,28},{12,20},{4,12},{0,4},{9,1},{1... | collective-permute-start | bytes 1572872 | tf_op jit(solution)/shard_map/ppermute | solution.py:315
  4.3 0.9 copy-start.6
  5.8 10.3 %all-to-all-start = ((bf16[4,2,56,128]{3,2,1,0:T(8,128)(2,1)}), bf16[4,2,56,128]{3,2,1,0:T(8,128)(2,1)S(1)}, u32[]{:S(2)}, u32[]{:S(2)}) async-start(bf16[4,2,56,128]{3,2,1,0:T(8,128)(2,1)} %shard_map.121), calls=%async_computation | async-start | bytes 229376 | tf_op jit(solution)/shard_map/all_to_all | solution.py:355
  9.2 6.9 %collective-permute-start.2 = (f32[56,33]{1,0:T(8,128)S(1)}, f32[56,33]{1,0:T(8,128)S(1)}, u32[]{:S(2)}, u32[]{:S(2)}) collective-permute-start(f32[56,33]{1,0:T(8,128)S(1)} %shard_map.120), channel_id=1, source_target_pairs={{0,0},{4,1},{8,2},{12,3},{16,4},{20,5},{24,6},{28,7},{1,8},{5,9},{... | collective-permute-start | bytes 22184 | tf_op jit(solution)/shard_map/ppermute | solution.py:350
  16.1 18.8 %collective-permute-start.3 = (bf16[128,2048]{1,0:T(8,128)(2,1)S(1)}, bf16[128,2048]{1,0:T(8,128)(2,1)S(1)}, u32[]{:S(2)}, u32[]{:S(2)}) collective-permute-start(bf16[128,2048]{1,0:T(8,128)(2,1)S(1)} %collective-permute-done.refs_1_.refs_5_), channel_id=1, source_target_pairs={{0,8},{8,16},{16,24},{24,28},{28,20},{20,12},{12,4},{4,0},{1,9},{9... | collective-permute-start | bytes 1572872 | tf_op jit(solution)/shard_map/ppermute | solution.py:315
  17.4 17.5 %collective-permute-start.4 = (bf16[128,2048]{1,0:T(8,128)(2,1)S(1)}, bf16[128,2048]{1,0:T(8,128)(2,1)S(1)}, u32[]{:S(2)}, u32[]{:S(2)}) collective-permute-start(bf16[128,2048]{1,0:T(8,128)(2,1)S(1)} %collective-permute-done.1.refs_2_.refs_6_), channel_id=1, source_target_pairs={{8,0},{16,8},{24,16},{28,24},{20,28},{12,20},{4,12},{0,4},{9,1},{1... | collective-permute-start | bytes 1572872 | tf_op jit(solution)/shard_map/ppermute | solution.py:315
  35.0 12.3 %collective-permute-start.5 = (bf16[128,2048]{1,0:T(8,128)(2,1)S(1)}, bf16[128,2048]{1,0:T(8,128)(2,1)S(1)}, u32[]{:S(2)}, u32[]{:S(2)}) collective-permute-start(bf16[128,2048]{1,0:T(8,128)(2,1)S(1)} %collective-permute-done.3.refs_3_.refs_7_), channel_id=1, source_target_pairs={{0,8},{8,16},{16,24},{24,28},{28,20},{20,12},{12,4},{4,0},{1,9},{9... | collective-permute-start | bytes 1572872 | tf_op jit(solution)/shard_map/ppermute | solution.py:315
  35.9 11.9 %collective-permute-start.6 = (bf16[128,2048]{1,0:T(8,128)(2,1)S(1)}, bf16[128,2048]{1,0:T(8,128)(2,1)S(1)}, u32[]{:S(2)}, u32[]{:S(2)}) collective-permute-start(bf16[128,2048]{1,0:T(8,128)(2,1)S(1)} %collective-permute-done.4.refs_4_.refs_8_), channel_id=1, source_target_pairs={{8,0},{16,8},{24,16},{28,24},{20,28},{12,20},{4,12},{0,4},{9,1},{1... | collective-permute-start | bytes 1572872 | tf_op jit(solution)/shard_map/ppermute | solution.py:315
  37.0 1.7 %copy-start.2 = (bf16[208,3,2048]{2,0,1:T(8,128)(2,1)S(1)}, bf16[208,3,2048]{2,0,1:T(8,128)(2,1)}, u32[]{:S(2)}) copy-start(bf16[208,3,2048]{2,0,1:T(8,128)(2,1)} %param.10) | copy-start | bytes 7667716
  38.7 1.0 %copy-start.4 = (bf16[128,2048]{1,0:T(8,128)(2,1)S(1)}, bf16[128,2048]{1,0:T(8,128)(2,1)}, u32[]{:S(2)}) copy-start(bf16[128,2048]{1,0:T(8,128)(2,1)} %refs_4_.1) | copy-start | bytes 1572868
  39.8 14.9 %copy-start.3 = (bf16[208,3,2048]{2,0,1:T(8,128)(2,1)S(1)}, bf16[208,3,2048]{2,0,1:T(8,128)(2,1)}, u32[]{:S(2)}) copy-start(bf16[208,3,2048]{2,0,1:T(8,128)(2,1)} %param.10) | copy-start | bytes 7667716
  43.2 17.3 %copy-start = (bf16[1024,1024]{1,0:T(8,128)(2,1)S(1)}, bf16[1024,1024]{1,0:T(8,128)(2,1)}, u32[]{:S(2)}) copy-start(bf16[1024,1024]{1,0:T(8,128)(2,1)} %constant.15.clone.cos_ref.refs_12_) | copy-start | bytes 6291460
  43.2 17.3 %copy-start.1 = (bf16[1024,1024]{1,0:T(8,128)(2,1)S(1)}, bf16[1024,1024]{1,0:T(8,128)(2,1)}, u32[]{:S(2)}) copy-start(bf16[1024,1024]{1,0:T(8,128)(2,1)} %constant.16.clone.sin_ref.refs_13_) | copy-start | bytes 6291460
  43.2 17.2 %copy-start.7 = (f32[2,1024]{1,0:T(2,128)S(1)}, f32[2,1024]{1,0:T(2,128)}, u32[]{:S(2)}) copy-start(f32[2,1024]{1,0:T(2,128)} %constant.17.clone.twist_ref.refs_14_) | copy-start | bytes 24580
  43.2 1.5 %collective-permute-start.7 = (bf16[3,56,640]{2,1,0:T(8,128)(2,1)S(1)}, bf16[3,56,640]{2,1,0:T(8,128)(2,1)S(1)}, u32[]{:S(2)}, u32[]{:S(2)}) collective-permute-start(bf16[3,56,640]{2,1,0:T(8,128)(2,1)S(1)} %get-tuple-element.51), channel_id=1, source_target_pairs={{0,1},{1,0},{2,3},{3,2},{4,5},{5,4},{6,7},{7,6},{8,9},{9,8},{10,11... | collective-permute-start | bytes 645128 | tf_op jit(solution)/shard_map/ppermute | solution.py:337
  47.9 6.4 %collective-permute-start.10 = (bf16[64,2048]{1,0:T(8,128)(2,1)S(1)}, bf16[64,2048]{1,0:T(8,128)(2,1)S(1)}, u32[]{:S(2)}, u32[]{:S(2)}) collective-permute-start(bf16[64,2048]{1,0:T(8,128)(2,1)S(1)} %slice.6), channel_id=1, source_target_pairs={{0,8},{8,16},{16,24},{24,28},{28,20},{20,12},{12,4},{4,0},{1,9},{9... | collective-permute-start | bytes 786440 | tf_op jit(solution)/shard_map/ppermute | solution.py:315
  48.3 6.4 %collective-permute-start.11 = (bf16[64,2048]{1,0:T(8,128)(2,1)S(1)}, bf16[64,2048]{1,0:T(8,128)(2,1)S(1)}, u32[]{:S(2)}, u32[]{:S(2)}) collective-permute-start(bf16[64,2048]{1,0:T(8,128)(2,1)S(1)} %slice.7), channel_id=1, source_target_pairs={{8,0},{16,8},{24,16},{28,24},{20,28},{12,20},{4,12},{0,4},{9,1},{1... | collective-permute-start | bytes 786440 | tf_op jit(solution)/shard_map/ppermute | solution.py:315
  50.0 12.1 %collective-permute-start.8 = (bf16[3,56,640]{2,1,0:T(8,128)(2,1)S(1)}, bf16[3,56,640]{2,1,0:T(8,128)(2,1)S(1)}, u32[]{:S(2)}, u32[]{:S(2)}) collective-permute-start(bf16[3,56,640]{2,1,0:T(8,128)(2,1)S(1)} %get-tuple-element.53), channel_id=1, source_target_pairs={{0,2},{1,3},{2,0},{3,1},{4,6},{5,7},{6,4},{7,5},{8,10},{9,11},{10,... | collective-permute-start | bytes 645128 | tf_op jit(solution)/shard_map/ppermute | solution.py:337
  53.1 8.9 %collective-permute-start.9 = (bf16[3,56,640]{2,1,0:T(8,128)(2,1)S(1)}, bf16[3,56,640]{2,1,0:T(8,128)(2,1)S(1)}, u32[]{:S(2)}, u32[]{:S(2)}) collective-permute-start(bf16[3,56,640]{2,1,0:T(8,128)(2,1)S(1)} %get-tuple-element.54), channel_id=1, source_target_pairs={{0,3},{1,2},{2,1},{3,0},{4,7},{5,6},{6,5},{7,4},{8,11},{9,10},{10,... | collective-permute-start | bytes 645128 | tf_op jit(solution)/shard_map/ppermute | solution.py:337
  57.1 5.0 %collective-permute-start.12 = (bf16[3,56,384]{2,1,0:T(8,128)(2,1)S(1)}, bf16[3,56,384]{2,1,0:T(8,128)(2,1)S(1)}, u32[]{:S(2)}, u32[]{:S(2)}) collective-permute-start(bf16[3,56,384]{2,1,0:T(8,128)(2,1)S(1)} %get-tuple-element.62), channel_id=1, source_target_pairs={{0,1},{1,0},{2,3},{3,2},{4,5},{5,4},{6,7},{7,6},{8,9},{9,8},{10,11... | collective-permute-start | bytes 387080 | tf_op jit(solution)/shard_map/ppermute | solution.py:337
  57.1 7.6 %collective-permute-start.13 = (bf16[3,56,384]{2,1,0:T(8,128)(2,1)S(1)}, bf16[3,56,384]{2,1,0:T(8,128)(2,1)S(1)}, u32[]{:S(2)}, u32[]{:S(2)}) collective-permute-start(bf16[3,56,384]{2,1,0:T(8,128)(2,1)S(1)} %get-tuple-element.63), channel_id=1, source_target_pairs={{0,2},{1,3},{2,0},{3,1},{4,6},{5,7},{6,4},{7,5},{8,10},{9,11},{10,... | collective-permute-start | bytes 387080 | tf_op jit(solution)/shard_map/ppermute | solution.py:337
  60.4 6.5 %collective-permute-start.14 = (bf16[3,56,384]{2,1,0:T(8,128)(2,1)S(1)}, bf16[3,56,384]{2,1,0:T(8,128)(2,1)S(1)}, u32[]{:S(2)}, u32[]{:S(2)}) collective-permute-start(bf16[3,56,384]{2,1,0:T(8,128)(2,1)S(1)} %get-tuple-element.64), channel_id=1, source_target_pairs={{0,3},{1,2},{2,1},{3,0},{4,7},{5,6},{6,5},{7,4},{8,11},{9,10},{10,... | collective-permute-start | bytes 387080 | tf_op jit(solution)/shard_map/ppermute | solution.py:337
  72.4 20.0 %copy-start.5 = (bf16[128,2048]{1,0:T(8,128)(2,1)S(1)}, bf16[128,2048]{1,0:T(8,128)(2,1)}, u32[]{:S(2)}) copy-start(bf16[128,2048]{1,0:T(8,128)(2,1)} %refs_4_.1) | copy-start | bytes 1572868
  72.4 10.8 %collective-permute-start.15 = (bf16[3,56,1024]{2,1,0:T(8,128)(2,1)S(1)}, bf16[3,56,1024]{2,1,0:T(8,128)(2,1)S(1)}, u32[]{:S(2)}, u32[]{:S(2)}) collective-permute-start(bf16[3,56,1024]{2,1,0:T(8,128)(2,1)S(1)} %get-tuple-element.69.refs_0_), channel_id=1, source_target_pairs={{0,2},{1,3},{2,0},{3,1},{4,6},{5,7},{6,4},{7,5},{8,10},{9,11},{10,... | collective-permute-start | bytes 1032200 | tf_op jit(solution)/shard_map/ppermute | solution.py:410
  76.1 7.1 %collective-permute-start.16 = (f32[56,33]{1,0:T(8,128)S(1)}, f32[56,33]{1,0:T(8,128)S(1)}, u32[]{:S(2)}, u32[]{:S(2)}) collective-permute-start(f32[56,33]{1,0:T(8,128)S(1)} %shard_map.126.refs_0_), channel_id=1, source_target_pairs={{0,2},{1,3},{2,0},{3,1},{4,6},{5,7},{6,4},{7,5},{8,10},{9,11},{10,... | collective-permute-start | bytes 22184 | tf_op jit(solution)/shard_map/ppermute | solution.py:410
  76.6 15.7 %collective-permute-start.17 = (bf16[3,56,1024]{2,1,0:T(8,128)(2,1)S(1)}, bf16[3,56,1024]{2,1,0:T(8,128)(2,1)S(1)}, u32[]{:S(2)}, u32[]{:S(2)}) collective-permute-start(bf16[3,56,1024]{2,1,0:T(8,128)(2,1)S(1)} %get-tuple-element.69.refs_0_), channel_id=1, source_target_pairs={{0,1},{1,0},{2,3},{3,2},{4,5},{5,4},{6,7},{7,6},{8,9},{9,8},{10,11... | collective-permute-start | bytes 1032200 | tf_op jit(solution)/shard_map/ppermute | solution.py:415
  83.1 9.2 %collective-permute-start.18 = (bf16[3,56,1024]{2,1,0:T(8,128)(2,1)S(1)}, bf16[3,56,1024]{2,1,0:T(8,128)(2,1)S(1)}, u32[]{:S(2)}, u32[]{:S(2)}) collective-permute-start(bf16[3,56,1024]{2,1,0:T(8,128)(2,1)S(1)} %collective-permute-done.15.refs_1_), channel_id=1, source_target_pairs={{0,1},{1,0},{2,3},{3,2},{4,5},{5,4},{6,7},{7,6},{8,9},{9,8},{10,11... | collective-permute-start | bytes 1032200 | tf_op jit(solution)/shard_map/ppermute | solution.py:424
  83.1 1.7 %collective-permute-start.19 = (f32[56,33]{1,0:T(8,128)S(1)}, f32[56,33]{1,0:T(8,128)S(1)}, u32[]{:S(2)}, u32[]{:S(2)}) collective-permute-start(f32[56,33]{1,0:T(8,128)S(1)} %shard_map.126.refs_0_), channel_id=1, source_target_pairs={{0,1},{1,0},{2,3},{3,2},{4,5},{5,4},{6,7},{7,6},{8,9},{9,8},{10,11... | collective-permute-start | bytes 22184 | tf_op jit(solution)/shard_map/ppermute | solution.py:425
  83.7 1.2 %collective-permute-start.20 = (f32[56,33]{1,0:T(8,128)S(1)}, f32[56,33]{1,0:T(8,128)S(1)}, u32[]{:S(2)}, u32[]{:S(2)}) collective-permute-start(f32[56,33]{1,0:T(8,128)S(1)} %collective-permute-done.16.refs_1_), channel_id=1, source_target_pairs={{0,1},{1,0},{2,3},{3,2},{4,5},{5,4},{6,7},{7,6},{8,9},{9,8},{10,11... | collective-permute-start | bytes 22184 | tf_op jit(solution)/shard_map/ppermute | solution.py:425
  85.4 13.7 %collective-permute-start.21 = (f32[208,33]{1,0:T(8,128)S(1)}, f32[208,33]{1,0:T(8,128)S(1)}, u32[]{:S(2)}, u32[]{:S(2)}) collective-permute-start(f32[208,33]{1,0:T(8,128)S(1)} %shard_map.128), channel_id=1, source_target_pairs={{0,0},{8,1},{16,2},{24,3},{4,4},{12,5},{20,6},{28,7},{1,8},{9,9},{... | collective-permute-start | bytes 82376 | tf_op jit(solution)/shard_map/ppermute | solution.py:438
  90.0 11.7 %collective-permute-start.22 = (f32[208,33]{1,0:T(8,128)S(1)}, f32[208,33]{1,0:T(8,128)S(1)}, u32[]{:S(2)}, u32[]{:S(2)}) collective-permute-start(f32[208,33]{1,0:T(8,128)S(1)} %shard_map.128), channel_id=1, source_target_pairs={{4,0},{12,1},{20,2},{28,3},{0,4},{8,5},{16,6},{24,7},{5,8},{13,9},... | collective-permute-start | bytes 82376 | tf_op jit(solution)/shard_map/ppermute | solution.py:438

commit v13 on v12

--- a/solution.py
+++ b/solution.py
@@ -437,7 +437,7 @@
         ]
         blocks.append(lax.ppermute(block_sums, ("seq", "ch"), route))
 
-    tile = min(512, width)
+    tile = min(256, width)
     weight_grad = pl.pallas_call(
         functools.partial(weight_kernel, shares=n_ch),
         out_shape=jax.ShapeDtypeStruct((gates, rows, width), F32),

time: 103 us -> 103 us (level)
  Pallas kernels: 23.6 us -> 25.1 us
  waiting for transfers between devices: 24.9 us -> 23.5 us
    pallas_call x1, Pallas kernels: 5.73 us -> 7.21 us  [local(): pl.pallas_call(functools.partial(weight_kernel, shares=n_ch), out_shape=j...]
    ppermute x2, waiting for transfers between devices: 3.66 us -> 2.2 us  [local(): blocks.append(lax.ppermute(block_sums, ('seq', 'ch'), route))]
    unnamed x16 -> x14, local copies, waits for them, and re-layouts: 3.68 us -> 3.68 us
  transfers between devices with their start and end apart: 24 -> 24, of which waited for: 12 -> 11; matrix products, arithmetic and copies ran while one was open for 1% -> 1% of each run, Pallas kernels for 16% -> 18%
where the time goes in v13:
time: 103 us
  starting transfers between devices  34.7 us (34%)
  Pallas kernels  25.1 us (24%)
  waiting for transfers between devices  23.5 us (23%)
  blocking collectives  14.2 us (14%)
  local copies, waits for them, and re-layouts  3.84 us (4%)
    pallas_call x9, Pallas kernels, call(): pl.pallas_call(kernel, out_shape=outs, in_specs=specs, out_specs=[whole]...  17.9 us
    all_to_all x1, blocking collectives, local(): lax.all_to_all(upper, 'seq', split_axis=0, concat_axis=0, tiled=True)  14.2 us
    pallas_call x1, Pallas kernels, local(): pl.pallas_call(functools.partial(weight_kernel, shares=n_ch), out_shape=j...  7.21 us
    ppermute x2, starting transfers between devices, local(): blocks.append(lax.ppermute(block_sums, ('seq', 'ch'), route))  6.86 us
    ppermute x6, starting transfers between devices, to_owners(): lax.ppermute(sums[d], 'ch', [(h, h ^ d) for h in range(n_ch)])  6.59 us
    ppermute x2, waiting for transfers between devices, chips(): lax.ppermute(array, 'ch', [(h, h ^ d) for h in range(n_ch)])  6.55 us
    ppermute x4, starting transfers between devices, send_on(): lax.ppermute(pair[1], 'seq', behind)  6.48 us
    ppermute x6, waiting for transfers between devices, to_owners(): lax.ppermute(sums[d], 'ch', [(h, h ^ d) for h in range(n_ch)])  6.37 us
  transfers between devices with their start and end apart: 24, of which 11 were waited for; matrix products, arithmetic and copies ran while one was open for 1% of the time, Pallas kernels for 18%

profile of v13, /device:TPU:4, one launch (start us, length us, event | category | flops | bytes accessed | tf_op | source)
XLA Modules:
  0.0 103.0 jit_solution(5502274973760866298)
XLA Ops:
  0.6 1.6 %collective-permute-start = (bf16[128,2048]{1,0:T(8,128)(2,1)}, bf16[128,2048]{1,0:T(8,128)(2,1)S(1)}, u32[]{:S(2)}, u32[]{:S(2)}) collective-permute-start(bf16[128,2048]{1,0:T(8,128)(2,1)} %refs_4_.1), channel_id=1, source_target_pairs={{0,8},{8,16},{16,24},{24,28},{28,20},{20,12},{12,4},{4,0},{1,9},{9... | collective-permute-start | bytes 1572872 | tf_op jit(solution)/shard_map/ppermute | solution.py:315
  5.8 3.3 %all-to-all-start = ((bf16[4,2,56,128]{3,2,1,0:T(8,128)(2,1)}), bf16[4,2,56,128]{3,2,1,0:T(8,128)(2,1)S(1)}, u32[]{:S(2)}, u32[]{:S(2)}) async-start(bf16[4,2,56,128]{3,2,1,0:T(8,128)(2,1)} %shard_map.121), calls=%async_computation | async-start | bytes 229376 | tf_op jit(solution)/shard_map/all_to_all | solution.py:355
  9.2 4.4 %collective-permute-start.2 = (f32[56,33]{1,0:T(8,128)S(1)}, f32[56,33]{1,0:T(8,128)S(1)}, u32[]{:S(2)}, u32[]{:S(2)}) collective-permute-start(f32[56,33]{1,0:T(8,128)S(1)} %shard_map.120), channel_id=1, source_target_pairs={{0,0},{4,1},{8,2},{12,3},{16,4},{20,5},{24,6},{28,7},{1,8},{5,9},{... | collective-permute-start | bytes 22184 | tf_op jit(solution)/shard_map/ppermute | solution.py:350
  13.6 2.5 %collective-permute-done.2.poles_ref.refs_9_ = f32[56,33]{1,0:T(8,128)S(1)} collective-permute-done((f32[56,33]{1,0:T(8,128)S(1)}, f32[56,33]{1,0:T(8,128)S(1)}, u32[]{:S(2)}, u32[]{:S(2)}) %collective-permute-start.2) | collective-permute-done | bytes 7424 | tf_op jit(solution)/shard_map/ppermute | solution.py:350
  16.1 1.3 %collective-permute-start.3 = (bf16[128,2048]{1,0:T(8,128)(2,1)S(1)}, bf16[128,2048]{1,0:T(8,128)(2,1)S(1)}, u32[]{:S(2)}, u32[]{:S(2)}) collective-permute-start(bf16[128,2048]{1,0:T(8,128)(2,1)S(1)} %collective-permute-done.refs_1_.refs_5_), channel_id=1, source_target_pairs={{0,8},{8,16},{16,24},{24,28},{28,20},{20,12},{12,4},{4,0},{1,9},{9... | collective-permute-start | bytes 1572872 | tf_op jit(solution)/shard_map/ppermute | solution.py:315
  17.4 3.3 %collective-permute-start.4 = (bf16[128,2048]{1,0:T(8,128)(2,1)S(1)}, bf16[128,2048]{1,0:T(8,128)(2,1)S(1)}, u32[]{:S(2)}, u32[]{:S(2)}) collective-permute-start(bf16[128,2048]{1,0:T(8,128)(2,1)S(1)} %collective-permute-done.1.refs_2_.refs_6_), channel_id=1, source_target_pairs={{8,0},{16,8},{24,16},{28,24},{20,28},{12,20},{4,12},{0,4},{9,1},{1... | collective-permute-start | bytes 1572872 | tf_op jit(solution)/shard_map/ppermute | solution.py:315
  20.7 14.2 %all_to_all.10.refs_8_ = bf16[8,56,128]{2,1,0:T(8,128)(2,1)S(1)} all-to-all(bf16[8,56,128]{2,1,0:T(8,128)(2,1)S(1)} %bitcast.12), channel_id=1, replica_groups=mesh['seq'=8,'ch'=4] {'seq'}, dimensions={0} | all-to-all | bytes 229376 | tf_op jit(solution)/shard_map/all_to_all | solution.py:358
  35.0 1.0 collective-permute-start.5
  35.9 1.1 %collective-permute-start.6 = (bf16[128,2048]{1,0:T(8,128)(2,1)S(1)}, bf16[128,2048]{1,0:T(8,128)(2,1)S(1)}, u32[]{:S(2)}, u32[]{:S(2)}) collective-permute-start(bf16[128,2048]{1,0:T(8,128)(2,1)S(1)} %collective-permute-done.4.refs_4_.refs_8_), channel_id=1, source_target_pairs={{8,0},{16,8},{24,16},{28,24},{20,28},{12,20},{4,12},{0,4},{9,1},{1... | collective-permute-start | bytes 1572872 | tf_op jit(solution)/shard_map/ppermute | solution.py:315
  37.0 1.7 %copy-done.2 = bf16[208,3,2048]{2,0,1:T(8,128)(2,1)S(1)} copy-done((bf16[208,3,2048]{2,0,1:T(8,128)(2,1)S(1)}, bf16[208,3,2048]{2,0,1:T(8,128)(2,1)}, u32[]{:S(2)}) %copy-start.2) | copy-done | bytes 2555928
  38.7 1.0 %copy-done.4 = bf16[128,2048]{1,0:T(8,128)(2,1)S(1)} copy-done((bf16[128,2048]{1,0:T(8,128)(2,1)S(1)}, bf16[128,2048]{1,0:T(8,128)(2,1)}, u32[]{:S(2)}) %copy-start.4) | copy-done | bytes 524312
  39.8 3.4 %shard_map.122 = (f32[3,56,640]{2,1,0:T(8,128)S(1)}, bf16[3,56,640]{2,1,0:T(8,128)(2,1)S(1)}, bf16[3,56,640]{2,1,0:T(8,128)(2,1)S(1)}, bf16[3,56,640]{2,1,0:T(8,128)(2,1)S(1)}) custom-call(s32[2]{0:T(128)S(1)} %pad_add_fusion.place_ref, bf16[3,208,2048]{2,1,0:T(8,128)(2,1)S(1)} %bitcast.9, bf16[128,2048]{1,0:T(8,128)(2,1)S(1)} %copy-done.4, ...), custom_call_target="tpu_custom_call" | custom-call | flops 1635778560 | bytes 6252552 | tf_op jit(solution)/shard_map/pallas_call | solution.py:279
  43.3 1.5 %collective-permute-done.7.refs_1_ = bf16[3,56,640]{2,1,0:T(8,128)(2,1)S(1)} collective-permute-done((bf16[3,56,640]{2,1,0:T(8,128)(2,1)S(1)}, bf16[3,56,640]{2,1,0:T(8,128)(2,1)S(1)}, u32[]{:S(2)}, u32[]{:S(2)}) %collective-permute-start.7) | collective-permute-done | bytes 215072 | tf_op jit(solution)/shard_map/ppermute | solution.py:337
  44.8 2.5 %collective-permute-done.5.refs_0_.refs_9_ = bf16[128,2048]{1,0:T(8,128)(2,1)S(1)} collective-permute-done((bf16[128,2048]{1,0:T(8,128)(2,1)S(1)}, bf16[128,2048]{1,0:T(8,128)(2,1)S(1)}, u32[]{:S(2)}, u32[]{:S(2)}) %collective-permute-start.5) | collective-permute-done | bytes 524320 | tf_op jit(solution)/shard_map/ppermute | solution.py:315
  48.3 1.7 %collective-permute-start.11 = (bf16[64,2048]{1,0:T(8,128)(2,1)S(1)}, bf16[64,2048]{1,0:T(8,128)(2,1)S(1)}, u32[]{:S(2)}, u32[]{:S(2)}) collective-permute-start(bf16[64,2048]{1,0:T(8,128)(2,1)S(1)} %slice.7), channel_id=1, source_target_pairs={{8,0},{16,8},{24,16},{28,24},{20,28},{12,20},{4,12},{0,4},{9,1},{1... | collective-permute-start | bytes 786440 | tf_op jit(solution)/shard_map/ppermute | solution.py:315
  50.0 3.1 %collective-permute-start.8 = (bf16[3,56,640]{2,1,0:T(8,128)(2,1)S(1)}, bf16[3,56,640]{2,1,0:T(8,128)(2,1)S(1)}, u32[]{:S(2)}, u32[]{:S(2)}) collective-permute-start(bf16[3,56,640]{2,1,0:T(8,128)(2,1)S(1)} %get-tuple-element.53), channel_id=1, source_target_pairs={{0,2},{1,3},{2,0},{3,1},{4,6},{5,7},{6,4},{7,5},{8,10},{9,11},{10,... | collective-permute-start | bytes 645128 | tf_op jit(solution)/shard_map/ppermute | solution.py:337
  53.1 1.2 %collective-permute-done.10.refs_2_.refs_11_ = bf16[64,2048]{1,0:T(8,128)(2,1)S(1)} collective-permute-done((bf16[64,2048]{1,0:T(8,128)(2,1)S(1)}, bf16[64,2048]{1,0:T(8,128)(2,1)S(1)}, u32[]{:S(2)}, u32[]{:S(2)}) %collective-permute-start.10) | collective-permute-done | bytes 262176 | tf_op jit(solution)/shard_map/ppermute | solution.py:315
  54.6 2.4 %shard_map.123 = (f32[3,56,384]{2,1,0:T(8,128)S(1)}, bf16[3,56,384]{2,1,0:T(8,128)(2,1)S(1)}, bf16[3,56,384]{2,1,0:T(8,128)(2,1)S(1)}, bf16[3,56,384]{2,1,0:T(8,128)(2,1)S(1)}) custom-call(s32[2]{0:T(128)S(1)} %pad_add_fusion.place_ref, bf16[3,208,2048]{2,1,0:T(8,128)(2,1)S(1)} %bitcast.10, bf16[128,2048]{1,0:T(8,128)(2,1)S(1)} %collective-permute-done.5.refs_0_.refs_9_, ...), custom_call_target="tpu_custom_call" | custom-call | flops 981467136 | bytes 4773896 | tf_op jit(solution)/shard_map/pallas_call | solution.py:279
  57.1 3.2 %collective-permute-start.13 = (bf16[3,56,384]{2,1,0:T(8,128)(2,1)S(1)}, bf16[3,56,384]{2,1,0:T(8,128)(2,1)S(1)}, u32[]{:S(2)}, u32[]{:S(2)}) collective-permute-start(bf16[3,56,384]{2,1,0:T(8,128)(2,1)S(1)} %get-tuple-element.63), channel_id=1, source_target_pairs={{0,2},{1,3},{2,0},{3,1},{4,6},{5,7},{6,4},{7,5},{8,10},{9,11},{10,... | collective-permute-start | bytes 387080 | tf_op jit(solution)/shard_map/ppermute | solution.py:337
  60.5 1.5 %shard_map.124 = (f32[56,1024]{1,0:T(8,128)S(1)}, f32[56,1024]{1,0:T(8,128)S(1)}) custom-call(f32[56,33]{1,0:T(8,128)S(1)} %collective-permute-done.2.poles_ref.refs_9_, bf16[1024,1024]{1,0:T(8,128)(2,1)S(1)} %copy-done, bf16[1024,1024]{1,0:T(8,128)(2,1)S(1)} %copy-done.1, f32[2,1024]{1,0:T(2,128)S(1)} %copy-done.6), custom_call_target="tpu_custom_call" | custom-call | flops 469762048 | bytes 4668640 | tf_op jit(solution)/shard_map/pallas_call | solution.py:279
  62.0 2.7 %collective-permute-done.13.refs_6_ = bf16[3,56,384]{2,1,0:T(8,128)(2,1)S(1)} collective-permute-done((bf16[3,56,384]{2,1,0:T(8,128)(2,1)S(1)}, bf16[3,56,384]{2,1,0:T(8,128)(2,1)S(1)}, u32[]{:S(2)}, u32[]{:S(2)}) %collective-permute-start.13) | collective-permute-done | bytes 129056 | tf_op jit(solution)/shard_map/ppermute | solution.py:337
  64.7 2.2 %collective-permute-done.14.refs_7_ = bf16[3,56,384]{2,1,0:T(8,128)(2,1)S(1)} collective-permute-done((bf16[3,56,384]{2,1,0:T(8,128)(2,1)S(1)}, bf16[3,56,384]{2,1,0:T(8,128)(2,1)S(1)}, u32[]{:S(2)}, u32[]{:S(2)}) %collective-permute-start.14) | collective-permute-done | bytes 129056 | tf_op jit(solution)/shard_map/ppermute | solution.py:337
  66.9 5.4 %shard_map.125 = (bf16[3,56,1024]{2,1,0:T(8,128)(2,1)S(1)}, f32[56,1024]{1,0:T(8,128)S(1)}, f32[56,1024]{1,0:T(8,128)S(1)}, f32[56,1]{1,0:T(8,128)S(1)}) custom-call(s32[2]{0:T(128)S(1)} %pad_add_fusion.place_ref, f32[3,56,640]{2,1,0:T(8,128)S(1)} %get-tuple-element.50.refs_0_, bf16[3,56,640]{2,1,0:T(8,128)(2,1)S(1)} %collective-permute-done.7.refs_1_, ...), custom_call_target="tpu_custom_call" | custom-call | flops 1879048192 | bytes 7306696 | tf_op jit(solution)/shard_map/pallas_call | solution.py:279
  72.4 1.6 %collective-permute-start.15 = (bf16[3,56,1024]{2,1,0:T(8,128)(2,1)S(1)}, bf16[3,56,1024]{2,1,0:T(8,128)(2,1)S(1)}, u32[]{:S(2)}, u32[]{:S(2)}) collective-permute-start(bf16[3,56,1024]{2,1,0:T(8,128)(2,1)S(1)} %get-tuple-element.69.refs_0_), channel_id=1, source_target_pairs={{0,2},{1,3},{2,0},{3,1},{4,6},{5,7},{6,4},{7,5},{8,10},{9,11},{10,... | collective-permute-start | bytes 1032200 | tf_op jit(solution)/shard_map/ppermute | solution.py:410
  74.0 2.0 %shard_map.126.refs_0_ = f32[56,33]{1,0:T(8,128)S(1)} custom-call(f32[56,33]{1,0:T(8,128)S(1)} %collective-permute-done.2.poles_ref.refs_9_, f32[56,1024]{1,0:T(8,128)S(1)} %get-tuple-element.70.tgc_ref, f32[56,1024]{1,0:T(8,128)S(1)} %get-tuple-element.71.tgs_ref, bf16[1024,1024]{1,0:T(8,128)(2,1)S(1)} %copy-done, bf16[1024,1024]{1,0:T(8,128)(2,1)S(1)} %copy-done.1, ...), custom_call_target="tpu_custom_call" | custom-call | flops 469762048 | bytes 4668064 | tf_op jit(solution)/shard_map/pallas_call | solution.py:279
  76.6 6.5 %collective-permute-done.16.refs_1_ = f32[56,33]{1,0:T(8,128)S(1)} collective-permute-done((f32[56,33]{1,0:T(8,128)S(1)}, f32[56,33]{1,0:T(8,128)S(1)}, u32[]{:S(2)}, u32[]{:S(2)}) %collective-permute-start.16) | collective-permute-done | bytes 7424 | tf_op jit(solution)/shard_map/ppermute | solution.py:410
  83.6 1.2 %collective-permute-done.19.refs_2_ = f32[56,33]{1,0:T(8,128)S(1)} collective-permute-done((f32[56,33]{1,0:T(8,128)S(1)}, f32[56,33]{1,0:T(8,128)S(1)}, u32[]{:S(2)}, u32[]{:S(2)}) %collective-permute-start.19) | collective-permute-done | bytes 7424 | tf_op jit(solution)/shard_map/ppermute | solution.py:425
  85.4 4.6 %collective-permute-start.21 = (f32[208,33]{1,0:T(8,128)S(1)}, f32[208,33]{1,0:T(8,128)S(1)}, u32[]{:S(2)}, u32[]{:S(2)}) collective-permute-start(f32[208,33]{1,0:T(8,128)S(1)} %shard_map.128), channel_id=1, source_target_pairs={{0,0},{8,1},{16,2},{24,3},{4,4},{12,5},{20,6},{28,7},{1,8},{9,9},{... | collective-permute-start | bytes 82376 | tf_op jit(solution)/shard_map/ppermute | solution.py:438
  90.0 2.3 %collective-permute-start.22 = (f32[208,33]{1,0:T(8,128)S(1)}, f32[208,33]{1,0:T(8,128)S(1)}, u32[]{:S(2)}, u32[]{:S(2)}) collective-permute-start(f32[208,33]{1,0:T(8,128)S(1)} %shard_map.128), channel_id=1, source_target_pairs={{4,0},{12,1},{20,2},{28,3},{0,4},{8,5},{16,6},{24,7},{5,8},{13,9},... | collective-permute-start | bytes 82376 | tf_op jit(solution)/shard_map/ppermute | solution.py:438
  92.3 7.2 %shard_map.127 = f32[3,208,2048]{2,1,0:T(8,128)} custom-call(s32[2]{0:T(128)S(1)} %pad_add_fusion.place_ref, bf16[3,56,1024]{2,1,0:T(8,128)(2,1)S(1)} %get-tuple-element.69.refs_0_, bf16[3,56,1024]{2,1,0:T(8,128)(2,1)S(1)} %collective-permute-done.15.refs_1_, bf16[3,56,1024]{2,1,0:T(8,128)(2,1)S(1)} %collective-permute-done.17.refs_2_, ...), custom_call_target="tpu_custom_call" | custom-call | flops 2617245696 | bytes 10584064 | tf_op jit(solution)/shard_map/pallas_call | solution.py:441
  99.5 2.2 %collective-permute-done.22.refs_1_ = f32[208,33]{1,0:T(8,128)S(1)} collective-permute-done((f32[208,33]{1,0:T(8,128)S(1)}, f32[208,33]{1,0:T(8,128)S(1)}, u32[]{:S(2)}, u32[]{:S(2)}) %collective-permute-start.22) | collective-permute-done | bytes 27488 | tf_op jit(solution)/shard_map/ppermute | solution.py:438
  101.7 1.3 %shard_map.129 = (f32[16,416]{1,0:T(8,128)}, f32[16,416]{1,0:T(8,128)}, f32[1,416]{1,0:T(1,128)}) custom-call(s32[2]{0:T(128)S(1)} %pad_add_fusion.place_ref, f32[208,33]{1,0:T(8,128)S(1)} %collective-permute-done.21.refs_0_, f32[208,33]{1,0:T(8,128)S(1)} %collective-permute-done.22.refs_1_), custom_call_target="tpu_custom_call" | custom-call | bytes 109832 | tf_op jit(solution)/shard_map/pallas_call | solution.py:279
  (46 shorter events, 6.8 us)
Async XLA Ops:
  0.6 15.5 %collective-permute-start = (bf16[128,2048]{1,0:T(8,128)(2,1)}, bf16[128,2048]{1,0:T(8,128)(2,1)S(1)}, u32[]{:S(2)}, u32[]{:S(2)}) collective-permute-start(bf16[128,2048]{1,0:T(8,128)(2,1)} %refs_4_.1), channel_id=1, source_target_pairs={{0,8},{8,16},{16,24},{24,28},{28,20},{20,12},{12,4},{4,0},{1,9},{9... | collective-permute-start | bytes 1572872 | tf_op jit(solution)/shard_map/ppermute | solution.py:315
  2.3 13.9 %collective-permute-start.1 = (bf16[128,2048]{1,0:T(8,128)(2,1)}, bf16[128,2048]{1,0:T(8,128)(2,1)S(1)}, u32[]{:S(2)}, u32[]{:S(2)}) collective-permute-start(bf16[128,2048]{1,0:T(8,128)(2,1)} %refs_4_.1), channel_id=1, source_target_pairs={{8,0},{16,8},{24,16},{28,24},{20,28},{12,20},{4,12},{0,4},{9,1},{1... | collective-permute-start | bytes 1572872 | tf_op jit(solution)/shard_map/ppermute | solution.py:315
  4.3 0.9 copy-start.5
  5.8 10.3 %all-to-all-start = ((bf16[4,2,56,128]{3,2,1,0:T(8,128)(2,1)}), bf16[4,2,56,128]{3,2,1,0:T(8,128)(2,1)S(1)}, u32[]{:S(2)}, u32[]{:S(2)}) async-start(bf16[4,2,56,128]{3,2,1,0:T(8,128)(2,1)} %shard_map.121), calls=%async_computation | async-start | bytes 229376 | tf_op jit(solution)/shard_map/all_to_all | solution.py:355
  9.2 6.9 %collective-permute-start.2 = (f32[56,33]{1,0:T(8,128)S(1)}, f32[56,33]{1,0:T(8,128)S(1)}, u32[]{:S(2)}, u32[]{:S(2)}) collective-permute-start(f32[56,33]{1,0:T(8,128)S(1)} %shard_map.120), channel_id=1, source_target_pairs={{0,0},{4,1},{8,2},{12,3},{16,4},{20,5},{24,6},{28,7},{1,8},{5,9},{... | collective-permute-start | bytes 22184 | tf_op jit(solution)/shard_map/ppermute | solution.py:350
  16.1 18.8 %collective-permute-start.3 = (bf16[128,2048]{1,0:T(8,128)(2,1)S(1)}, bf16[128,2048]{1,0:T(8,128)(2,1)S(1)}, u32[]{:S(2)}, u32[]{:S(2)}) collective-permute-start(bf16[128,2048]{1,0:T(8,128)(2,1)S(1)} %collective-permute-done.refs_1_.refs_5_), channel_id=1, source_target_pairs={{0,8},{8,16},{16,24},{24,28},{28,20},{20,12},{12,4},{4,0},{1,9},{9... | collective-permute-start | bytes 1572872 | tf_op jit(solution)/shard_map/ppermute | solution.py:315
  17.4 17.5 %collective-permute-start.4 = (bf16[128,2048]{1,0:T(8,128)(2,1)S(1)}, bf16[128,2048]{1,0:T(8,128)(2,1)S(1)}, u32[]{:S(2)}, u32[]{:S(2)}) collective-permute-start(bf16[128,2048]{1,0:T(8,128)(2,1)S(1)} %collective-permute-done.1.refs_2_.refs_6_), channel_id=1, source_target_pairs={{8,0},{16,8},{24,16},{28,24},{20,28},{12,20},{4,12},{0,4},{9,1},{1... | collective-permute-start | bytes 1572872 | tf_op jit(solution)/shard_map/ppermute | solution.py:315
  35.0 12.3 %collective-permute-start.5 = (bf16[128,2048]{1,0:T(8,128)(2,1)S(1)}, bf16[128,2048]{1,0:T(8,128)(2,1)S(1)}, u32[]{:S(2)}, u32[]{:S(2)}) collective-permute-start(bf16[128,2048]{1,0:T(8,128)(2,1)S(1)} %collective-permute-done.3.refs_3_.refs_7_), channel_id=1, source_target_pairs={{0,8},{8,16},{16,24},{24,28},{28,20},{20,12},{12,4},{4,0},{1,9},{9... | collective-permute-start | bytes 1572872 | tf_op jit(solution)/shard_map/ppermute | solution.py:315
  35.9 11.9 %collective-permute-start.6 = (bf16[128,2048]{1,0:T(8,128)(2,1)S(1)}, bf16[128,2048]{1,0:T(8,128)(2,1)S(1)}, u32[]{:S(2)}, u32[]{:S(2)}) collective-permute-start(bf16[128,2048]{1,0:T(8,128)(2,1)S(1)} %collective-permute-done.4.refs_4_.refs_8_), channel_id=1, source_target_pairs={{8,0},{16,8},{24,16},{28,24},{20,28},{12,20},{4,12},{0,4},{9,1},{1... | collective-permute-start | bytes 1572872 | tf_op jit(solution)/shard_map/ppermute | solution.py:315
  37.0 1.7 %copy-start.2 = (bf16[208,3,2048]{2,0,1:T(8,128)(2,1)S(1)}, bf16[208,3,2048]{2,0,1:T(8,128)(2,1)}, u32[]{:S(2)}) copy-start(bf16[208,3,2048]{2,0,1:T(8,128)(2,1)} %param.10) | copy-start | bytes 7667716
  38.7 1.0 %copy-start.4 = (bf16[128,2048]{1,0:T(8,128)(2,1)S(1)}, bf16[128,2048]{1,0:T(8,128)(2,1)}, u32[]{:S(2)}) copy-start(bf16[128,2048]{1,0:T(8,128)(2,1)} %refs_4_.1) | copy-start | bytes 1572868
  39.8 14.9 %copy-start.3 = (bf16[208,3,2048]{2,0,1:T(8,128)(2,1)S(1)}, bf16[208,3,2048]{2,0,1:T(8,128)(2,1)}, u32[]{:S(2)}) copy-start(bf16[208,3,2048]{2,0,1:T(8,128)(2,1)} %param.10) | copy-start | bytes 7667716
  43.2 17.3 %copy-start = (bf16[1024,1024]{1,0:T(8,128)(2,1)S(1)}, bf16[1024,1024]{1,0:T(8,128)(2,1)}, u32[]{:S(2)}) copy-start(bf16[1024,1024]{1,0:T(8,128)(2,1)} %constant.15.clone.cos_ref.refs_12_) | copy-start | bytes 6291460
  43.2 17.3 %copy-start.1 = (bf16[1024,1024]{1,0:T(8,128)(2,1)S(1)}, bf16[1024,1024]{1,0:T(8,128)(2,1)}, u32[]{:S(2)}) copy-start(bf16[1024,1024]{1,0:T(8,128)(2,1)} %constant.16.clone.sin_ref.refs_13_) | copy-start | bytes 6291460
  43.2 17.2 %copy-start.6 = (f32[2,1024]{1,0:T(2,128)S(1)}, f32[2,1024]{1,0:T(2,128)}, u32[]{:S(2)}) copy-start(f32[2,1024]{1,0:T(2,128)} %constant.17.clone.twist_ref.refs_14_) | copy-start | bytes 24580
  43.2 1.5 %collective-permute-start.7 = (bf16[3,56,640]{2,1,0:T(8,128)(2,1)S(1)}, bf16[3,56,640]{2,1,0:T(8,128)(2,1)S(1)}, u32[]{:S(2)}, u32[]{:S(2)}) collective-permute-start(bf16[3,56,640]{2,1,0:T(8,128)(2,1)S(1)} %get-tuple-element.51), channel_id=1, source_target_pairs={{0,1},{1,0},{2,3},{3,2},{4,5},{5,4},{6,7},{7,6},{8,9},{9,8},{10,11... | collective-permute-start | bytes 645128 | tf_op jit(solution)/shard_map/ppermute | solution.py:337
  47.9 6.4 %collective-permute-start.10 = (bf16[64,2048]{1,0:T(8,128)(2,1)S(1)}, bf16[64,2048]{1,0:T(8,128)(2,1)S(1)}, u32[]{:S(2)}, u32[]{:S(2)}) collective-permute-start(bf16[64,2048]{1,0:T(8,128)(2,1)S(1)} %slice.6), channel_id=1, source_target_pairs={{0,8},{8,16},{16,24},{24,28},{28,20},{20,12},{12,4},{4,0},{1,9},{9... | collective-permute-start | bytes 786440 | tf_op jit(solution)/shard_map/ppermute | solution.py:315
  48.3 6.4 %collective-permute-start.11 = (bf16[64,2048]{1,0:T(8,128)(2,1)S(1)}, bf16[64,2048]{1,0:T(8,128)(2,1)S(1)}, u32[]{:S(2)}, u32[]{:S(2)}) collective-permute-start(bf16[64,2048]{1,0:T(8,128)(2,1)S(1)} %slice.7), channel_id=1, source_target_pairs={{8,0},{16,8},{24,16},{28,24},{20,28},{12,20},{4,12},{0,4},{9,1},{1... | collective-permute-start | bytes 786440 | tf_op jit(solution)/shard_map/ppermute | solution.py:315
  50.0 12.0 %collective-permute-start.8 = (bf16[3,56,640]{2,1,0:T(8,128)(2,1)S(1)}, bf16[3,56,640]{2,1,0:T(8,128)(2,1)S(1)}, u32[]{:S(2)}, u32[]{:S(2)}) collective-permute-start(bf16[3,56,640]{2,1,0:T(8,128)(2,1)S(1)} %get-tuple-element.53), channel_id=1, source_target_pairs={{0,2},{1,3},{2,0},{3,1},{4,6},{5,7},{6,4},{7,5},{8,10},{9,11},{10,... | collective-permute-start | bytes 645128 | tf_op jit(solution)/shard_map/ppermute | solution.py:337
  53.1 8.9 %collective-permute-start.9 = (bf16[3,56,640]{2,1,0:T(8,128)(2,1)S(1)}, bf16[3,56,640]{2,1,0:T(8,128)(2,1)S(1)}, u32[]{:S(2)}, u32[]{:S(2)}) collective-permute-start(bf16[3,56,640]{2,1,0:T(8,128)(2,1)S(1)} %get-tuple-element.54), channel_id=1, source_target_pairs={{0,3},{1,2},{2,1},{3,0},{4,7},{5,6},{6,5},{7,4},{8,11},{9,10},{10,... | collective-permute-start | bytes 645128 | tf_op jit(solution)/shard_map/ppermute | solution.py:337
  57.1 5.0 %collective-permute-start.12 = (bf16[3,56,384]{2,1,0:T(8,128)(2,1)S(1)}, bf16[3,56,384]{2,1,0:T(8,128)(2,1)S(1)}, u32[]{:S(2)}, u32[]{:S(2)}) collective-permute-start(bf16[3,56,384]{2,1,0:T(8,128)(2,1)S(1)} %get-tuple-element.62), channel_id=1, source_target_pairs={{0,1},{1,0},{2,3},{3,2},{4,5},{5,4},{6,7},{7,6},{8,9},{9,8},{10,11... | collective-permute-start | bytes 387080 | tf_op jit(solution)/shard_map/ppermute | solution.py:337
  57.1 7.6 %collective-permute-start.13 = (bf16[3,56,384]{2,1,0:T(8,128)(2,1)S(1)}, bf16[3,56,384]{2,1,0:T(8,128)(2,1)S(1)}, u32[]{:S(2)}, u32[]{:S(2)}) collective-permute-start(bf16[3,56,384]{2,1,0:T(8,128)(2,1)S(1)} %get-tuple-element.63), channel_id=1, source_target_pairs={{0,2},{1,3},{2,0},{3,1},{4,6},{5,7},{6,4},{7,5},{8,10},{9,11},{10,... | collective-permute-start | bytes 387080 | tf_op jit(solution)/shard_map/ppermute | solution.py:337
  60.4 6.5 %collective-permute-start.14 = (bf16[3,56,384]{2,1,0:T(8,128)(2,1)S(1)}, bf16[3,56,384]{2,1,0:T(8,128)(2,1)S(1)}, u32[]{:S(2)}, u32[]{:S(2)}) collective-permute-start(bf16[3,56,384]{2,1,0:T(8,128)(2,1)S(1)} %get-tuple-element.64), channel_id=1, source_target_pairs={{0,3},{1,2},{2,1},{3,0},{4,7},{5,6},{6,5},{7,4},{8,11},{9,10},{10,... | collective-permute-start | bytes 387080 | tf_op jit(solution)/shard_map/ppermute | solution.py:337
  72.4 10.8 %collective-permute-start.15 = (bf16[3,56,1024]{2,1,0:T(8,128)(2,1)S(1)}, bf16[3,56,1024]{2,1,0:T(8,128)(2,1)S(1)}, u32[]{:S(2)}, u32[]{:S(2)}) collective-permute-start(bf16[3,56,1024]{2,1,0:T(8,128)(2,1)S(1)} %get-tuple-element.69.refs_0_), channel_id=1, source_target_pairs={{0,2},{1,3},{2,0},{3,1},{4,6},{5,7},{6,4},{7,5},{8,10},{9,11},{10,... | collective-permute-start | bytes 1032200 | tf_op jit(solution)/shard_map/ppermute | solution.py:410
  76.1 7.1 %collective-permute-start.16 = (f32[56,33]{1,0:T(8,128)S(1)}, f32[56,33]{1,0:T(8,128)S(1)}, u32[]{:S(2)}, u32[]{:S(2)}) collective-permute-start(f32[56,33]{1,0:T(8,128)S(1)} %shard_map.126.refs_0_), channel_id=1, source_target_pairs={{0,2},{1,3},{2,0},{3,1},{4,6},{5,7},{6,4},{7,5},{8,10},{9,11},{10,... | collective-permute-start | bytes 22184 | tf_op jit(solution)/shard_map/ppermute | solution.py:410
  76.6 15.7 %collective-permute-start.17 = (bf16[3,56,1024]{2,1,0:T(8,128)(2,1)S(1)}, bf16[3,56,1024]{2,1,0:T(8,128)(2,1)S(1)}, u32[]{:S(2)}, u32[]{:S(2)}) collective-permute-start(bf16[3,56,1024]{2,1,0:T(8,128)(2,1)S(1)} %get-tuple-element.69.refs_0_), channel_id=1, source_target_pairs={{0,1},{1,0},{2,3},{3,2},{4,5},{5,4},{6,7},{7,6},{8,9},{9,8},{10,11... | collective-permute-start | bytes 1032200 | tf_op jit(solution)/shard_map/ppermute | solution.py:415
  83.1 9.2 %collective-permute-start.18 = (bf16[3,56,1024]{2,1,0:T(8,128)(2,1)S(1)}, bf16[3,56,1024]{2,1,0:T(8,128)(2,1)S(1)}, u32[]{:S(2)}, u32[]{:S(2)}) collective-permute-start(bf16[3,56,1024]{2,1,0:T(8,128)(2,1)S(1)} %collective-permute-done.15.refs_1_), channel_id=1, source_target_pairs={{0,1},{1,0},{2,3},{3,2},{4,5},{5,4},{6,7},{7,6},{8,9},{9,8},{10,11... | collective-permute-start | bytes 1032200 | tf_op jit(solution)/shard_map/ppermute | solution.py:424
  83.1 1.7 %collective-permute-start.19 = (f32[56,33]{1,0:T(8,128)S(1)}, f32[56,33]{1,0:T(8,128)S(1)}, u32[]{:S(2)}, u32[]{:S(2)}) collective-permute-start(f32[56,33]{1,0:T(8,128)S(1)} %shard_map.126.refs_0_), channel_id=1, source_target_pairs={{0,1},{1,0},{2,3},{3,2},{4,5},{5,4},{6,7},{7,6},{8,9},{9,8},{10,11... | collective-permute-start | bytes 22184 | tf_op jit(solution)/shard_map/ppermute | solution.py:425
  83.6 1.2 %collective-permute-start.20 = (f32[56,33]{1,0:T(8,128)S(1)}, f32[56,33]{1,0:T(8,128)S(1)}, u32[]{:S(2)}, u32[]{:S(2)}) collective-permute-start(f32[56,33]{1,0:T(8,128)S(1)} %collective-permute-done.16.refs_1_), channel_id=1, source_target_pairs={{0,1},{1,0},{2,3},{3,2},{4,5},{5,4},{6,7},{7,6},{8,9},{9,8},{10,11... | collective-permute-start | bytes 22184 | tf_op jit(solution)/shard_map/ppermute | solution.py:425
  85.4 14.1 %collective-permute-start.21 = (f32[208,33]{1,0:T(8,128)S(1)}, f32[208,33]{1,0:T(8,128)S(1)}, u32[]{:S(2)}, u32[]{:S(2)}) collective-permute-start(f32[208,33]{1,0:T(8,128)S(1)} %shard_map.128), channel_id=1, source_target_pairs={{0,0},{8,1},{16,2},{24,3},{4,4},{12,5},{20,6},{28,7},{1,8},{9,9},{... | collective-permute-start | bytes 82376 | tf_op jit(solution)/shard_map/ppermute | solution.py:438
  90.0 11.7 %collective-permute-start.22 = (f32[208,33]{1,0:T(8,128)S(1)}, f32[208,33]{1,0:T(8,128)S(1)}, u32[]{:S(2)}, u32[]{:S(2)}) collective-permute-start(f32[208,33]{1,0:T(8,128)S(1)} %shard_map.128), channel_id=1, source_target_pairs={{4,0},{12,1},{20,2},{28,3},{0,4},{8,5},{16,6},{24,7},{5,8},{13,9},... | collective-permute-start | bytes 82376 | tf_op jit(solution)/shard_map/ppermute | solution.py:438
